TPU v7x, 128 devices: a whole 4x4x4 slice. The times are simulated.
128 devices in a mesh: row: 8 (over y, core), col: 16 (over z, x).
Axes of the slice: x: 4, y: 4, z: 4, core: 2. Of those that a mesh axis runs over, the one named last changes fastest.
Arguments:
- sigma_top: float32 [6144, 6144], P('row', 'col')
- factor_cross: float32 [6144, 6144], P('row', 'col'), may hold values from -0.078125 to 0.078125
- factor_inverse: float32 [6144, 6144], P('row', 'col')
- block_inverse: float32 [6144, 6144], P('row', 'col')
- ancestors: int32 [12], replicated, may hold values from 0 to 23, as said below
Outputs:
- sigma_cross: float32 [6144, 6144], P('row', 'col')
- sigma_child: float32 [6144, 6144], P('row', 'col')
Inputs may be any that keep to these rules, and one draw needn't show every extreme that they name: `ancestors`: 12 distinct block numbers; block 0 and block 23 are always among them.
All inputs are finite; a program needn't handle non-finite values.
Results may differ from a plain program's by a relative error of at most 0.000078.
Values sent between devices are 32-bit elements; how exact they have to be, the bound alone decides.
No kernel may reach another device: no remote copies, remote signals or barrier semaphores. Data moves between devices by JAX's collectives and lax.ppermute only.
A program may use at most 128 MiB of HBM per device.

v0:
```python
import jax
import jax.numpy as jnp
from jax import lax
from jax.sharding import PartitionSpec as P

BLK = 256


def transposed_rows(gathered, right_side):
    return lax.dot_general(
        gathered,
        right_side,
        (((0,), (0,)), ((), ())),
        precision=lax.Precision.HIGHEST,
        preferred_element_type=jnp.float32,
    )


def per_device(sigma_top, factor_cross, factor_inverse, block_inverse, ancestors):
    height = sigma_top.shape[0]
    first_row = lax.axis_index("row") * height
    blocks = (first_row + lax.iota(jnp.int32, height)) // BLK
    living = jnp.any(blocks[:, None] == ancestors[None, :], axis=1)
    masked = jnp.where(living[:, None], factor_cross, jnp.float32(0.0))
    inverse_strip = lax.all_gather(factor_inverse, "row", axis=0, tiled=True)
    rows_used = inverse_strip
    update = jnp.dot(
        lax.all_gather(masked, "col", axis=1, tiled=True),
        rows_used,
        precision=lax.Precision.HIGHEST,
        preferred_element_type=jnp.float32,
    )
    update_strip = lax.all_gather(update, "row", axis=0, tiled=True)
    rows_used = update_strip
    product = jnp.dot(
        lax.all_gather(sigma_top, "col", axis=1, tiled=True),
        rows_used,
        precision=lax.Precision.HIGHEST,
        preferred_element_type=jnp.float32,
    )
    sigma_cross = jnp.where(living[:, None], -product, jnp.float32(0.0))
    gathered = lax.all_gather(sigma_cross, "col", axis=1, tiled=True)
    correction = lax.psum_scatter(
        transposed_rows(gathered, update), "row", scatter_dimension=0, tiled=True
    )
    sigma_child = block_inverse - correction
    return (sigma_cross, sigma_child)


def solution(mesh):
    return jax.shard_map(
        per_device,
        mesh=mesh,
        in_specs=(P("row", "col"), P("row", "col"), P("row", "col"), P("row", "col"), P()),
        out_specs=(P("row", "col"), P("row", "col")),
        check_vma=False,
    )
```

profile of v0, /device:TPU:1, one launch (start us, length us, event | category | flops | bytes accessed | tf_op | source)
XLA Modules:
  0.0 643.4 jit_solution(8413906918570889155)
XLA Ops:
  7.2 0.0 all-gather.8.cloned.1.call-start
  7.2 0.7 all-gather.8.cloned.1.call-update
  7.9 0.0 all-gather.6.cloned.1.call-start
  8.0 0.7 compare_reduce_fusion
  8.7 2.5 broadcast_select_fusion
  11.2 0.0 all-gather.6.cloned.1.call-update
  11.2 0.0 all-gather.12.cloned.1.call-start
  11.2 0.7 all-gather.12.cloned.1.call-update
  11.9 0.0 all-gather.10.cloned.1.call-start
  12.0 55.5 %all-gather.8.cloned.1.call-done = f32[6144,384]{1,0:T(8,128)} async-done(((f32[768,384]{1,0:T(8,128)}), f32[6144,384]{1,0:T(8,128)}) %all-gather.8.cloned.1.call-update) | async-done | bytes 9437200 | tf_op jit(solution)/shard_map/all_gather | solution.py:25
  67.5 124.8 %all-gather.6.cloned.1.call-done = f32[768,6144]{1,0:T(8,128)} async-done(((f32[768,384]{1,0:T(8,128)}), f32[768,6144]{1,0:T(8,128)}) %all-gather.6.cloned.1.call-update) | async-done | bytes 18874384 | tf_op jit(solution)/shard_map/all_gather | solution.py:28
  192.3 34.1 %fusion.5 = f32[768,384]{1,0:T(8,128)} fusion(f32[768,6144]{1,0:T(8,128)} %all-gather.6.cloned.1.call-done, f32[6144,384]{1,0:T(8,128)} %all-gather.8.cloned.1.call-done), kind=kOutput, calls=%fused_computation.14 | convolution fusion | flops 21743271936 | bytes 29491200 | tf_op jit(solution)/shard_map/dot_general | solution.py:27
  226.4 0.0 all-gather.10.cloned.1.call-update
  226.4 0.0 copy-start
  226.4 0.2 all-gather.14.cloned.1.call-start
  226.6 89.7 %all-gather.12.cloned.1.call-done = f32[768,6144]{1,0:T(8,128)} async-done(((f32[768,384]{1,0:T(8,128)}), f32[768,6144]{1,0:T(8,128)}) %all-gather.12.cloned.1.call-update) | async-done | bytes 18874384 | tf_op jit(solution)/shard_map/all_gather | solution.py:36
  316.3 56.3 %all-gather.10.cloned.1.call-done = f32[6144,384]{1,0:T(8,128)} async-done(((f32[768,384]{1,0:T(8,128)}), f32[6144,384]{1,0:T(8,128)}) %all-gather.10.cloned.1.call-update) | async-done | bytes 9437200 | tf_op jit(solution)/shard_map/all_gather | solution.py:33
  372.6 48.7 %fusion.1 = f32[768,384]{0,1:T(8,128)} fusion(f32[6144,384]{1,0:T(8,128)} %all-gather.10.cloned.1.call-done, f32[768,6144]{1,0:T(8,128)} %all-gather.12.cloned.1.call-done, pred[768]{0:T(1024)(128)(4,1)S(1)} %compare_reduce_fusion), kind=kOutput, calls=%fused_computation.2 | convolution fusion | flops 21743861760 | bytes 29491968 | tf_op jit(solution)/shard_map/dot_general | solution.py:35
  421.3 0.0 all-gather.14.cloned.1.call-update
  421.3 0.3 reduce-scatter.2.cloned.1.call-start
  421.6 121.8 %all-gather.14.cloned.1.call-done = f32[768,6144]{0,1:T(8,128)} async-done(((f32[768,384]{0,1:T(8,128)}), f32[768,6144]{0,1:T(8,128)}) %all-gather.14.cloned.1.call-update) | async-done | bytes 18874384 | tf_op jit(solution)/shard_map/all_gather | solution.py:42
  543.4 0.0 copy-done
  543.4 34.0 %fusion.6 = f32[6144,384]{1,0:T(8,128)} fusion(f32[768,6144]{0,1:T(8,128)} %all-gather.14.cloned.1.call-done, f32[768,384]{1,0:T(8,128)S(1)} %copy-done), kind=kOutput, calls=%fused_computation.15 | convolution fusion | flops 21743271936 | bytes 29491200 | tf_op jit(solution)/shard_map/dot_general | solution.py:10
  577.5 0.0 copy-start.1
  577.5 0.0 copy-start.2
  577.5 0.0 reduce-scatter.2.cloned.1.call-update
  577.5 1.2 copy-done.1
  578.8 1.4 copy.8
  580.2 54.0 %reduce-scatter.2.cloned.1.call-done = f32[768,384]{1,0:T(8,128)} async-done(((f32[6144,384]{1,0:T(8,128)}), f32[768,384]{1,0:T(8,128)}) %reduce-scatter.2.cloned.1.call-update) | async-done | bytes 1179664 | tf_op jit(solution)/shard_map/reduce_scatter | solution.py:43
  634.2 0.0 copy-done.2
  634.2 2.4 sub.10
  (1 shorter events, 0.0 us)
Async XLA Ops:
  7.2 60.3 %all-gather.8.cloned.1.call-start = ((), (), s32[]{:S(2)}) async-start(), calls=%async_computation.2 | async-start | bytes 10616832 | tf_op jit(solution)/shard_map/all_gather | solution.py:25
  7.9 184.4 %all-gather.6.cloned.1.call-start = ((), (), s32[]{:S(2)}) async-start(), calls=%async_computation.1 | async-start | bytes 20054016 | tf_op jit(solution)/shard_map/all_gather | solution.py:28
  11.2 305.1 %all-gather.12.cloned.1.call-start = ((), (), s32[]{:S(2)}) async-start(), calls=%async_computation.4 | async-start | bytes 20054016 | tf_op jit(solution)/shard_map/all_gather | solution.py:36
  11.9 360.6 %all-gather.10.cloned.1.call-start = ((), (), s32[]{:S(2)}) async-start(), calls=%async_computation.3 | async-start | bytes 10616832 | tf_op jit(solution)/shard_map/all_gather | solution.py:33
  226.4 317.1 %copy-start = (f32[768,384]{1,0:T(8,128)S(1)}, f32[768,384]{1,0:T(8,128)}, u32[]{:S(2)}) copy-start(f32[768,384]{1,0:T(8,128)} %fusion.5) | copy-start | bytes 3538948
  226.4 317.0 %all-gather.14.cloned.1.call-start = ((), (), s32[]{:S(2)}) async-start(), calls=%async_computation.5 | async-start | bytes 20054016 | tf_op jit(solution)/shard_map/all_gather | solution.py:42
  421.3 212.8 %reduce-scatter.2.cloned.1.call-start = ((), (), s32[]{:S(2)}) async-start(), calls=%async_computation.6 | async-start | bytes 10616832 | tf_op jit(solution)/shard_map/reduce_scatter | solution.py:43
  577.5 1.3 copy-start.1
  577.5 56.7 %copy-start.2 = (f32[768,384]{1,0:T(8,128)S(1)}, f32[768,384]{1,0:T(8,128)}, u32[]{:S(2)}) copy-start(f32[768,384]{1,0:T(8,128)} %param.8) | copy-start | bytes 3538948
Sparse Core Ops, SparseCore 0:
  9.7 57.7 all-gather.7
  70.3 121.9 all-gather.5
  194.5 121.7 all-gather.11
  318.4 54.1 all-gather.9
  421.5 121.9 all-gather.13
  577.6 56.4 reduce-scatter.1
where the time goes:
time: 644 us; the launch traced here: 643 us
  waiting for transfers between devices  504 us (78%)
  matrix products  117 us (18%)
  between operations  14.1 us (2%)
    all_gather x1, waiting for transfers between devices, per_device(): lax.all_gather(masked, 'col', axis=1, tiled=True)  125 us
    all_gather x1, waiting for transfers between devices, per_device(): gathered = lax.all_gather(sigma_cross, 'col', axis=1, tiled=True)  122 us
    all_gather x1, waiting for transfers between devices, per_device(): lax.all_gather(sigma_top, 'col', axis=1, tiled=True)  89.7 us
    all_gather x1, waiting for transfers between devices, per_device(): update_strip = lax.all_gather(update, 'row', axis=0, tiled=True)  56.3 us
    all_gather x1, waiting for transfers between devices, per_device(): inverse_strip = lax.all_gather(factor_inverse, 'row', axis=0, tiled=True)  55.5 us
    reduce_scatter x1, waiting for transfers between devices, per_device(): lax.psum_scatter(transposed_rows(gathered, update), 'row', scatter_dimens...  54 us
    dot_general x1, matrix products, per_device(): jnp.dot(lax.all_gather(sigma_top, 'col', axis=1, tiled=True), rows_used,...  48.7 us
    dot_general x1, matrix products, per_device(): jnp.dot(lax.all_gather(masked, 'col', axis=1, tiled=True), rows_used, pre...  34.1 us
  transfers between devices with their start and end apart: 6, of which 6 were waited for; matrix products, arithmetic and copies ran while one was open for 6% of the time, Pallas kernels for 0%

commit v1 on v0

v1 whole, which is shorter than its diff:
```python
import jax
import jax.numpy as jnp
import numpy as np
from jax import lax
from jax.sharding import Mesh, PartitionSpec as P

NB = 24
NANC = 12
ROW = ("y", "core")
COL = ("z", "x")
ALL = ("y", "core", "z", "x")


def shift(x, axis, n, k):
    return lax.ppermute(x, axis, [(i, (i + k) % n) for i in range(n)])


def gather_rows(x):
    y, core = lax.axis_index("y"), lax.axis_index("core")
    half = x.shape[0] // 2
    left = shift(x, "y", 4, 1)
    right = shift(x, "y", 4, -1)
    far = jnp.concatenate([shift(left[:half], "y", 4, 1), shift(right[half:], "y", 4, -1)])
    mine = [x, left, right, far]
    at = [y, (y + 3) % 4, (y + 1) % 4, (y + 2) % 4]
    out = [(2 * a + core, t) for a, t in zip(at, mine)]
    out += [(2 * a + 1 - core, shift(t, "core", 2, 1)) for a, t in zip(at, mine)]
    return out


def spread(x):
    h, w = x.shape
    sub = h // 24
    return lax.all_to_all(x.reshape(3, 8, sub, w), ROW, 1, 0, tiled=True).reshape(NB, sub, w)


def pick(x, ancestors):
    return jnp.concatenate([lax.dynamic_slice_in_dim(x, ancestors[i], 1, 0) for i in range(NANC)])


def dot(a, b, dims):
    return lax.dot_general(a, b, (dims, ((), ())), precision=lax.Precision.HIGH, preferred_element_type=jnp.float32)


def per_device(sigma_top, factor_cross, factor_inverse, block_inverse, ancestors):
    h, w = sigma_top.shape
    sub = h // 24
    part = NANC * sub

    f = pick(spread(factor_cross), ancestors).reshape(part, w)
    f_all = lax.all_gather(f, COL, axis=1, tiled=True)
    strip = jnp.zeros((8 * h, w), jnp.float32)
    for r, t in gather_rows(factor_inverse):
        strip = lax.dynamic_update_slice(strip, t, (r * h, 0))
    s = pick(spread(sigma_top), ancestors).reshape(part, w)
    s_all = lax.all_gather(s, COL, axis=1, tiled=True)

    u = dot(f_all, strip, ((1,), (0,)))

    moved = lax.ppermute(u, ALL, [(16 * r + c, 16 * (c // 2) + 2 * r + c % 2) for r in range(8) for c in range(16)])
    u_side = lax.all_gather(moved, COL, axis=0, tiled=False).reshape(8, 2, part, w)

    u_col = jnp.zeros((NANC, 8, sub, w), jnp.float32)
    for r, t in gather_rows(u):
        u_col = lax.dynamic_update_slice(u_col, t.reshape(NANC, 1, sub, w), (0, r, 0, 0))
    s_sel = jnp.concatenate(
        [lax.dynamic_slice_in_dim(s_all, ancestors[i] * 8 * sub, 8 * sub, 1) for i in range(NANC)], axis=1
    )
    sigma = -dot(s_sel, u_col.reshape(8 * part, w), ((1,), (0,)))

    sigma_col = jnp.zeros((8, part, w), jnp.float32)
    for r, t in gather_rows(sigma):
        sigma_col = lax.dynamic_update_slice(sigma_col, t[None], (r, 0, 0))
    correction = jnp.concatenate([dot(u_side[:, p], sigma_col, ((0, 1), (0, 1))) for p in range(2)])
    sigma_child = block_inverse - correction

    blocks = sigma.reshape(NANC, sub, w)
    hit = ancestors[None, :] == lax.iota(jnp.int32, NB)[:, None]
    place = jnp.argmax(hit, axis=1)
    living = jnp.any(hit, axis=1)
    full = jnp.concatenate([lax.dynamic_slice_in_dim(blocks, place[b], 1, 0) for b in range(NB)])
    full = jnp.where(living[:, None, None], full, jnp.float32(0.0))
    back = lax.all_to_all(full.reshape(8, 3, sub, w), ROW, 0, 0, tiled=True)
    sigma_cross = back.reshape(8, 3, sub, w).transpose(1, 0, 2, 3).reshape(h, w)
    return (sigma_cross, sigma_child)


def solution(mesh):
    fine = Mesh(np.asarray(mesh.devices).reshape(4, 2, 4, 4), ALL)
    tile = P(ROW, COL)
    return jax.shard_map(
        per_device,
        mesh=fine,
        in_specs=(tile, tile, tile, tile, P()),
        out_specs=(tile, tile),
        check_vma=False,
    )
```

time: 644 us -> 345 us (0.54)
  waiting for transfers between devices: 504 us -> 102 us
  matrix products: 117 us -> 30.6 us
  between operations: 14.1 us -> 89 us
  starting transfers between devices: 0.64 us -> 62.1 us
  local copies, waits for them, and re-layouts: 2.64 us -> 56.3 us
    all_gather x5 -> x3, waiting for transfers between devices: 448 us -> 11.1 us  [the longest x1 11.1 us: per_device(): f_all = lax.all_gather(f, COL, axis=1, tiled=True)]
    dot_general x3 -> x4, matrix products: 117 us -> 30.6 us  [dot(): lax.dot_general(a, b, (dims, ((), ())), precision=lax.Precision.HIGH, pre...]
    ppermute x0 -> x25, waiting for transfers between devices: none -> 75.6 us  [the longest x24 61.1 us: shift(): return lax.ppermute(x, axis, [(i, (i + k) % n) for i in range(n)])]
    reduce_scatter x1 -> x0, waiting for transfers between devices: 54 us -> none  [per_device(): lax.psum_scatter(transposed_rows(gathered, update), 'row', scatter_dimens...]
    ppermute x0 -> x25, starting transfers between devices: none -> 48.2 us  [the longest x24 43.1 us: shift(): return lax.ppermute(x, axis, [(i, (i + k) % n) for i in range(n)])]
    dynamic_update_slice x0 -> x23, local copies, waits for them, and re-layouts: none -> 26.2 us  [the longest x8 15.4 us: per_device(): strip = lax.dynamic_update_slice(strip, t, (r * h, 0))]
    all_to_all x0 -> x3, waiting for transfers between devices: none -> 15.4 us  [the longest x2 15.4 us: spread(): lax.all_to_all(x.reshape(3, 8, sub, w), ROW, 1, 0, tiled=True)]
    all_to_all x0 -> x3, starting transfers between devices: none -> 13.8 us  [the longest x2 10.3 us: spread(): lax.all_to_all(x.reshape(3, 8, sub, w), ROW, 1, 0, tiled=True)]
  transfers between devices with their start and end apart: 6 -> 31, of which waited for: 6 -> 10; matrix products, arithmetic and copies ran while one was open for 6% -> 20% of each run, Pallas kernels for 0% -> 0%
where the time goes in v1:
time: 345 us; the launch traced here: 343 us
  waiting for transfers between devices  102 us (30%)
  between operations  89 us (26%)
  starting transfers between devices  62.1 us (18%)
  local copies, waits for them, and re-layouts  56.3 us (16%)
  matrix products  30.6 us (9%)
    ppermute x24, waiting for transfers between devices, shift(): return lax.ppermute(x, axis, [(i, (i + k) % n) for i in range(n)])  61.1 us
    ppermute x24, starting transfers between devices, shift(): return lax.ppermute(x, axis, [(i, (i + k) % n) for i in range(n)])  43.1 us
    dot_general x4, matrix products, dot(): lax.dot_general(a, b, (dims, ((), ())), precision=lax.Precision.HIGH, pre...  30.6 us
    dynamic_update_slice x8, local copies, waits for them, and re-layouts, per_device(): strip = lax.dynamic_update_slice(strip, t, (r * h, 0))  15.4 us
    all_to_all x2, waiting for transfers between devices, spread(): lax.all_to_all(x.reshape(3, 8, sub, w), ROW, 1, 0, tiled=True)  15.4 us
    unnamed x72, local copies, waits for them, and re-layouts  14.6 us
    ppermute x1, waiting for transfers between devices, per_device(): lax.ppermute(u, ALL, [(16 * r + c, 16 * (c // 2) + 2 * r + c % 2) for r i...  14.5 us
    all_gather x1, waiting for transfers between devices, per_device(): f_all = lax.all_gather(f, COL, axis=1, tiled=True)  11.1 us
  transfers between devices with their start and end apart: 31, of which 10 were waited for; matrix products, arithmetic and copies ran while one was open for 20% of the time, Pallas kernels for 0%

profile of v1, /device:TPU:1, one launch (start us, length us, event | category | flops | bytes accessed | tf_op | source)
XLA Modules:
  0.0 343.1 jit_solution(14482909959101323158)
XLA Ops:
  7.2 2.5 copy.63
  9.6 6.0 %all-to-all-start.1 = ((f32[3,8,32,384]{3,2,0,1:T(8,128)}), f32[3,8,32,384]{3,2,0,1:T(8,128)S(1)}, u32[]{:S(2)}, u32[]{:S(2)}) async-start(f32[3,8,32,384]{3,2,0,1:T(8,128)} %copy.63), calls=%async_computation.1 | async-start | bytes 2359296 | tf_op jit(solution)/shard_map/all_to_all | solution.py:34
  15.6 1.1 copy.62
  16.7 15.4 %all-to-all-done.1 = f32[3,8,32,384]{3,2,0,1:T(8,128)S(1)} async-done(((f32[3,8,32,384]{3,2,0,1:T(8,128)}), f32[3,8,32,384]{3,2,0,1:T(8,128)S(1)}, u32[]{:S(2)}, u32[]{:S(2)}) %all-to-all-start.1) | async-done | bytes 1179680 | tf_op jit(solution)/shard_map/all_to_all | solution.py:34
  32.1 4.3 %all-to-all-start = ((f32[3,8,32,384]{3,2,0,1:T(8,128)}), f32[3,8,32,384]{3,2,0,1:T(8,128)S(1)}, u32[]{:S(2)}, u32[]{:S(2)}) async-start(f32[3,8,32,384]{3,2,0,1:T(8,128)} %copy.62), calls=%async_computation | async-start | bytes 2359296 | tf_op jit(solution)/shard_map/all_to_all | solution.py:34
  61.3 1.5 collective-permute-start
  62.8 1.3 collective-permute-start.1
  64.1 26.1 %collective-permute-done = f32[768,384]{1,0:T(8,128)S(1)} collective-permute-done((f32[768,384]{1,0:T(8,128)}, f32[768,384]{1,0:T(8,128)S(1)}, u32[]{:S(2)}, u32[]{:S(2)}) %collective-permute-start) | collective-permute-done | bytes 1179680 | tf_op jit(solution)/shard_map/ppermute | solution.py:15
  90.4 2.7 collective-permute-start.3
  93.1 1.5 collective-permute-start.4
  95.2 10.4 %collective-permute-done.2 = f32[384,384]{1,0:T(8,128)S(1)} collective-permute-done((f32[384,384]{1,0:T(8,128)S(1)}, f32[384,384]{1,0:T(8,128)S(1)}, u32[]{:S(2)}, u32[]{:S(2)}) %collective-permute-start.2) | collective-permute-done | bytes 589856 | tf_op jit(solution)/shard_map/ppermute | solution.py:15
  105.6 1.8 collective-permute-start.7
  107.5 4.3 %broadcast_in_dim.53 = f32[6144,384]{1,0:T(8,128)} broadcast(f32[]{:T(128)} %constant.74.clone.1), dimensions={} | broadcast | bytes 9437188 | tf_op jit(solution)/shard_map/broadcast_in_dim | solution.py:52
  111.8 2.4 constant_dynamic-update-slice_fusion.69
  114.1 1.1 constant_dynamic-update-slice_fusion.68
  115.2 1.1 constant_dynamic-update-slice_fusion.67
  116.4 1.2 constant_dynamic-update-slice_fusion.66
  117.5 2.4 constant_dynamic-update-slice_fusion.65
  120.0 2.4 constant_dynamic-update-slice_fusion.64
  122.4 2.4 constant_dynamic-update-slice_fusion.63
  124.8 2.4 constant_dynamic-update-slice_fusion.62
  127.2 11.1 %all-gather.7.cloned.1.call-done = f32[384,6144]{1,0:T(8,128)} async-done(((f32[384,384]{1,0:T(8,128)}), f32[384,6144]{1,0:T(8,128)}) %all-gather.7.cloned.1.call-update) | async-done | bytes 9437200 | tf_op jit(solution)/shard_map/all_gather | solution.py:51
  138.3 11.7 %fusion.8 = f32[384,384]{1,0:T(8,128)S(1)} fusion(f32[384,6144]{1,0:T(8,128)} %all-gather.7.cloned.1.call-done, f32[6144,384]{1,0:T(8,128)} %constant_dynamic-update-slice_fusion.62), kind=kOutput, calls=%fused_computation.105 | convolution fusion | flops 5435817984 | bytes 19464192 | tf_op jit(solution)/shard_map/dot_general | solution.py:42
  150.0 5.2 %collective-permute-start.16 = (f32[384,384]{1,0:T(8,128)S(1)}, f32[384,384]{1,0:T(8,128)S(1)}, u32[]{:S(2)}, u32[]{:S(2)}) collective-permute-start(f32[384,384]{1,0:T(8,128)S(1)} %fusion.8), channel_id=1, source_target_pairs={{0,0},{1,1},{2,16},{3,17},{4,32},{5,33},{6,48},{7,49},{8,64},{9,65... | collective-permute-start | bytes 1769480 | tf_op jit(solution)/shard_map/ppermute | solution.py:60
  155.2 14.5 %collective-permute-done.16 = f32[384,384]{1,0:T(8,128)S(1)} collective-permute-done((f32[384,384]{1,0:T(8,128)S(1)}, f32[384,384]{1,0:T(8,128)S(1)}, u32[]{:S(2)}, u32[]{:S(2)}) %collective-permute-start.16) | collective-permute-done | bytes 589856 | tf_op jit(solution)/shard_map/ppermute | solution.py:60
  225.2 4.2 %collective-permute-start.8 = (f32[384,384]{1,0:T(8,128)S(1)}, f32[384,384]{1,0:T(8,128)S(1)}, u32[]{:S(2)}, u32[]{:S(2)}) collective-permute-start(f32[384,384]{1,0:T(8,128)S(1)} %fusion.8), channel_id=1, source_target_pairs={{0,32},{32,64},{64,96},{96,0},{1,33},{33,65},{65,97},{97,1},{2,34}... | collective-permute-start | bytes 1769480 | tf_op jit(solution)/shard_map/ppermute | solution.py:15
  229.4 4.4 %collective-permute-start.9 = (f32[384,384]{1,0:T(8,128)S(1)}, f32[384,384]{1,0:T(8,128)S(1)}, u32[]{:S(2)}, u32[]{:S(2)}) collective-permute-start(f32[384,384]{1,0:T(8,128)S(1)} %fusion.8), channel_id=1, source_target_pairs={{0,96},{32,0},{64,32},{96,64},{1,97},{33,1},{65,33},{97,65},{2,98}... | collective-permute-start | bytes 1769480 | tf_op jit(solution)/shard_map/ppermute | solution.py:15
  233.8 9.4 %collective-permute-start.12 = (f32[384,384]{1,0:T(8,128)S(1)}, f32[384,384]{1,0:T(8,128)S(1)}, u32[]{:S(2)}, u32[]{:S(2)}) collective-permute-start(f32[384,384]{1,0:T(8,128)S(1)} %fusion.8), channel_id=1, source_target_pairs={{0,16},{16,0},{1,17},{17,1},{2,18},{18,2},{3,19},{19,3},{4,20},{20... | collective-permute-start | bytes 1769480 | tf_op jit(solution)/shard_map/ppermute | solution.py:15
  243.1 1.0 dynamic-slice_dynamic-update-slice_fusion.11
  244.2 1.0 dynamic-slice_dynamic-update-slice_fusion.10
  245.2 1.0 dynamic-slice_dynamic-update-slice_fusion.9
  246.3 1.0 dynamic-slice_dynamic-update-slice_fusion.8
  247.3 1.0 dynamic-slice_dynamic-update-slice_fusion.7
  248.4 1.0 dynamic-slice_dynamic-update-slice_fusion.6
  249.4 1.0 dynamic-slice_dynamic-update-slice_fusion.5
  250.5 1.0 dynamic-slice_dynamic-update-slice_fusion.4
  251.5 1.1 dynamic-slice_dynamic-update-slice_fusion.3
  252.6 1.1 dynamic-slice_dynamic-update-slice_fusion.2
  254.4 1.0 dynamic-slice_dynamic-update-slice_fusion.1
  255.5 2.7 collective-permute-start.11
  258.3 1.0 dynamic-slice_dynamic-update-slice_fusion
  260.1 4.4 %collective-permute-done.10 = f32[192,384]{1,0:T(8,128)S(1)} collective-permute-done((f32[192,384]{1,0:T(8,128)S(1)}, f32[192,384]{1,0:T(8,128)S(1)}, u32[]{:S(2)}, u32[]{:S(2)}) %collective-permute-start.10) | collective-permute-done | bytes 294944 | tf_op jit(solution)/shard_map/ppermute | solution.py:15
  264.5 1.1 collective-permute-start.15
  265.9 1.3 collective-permute-done.15
  267.3 2.5 broadcast_in_dim.55
  269.8 5.0 %bitcast_dynamic-update-slice_fusion.7 = (f32[8,384,384]{2,1,0:T(8,128)}, f32[384,384]{1,0:T(8,128)S(1)}) fusion(f32[8,384,384]{2,1,0:T(8,128)} %broadcast_in_dim.55, s32[]{:T(128)S(6)} %select_n.283, f32[384,3072]{1,0:T(8,128)S(1)} %dynamic-slice_dynamic-update-slice_fusion, f32[3072,384]{1,0:T(8,128)S(1)} %bitcast.119), kind=kOutput, calls=%fused_computation.15 | convolution fusion | flops 2718056448 | bytes 10616836 | tf_op jit(solution)/shard_map/dot_general | solution.py:42
  275.4 2.9 collective-permute-start.18
  279.4 1.2 broadcast_select_fusion
  280.5 3.5 %all-to-all-start.2 = ((f32[8,3,32,384]{3,2,1,0:T(8,128)}), f32[8,3,32,384]{3,2,1,0:T(8,128)S(1)}, u32[]{:S(2)}, u32[]{:S(2)}) async-start(f32[8,3,32,384]{3,2,1,0:T(8,128)} %broadcast_select_fusion), calls=%async_computation.2 | async-start | bytes 2359296 | tf_op jit(solution)/shard_map/all_to_all | solution.py:83
  284.0 7.7 %collective-permute-done.17 = f32[384,384]{1,0:T(8,128)S(1)} collective-permute-done((f32[384,384]{1,0:T(8,128)S(1)}, f32[384,384]{1,0:T(8,128)S(1)}, u32[]{:S(2)}, u32[]{:S(2)}) %collective-permute-start.17) | collective-permute-done | bytes 589856 | tf_op jit(solution)/shard_map/ppermute | solution.py:15
  292.0 3.7 %collective-permute-start.20 = (f32[192,384]{1,0:T(8,128)S(1)}, f32[192,384]{1,0:T(8,128)S(1)}, u32[]{:S(2)}, u32[]{:S(2)}) collective-permute-start(f32[192,384]{1,0:T(8,128)S(1)} %slice.206), channel_id=1, source_target_pairs={{0,96},{32,0},{64,32},{96,64},{1,97},{33,1},{65,33},{97,65},{2,98}... | collective-permute-start | bytes 884744 | tf_op jit(solution)/shard_map/ppermute | solution.py:15
  295.8 2.2 collective-permute-start.22
  297.9 0.9 bitcast_dynamic-update-slice_fusion.6
  299.6 11.1 %collective-permute-done.19 = f32[192,384]{1,0:T(8,128)S(1)} collective-permute-done((f32[192,384]{1,0:T(8,128)S(1)}, f32[192,384]{1,0:T(8,128)S(1)}, u32[]{:S(2)}, u32[]{:S(2)}) %collective-permute-start.19) | collective-permute-done | bytes 294944 | tf_op jit(solution)/shard_map/ppermute | solution.py:15
  310.8 1.1 collective-permute-start.24
  311.8 0.9 bitcast_dynamic-update-slice_fusion.4
  312.7 1.9 bitcast_dynamic-update-slice_fusion.3
  314.6 1.1 copy.72
  315.7 1.9 bitcast_dynamic-update-slice_fusion.2
  317.6 1.9 bitcast_dynamic-update-slice_fusion.1
  319.6 1.9 bitcast_dynamic-update-slice_fusion
  321.5 7.8 %fusion.2 = f32[384,384]{1,0:T(8,128)S(1)} fusion(f32[8,384,384]{2,1,0:T(8,128)} %bitcast_dynamic-update-slice_fusion, f32[8,2,384,384]{3,2,1,0:T(8,128)} %bitcast.120), kind=kOutput, calls=%fused_computation.4 | convolution fusion | flops 2717908992 | bytes 10027008 | tf_op jit(solution)/shard_map/dot_general | solution.py:42
  329.3 6.1 %fusion.3 = f32[384,384]{1,0:T(8,128)S(1)} fusion(f32[8,384,384]{2,1,0:T(8,128)} %bitcast_dynamic-update-slice_fusion, f32[8,2,384,384]{3,2,1,0:T(8,128)S(1)} %bitcast.121), kind=kOutput, calls=%fused_computation.5 | convolution fusion | flops 2717908992 | bytes 10027008 | tf_op jit(solution)/shard_map/dot_general | solution.py:42
  335.4 1.1 maximum_subtract_fusion
  (127 shorter events, 11.1 us)
Async XLA Ops:
  7.2 8.4 %copy-start.2 = (f32[768,384]{1,0:T(8,128)S(1)}, f32[768,384]{1,0:T(8,128)}, u32[]{:S(2)}) copy-start(f32[768,384]{1,0:T(8,128)} %param.5) | copy-start | bytes 3538948
  7.2 29.3 %copy-start.6 = (s32[12]{0:T(128)S(1)}, s32[12]{0:T(128)}, u32[]{:S(2)}) copy-start(s32[12]{0:T(128)} %param.9) | copy-start | bytes 148
  9.6 22.5 %all-to-all-start.1 = ((f32[3,8,32,384]{3,2,0,1:T(8,128)}), f32[3,8,32,384]{3,2,0,1:T(8,128)S(1)}, u32[]{:S(2)}, u32[]{:S(2)}) async-start(f32[3,8,32,384]{3,2,0,1:T(8,128)} %copy.63), calls=%async_computation.1 | async-start | bytes 2359296 | tf_op jit(solution)/shard_map/all_to_all | solution.py:34
  32.1 26.9 %all-to-all-start = ((f32[3,8,32,384]{3,2,0,1:T(8,128)}), f32[3,8,32,384]{3,2,0,1:T(8,128)S(1)}, u32[]{:S(2)}, u32[]{:S(2)}) async-start(f32[3,8,32,384]{3,2,0,1:T(8,128)} %copy.62), calls=%async_computation | async-start | bytes 2359296 | tf_op jit(solution)/shard_map/all_to_all | solution.py:34
  36.5 101.8 %all-gather.7.cloned.1.call-start = ((), (), s32[]{:S(2)}) async-start(), calls=%async_computation.4 | async-start | bytes 10027008 | tf_op jit(solution)/shard_map/all_gather | solution.py:51
  59.3 0.8 copy-start.4
  60.2 183.0 %all-gather.5.cloned.1.call-start = ((), (), s32[]{:S(2)}) async-start(), calls=%async_computation.3 | async-start | bytes 10027008 | tf_op jit(solution)/shard_map/all_gather | solution.py:56
  60.4 0.8 copy-start.3
  61.3 260.2 %all-gather.9.cloned.1.call-start = ((), (), s32[]{:S(2)}) async-start(), calls=%async_computation.5 | async-start | bytes 10027008 | tf_op jit(solution)/shard_map/all_gather | solution.py:61
  61.3 28.9 %collective-permute-start = (f32[768,384]{1,0:T(8,128)}, f32[768,384]{1,0:T(8,128)S(1)}, u32[]{:S(2)}, u32[]{:S(2)}) collective-permute-start(f32[768,384]{1,0:T(8,128)} %param.7), channel_id=1, source_target_pairs={{0,32},{32,64},{64,96},{96,0},{1,33},{33,65},{65,97},{97,1},{2,34}... | collective-permute-start | bytes 3538952 | tf_op jit(solution)/shard_map/ppermute | solution.py:15
  62.8 27.6 %collective-permute-start.1 = (f32[768,384]{1,0:T(8,128)}, f32[768,384]{1,0:T(8,128)S(1)}, u32[]{:S(2)}, u32[]{:S(2)}) collective-permute-start(f32[768,384]{1,0:T(8,128)} %param.7), channel_id=1, source_target_pairs={{0,96},{32,0},{64,32},{96,64},{1,97},{33,1},{65,33},{97,65},{2,98}... | collective-permute-start | bytes 3538952 | tf_op jit(solution)/shard_map/ppermute | solution.py:15
  90.3 15.3 %collective-permute-start.2 = (f32[384,384]{1,0:T(8,128)S(1)}, f32[384,384]{1,0:T(8,128)S(1)}, u32[]{:S(2)}, u32[]{:S(2)}) collective-permute-start(f32[384,384]{1,0:T(8,128)S(1)} %slice.200), channel_id=1, source_target_pairs={{0,32},{32,64},{64,96},{96,0},{1,33},{33,65},{65,97},{97,1},{2,34}... | collective-permute-start | bytes 1769480 | tf_op jit(solution)/shard_map/ppermute | solution.py:15
  90.4 15.2 %collective-permute-start.3 = (f32[384,384]{1,0:T(8,128)S(1)}, f32[384,384]{1,0:T(8,128)S(1)}, u32[]{:S(2)}, u32[]{:S(2)}) collective-permute-start(f32[384,384]{1,0:T(8,128)S(1)} %slice.201), channel_id=1, source_target_pairs={{0,96},{32,0},{64,32},{96,64},{1,97},{33,1},{65,33},{97,65},{2,98}... | collective-permute-start | bytes 1769480 | tf_op jit(solution)/shard_map/ppermute | solution.py:15
  93.1 24.4 %collective-permute-start.4 = (f32[768,384]{1,0:T(8,128)}, f32[768,384]{1,0:T(8,128)}, u32[]{:S(2)}, u32[]{:S(2)}) collective-permute-start(f32[768,384]{1,0:T(8,128)} %param.7), channel_id=1, source_target_pairs={{0,16},{16,0},{1,17},{17,1},{2,18},{18,2},{3,19},{19,3},{4,20},{20... | collective-permute-start | bytes 3538952 | tf_op jit(solution)/shard_map/ppermute | solution.py:15
  94.7 25.3 %collective-permute-start.5 = (f32[768,384]{1,0:T(8,128)S(1)}, f32[768,384]{1,0:T(8,128)}, u32[]{:S(2)}, u32[]{:S(2)}) collective-permute-start(f32[768,384]{1,0:T(8,128)S(1)} %collective-permute-done), channel_id=1, source_target_pairs={{0,16},{16,0},{1,17},{17,1},{2,18},{18,2},{3,19},{19,3},{4,20},{20... | collective-permute-start | bytes 3538952 | tf_op jit(solution)/shard_map/ppermute | solution.py:15
  94.7 27.7 %collective-permute-start.6 = (f32[768,384]{1,0:T(8,128)S(1)}, f32[768,384]{1,0:T(8,128)}, u32[]{:S(2)}, u32[]{:S(2)}) collective-permute-start(f32[768,384]{1,0:T(8,128)S(1)} %collective-permute-done.1), channel_id=1, source_target_pairs={{0,16},{16,0},{1,17},{17,1},{2,18},{18,2},{3,19},{19,3},{4,20},{20... | collective-permute-start | bytes 3538952 | tf_op jit(solution)/shard_map/ppermute | solution.py:15
  105.6 19.2 %collective-permute-start.7 = (f32[768,384]{1,0:T(8,128)S(1)}, f32[768,384]{1,0:T(8,128)}, u32[]{:S(2)}, u32[]{:S(2)}) collective-permute-start(f32[768,384]{1,0:T(8,128)S(1)} %constant_dynamic-update-slice_fusion.24), channel_id=1, source_target_pairs={{0,16},{16,0},{1,17},{17,1},{2,18},{18,2},{3,19},{19,3},{4,20},{20... | collective-permute-start | bytes 3538952 | tf_op jit(solution)/shard_map/ppermute | solution.py:15
  150.0 19.7 %collective-permute-start.16 = (f32[384,384]{1,0:T(8,128)S(1)}, f32[384,384]{1,0:T(8,128)S(1)}, u32[]{:S(2)}, u32[]{:S(2)}) collective-permute-start(f32[384,384]{1,0:T(8,128)S(1)} %fusion.8), channel_id=1, source_target_pairs={{0,0},{1,1},{2,16},{3,17},{4,32},{5,33},{6,48},{7,49},{8,64},{9,65... | collective-permute-start | bytes 1769480 | tf_op jit(solution)/shard_map/ppermute | solution.py:60
  169.6 0.8 copy-start.5
  225.2 29.1 %collective-permute-start.8 = (f32[384,384]{1,0:T(8,128)S(1)}, f32[384,384]{1,0:T(8,128)S(1)}, u32[]{:S(2)}, u32[]{:S(2)}) collective-permute-start(f32[384,384]{1,0:T(8,128)S(1)} %fusion.8), channel_id=1, source_target_pairs={{0,32},{32,64},{64,96},{96,0},{1,33},{33,65},{65,97},{97,1},{2,34}... | collective-permute-start | bytes 1769480 | tf_op jit(solution)/shard_map/ppermute | solution.py:15
  229.4 26.1 %collective-permute-start.9 = (f32[384,384]{1,0:T(8,128)S(1)}, f32[384,384]{1,0:T(8,128)S(1)}, u32[]{:S(2)}, u32[]{:S(2)}) collective-permute-start(f32[384,384]{1,0:T(8,128)S(1)} %fusion.8), channel_id=1, source_target_pairs={{0,96},{32,0},{64,32},{96,64},{1,97},{33,1},{65,33},{97,65},{2,98}... | collective-permute-start | bytes 1769480 | tf_op jit(solution)/shard_map/ppermute | solution.py:15
  233.8 32.0 %collective-permute-start.12 = (f32[384,384]{1,0:T(8,128)S(1)}, f32[384,384]{1,0:T(8,128)S(1)}, u32[]{:S(2)}, u32[]{:S(2)}) collective-permute-start(f32[384,384]{1,0:T(8,128)S(1)} %fusion.8), channel_id=1, source_target_pairs={{0,16},{16,0},{1,17},{17,1},{2,18},{18,2},{3,19},{19,3},{4,20},{20... | collective-permute-start | bytes 1769480 | tf_op jit(solution)/shard_map/ppermute | solution.py:15
  254.4 10.1 %collective-permute-start.10 = (f32[192,384]{1,0:T(8,128)S(1)}, f32[192,384]{1,0:T(8,128)S(1)}, u32[]{:S(2)}, u32[]{:S(2)}) collective-permute-start(f32[192,384]{1,0:T(8,128)S(1)} %slice.202), channel_id=1, source_target_pairs={{0,32},{32,64},{64,96},{96,0},{1,33},{33,65},{65,97},{97,1},{2,34}... | collective-permute-start | bytes 884744 | tf_op jit(solution)/shard_map/ppermute | solution.py:15
  255.5 8.9 %collective-permute-start.11 = (f32[192,384]{1,0:T(8,128)S(1)}, f32[192,384]{1,0:T(8,128)S(1)}, u32[]{:S(2)}, u32[]{:S(2)}) collective-permute-start(f32[192,384]{1,0:T(8,128)S(1)} %slice.203), channel_id=1, source_target_pairs={{0,96},{32,0},{64,32},{96,64},{1,97},{33,1},{65,33},{97,65},{2,98}... | collective-permute-start | bytes 884744 | tf_op jit(solution)/shard_map/ppermute | solution.py:15
  259.3 6.5 %collective-permute-start.13 = (f32[384,384]{1,0:T(8,128)S(1)}, f32[384,384]{1,0:T(8,128)S(1)}, u32[]{:S(2)}, u32[]{:S(2)}) collective-permute-start(f32[384,384]{1,0:T(8,128)S(1)} %collective-permute-done.8), channel_id=1, source_target_pairs={{0,16},{16,0},{1,17},{17,1},{2,18},{18,2},{3,19},{19,3},{4,20},{20... | collective-permute-start | bytes 1769480 | tf_op jit(solution)/shard_map/ppermute | solution.py:15
  259.9 6.0 %collective-permute-start.14 = (f32[384,384]{1,0:T(8,128)S(1)}, f32[384,384]{1,0:T(8,128)S(1)}, u32[]{:S(2)}, u32[]{:S(2)}) collective-permute-start(f32[384,384]{1,0:T(8,128)S(1)} %collective-permute-done.9), channel_id=1, source_target_pairs={{0,16},{16,0},{1,17},{17,1},{2,18},{18,2},{3,19},{19,3},{4,20},{20... | collective-permute-start | bytes 1769480 | tf_op jit(solution)/shard_map/ppermute | solution.py:15
  264.5 2.7 collective-permute-start.15
  274.9 16.9 %collective-permute-start.17 = (f32[384,384]{1,0:T(8,128)S(1)}, f32[384,384]{1,0:T(8,128)S(1)}, u32[]{:S(2)}, u32[]{:S(2)}) collective-permute-start(f32[384,384]{1,0:T(8,128)S(1)} %get-tuple-element.41), channel_id=1, source_target_pairs={{0,32},{32,64},{64,96},{96,0},{1,33},{33,65},{65,97},{97,1},{2,34}... | collective-permute-start | bytes 1769480 | tf_op jit(solution)/shard_map/ppermute | solution.py:15
  275.4 16.7 %collective-permute-start.18 = (f32[384,384]{1,0:T(8,128)S(1)}, f32[384,384]{1,0:T(8,128)S(1)}, u32[]{:S(2)}, u32[]{:S(2)}) collective-permute-start(f32[384,384]{1,0:T(8,128)S(1)} %get-tuple-element.41), channel_id=1, source_target_pairs={{0,96},{32,0},{64,32},{96,64},{1,97},{33,1},{65,33},{97,65},{2,98}... | collective-permute-start | bytes 1769480 | tf_op jit(solution)/shard_map/ppermute | solution.py:15
  278.2 34.5 %collective-permute-start.21 = (f32[384,384]{1,0:T(8,128)S(1)}, f32[384,384]{1,0:T(8,128)}, u32[]{:S(2)}, u32[]{:S(2)}) collective-permute-start(f32[384,384]{1,0:T(8,128)S(1)} %get-tuple-element.41), channel_id=1, source_target_pairs={{0,16},{16,0},{1,17},{17,1},{2,18},{18,2},{3,19},{19,3},{4,20},{20... | collective-permute-start | bytes 1769480 | tf_op jit(solution)/shard_map/ppermute | solution.py:15
  280.5 34.1 %all-to-all-start.2 = ((f32[8,3,32,384]{3,2,1,0:T(8,128)}), f32[8,3,32,384]{3,2,1,0:T(8,128)S(1)}, u32[]{:S(2)}, u32[]{:S(2)}) async-start(f32[8,3,32,384]{3,2,1,0:T(8,128)} %broadcast_select_fusion), calls=%async_computation.2 | async-start | bytes 2359296 | tf_op jit(solution)/shard_map/all_to_all | solution.py:83
  291.8 18.9 %collective-permute-start.19 = (f32[192,384]{1,0:T(8,128)S(1)}, f32[192,384]{1,0:T(8,128)S(1)}, u32[]{:S(2)}, u32[]{:S(2)}) collective-permute-start(f32[192,384]{1,0:T(8,128)S(1)} %slice.205), channel_id=1, source_target_pairs={{0,32},{32,64},{64,96},{96,0},{1,33},{33,65},{65,97},{97,1},{2,34}... | collective-permute-start | bytes 884744 | tf_op jit(solution)/shard_map/ppermute | solution.py:15
  292.0 18.7 %collective-permute-start.20 = (f32[192,384]{1,0:T(8,128)S(1)}, f32[192,384]{1,0:T(8,128)S(1)}, u32[]{:S(2)}, u32[]{:S(2)}) collective-permute-start(f32[192,384]{1,0:T(8,128)S(1)} %slice.206), channel_id=1, source_target_pairs={{0,96},{32,0},{64,32},{96,64},{1,97},{33,1},{65,33},{97,65},{2,98}... | collective-permute-start | bytes 884744 | tf_op jit(solution)/shard_map/ppermute | solution.py:15
  295.8 20.0 %collective-permute-start.22 = (f32[384,384]{1,0:T(8,128)S(1)}, f32[384,384]{1,0:T(8,128)}, u32[]{:S(2)}, u32[]{:S(2)}) collective-permute-start(f32[384,384]{1,0:T(8,128)S(1)} %collective-permute-done.17), channel_id=1, source_target_pairs={{0,16},{16,0},{1,17},{17,1},{2,18},{18,2},{3,19},{19,3},{4,20},{20... | collective-permute-start | bytes 1769480 | tf_op jit(solution)/shard_map/ppermute | solution.py:15
  297.9 19.7 %collective-permute-start.23 = (f32[384,384]{1,0:T(8,128)S(1)}, f32[384,384]{1,0:T(8,128)}, u32[]{:S(2)}, u32[]{:S(2)}) collective-permute-start(f32[384,384]{1,0:T(8,128)S(1)} %collective-permute-done.18), channel_id=1, source_target_pairs={{0,16},{16,0},{1,17},{17,1},{2,18},{18,2},{3,19},{19,3},{4,20},{20... | collective-permute-start | bytes 1769480 | tf_op jit(solution)/shard_map/ppermute | solution.py:15
  310.8 8.8 %collective-permute-start.24 = (f32[384,384]{1,0:T(8,128)S(1)}, f32[384,384]{1,0:T(8,128)}, u32[]{:S(2)}, u32[]{:S(2)}) collective-permute-start(f32[384,384]{1,0:T(8,128)S(1)} %constant_dynamic-update-slice_fusion.52), channel_id=1, source_target_pairs={{0,16},{16,0},{1,17},{17,1},{2,18},{18,2},{3,19},{19,3},{4,20},{20... | collective-permute-start | bytes 1769480 | tf_op jit(solution)/shard_map/ppermute | solution.py:15
  321.5 7.8 %copy-start = (f32[6144,384]{1,0:T(8,128)S(1)}, f32[6144,384]{1,0:T(8,128)}, u32[]{:S(2)}) copy-start(f32[6144,384]{1,0:T(8,128)} %all-gather.9.cloned.1.call-done) | copy-start | bytes 28311556
  329.3 6.1 %copy-start.1 = (f32[768,384]{1,0:T(8,128)S(1)}, f32[768,384]{1,0:T(8,128)}, u32[]{:S(2)}) copy-start(f32[768,384]{1,0:T(8,128)} %param.8) | copy-start | bytes 3538948
Sparse Core Ops, SparseCore 0:
  60.3 77.9 all-gather.6
  141.0 100.0 all-gather.4
  243.3 75.4 all-gather.8

commit v2 on v1

v2 whole, which is shorter than its diff:
```python
import jax
import jax.numpy as jnp
import numpy as np
from jax import lax
from jax.experimental import pallas as pl
from jax.experimental.pallas import tpu as pltpu
from jax.sharding import Mesh, PartitionSpec as P

NB = 24
NANC = 12
ROW = ("y", "core")
COL = ("z", "x")
ALL = ("y", "core", "z", "x")
VMEM = pl.BlockSpec(memory_space=pltpu.VMEM)
SMEM = pl.BlockSpec(memory_space=pltpu.SMEM)
ANY = pl.BlockSpec(memory_space=pl.ANY)
F32 = jnp.float32


def params(mib):
    return pltpu.CompilerParams(vmem_limit_bytes=mib * 1024 * 1024)


def cost(m, k, n, in_bytes):
    return pl.CostEstimate(flops=6 * m * k * n, bytes_accessed=in_bytes, transcendentals=0)


def step(x, axis):
    if axis == "y":
        return lax.ppermute(x, ROW, [(2 * i + c, 2 * ((i + 1 - 2 * c) % 4) + c) for i in range(4) for c in range(2)])
    return lax.ppermute(x, ("core", axis), [(4 * c + i, 4 * c + (i + 1 - 2 * c) % 4) for i in range(4) for c in range(2)])


def swap(x):
    return lax.ppermute(x, "core", [(0, 1), (1, 0)])


def ring(x, axis):
    out = [x]
    for _ in range(3):
        out.append(step(out[-1], axis))
    return out


def gather_rows(x):
    mine = ring(x, "y")
    return mine + [swap(t) for t in mine]


def gather_cols(a, b):
    first = jnp.stack(ring(a, "x"))
    second = jnp.stack(ring(b, "z"))
    return ring(first, "z") + ring(second, "x")


def places():
    y, core, z, x = (lax.axis_index(n) for n in ALL)
    s = 1 - 2 * core
    back = lambda i, k: lax.rem(i - s * k + 8, 4)
    rows = [2 * back(y, k) + core for k in range(4)] + [2 * lax.rem(y + s * k + 8, 4) + 1 - core for k in range(4)]
    cols = [4 * back(z, i) + back(x, j) for i in range(4) for j in range(4)]
    cols += [4 * back(z, j) + back(x, i) for i in range(4) for j in range(4)]
    return jnp.stack(rows + cols).astype(jnp.int32)


def dot3(a, b):
    a_hi, b_hi = a.astype(jnp.bfloat16), b.astype(jnp.bfloat16)
    a_lo = (a - a_hi.astype(F32)).astype(jnp.bfloat16)
    b_lo = (b - b_hi.astype(F32)).astype(jnp.bfloat16)
    mul = lambda p, q: jnp.dot(p, q, preferred_element_type=F32)
    return mul(a_hi, b_hi) + (mul(a_hi, b_lo) + mul(a_lo, b_hi))


def col_copies(at, pieces, buf, sem, rows):
    out = []
    for i in range(32):
        half, c = i // 16, at[8 + i]
        out.append(
            pltpu.make_async_copy(
                pieces[i // 4].at[i % 4], buf.at[c, pl.ds(half * rows, rows)], sem.at[half, c]
            )
        )
    return out


def update_kernel(at, *refs):
    pieces, tiles, (u, ut), (a_buf, b_buf, a_sem, b_sem) = refs[:8], refs[8:16], refs[16:18], refs[18:]
    for i in range(8):
        pltpu.make_async_copy(tiles[i], b_buf.at[at[i]], b_sem.at[at[i]]).start()
    for copy in col_copies(at, pieces, a_buf, a_sem, a_buf.shape[1] // 2):
        copy.start()
    u[...] = jnp.zeros_like(u)
    rows = a_buf.shape[1] // 2

    def body(j, carry):
        pltpu.make_async_copy(tiles[0], b_buf.at[j], b_sem.at[j]).wait()
        for k in range(2):
            for half in range(2):
                pltpu.make_async_copy(
                    pieces[0].at[0], a_buf.at[2 * j + k, pl.ds(half * rows, rows)], a_sem.at[half, 2 * j + k]
                ).wait()
        lhs = jnp.concatenate([a_buf[2 * j], a_buf[2 * j + 1]], axis=1)
        u[...] += dot3(lhs, b_buf[j])
        return carry

    lax.fori_loop(0, 8, body, 0)
    ut[...] = u[...].T


def update_product(at, pieces, tiles):
    m, w = 2 * pieces[0].shape[1], pieces[0].shape[2]
    h = tiles[0].shape[0]
    out = jax.ShapeDtypeStruct((m, w), F32)
    return pl.pallas_call(
        update_kernel,
        out_shape=(out, jax.ShapeDtypeStruct((w, m), F32)),
        in_specs=[SMEM] + [ANY] * 16,
        out_specs=(VMEM, VMEM),
        scratch_shapes=[
            pltpu.VMEM((16, m, w), F32),
            pltpu.VMEM((8, h, w), F32),
            pltpu.SemaphoreType.DMA((2, 16)),
            pltpu.SemaphoreType.DMA((8,)),
        ],
        compiler_params=params(40),
        cost_estimate=cost(m, 8 * h, w, 4 * 16 * w * (m + w)),
        name="update",
    )(at, *pieces, *tiles)


def cross_kernel(at, *refs):
    pieces, tiles, (sigma,), (s_buf, u_buf, s_sem, u_sem) = refs[:8], refs[8:16], refs[16:17], refs[17:]
    width = s_buf.shape[2] // 2
    copies = []
    for i in range(32):
        half, c = i // 16, at[8 + i]
        copies.append(
            pltpu.make_async_copy(
                pieces[i // 4].at[i % 4], s_buf.at[c, :, pl.ds(half * width, width)], s_sem.at[half, c]
            )
        )
    for i in range(8):
        copies.append(pltpu.make_async_copy(tiles[i], u_buf.at[:, at[i]], u_sem.at[at[i]]))
    for copy in copies:
        copy.start()
    sigma[...] = jnp.zeros_like(sigma)
    for copy in copies:
        copy.wait()
    m, w = sigma.shape

    def body(k, carry):
        lhs = s_buf[:, :, pl.ds(pl.multiple_of(k * 768, 128), 768)].reshape(m, 768)
        rhs = u_buf[pl.ds(3 * k, 3)].reshape(768, w)
        sigma[...] -= dot3(lhs, rhs)
        return carry

    lax.fori_loop(0, 4, body, 0)


def cross_product(at, pieces, tiles):
    q, half = pieces[0].shape[1:]
    sub, w = tiles[0].shape[1:]
    return pl.pallas_call(
        cross_kernel,
        out_shape=jax.ShapeDtypeStruct((16 * q, w), F32),
        in_specs=[SMEM] + [ANY] * 16,
        out_specs=VMEM,
        scratch_shapes=[
            pltpu.VMEM((16, q, 2 * half), F32),
            pltpu.VMEM((NANC, 8, sub, w), F32),
            pltpu.SemaphoreType.DMA((2, 16)),
            pltpu.SemaphoreType.DMA((8,)),
        ],
        compiler_params=params(40),
        cost_estimate=cost(16 * q, 2 * half, w, 4 * 2 * half * (16 * q + w)),
        name="cross",
    )(at, *pieces, *tiles)


def child_kernel(at, base, *refs):
    pieces, tiles, (child,), (a_buf, b_buf, a_sem, b_sem) = refs[:8], refs[8:16], refs[16:17], refs[17:]
    w = a_buf.shape[2]
    copies = col_copies(at, pieces, a_buf, a_sem, w // 2)
    for i in range(8):
        copies.append(pltpu.make_async_copy(tiles[i], b_buf.at[at[i]], b_sem.at[at[i]]))
    for copy in copies:
        copy.start()
    child[...] = base[...]
    for copy in copies:
        copy.wait()

    def body(j, carry):
        rhs = b_buf[pl.ds(2 * j, 2)].reshape(2 * w, w)
        for p in range(2):
            lhs = jnp.concatenate([a_buf[4 * j + p], a_buf[4 * j + 2 + p]], axis=1)
            child[pl.ds(p * w, w)] -= dot3(lhs, rhs)
        return carry

    lax.fori_loop(0, 4, body, 0)


def child_product(at, base, pieces, tiles):
    h, w = base.shape
    return pl.pallas_call(
        child_kernel,
        out_shape=jax.ShapeDtypeStruct((h, w), F32),
        in_specs=[SMEM, VMEM] + [ANY] * 16,
        out_specs=VMEM,
        scratch_shapes=[
            pltpu.VMEM((16, w, w), F32),
            pltpu.VMEM((8, w, w), F32),
            pltpu.SemaphoreType.DMA((2, 16)),
            pltpu.SemaphoreType.DMA((8,)),
        ],
        compiler_params=params(40),
        cost_estimate=cost(h, 8 * w, w, 4 * w * 8 * (h + w)),
        name="child",
    )(at, base, *pieces, *tiles)


def spread(x):
    h, w = x.shape
    sub = h // 24
    return lax.all_to_all(x.reshape(3, 8, sub, w), ROW, 1, 0, tiled=True).reshape(NB, sub, w)


def pick_rows_kernel(anc, x, a, b):
    for i in range(NANC // 2):
        a[i] = x[anc[i]]
        b[i] = x[anc[i + NANC // 2]]


def pick_rows(ancestors, x):
    sub, w = x.shape[1:]
    out = jax.ShapeDtypeStruct((NANC // 2, sub, w), F32)
    a, b = pl.pallas_call(
        pick_rows_kernel,
        out_shape=(out, out),
        in_specs=[SMEM, VMEM],
        out_specs=(VMEM, VMEM),
        compiler_params=params(8),
        name="pick_rows",
    )(ancestors, x)
    return a.reshape(-1, w), b.reshape(-1, w)


def pick_cols_kernel(anc, x, a, b):
    for out, first in ((a, 0), (b, NANC // 2)):
        for i in range(NANC // 2):
            for k in range(2):
                t = 2 * anc[first + i] + k
                off = pl.multiple_of(lax.rem(t, 3) * 128, 128)
                out[:, pl.ds(i * 256 + k * 128, 128)] = x[lax.div(t, 3), :, pl.ds(off, 128)]


def pick_cols(ancestors, x):
    q = x.shape[1]
    out = jax.ShapeDtypeStruct((q, NANC * 128), F32)
    return pl.pallas_call(
        pick_cols_kernel,
        out_shape=(out, out),
        in_specs=[SMEM, VMEM],
        out_specs=(VMEM, VMEM),
        compiler_params=params(8),
        name="pick_cols",
    )(ancestors, x)


def place_kernel(anc, x, out):
    out[...] = jnp.zeros_like(out)
    for i in range(NANC):
        out[anc[i]] = x[i]


def place_rows(ancestors, x):
    sub, w = x.shape[1:]
    return pl.pallas_call(
        place_kernel,
        out_shape=jax.ShapeDtypeStruct((NB, sub, w), F32),
        in_specs=[SMEM, VMEM],
        out_specs=VMEM,
        compiler_params=params(8),
        name="place_rows",
    )(ancestors, x)


def per_device(sigma_top, factor_cross, factor_inverse, block_inverse, ancestors):
    h, w = sigma_top.shape
    sub = h // 24
    at = places()

    f_pieces = gather_cols(*pick_rows(ancestors, spread(factor_cross)))
    inverse_tiles = gather_rows(factor_inverse)

    s_rows = jnp.concatenate(pick_rows(ancestors, spread(sigma_top)))
    s_cols = lax.all_to_all(s_rows.reshape(16, -1, w), COL, 0, 0, tiled=True)
    s_pieces = gather_cols(*pick_cols(ancestors, s_cols))

    u, ut = update_product(at, f_pieces, inverse_tiles)
    moved = lax.ppermute(ut, ALL, [(16 * r + c, 16 * (c // 2) + 2 * r + c % 2) for r in range(8) for c in range(16)])
    u_pieces = gather_cols(moved[: w // 2], moved[w // 2 :])
    u_tiles = gather_rows(u.reshape(NANC, sub, w))

    sigma = cross_product(at, s_pieces, u_tiles)
    sigma_tiles = gather_rows(sigma)
    sigma_child = child_product(at, block_inverse, u_pieces, sigma_tiles)

    full = place_rows(ancestors, sigma.reshape(NANC, sub, w))
    back = lax.all_to_all(full.reshape(8, 3, sub, w), ROW, 0, 0, tiled=True)
    sigma_cross = back.reshape(8, 3, sub, w).transpose(1, 0, 2, 3).reshape(h, w)
    return (sigma_cross, sigma_child)


def solution(mesh):
    fine = Mesh(np.asarray(mesh.devices).reshape(4, 2, 4, 4), ALL)
    tile = P(ROW, COL)
    return jax.shard_map(
        per_device,
        mesh=fine,
        in_specs=(tile, tile, tile, tile, P()),
        out_specs=(tile, tile),
        check_vma=False,
    )
```

time: 345 us -> 299 us (0.87)
  between operations: 89 us -> 1.16 us
  starting transfers between devices: 62.1 us -> 143 us
  local copies, waits for them, and re-layouts: 56.3 us -> 8.49 us
  Pallas kernels: 0 us -> 40.5 us
  matrix products: 30.6 us -> 0 us
  blocking collectives: 0 us -> 17.6 us
  waiting for transfers between devices: 102 us -> 87.5 us
    ppermute x25 -> x58, starting transfers between devices: 48.2 us -> 127 us  [the longest x36 71.7 us: step(): lax.ppermute(x, ('core', axis), [(4 * c + i, 4 * c + (i + 1 - 2 * c) % 4)...]
    pallas_call x0 -> x7, Pallas kernels: none -> 40.5 us  [the longest x1 14.8 us: update_product(): pl.pallas_call(update_kernel, out_shape=(out, jax.ShapeDtypeStruct((w, m)...]
    dot_general x4 -> x0, matrix products: 30.6 us -> none  [dot(): lax.dot_general(a, b, (dims, ((), ())), precision=lax.Precision.HIGH, pre...]
    dynamic_update_slice x23 -> x0, local copies, waits for them, and re-layouts: 26.2 us -> none  [the longest x8 15.4 us: per_device(): strip = lax.dynamic_update_slice(strip, t, (r * h, 0))]
    ppermute x25 -> x58, waiting for transfers between devices: 75.6 us -> 57.9 us  [the longest x36 37 us: step(): lax.ppermute(x, ('core', axis), [(4 * c + i, 4 * c + (i + 1 - 2 * c) % 4)...]
    all_to_all x0 -> x1, blocking collectives: none -> 17.6 us  [per_device(): s_cols = lax.all_to_all(s_rows.reshape(16, -1, w), COL, 0, 0, tiled=True)]
    unnamed x72 -> x18, local copies, waits for them, and re-layouts: 14.6 us -> 2.32 us
    all_gather x3 -> x0, waiting for transfers between devices: 11.1 us -> none  [the longest x1 11.1 us: per_device(): f_all = lax.all_gather(f, COL, axis=1, tiled=True)]
  transfers between devices with their start and end apart: 31 -> 61, of which waited for: 10 -> 20; matrix products, arithmetic and copies ran while one was open for 20% -> 1% of each run, Pallas kernels for 0% -> 9%
where the time goes in v2:
time: 299 us
  starting transfers between devices  143 us (48%)
  waiting for transfers between devices  87.5 us (29%)
  Pallas kernels  40.5 us (14%)
  blocking collectives  17.6 us (6%)
  local copies, waits for them, and re-layouts  8.49 us (3%)
    ppermute x36, starting transfers between devices, step(): lax.ppermute(x, ('core', axis), [(4 * c + i, 4 * c + (i + 1 - 2 * c) % 4)...  71.7 us
    ppermute x36, waiting for transfers between devices, step(): lax.ppermute(x, ('core', axis), [(4 * c + i, 4 * c + (i + 1 - 2 * c) % 4)...  37 us
    ppermute x12, starting transfers between devices, swap(): return lax.ppermute(x, 'core', [(0, 1), (1, 0)])  30.8 us
    ppermute x9, starting transfers between devices, step(): lax.ppermute(x, ROW, [(2 * i + c, 2 * ((i + 1 - 2 * c) % 4) + c) for i in...  20.2 us
    all_to_all x2, waiting for transfers between devices, spread(): lax.all_to_all(x.reshape(3, 8, sub, w), ROW, 1, 0, tiled=True)  19.9 us
    all_to_all x1, blocking collectives, per_device(): s_cols = lax.all_to_all(s_rows.reshape(16, -1, w), COL, 0, 0, tiled=True)  17.6 us
    ppermute x9, waiting for transfers between devices, step(): lax.ppermute(x, ROW, [(2 * i + c, 2 * ((i + 1 - 2 * c) % 4) + c) for i in...  15.3 us
    pallas_call x1, Pallas kernels, update_product(): pl.pallas_call(update_kernel, out_shape=(out, jax.ShapeDtypeStruct((w, m)...  14.8 us
  transfers between devices with their start and end apart: 61, of which 20 were waited for; matrix products, arithmetic and copies ran while one was open for 1% of the time, Pallas kernels for 9%

profile of v2, /device:TPU:1, one launch (start us, length us, event | category | flops | bytes accessed | tf_op | source)
XLA Modules:
  0.0 298.6 jit_solution(5519153658792416753)
XLA Ops:
  0.6 2.4 copy.8
  3.0 6.1 %all-to-all-start.2 = ((f32[3,8,32,384]{3,2,0,1:T(8,128)}), f32[3,8,32,384]{3,2,0,1:T(8,128)S(1)}, u32[]{:S(2)}, u32[]{:S(2)}) async-start(f32[3,8,32,384]{3,2,0,1:T(8,128)} %copy.8), calls=%async_computation.2 | async-start | bytes 2359296 | tf_op jit(solution)/shard_map/all_to_all | solution.py:224
  9.1 2.6 collective-permute-start.24
  11.7 13.9 %all-to-all-done.2 = f32[3,8,32,384]{3,2,0,1:T(8,128)S(1)} async-done(((f32[3,8,32,384]{3,2,0,1:T(8,128)}), f32[3,8,32,384]{3,2,0,1:T(8,128)S(1)}, u32[]{:S(2)}, u32[]{:S(2)}) %all-to-all-start.2) | async-done | bytes 1179680 | tf_op jit(solution)/shard_map/all_to_all | solution.py:224
  26.2 2.5 collective-permute-start.12
  28.8 3.8 %collective-permute-start.18 = (f32[192,384]{1,0:T(8,128)S(1)}, f32[192,384]{1,0:T(8,128)S(1)}, u32[]{:S(2)}, u32[]{:S(2)}) collective-permute-start(f32[192,384]{1,0:T(8,128)S(1)} %bitcast.75), channel_id=1, source_target_pairs={{0,4},{16,28},{4,8},{20,16},{8,12},{24,20},{12,0},{28,24},{1,5},{1... | collective-permute-start | bytes 884744 | tf_op jit(solution)/shard_map/ppermute | solution.py:31
  32.6 3.4 %collective-permute-start.13 = (f32[192,384]{1,0:T(8,128)S(1)}, f32[192,384]{1,0:T(8,128)S(1)}, u32[]{:S(2)}, u32[]{:S(2)}) collective-permute-start(f32[192,384]{1,0:T(8,128)S(1)} %collective-permute-done.12), channel_id=1, source_target_pairs={{0,1},{16,19},{1,2},{17,16},{2,3},{18,17},{3,0},{19,18},{4,5},{20,... | collective-permute-start | bytes 884744 | tf_op jit(solution)/shard_map/ppermute | solution.py:31
  36.2 3.5 %collective-permute-start.19 = (f32[192,384]{1,0:T(8,128)S(1)}, f32[192,384]{1,0:T(8,128)S(1)}, u32[]{:S(2)}, u32[]{:S(2)}) collective-permute-start(f32[192,384]{1,0:T(8,128)S(1)} %collective-permute-done.18), channel_id=1, source_target_pairs={{0,4},{16,28},{4,8},{20,16},{8,12},{24,20},{12,0},{28,24},{1,5},{1... | collective-permute-start | bytes 884744 | tf_op jit(solution)/shard_map/ppermute | solution.py:31
  39.7 3.0 %collective-permute-start.14 = (f32[192,384]{1,0:T(8,128)S(1)}, f32[192,384]{1,0:T(8,128)S(1)}, u32[]{:S(2)}, u32[]{:S(2)}) collective-permute-start(f32[192,384]{1,0:T(8,128)S(1)} %collective-permute-done.13), channel_id=1, source_target_pairs={{0,1},{16,19},{1,2},{17,16},{2,3},{18,17},{3,0},{19,18},{4,5},{20,... | collective-permute-start | bytes 884744 | tf_op jit(solution)/shard_map/ppermute | solution.py:31
  43.4 3.1 %collective-permute-start.20 = (f32[192,384]{1,0:T(8,128)S(1)}, f32[192,384]{1,0:T(8,128)S(1)}, u32[]{:S(2)}, u32[]{:S(2)}) collective-permute-start(f32[192,384]{1,0:T(8,128)S(1)} %collective-permute-done.19), channel_id=1, source_target_pairs={{0,4},{16,28},{4,8},{20,16},{8,12},{24,20},{12,0},{28,24},{1,5},{1... | collective-permute-start | bytes 884744 | tf_op jit(solution)/shard_map/ppermute | solution.py:31
  47.4 2.9 collective-permute-start.15
  50.4 3.2 %collective-permute-start.21 = (f32[4,192,384]{2,1,0:T(8,128)S(1)}, f32[4,192,384]{2,1,0:T(8,128)}, u32[]{:S(2)}, u32[]{:S(2)}) collective-permute-start(f32[4,192,384]{2,1,0:T(8,128)S(1)} %pad_maximum_fusion.1.refs_4_), channel_id=1, source_target_pairs={{0,1},{16,19},{1,2},{17,16},{2,3},{18,17},{3,0},{19,18},{4,5},{20,... | collective-permute-start | bytes 3538952 | tf_op jit(solution)/shard_map/ppermute | solution.py:31
  53.6 1.1 copy.7
  54.7 4.8 %all-to-all-start = ((f32[3,8,32,384]{3,2,0,1:T(8,128)}), f32[3,8,32,384]{3,2,0,1:T(8,128)S(1)}, u32[]{:S(2)}, u32[]{:S(2)}) async-start(f32[3,8,32,384]{3,2,0,1:T(8,128)} %copy.7), calls=%async_computation | async-start | bytes 2359296 | tf_op jit(solution)/shard_map/all_to_all | solution.py:224
  59.7 2.5 collective-permute-done.25.refs_10_
  62.2 2.1 collective-permute-start.26
  64.3 2.7 collective-permute-start.16
  67.0 3.2 %collective-permute-start.22 = (f32[4,192,384]{2,1,0:T(8,128)}, f32[4,192,384]{2,1,0:T(8,128)}, u32[]{:S(2)}, u32[]{:S(2)}) collective-permute-start(f32[4,192,384]{2,1,0:T(8,128)} %collective-permute-done.21.refs_5_), channel_id=1, source_target_pairs={{0,1},{16,19},{1,2},{17,16},{2,3},{18,17},{3,0},{19,18},{4,5},{20,... | collective-permute-start | bytes 3538952 | tf_op jit(solution)/shard_map/ppermute | solution.py:31
  70.2 5.9 %all-to-all-done = f32[3,8,32,384]{3,2,0,1:T(8,128)S(1)} async-done(((f32[3,8,32,384]{3,2,0,1:T(8,128)}), f32[3,8,32,384]{3,2,0,1:T(8,128)S(1)}, u32[]{:S(2)}, u32[]{:S(2)}) %all-to-all-start) | async-done | bytes 1179680 | tf_op jit(solution)/shard_map/all_to_all | solution.py:224
  76.8 17.6 %all_to_all.40.x = f32[16,24,384]{2,1,0:T(8,128)S(1)} all-to-all(f32[16,24,384]{2,1,0:T(8,128)S(1)} %bitcast.86), channel_id=1, replica_groups=mesh['y'=4,'core'=2,'z'=4,'x'=4] {'z','x'}, dimensions={0} | all-to-all | bytes 1179648 | tf_op jit(solution)/shard_map/all_to_all | solution.py:296
  95.6 3.4 %collective-permute-done.6 = f32[24,1536]{1,0:T(8,128)S(1)} collective-permute-done((f32[24,1536]{1,0:T(8,128)S(1)}, f32[24,1536]{1,0:T(8,128)S(1)}, u32[]{:S(2)}, u32[]{:S(2)}) %collective-permute-start.6) | collective-permute-done | bytes 147488 | tf_op jit(solution)/shard_map/ppermute | solution.py:31
  99.0 1.8 collective-permute-start.7
  100.8 2.5 collective-permute-done.7
  103.3 2.7 collective-permute-start.8
  106.1 5.1 %collective-permute-start.28 = (f32[768,384]{1,0:T(8,128)}, f32[768,384]{1,0:T(8,128)}, u32[]{:S(2)}, u32[]{:S(2)}) collective-permute-start(f32[768,384]{1,0:T(8,128)} %collective-permute-done.24.refs_9_), channel_id=1, source_target_pairs={{0,16},{16,0},{1,17},{17,1},{2,18},{18,2},{3,19},{19,3},{4,20},{20... | collective-permute-start | bytes 3538952 | tf_op jit(solution)/shard_map/ppermute | solution.py:35
  111.1 6.3 %collective-permute-start.29 = (f32[768,384]{1,0:T(8,128)}, f32[768,384]{1,0:T(8,128)}, u32[]{:S(2)}, u32[]{:S(2)}) collective-permute-start(f32[768,384]{1,0:T(8,128)} %collective-permute-done.25.refs_10_), channel_id=1, source_target_pairs={{0,16},{16,0},{1,17},{17,1},{2,18},{18,2},{3,19},{19,3},{4,20},{20... | collective-permute-start | bytes 3538952 | tf_op jit(solution)/shard_map/ppermute | solution.py:35
  118.0 2.3 collective-permute-done.29.refs_14_
  120.3 1.7 collective-permute-done.30.refs_15_
  122.0 11.2 %collective-permute-done.17.refs_3_ = f32[4,192,384]{2,1,0:T(8,128)} collective-permute-done((f32[4,192,384]{2,1,0:T(8,128)}, f32[4,192,384]{2,1,0:T(8,128)}, u32[]{:S(2)}, u32[]{:S(2)}) %collective-permute-start.17) | collective-permute-done | bytes 1179680 | tf_op jit(solution)/shard_map/ppermute | solution.py:31
  133.3 14.8 %update.1 = (f32[384,384]{1,0:T(8,128)S(1)}, f32[384,384]{1,0:T(8,128)S(1)}) custom-call(s32[40]{0:T(128)S(1)} %stack.199.at, f32[4,192,384]{2,1,0:T(8,128)S(1)} %pad_maximum_fusion.refs_0_, f32[4,192,384]{2,1,0:T(8,128)} %collective-permute-done.15.refs_1_, f32[4,192,384]{2,1,0:T(8,128)} %collective-permute-done.16.refs_2_, ...), custom_call_target="tpu_custom_call" | custom-call | flops 5435817984 | bytes 18874368 | tf_op jit(solution)/shard_map/update/pallas_call | solution.py:114
  148.1 4.4 %collective-permute-start.38 = (f32[384,384]{1,0:T(8,128)S(1)}, f32[384,384]{1,0:T(8,128)S(1)}, u32[]{:S(2)}, u32[]{:S(2)}) collective-permute-start(f32[384,384]{1,0:T(8,128)S(1)} %get-tuple-element.17), channel_id=1, source_target_pairs={{0,0},{1,1},{2,16},{3,17},{4,32},{5,33},{6,48},{7,49},{8,64},{9,65... | collective-permute-start | bytes 1769480 | tf_op jit(solution)/shard_map/ppermute | solution.py:300
  152.8 9.3 %collective-permute-done.1 = f32[24,1536]{1,0:T(8,128)S(1)} collective-permute-done((f32[24,1536]{1,0:T(8,128)S(1)}, f32[24,1536]{1,0:T(8,128)S(1)}, u32[]{:S(2)}, u32[]{:S(2)}) %collective-permute-start.1) | collective-permute-done | bytes 147488 | tf_op jit(solution)/shard_map/ppermute | solution.py:31
  162.1 2.1 collective-permute-start.2
  164.1 2.1 collective-permute-done.2
  166.3 6.3 %collective-permute-start.3 = (f32[4,24,1536]{2,1,0:T(8,128)S(1)}, f32[4,24,1536]{2,1,0:T(8,128)S(1)}, u32[]{:S(2)}, u32[]{:S(2)}) collective-permute-start(f32[4,24,1536]{2,1,0:T(8,128)S(1)} %pad_maximum_fusion.5.refs_0_), channel_id=1, source_target_pairs={{0,4},{16,28},{4,8},{20,16},{8,12},{24,20},{12,0},{28,24},{1,5},{1... | collective-permute-start | bytes 1769480 | tf_op jit(solution)/shard_map/ppermute | solution.py:31
  172.5 2.4 collective-permute-start.31
  176.0 7.5 %collective-permute-start.39 = (f32[192,384]{1,0:T(8,128)S(1)}, f32[192,384]{1,0:T(8,128)S(1)}, u32[]{:S(2)}, u32[]{:S(2)}) collective-permute-start(f32[192,384]{1,0:T(8,128)S(1)} %get-tuple-element.21), channel_id=1, source_target_pairs={{0,1},{16,19},{1,2},{17,16},{2,3},{18,17},{3,0},{19,18},{4,5},{20,... | collective-permute-start | bytes 884744 | tf_op jit(solution)/shard_map/ppermute | solution.py:31
  183.5 1.2 collective-permute-done.3.refs_1_
  184.7 3.1 %collective-permute-start.4 = (f32[4,24,1536]{2,1,0:T(8,128)S(1)}, f32[4,24,1536]{2,1,0:T(8,128)S(1)}, u32[]{:S(2)}, u32[]{:S(2)}) collective-permute-start(f32[4,24,1536]{2,1,0:T(8,128)S(1)} %collective-permute-done.3.refs_1_), channel_id=1, source_target_pairs={{0,4},{16,28},{4,8},{20,16},{8,12},{24,20},{12,0},{28,24},{1,5},{1... | collective-permute-start | bytes 1769480 | tf_op jit(solution)/shard_map/ppermute | solution.py:31
  187.9 3.9 %collective-permute-start.46 = (f32[192,384]{1,0:T(8,128)S(1)}, f32[192,384]{1,0:T(8,128)S(1)}, u32[]{:S(2)}, u32[]{:S(2)}) collective-permute-start(f32[192,384]{1,0:T(8,128)S(1)} %collective-permute-done.45), channel_id=1, source_target_pairs={{0,4},{16,28},{4,8},{20,16},{8,12},{24,20},{12,0},{28,24},{1,5},{1... | collective-permute-start | bytes 884744 | tf_op jit(solution)/shard_map/ppermute | solution.py:31
  192.6 5.3 %collective-permute-done.46 = f32[192,384]{1,0:T(8,128)S(1)} collective-permute-done((f32[192,384]{1,0:T(8,128)S(1)}, f32[192,384]{1,0:T(8,128)S(1)}, u32[]{:S(2)}, u32[]{:S(2)}) %collective-permute-start.46) | collective-permute-done | bytes 294944 | tf_op jit(solution)/shard_map/ppermute | solution.py:31
  197.8 3.4 %collective-permute-start.47 = (f32[192,384]{1,0:T(8,128)S(1)}, f32[192,384]{1,0:T(8,128)S(1)}, u32[]{:S(2)}, u32[]{:S(2)}) collective-permute-start(f32[192,384]{1,0:T(8,128)S(1)} %collective-permute-done.46), channel_id=1, source_target_pairs={{0,4},{16,28},{4,8},{20,16},{8,12},{24,20},{12,0},{28,24},{1,5},{1... | collective-permute-start | bytes 884744 | tf_op jit(solution)/shard_map/ppermute | solution.py:31
  201.3 2.6 collective-permute-start.34
  203.9 1.0 collective-permute-done.47
  204.9 4.3 %collective-permute-start.33 = (f32[12,32,384]{2,1,0:T(8,128)S(1)}, f32[12,32,384]{2,1,0:T(8,128)S(1)}, u32[]{:S(2)}, u32[]{:S(2)}) collective-permute-start(f32[12,32,384]{2,1,0:T(8,128)S(1)} %collective-permute-done.32.refs_10_), channel_id=1, source_target_pairs={{0,32},{16,112},{32,64},{48,16},{64,96},{80,48},{96,0},{112,80},{1... | collective-permute-start | bytes 1769480 | tf_op jit(solution)/shard_map/ppermute | solution.py:30
  209.3 2.9 collective-permute-start.48
  212.3 3.0 %collective-permute-start.42 = (f32[4,192,384]{2,1,0:T(8,128)S(1)}, f32[4,192,384]{2,1,0:T(8,128)S(1)}, u32[]{:S(2)}, u32[]{:S(2)}) collective-permute-start(f32[4,192,384]{2,1,0:T(8,128)S(1)} %pad_maximum_fusion.2.refs_0_), channel_id=1, source_target_pairs={{0,4},{16,28},{4,8},{20,16},{8,12},{24,20},{12,0},{28,24},{1,5},{1... | collective-permute-start | bytes 3538952 | tf_op jit(solution)/shard_map/ppermute | solution.py:31
  215.3 1.8 collective-permute-start.35
  217.1 7.9 %collective-permute-start.37 = (f32[12,32,384]{2,1,0:T(8,128)S(1)}, f32[12,32,384]{2,1,0:T(8,128)S(1)}, u32[]{:S(2)}, u32[]{:S(2)}) collective-permute-start(f32[12,32,384]{2,1,0:T(8,128)S(1)} %collective-permute-done.33.refs_11_), channel_id=1, source_target_pairs={{0,16},{16,0},{1,17},{17,1},{2,18},{18,2},{3,19},{19,3},{4,20},{20... | collective-permute-start | bytes 1769480 | tf_op jit(solution)/shard_map/ppermute | solution.py:35
  225.0 1.6 collective-permute-done.37.refs_15_
  226.7 8.3 %cross.1.refs_8_ = f32[384,384]{1,0:T(8,128)S(1)} custom-call(s32[40]{0:T(128)S(1)} %stack.199.at, f32[4,24,1536]{2,1,0:T(8,128)S(1)} %pad_maximum_fusion.5.refs_0_, f32[4,24,1536]{2,1,0:T(8,128)S(1)} %collective-permute-done.3.refs_1_, f32[4,24,1536]{2,1,0:T(8,128)S(1)} %collective-permute-done.4.refs_2_, ...), custom_call_target="tpu_custom_call" | custom-call | flops 2717908992 | bytes 9437184 | tf_op jit(solution)/shard_map/cross/pallas_call | solution.py:163
  234.9 1.8 collective-permute-start.51
  237.1 1.0 copy-done.6
  238.2 6.0 %collective-permute-done.51.refs_9_ = f32[384,384]{1,0:T(8,128)S(1)} collective-permute-done((f32[384,384]{1,0:T(8,128)S(1)}, f32[384,384]{1,0:T(8,128)S(1)}, u32[]{:S(2)}, u32[]{:S(2)}) %collective-permute-start.51) | collective-permute-done | bytes 589856 | tf_op jit(solution)/shard_map/ppermute | solution.py:30
  244.1 3.0 collective-permute-start.52
  247.1 6.8 %collective-permute-done.52.refs_10_ = f32[384,384]{1,0:T(8,128)} collective-permute-done((f32[384,384]{1,0:T(8,128)S(1)}, f32[384,384]{1,0:T(8,128)}, u32[]{:S(2)}, u32[]{:S(2)}) %collective-permute-start.52) | collective-permute-done | bytes 589856 | tf_op jit(solution)/shard_map/ppermute | solution.py:30
  253.9 3.2 %collective-permute-start.53 = (f32[384,384]{1,0:T(8,128)}, f32[384,384]{1,0:T(8,128)}, u32[]{:S(2)}, u32[]{:S(2)}) collective-permute-start(f32[384,384]{1,0:T(8,128)} %collective-permute-done.52.refs_10_), channel_id=1, source_target_pairs={{0,32},{16,112},{32,64},{48,16},{64,96},{80,48},{96,0},{112,80},{1... | collective-permute-start | bytes 1769480 | tf_op jit(solution)/shard_map/ppermute | solution.py:30
  257.3 1.7 place_rows.1
  259.0 5.0 %all-to-all-start.3 = ((f32[8,3,32,384]{3,2,1,0:T(8,128)}), f32[8,3,32,384]{3,2,1,0:T(8,128)}, u32[]{:S(2)}, u32[]{:S(2)}) async-start(f32[8,3,32,384]{3,2,1,0:T(8,128)} %bitcast.55), calls=%async_computation.3 | async-start | bytes 2359296 | tf_op jit(solution)/shard_map/all_to_all | solution.py:309
  264.5 6.4 %collective-permute-start.57 = (f32[384,384]{1,0:T(8,128)}, f32[384,384]{1,0:T(8,128)}, u32[]{:S(2)}, u32[]{:S(2)}) collective-permute-start(f32[384,384]{1,0:T(8,128)} %collective-permute-done.53.refs_11_), channel_id=1, source_target_pairs={{0,16},{16,0},{1,17},{17,1},{2,18},{18,2},{3,19},{19,3},{4,20},{20... | collective-permute-start | bytes 1769480 | tf_op jit(solution)/shard_map/ppermute | solution.py:35
  270.9 9.7 %all-to-all-done.3 = f32[8,3,32,384]{3,2,1,0:T(8,128)} async-done(((f32[8,3,32,384]{3,2,1,0:T(8,128)}), f32[8,3,32,384]{3,2,1,0:T(8,128)}, u32[]{:S(2)}, u32[]{:S(2)}) %all-to-all-start.3) | async-done | bytes 1179680 | tf_op jit(solution)/shard_map/all_to_all | solution.py:309
  280.6 2.5 copy.9
  283.2 1.3 copy-done.7
  284.5 14.0 %child.1 = f32[768,384]{1,0:T(8,128)} custom-call(s32[40]{0:T(128)S(1)} %stack.199.at, f32[768,384]{1,0:T(8,128)S(1)} %copy-done.3, f32[4,192,384]{2,1,0:T(8,128)S(1)} %pad_maximum_fusion.2.refs_0_, f32[4,192,384]{2,1,0:T(8,128)S(1)} %copy-done.7, f32[4,192,384]{2,1,0:T(8,128)} %collective-permute-done.43.refs_2_, ...), custom_call_target="tpu_custom_call" | custom-call | flops 5435817984 | bytes 14155776 | tf_op jit(solution)/shard_map/child/pallas_call | solution.py:204
  (96 shorter events, 8.7 us)
Async XLA Ops:
  3.0 22.7 %copy-start = (s32[12]{0:T(128)S(1)}, s32[12]{0:T(128)}, u32[]{:S(2)}) copy-start(s32[12]{0:T(128)} %anc.7) | copy-start | bytes 148
  3.0 22.7 %all-to-all-start.2 = ((f32[3,8,32,384]{3,2,0,1:T(8,128)}), f32[3,8,32,384]{3,2,0,1:T(8,128)S(1)}, u32[]{:S(2)}, u32[]{:S(2)}) async-start(f32[3,8,32,384]{3,2,0,1:T(8,128)} %copy.8), calls=%async_computation.2 | async-start | bytes 2359296 | tf_op jit(solution)/shard_map/all_to_all | solution.py:224
  9.1 37.4 %collective-permute-start.24 = (f32[768,384]{1,0:T(8,128)S(1)}, f32[768,384]{1,0:T(8,128)}, u32[]{:S(2)}, u32[]{:S(2)}) collective-permute-start(f32[768,384]{1,0:T(8,128)S(1)} %copy-done.1), channel_id=1, source_target_pairs={{0,32},{16,112},{32,64},{48,16},{64,96},{80,48},{96,0},{112,80},{1... | collective-permute-start | bytes 3538952 | tf_op jit(solution)/shard_map/ppermute | solution.py:30
  26.2 6.3 %collective-permute-start.12 = (f32[192,384]{1,0:T(8,128)S(1)}, f32[192,384]{1,0:T(8,128)S(1)}, u32[]{:S(2)}, u32[]{:S(2)}) collective-permute-start(f32[192,384]{1,0:T(8,128)S(1)} %bitcast.77), channel_id=1, source_target_pairs={{0,1},{16,19},{1,2},{17,16},{2,3},{18,17},{3,0},{19,18},{4,5},{20,... | collective-permute-start | bytes 884744 | tf_op jit(solution)/shard_map/ppermute | solution.py:31
  28.8 7.4 %collective-permute-start.18 = (f32[192,384]{1,0:T(8,128)S(1)}, f32[192,384]{1,0:T(8,128)S(1)}, u32[]{:S(2)}, u32[]{:S(2)}) collective-permute-start(f32[192,384]{1,0:T(8,128)S(1)} %bitcast.75), channel_id=1, source_target_pairs={{0,4},{16,28},{4,8},{20,16},{8,12},{24,20},{12,0},{28,24},{1,5},{1... | collective-permute-start | bytes 884744 | tf_op jit(solution)/shard_map/ppermute | solution.py:31
  32.6 7.2 %collective-permute-start.13 = (f32[192,384]{1,0:T(8,128)S(1)}, f32[192,384]{1,0:T(8,128)S(1)}, u32[]{:S(2)}, u32[]{:S(2)}) collective-permute-start(f32[192,384]{1,0:T(8,128)S(1)} %collective-permute-done.12), channel_id=1, source_target_pairs={{0,1},{16,19},{1,2},{17,16},{2,3},{18,17},{3,0},{19,18},{4,5},{20,... | collective-permute-start | bytes 884744 | tf_op jit(solution)/shard_map/ppermute | solution.py:31
  36.2 7.2 %collective-permute-start.19 = (f32[192,384]{1,0:T(8,128)S(1)}, f32[192,384]{1,0:T(8,128)S(1)}, u32[]{:S(2)}, u32[]{:S(2)}) collective-permute-start(f32[192,384]{1,0:T(8,128)S(1)} %collective-permute-done.18), channel_id=1, source_target_pairs={{0,4},{16,28},{4,8},{20,16},{8,12},{24,20},{12,0},{28,24},{1,5},{1... | collective-permute-start | bytes 884744 | tf_op jit(solution)/shard_map/ppermute | solution.py:31
  39.7 7.6 %collective-permute-start.14 = (f32[192,384]{1,0:T(8,128)S(1)}, f32[192,384]{1,0:T(8,128)S(1)}, u32[]{:S(2)}, u32[]{:S(2)}) collective-permute-start(f32[192,384]{1,0:T(8,128)S(1)} %collective-permute-done.13), channel_id=1, source_target_pairs={{0,1},{16,19},{1,2},{17,16},{2,3},{18,17},{3,0},{19,18},{4,5},{20,... | collective-permute-start | bytes 884744 | tf_op jit(solution)/shard_map/ppermute | solution.py:31
  43.4 6.9 %collective-permute-start.20 = (f32[192,384]{1,0:T(8,128)S(1)}, f32[192,384]{1,0:T(8,128)S(1)}, u32[]{:S(2)}, u32[]{:S(2)}) collective-permute-start(f32[192,384]{1,0:T(8,128)S(1)} %collective-permute-done.19), channel_id=1, source_target_pairs={{0,4},{16,28},{4,8},{20,16},{8,12},{24,20},{12,0},{28,24},{1,5},{1... | collective-permute-start | bytes 884744 | tf_op jit(solution)/shard_map/ppermute | solution.py:31
  46.5 15.7 %collective-permute-start.25 = (f32[768,384]{1,0:T(8,128)}, f32[768,384]{1,0:T(8,128)}, u32[]{:S(2)}, u32[]{:S(2)}) collective-permute-start(f32[768,384]{1,0:T(8,128)} %collective-permute-done.24.refs_9_), channel_id=1, source_target_pairs={{0,32},{16,112},{32,64},{48,16},{64,96},{80,48},{96,0},{112,80},{1... | collective-permute-start | bytes 3538952 | tf_op jit(solution)/shard_map/ppermute | solution.py:30
  47.4 16.9 %collective-permute-start.15 = (f32[4,192,384]{2,1,0:T(8,128)S(1)}, f32[4,192,384]{2,1,0:T(8,128)}, u32[]{:S(2)}, u32[]{:S(2)}) collective-permute-start(f32[4,192,384]{2,1,0:T(8,128)S(1)} %pad_maximum_fusion.refs_0_), channel_id=1, source_target_pairs={{0,4},{16,28},{4,8},{20,16},{8,12},{24,20},{12,0},{28,24},{1,5},{1... | collective-permute-start | bytes 3538952 | tf_op jit(solution)/shard_map/ppermute | solution.py:31
  50.4 16.6 %collective-permute-start.21 = (f32[4,192,384]{2,1,0:T(8,128)S(1)}, f32[4,192,384]{2,1,0:T(8,128)}, u32[]{:S(2)}, u32[]{:S(2)}) collective-permute-start(f32[4,192,384]{2,1,0:T(8,128)S(1)} %pad_maximum_fusion.1.refs_4_), channel_id=1, source_target_pairs={{0,1},{16,19},{1,2},{17,16},{2,3},{18,17},{3,0},{19,18},{4,5},{20,... | collective-permute-start | bytes 3538952 | tf_op jit(solution)/shard_map/ppermute | solution.py:31
  54.7 21.4 %all-to-all-start = ((f32[3,8,32,384]{3,2,0,1:T(8,128)}), f32[3,8,32,384]{3,2,0,1:T(8,128)S(1)}, u32[]{:S(2)}, u32[]{:S(2)}) async-start(f32[3,8,32,384]{3,2,0,1:T(8,128)} %copy.7), calls=%async_computation | async-start | bytes 2359296 | tf_op jit(solution)/shard_map/all_to_all | solution.py:224
  59.5 46.5 %collective-permute-start.27 = (f32[768,384]{1,0:T(8,128)}, f32[768,384]{1,0:T(8,128)}, u32[]{:S(2)}, u32[]{:S(2)}) collective-permute-start(f32[768,384]{1,0:T(8,128)} %refs_8_.1), channel_id=1, source_target_pairs={{0,16},{16,0},{1,17},{17,1},{2,18},{18,2},{3,19},{19,3},{4,20},{20... | collective-permute-start | bytes 3538952 | tf_op jit(solution)/shard_map/ppermute | solution.py:35
  62.2 55.3 %collective-permute-start.26 = (f32[768,384]{1,0:T(8,128)}, f32[768,384]{1,0:T(8,128)}, u32[]{:S(2)}, u32[]{:S(2)}) collective-permute-start(f32[768,384]{1,0:T(8,128)} %collective-permute-done.25.refs_10_), channel_id=1, source_target_pairs={{0,32},{16,112},{32,64},{48,16},{64,96},{80,48},{96,0},{112,80},{1... | collective-permute-start | bytes 3538952 | tf_op jit(solution)/shard_map/ppermute | solution.py:30
  64.3 53.2 %collective-permute-start.16 = (f32[4,192,384]{2,1,0:T(8,128)}, f32[4,192,384]{2,1,0:T(8,128)}, u32[]{:S(2)}, u32[]{:S(2)}) collective-permute-start(f32[4,192,384]{2,1,0:T(8,128)} %collective-permute-done.15.refs_1_), channel_id=1, source_target_pairs={{0,4},{16,28},{4,8},{20,16},{8,12},{24,20},{12,0},{28,24},{1,5},{1... | collective-permute-start | bytes 3538952 | tf_op jit(solution)/shard_map/ppermute | solution.py:31
  67.0 50.6 %collective-permute-start.22 = (f32[4,192,384]{2,1,0:T(8,128)}, f32[4,192,384]{2,1,0:T(8,128)}, u32[]{:S(2)}, u32[]{:S(2)}) collective-permute-start(f32[4,192,384]{2,1,0:T(8,128)} %collective-permute-done.21.refs_5_), channel_id=1, source_target_pairs={{0,1},{16,19},{1,2},{17,16},{2,3},{18,17},{3,0},{19,18},{4,5},{20,... | collective-permute-start | bytes 3538952 | tf_op jit(solution)/shard_map/ppermute | solution.py:31
  95.0 4.1 %collective-permute-start.6 = (f32[24,1536]{1,0:T(8,128)S(1)}, f32[24,1536]{1,0:T(8,128)S(1)}, u32[]{:S(2)}, u32[]{:S(2)}) collective-permute-start(f32[24,1536]{1,0:T(8,128)S(1)} %get-tuple-element.13), channel_id=1, source_target_pairs={{0,4},{16,28},{4,8},{20,16},{8,12},{24,20},{12,0},{28,24},{1,5},{1... | collective-permute-start | bytes 442376 | tf_op jit(solution)/shard_map/ppermute | solution.py:31
  99.0 4.3 %collective-permute-start.7 = (f32[24,1536]{1,0:T(8,128)S(1)}, f32[24,1536]{1,0:T(8,128)S(1)}, u32[]{:S(2)}, u32[]{:S(2)}) collective-permute-start(f32[24,1536]{1,0:T(8,128)S(1)} %collective-permute-done.6), channel_id=1, source_target_pairs={{0,4},{16,28},{4,8},{20,16},{8,12},{24,20},{12,0},{28,24},{1,5},{1... | collective-permute-start | bytes 442376 | tf_op jit(solution)/shard_map/ppermute | solution.py:31
  103.3 7.8 %collective-permute-start.8 = (f32[24,1536]{1,0:T(8,128)S(1)}, f32[24,1536]{1,0:T(8,128)S(1)}, u32[]{:S(2)}, u32[]{:S(2)}) collective-permute-start(f32[24,1536]{1,0:T(8,128)S(1)} %collective-permute-done.7), channel_id=1, source_target_pairs={{0,4},{16,28},{4,8},{20,16},{8,12},{24,20},{12,0},{28,24},{1,5},{1... | collective-permute-start | bytes 442376 | tf_op jit(solution)/shard_map/ppermute | solution.py:31
  106.1 11.8 %collective-permute-start.28 = (f32[768,384]{1,0:T(8,128)}, f32[768,384]{1,0:T(8,128)}, u32[]{:S(2)}, u32[]{:S(2)}) collective-permute-start(f32[768,384]{1,0:T(8,128)} %collective-permute-done.24.refs_9_), channel_id=1, source_target_pairs={{0,16},{16,0},{1,17},{17,1},{2,18},{18,2},{3,19},{19,3},{4,20},{20... | collective-permute-start | bytes 3538952 | tf_op jit(solution)/shard_map/ppermute | solution.py:35
  111.1 9.2 %collective-permute-start.29 = (f32[768,384]{1,0:T(8,128)}, f32[768,384]{1,0:T(8,128)}, u32[]{:S(2)}, u32[]{:S(2)}) collective-permute-start(f32[768,384]{1,0:T(8,128)} %collective-permute-done.25.refs_10_), channel_id=1, source_target_pairs={{0,16},{16,0},{1,17},{17,1},{2,18},{18,2},{3,19},{19,3},{4,20},{20... | collective-permute-start | bytes 3538952 | tf_op jit(solution)/shard_map/ppermute | solution.py:35
  117.5 4.5 %collective-permute-start.30 = (f32[768,384]{1,0:T(8,128)}, f32[768,384]{1,0:T(8,128)}, u32[]{:S(2)}, u32[]{:S(2)}) collective-permute-start(f32[768,384]{1,0:T(8,128)} %collective-permute-done.26.refs_11_), channel_id=1, source_target_pairs={{0,16},{16,0},{1,17},{17,1},{2,18},{18,2},{3,19},{19,3},{4,20},{20... | collective-permute-start | bytes 3538952 | tf_op jit(solution)/shard_map/ppermute | solution.py:35
  117.5 15.7 %collective-permute-start.17 = (f32[4,192,384]{2,1,0:T(8,128)}, f32[4,192,384]{2,1,0:T(8,128)}, u32[]{:S(2)}, u32[]{:S(2)}) collective-permute-start(f32[4,192,384]{2,1,0:T(8,128)} %collective-permute-done.16.refs_2_), channel_id=1, source_target_pairs={{0,4},{16,28},{4,8},{20,16},{8,12},{24,20},{12,0},{28,24},{1,5},{1... | collective-permute-start | bytes 3538952 | tf_op jit(solution)/shard_map/ppermute | solution.py:31
  117.6 15.7 %collective-permute-start.23 = (f32[4,192,384]{2,1,0:T(8,128)}, f32[4,192,384]{2,1,0:T(8,128)}, u32[]{:S(2)}, u32[]{:S(2)}) collective-permute-start(f32[4,192,384]{2,1,0:T(8,128)} %collective-permute-done.22.refs_6_), channel_id=1, source_target_pairs={{0,1},{16,19},{1,2},{17,16},{2,3},{18,17},{3,0},{19,18},{4,5},{20,... | collective-permute-start | bytes 3538952 | tf_op jit(solution)/shard_map/ppermute | solution.py:31
  117.8 15.5 %copy-start.2 = (f32[768,384]{1,0:T(8,128)S(1)}, f32[768,384]{1,0:T(8,128)}, u32[]{:S(2)}) copy-start(f32[768,384]{1,0:T(8,128)} %refs_8_.1) | copy-start | bytes 3538948
  117.9 34.6 %collective-permute-start = (f32[24,1536]{1,0:T(8,128)S(1)}, f32[24,1536]{1,0:T(8,128)S(1)}, u32[]{:S(2)}, u32[]{:S(2)}) collective-permute-start(f32[24,1536]{1,0:T(8,128)S(1)} %get-tuple-element.12), channel_id=1, source_target_pairs={{0,1},{16,19},{1,2},{17,16},{2,3},{18,17},{3,0},{19,18},{4,5},{20,... | collective-permute-start | bytes 442376 | tf_op jit(solution)/shard_map/ppermute | solution.py:31
  120.3 54.6 %collective-permute-start.9 = (f32[4,24,1536]{2,1,0:T(8,128)S(1)}, f32[4,24,1536]{2,1,0:T(8,128)S(1)}, u32[]{:S(2)}, u32[]{:S(2)}) collective-permute-start(f32[4,24,1536]{2,1,0:T(8,128)S(1)} %pad_maximum_fusion.6.refs_4_), channel_id=1, source_target_pairs={{0,1},{16,19},{1,2},{17,16},{2,3},{18,17},{3,0},{19,18},{4,5},{20,... | collective-permute-start | bytes 1769480 | tf_op jit(solution)/shard_map/ppermute | solution.py:31
  148.1 27.7 %collective-permute-start.38 = (f32[384,384]{1,0:T(8,128)S(1)}, f32[384,384]{1,0:T(8,128)S(1)}, u32[]{:S(2)}, u32[]{:S(2)}) collective-permute-start(f32[384,384]{1,0:T(8,128)S(1)} %get-tuple-element.17), channel_id=1, source_target_pairs={{0,0},{1,1},{2,16},{3,17},{4,32},{5,33},{6,48},{7,49},{8,64},{9,65... | collective-permute-start | bytes 1769480 | tf_op jit(solution)/shard_map/ppermute | solution.py:300
  152.5 9.6 %collective-permute-start.1 = (f32[24,1536]{1,0:T(8,128)S(1)}, f32[24,1536]{1,0:T(8,128)S(1)}, u32[]{:S(2)}, u32[]{:S(2)}) collective-permute-start(f32[24,1536]{1,0:T(8,128)S(1)} %collective-permute-done), channel_id=1, source_target_pairs={{0,1},{16,19},{1,2},{17,16},{2,3},{18,17},{3,0},{19,18},{4,5},{20,... | collective-permute-start | bytes 442376 | tf_op jit(solution)/shard_map/ppermute | solution.py:31
  162.1 4.2 %collective-permute-start.2 = (f32[24,1536]{1,0:T(8,128)S(1)}, f32[24,1536]{1,0:T(8,128)S(1)}, u32[]{:S(2)}, u32[]{:S(2)}) collective-permute-start(f32[24,1536]{1,0:T(8,128)S(1)} %collective-permute-done.1), channel_id=1, source_target_pairs={{0,1},{16,19},{1,2},{17,16},{2,3},{18,17},{3,0},{19,18},{4,5},{20,... | collective-permute-start | bytes 442376 | tf_op jit(solution)/shard_map/ppermute | solution.py:31
  166.3 18.4 %collective-permute-start.3 = (f32[4,24,1536]{2,1,0:T(8,128)S(1)}, f32[4,24,1536]{2,1,0:T(8,128)S(1)}, u32[]{:S(2)}, u32[]{:S(2)}) collective-permute-start(f32[4,24,1536]{2,1,0:T(8,128)S(1)} %pad_maximum_fusion.5.refs_0_), channel_id=1, source_target_pairs={{0,4},{16,28},{4,8},{20,16},{8,12},{24,20},{12,0},{28,24},{1,5},{1... | collective-permute-start | bytes 1769480 | tf_op jit(solution)/shard_map/ppermute | solution.py:31
  172.5 15.3 %collective-permute-start.31 = (f32[12,32,384]{2,1,0:T(8,128)S(1)}, f32[12,32,384]{2,1,0:T(8,128)S(1)}, u32[]{:S(2)}, u32[]{:S(2)}) collective-permute-start(f32[12,32,384]{2,1,0:T(8,128)S(1)} %bitcast.83), channel_id=1, source_target_pairs={{0,32},{16,112},{32,64},{48,16},{64,96},{80,48},{96,0},{112,80},{1... | collective-permute-start | bytes 1769480 | tf_op jit(solution)/shard_map/ppermute | solution.py:30
  174.9 17.0 %collective-permute-start.10 = (f32[4,24,1536]{2,1,0:T(8,128)S(1)}, f32[4,24,1536]{2,1,0:T(8,128)S(1)}, u32[]{:S(2)}, u32[]{:S(2)}) collective-permute-start(f32[4,24,1536]{2,1,0:T(8,128)S(1)} %collective-permute-done.9.refs_5_), channel_id=1, source_target_pairs={{0,1},{16,19},{1,2},{17,16},{2,3},{18,17},{3,0},{19,18},{4,5},{20,... | collective-permute-start | bytes 1769480 | tf_op jit(solution)/shard_map/ppermute | solution.py:31
  175.9 12.0 %collective-permute-start.45 = (f32[192,384]{1,0:T(8,128)S(1)}, f32[192,384]{1,0:T(8,128)S(1)}, u32[]{:S(2)}, u32[]{:S(2)}) collective-permute-start(f32[192,384]{1,0:T(8,128)S(1)} %get-tuple-element.20), channel_id=1, source_target_pairs={{0,4},{16,28},{4,8},{20,16},{8,12},{24,20},{12,0},{28,24},{1,5},{1... | collective-permute-start | bytes 884744 | tf_op jit(solution)/shard_map/ppermute | solution.py:31
  176.0 15.9 %collective-permute-start.39 = (f32[192,384]{1,0:T(8,128)S(1)}, f32[192,384]{1,0:T(8,128)S(1)}, u32[]{:S(2)}, u32[]{:S(2)}) collective-permute-start(f32[192,384]{1,0:T(8,128)S(1)} %get-tuple-element.21), channel_id=1, source_target_pairs={{0,1},{16,19},{1,2},{17,16},{2,3},{18,17},{3,0},{19,18},{4,5},{20,... | collective-permute-start | bytes 884744 | tf_op jit(solution)/shard_map/ppermute | solution.py:31
  184.7 16.5 %collective-permute-start.4 = (f32[4,24,1536]{2,1,0:T(8,128)S(1)}, f32[4,24,1536]{2,1,0:T(8,128)S(1)}, u32[]{:S(2)}, u32[]{:S(2)}) collective-permute-start(f32[4,24,1536]{2,1,0:T(8,128)S(1)} %collective-permute-done.3.refs_1_), channel_id=1, source_target_pairs={{0,4},{16,28},{4,8},{20,16},{8,12},{24,20},{12,0},{28,24},{1,5},{1... | collective-permute-start | bytes 1769480 | tf_op jit(solution)/shard_map/ppermute | solution.py:31
  187.8 13.5 %collective-permute-start.32 = (f32[12,32,384]{2,1,0:T(8,128)S(1)}, f32[12,32,384]{2,1,0:T(8,128)S(1)}, u32[]{:S(2)}, u32[]{:S(2)}) collective-permute-start(f32[12,32,384]{2,1,0:T(8,128)S(1)} %collective-permute-done.31.refs_9_), channel_id=1, source_target_pairs={{0,32},{16,112},{32,64},{48,16},{64,96},{80,48},{96,0},{112,80},{1... | collective-permute-start | bytes 1769480 | tf_op jit(solution)/shard_map/ppermute | solution.py:30
  187.9 9.9 %collective-permute-start.46 = (f32[192,384]{1,0:T(8,128)S(1)}, f32[192,384]{1,0:T(8,128)S(1)}, u32[]{:S(2)}, u32[]{:S(2)}) collective-permute-start(f32[192,384]{1,0:T(8,128)S(1)} %collective-permute-done.45), channel_id=1, source_target_pairs={{0,4},{16,28},{4,8},{20,16},{8,12},{24,20},{12,0},{28,24},{1,5},{1... | collective-permute-start | bytes 884744 | tf_op jit(solution)/shard_map/ppermute | solution.py:31
  191.9 9.3 %collective-permute-start.40 = (f32[192,384]{1,0:T(8,128)S(1)}, f32[192,384]{1,0:T(8,128)S(1)}, u32[]{:S(2)}, u32[]{:S(2)}) collective-permute-start(f32[192,384]{1,0:T(8,128)S(1)} %collective-permute-done.39), channel_id=1, source_target_pairs={{0,1},{16,19},{1,2},{17,16},{2,3},{18,17},{3,0},{19,18},{4,5},{20,... | collective-permute-start | bytes 884744 | tf_op jit(solution)/shard_map/ppermute | solution.py:31
  191.9 20.4 %collective-permute-start.11 = (f32[4,24,1536]{2,1,0:T(8,128)S(1)}, f32[4,24,1536]{2,1,0:T(8,128)S(1)}, u32[]{:S(2)}, u32[]{:S(2)}) collective-permute-start(f32[4,24,1536]{2,1,0:T(8,128)S(1)} %collective-permute-done.10.refs_6_), channel_id=1, source_target_pairs={{0,1},{16,19},{1,2},{17,16},{2,3},{18,17},{3,0},{19,18},{4,5},{20,... | collective-permute-start | bytes 1769480 | tf_op jit(solution)/shard_map/ppermute | solution.py:31
  197.8 7.1 %collective-permute-start.47 = (f32[192,384]{1,0:T(8,128)S(1)}, f32[192,384]{1,0:T(8,128)S(1)}, u32[]{:S(2)}, u32[]{:S(2)}) collective-permute-start(f32[192,384]{1,0:T(8,128)S(1)} %collective-permute-done.46), channel_id=1, source_target_pairs={{0,4},{16,28},{4,8},{20,16},{8,12},{24,20},{12,0},{28,24},{1,5},{1... | collective-permute-start | bytes 884744 | tf_op jit(solution)/shard_map/ppermute | solution.py:31
  201.2 8.0 %collective-permute-start.41 = (f32[192,384]{1,0:T(8,128)S(1)}, f32[192,384]{1,0:T(8,128)S(1)}, u32[]{:S(2)}, u32[]{:S(2)}) collective-permute-start(f32[192,384]{1,0:T(8,128)S(1)} %collective-permute-done.40), channel_id=1, source_target_pairs={{0,1},{16,19},{1,2},{17,16},{2,3},{18,17},{3,0},{19,18},{4,5},{20,... | collective-permute-start | bytes 884744 | tf_op jit(solution)/shard_map/ppermute | solution.py:31
  201.2 14.1 %collective-permute-start.5 = (f32[4,24,1536]{2,1,0:T(8,128)S(1)}, f32[4,24,1536]{2,1,0:T(8,128)S(1)}, u32[]{:S(2)}, u32[]{:S(2)}) collective-permute-start(f32[4,24,1536]{2,1,0:T(8,128)S(1)} %collective-permute-done.4.refs_2_), channel_id=1, source_target_pairs={{0,4},{16,28},{4,8},{20,16},{8,12},{24,20},{12,0},{28,24},{1,5},{1... | collective-permute-start | bytes 1769480 | tf_op jit(solution)/shard_map/ppermute | solution.py:31
  201.3 15.8 %collective-permute-start.34 = (f32[12,32,384]{2,1,0:T(8,128)S(1)}, f32[12,32,384]{2,1,0:T(8,128)S(1)}, u32[]{:S(2)}, u32[]{:S(2)}) collective-permute-start(f32[12,32,384]{2,1,0:T(8,128)S(1)} %bitcast.84), channel_id=1, source_target_pairs={{0,16},{16,0},{1,17},{17,1},{2,18},{18,2},{3,19},{19,3},{4,20},{20... | collective-permute-start | bytes 1769480 | tf_op jit(solution)/shard_map/ppermute | solution.py:35
  204.9 12.2 %collective-permute-start.33 = (f32[12,32,384]{2,1,0:T(8,128)S(1)}, f32[12,32,384]{2,1,0:T(8,128)S(1)}, u32[]{:S(2)}, u32[]{:S(2)}) collective-permute-start(f32[12,32,384]{2,1,0:T(8,128)S(1)} %collective-permute-done.32.refs_10_), channel_id=1, source_target_pairs={{0,32},{16,112},{32,64},{48,16},{64,96},{80,48},{96,0},{112,80},{1... | collective-permute-start | bytes 1769480 | tf_op jit(solution)/shard_map/ppermute | solution.py:30
  209.3 27.5 %collective-permute-start.48 = (f32[4,192,384]{2,1,0:T(8,128)S(1)}, f32[4,192,384]{2,1,0:T(8,128)S(1)}, u32[]{:S(2)}, u32[]{:S(2)}) collective-permute-start(f32[4,192,384]{2,1,0:T(8,128)S(1)} %pad_maximum_fusion.3.refs_4_), channel_id=1, source_target_pairs={{0,1},{16,19},{1,2},{17,16},{2,3},{18,17},{3,0},{19,18},{4,5},{20,... | collective-permute-start | bytes 3538952 | tf_op jit(solution)/shard_map/ppermute | solution.py:31
  212.3 24.4 %collective-permute-start.42 = (f32[4,192,384]{2,1,0:T(8,128)S(1)}, f32[4,192,384]{2,1,0:T(8,128)S(1)}, u32[]{:S(2)}, u32[]{:S(2)}) collective-permute-start(f32[4,192,384]{2,1,0:T(8,128)S(1)} %pad_maximum_fusion.2.refs_0_), channel_id=1, source_target_pairs={{0,4},{16,28},{4,8},{20,16},{8,12},{24,20},{12,0},{28,24},{1,5},{1... | collective-permute-start | bytes 3538952 | tf_op jit(solution)/shard_map/ppermute | solution.py:31
  215.3 9.7 %collective-permute-start.35 = (f32[12,32,384]{2,1,0:T(8,128)S(1)}, f32[12,32,384]{2,1,0:T(8,128)S(1)}, u32[]{:S(2)}, u32[]{:S(2)}) collective-permute-start(f32[12,32,384]{2,1,0:T(8,128)S(1)} %collective-permute-done.31.refs_9_), channel_id=1, source_target_pairs={{0,16},{16,0},{1,17},{17,1},{2,18},{18,2},{3,19},{19,3},{4,20},{20... | collective-permute-start | bytes 1769480 | tf_op jit(solution)/shard_map/ppermute | solution.py:35
  217.1 7.9 %collective-permute-start.36 = (f32[12,32,384]{2,1,0:T(8,128)S(1)}, f32[12,32,384]{2,1,0:T(8,128)S(1)}, u32[]{:S(2)}, u32[]{:S(2)}) collective-permute-start(f32[12,32,384]{2,1,0:T(8,128)S(1)} %collective-permute-done.32.refs_10_), channel_id=1, source_target_pairs={{0,16},{16,0},{1,17},{17,1},{2,18},{18,2},{3,19},{19,3},{4,20},{20... | collective-permute-start | bytes 1769480 | tf_op jit(solution)/shard_map/ppermute | solution.py:35
  217.1 9.5 %collective-permute-start.37 = (f32[12,32,384]{2,1,0:T(8,128)S(1)}, f32[12,32,384]{2,1,0:T(8,128)S(1)}, u32[]{:S(2)}, u32[]{:S(2)}) collective-permute-start(f32[12,32,384]{2,1,0:T(8,128)S(1)} %collective-permute-done.33.refs_11_), channel_id=1, source_target_pairs={{0,16},{16,0},{1,17},{17,1},{2,18},{18,2},{3,19},{19,3},{4,20},{20... | collective-permute-start | bytes 1769480 | tf_op jit(solution)/shard_map/ppermute | solution.py:35
  234.9 9.2 %collective-permute-start.51 = (f32[384,384]{1,0:T(8,128)S(1)}, f32[384,384]{1,0:T(8,128)S(1)}, u32[]{:S(2)}, u32[]{:S(2)}) collective-permute-start(f32[384,384]{1,0:T(8,128)S(1)} %cross.1.refs_8_), channel_id=1, source_target_pairs={{0,32},{16,112},{32,64},{48,16},{64,96},{80,48},{96,0},{112,80},{1... | collective-permute-start | bytes 1769480 | tf_op jit(solution)/shard_map/ppermute | solution.py:30
  236.7 22.3 %copy-start.4 = (f32[4,192,384]{2,1,0:T(8,128)}, f32[4,192,384]{2,1,0:T(8,128)S(1)}, u32[]{:S(2)}) copy-start(f32[4,192,384]{2,1,0:T(8,128)S(1)} %collective-permute-done.48.refs_5_) | copy-start | bytes 3538948
  236.7 20.4 %collective-permute-start.49 = (f32[4,192,384]{2,1,0:T(8,128)S(1)}, f32[4,192,384]{2,1,0:T(8,128)}, u32[]{:S(2)}, u32[]{:S(2)}) collective-permute-start(f32[4,192,384]{2,1,0:T(8,128)S(1)} %collective-permute-done.48.refs_5_), channel_id=1, source_target_pairs={{0,1},{16,19},{1,2},{17,16},{2,3},{18,17},{3,0},{19,18},{4,5},{20,... | collective-permute-start | bytes 3538952 | tf_op jit(solution)/shard_map/ppermute | solution.py:31
  236.8 20.6 %collective-permute-start.43 = (f32[4,192,384]{2,1,0:T(8,128)S(1)}, f32[4,192,384]{2,1,0:T(8,128)}, u32[]{:S(2)}, u32[]{:S(2)}) collective-permute-start(f32[4,192,384]{2,1,0:T(8,128)S(1)} %collective-permute-done.42.refs_1_), channel_id=1, source_target_pairs={{0,4},{16,28},{4,8},{20,16},{8,12},{24,20},{12,0},{28,24},{1,5},{1... | collective-permute-start | bytes 3538952 | tf_op jit(solution)/shard_map/ppermute | solution.py:31
  244.1 9.8 %collective-permute-start.52 = (f32[384,384]{1,0:T(8,128)S(1)}, f32[384,384]{1,0:T(8,128)}, u32[]{:S(2)}, u32[]{:S(2)}) collective-permute-start(f32[384,384]{1,0:T(8,128)S(1)} %collective-permute-done.51.refs_9_), channel_id=1, source_target_pairs={{0,32},{16,112},{32,64},{48,16},{64,96},{80,48},{96,0},{112,80},{1... | collective-permute-start | bytes 1769480 | tf_op jit(solution)/shard_map/ppermute | solution.py:30
  247.1 16.9 %collective-permute-start.54 = (f32[384,384]{1,0:T(8,128)S(1)}, f32[384,384]{1,0:T(8,128)}, u32[]{:S(2)}, u32[]{:S(2)}) collective-permute-start(f32[384,384]{1,0:T(8,128)S(1)} %cross.1.refs_8_), channel_id=1, source_target_pairs={{0,16},{16,0},{1,17},{17,1},{2,18},{18,2},{3,19},{19,3},{4,20},{20... | collective-permute-start | bytes 1769480 | tf_op jit(solution)/shard_map/ppermute | solution.py:35
  253.9 10.6 %collective-permute-start.53 = (f32[384,384]{1,0:T(8,128)}, f32[384,384]{1,0:T(8,128)}, u32[]{:S(2)}, u32[]{:S(2)}) collective-permute-start(f32[384,384]{1,0:T(8,128)} %collective-permute-done.52.refs_10_), channel_id=1, source_target_pairs={{0,32},{16,112},{32,64},{48,16},{64,96},{80,48},{96,0},{112,80},{1... | collective-permute-start | bytes 1769480 | tf_op jit(solution)/shard_map/ppermute | solution.py:30
  257.1 26.0 %collective-permute-start.50 = (f32[4,192,384]{2,1,0:T(8,128)}, f32[4,192,384]{2,1,0:T(8,128)}, u32[]{:S(2)}, u32[]{:S(2)}) collective-permute-start(f32[4,192,384]{2,1,0:T(8,128)} %collective-permute-done.49.refs_6_), channel_id=1, source_target_pairs={{0,1},{16,19},{1,2},{17,16},{2,3},{18,17},{3,0},{19,18},{4,5},{20,... | collective-permute-start | bytes 3538952 | tf_op jit(solution)/shard_map/ppermute | solution.py:31
  257.3 25.8 %collective-permute-start.44 = (f32[4,192,384]{2,1,0:T(8,128)}, f32[4,192,384]{2,1,0:T(8,128)}, u32[]{:S(2)}, u32[]{:S(2)}) collective-permute-start(f32[4,192,384]{2,1,0:T(8,128)} %collective-permute-done.43.refs_2_), channel_id=1, source_target_pairs={{0,4},{16,28},{4,8},{20,16},{8,12},{24,20},{12,0},{28,24},{1,5},{1... | collective-permute-start | bytes 3538952 | tf_op jit(solution)/shard_map/ppermute | solution.py:31
  259.0 21.6 %all-to-all-start.3 = ((f32[8,3,32,384]{3,2,1,0:T(8,128)}), f32[8,3,32,384]{3,2,1,0:T(8,128)}, u32[]{:S(2)}, u32[]{:S(2)}) async-start(f32[8,3,32,384]{3,2,1,0:T(8,128)} %bitcast.55), calls=%async_computation.3 | async-start | bytes 2359296 | tf_op jit(solution)/shard_map/all_to_all | solution.py:309
  264.0 19.2 %collective-permute-start.55 = (f32[384,384]{1,0:T(8,128)S(1)}, f32[384,384]{1,0:T(8,128)}, u32[]{:S(2)}, u32[]{:S(2)}) collective-permute-start(f32[384,384]{1,0:T(8,128)S(1)} %collective-permute-done.51.refs_9_), channel_id=1, source_target_pairs={{0,16},{16,0},{1,17},{17,1},{2,18},{18,2},{3,19},{19,3},{4,20},{20... | collective-permute-start | bytes 1769480 | tf_op jit(solution)/shard_map/ppermute | solution.py:35
  264.0 19.2 %collective-permute-start.56 = (f32[384,384]{1,0:T(8,128)}, f32[384,384]{1,0:T(8,128)}, u32[]{:S(2)}, u32[]{:S(2)}) collective-permute-start(f32[384,384]{1,0:T(8,128)} %collective-permute-done.52.refs_10_), channel_id=1, source_target_pairs={{0,16},{16,0},{1,17},{17,1},{2,18},{18,2},{3,19},{19,3},{4,20},{20... | collective-permute-start | bytes 1769480 | tf_op jit(solution)/shard_map/ppermute | solution.py:35
  264.5 18.7 %collective-permute-start.57 = (f32[384,384]{1,0:T(8,128)}, f32[384,384]{1,0:T(8,128)}, u32[]{:S(2)}, u32[]{:S(2)}) collective-permute-start(f32[384,384]{1,0:T(8,128)} %collective-permute-done.53.refs_11_), channel_id=1, source_target_pairs={{0,16},{16,0},{1,17},{17,1},{2,18},{18,2},{3,19},{19,3},{4,20},{20... | collective-permute-start | bytes 1769480 | tf_op jit(solution)/shard_map/ppermute | solution.py:35
  (6 other events, 16.8 us)

commit v3 on v2

--- a/solution.py
+++ b/solution.py
@@ -35,22 +35,48 @@
     return lax.ppermute(x, "core", [(0, 1), (1, 0)])
 
 
-def ring(x, axis):
+def after(x, *others):
+    return lax.optimization_barrier((x, *others))[0]
+
+
+def ring(x, axis, gates=((), (), ())):
     out = [x]
-    for _ in range(3):
-        out.append(step(out[-1], axis))
+    for gate in gates:
+        out.append(step(after(out[-1], *gate) if gate else out[-1], axis))
     return out
 
 
-def gather_rows(x):
-    mine = ring(x, "y")
+def gather_rows(x, gates=((), (), ())):
+    mine = ring(x, "y", gates)
     return mine + [swap(t) for t in mine]
 
 
-def gather_cols(a, b):
-    first = jnp.stack(ring(a, "x"))
-    second = jnp.stack(ring(b, "z"))
-    return ring(first, "z") + ring(second, "x")
+def first_axis(a, b, gates=((), (), ())):
+    return jnp.stack(ring(a, "x", gates)), jnp.stack(ring(b, "z", gates))
+
+
+def second_axis(first, second, gates=((), (), ())):
+    return ring(first, "z", gates) + ring(second, "x", gates)
+
+
+def gather_cols(a, b, gates=((), (), ())):
+    return second_axis(*first_axis(a, b, gates))
+
+
+def deal_cols(x, gate):
+    x = x.reshape(4, 4, -1, x.shape[1])
+    at = lax.axis_index("x")
+    out = [lax.dynamic_index_in_dim(x, at, 1, False)]
+    for k in range(1, 4):
+        part = lax.dynamic_index_in_dim(x, lax.rem(at + k, 4), 1, False)
+        out.append(lax.ppermute(part, "x", [(i, (i + k) % 4) for i in range(4)]))
+    x = after(jnp.stack(out, axis=1), *gate)
+    at = lax.axis_index("z")
+    out = [lax.dynamic_index_in_dim(x, at, 0, False)]
+    for k in range(1, 4):
+        part = lax.dynamic_index_in_dim(x, lax.rem(at + k, 4), 0, False)
+        out.append(lax.ppermute(part, "z", [(i, (i + k) % 4) for i in range(4)]))
+    return jnp.stack(out)
 
 
 def places():
@@ -244,26 +270,30 @@
     return a.reshape(-1, w), b.reshape(-1, w)
 
 
-def pick_cols_kernel(anc, x, a, b):
+def pick_cols_kernel(anc, at, x, a, b):
     for out, first in ((a, 0), (b, NANC // 2)):
         for i in range(NANC // 2):
             for k in range(2):
                 t = 2 * anc[first + i] + k
                 off = pl.multiple_of(lax.rem(t, 3) * 128, 128)
-                out[:, pl.ds(i * 256 + k * 128, 128)] = x[lax.div(t, 3), :, pl.ds(off, 128)]
+                c = lax.div(t, 3)
+                back_z = lax.rem(at[0] - lax.div(c, 4) + 4, 4)
+                back_x = lax.rem(at[1] - lax.rem(c, 4) + 4, 4)
+                out[:, pl.ds(i * 256 + k * 128, 128)] = x[back_z, back_x, :, pl.ds(off, 128)]
 
 
 def pick_cols(ancestors, x):
-    q = x.shape[1]
+    q = x.shape[2]
+    at = jnp.stack([lax.axis_index(n) for n in COL]).astype(jnp.int32)
     out = jax.ShapeDtypeStruct((q, NANC * 128), F32)
     return pl.pallas_call(
         pick_cols_kernel,
         out_shape=(out, out),
-        in_specs=[SMEM, VMEM],
+        in_specs=[SMEM, SMEM, VMEM],
         out_specs=(VMEM, VMEM),
         compiler_params=params(8),
         name="pick_cols",
-    )(ancestors, x)
+    )(ancestors, at, x)
 
 
 def place_kernel(anc, x, out):
@@ -289,15 +319,17 @@
     sub = h // 24
     at = places()
 
-    f_pieces = gather_cols(*pick_rows(ancestors, spread(factor_cross)))
-    inverse_tiles = gather_rows(factor_inverse)
-
-    s_rows = jnp.concatenate(pick_rows(ancestors, spread(sigma_top)))
-    s_cols = lax.all_to_all(s_rows.reshape(16, -1, w), COL, 0, 0, tiled=True)
-    s_pieces = gather_cols(*pick_cols(ancestors, s_cols))
+    f_once = first_axis(*pick_rows(ancestors, spread(factor_cross)))
+    f_pieces = second_axis(*f_once)
+    inverse_tiles = gather_rows(factor_inverse, ((), (), (f_pieces[1], f_pieces[5])))
+
+    s_rows = jnp.concatenate(pick_rows(ancestors, spread(after(sigma_top, *f_once))))
+    s_cols = deal_cols(after(s_rows, f_pieces[1], f_pieces[5]), (f_pieces[2], f_pieces[6]))
+    s_once = first_axis(*pick_cols(ancestors, s_cols))
 
     u, ut = update_product(at, f_pieces, inverse_tiles)
     moved = lax.ppermute(ut, ALL, [(16 * r + c, 16 * (c // 2) + 2 * r + c % 2) for r in range(8) for c in range(16)])
+    s_pieces = second_axis(*s_once)
     u_pieces = gather_cols(moved[: w // 2], moved[w // 2 :])
     u_tiles = gather_rows(u.reshape(NANC, sub, w))
 

time: 299 us -> 306 us (1.023)
  waiting for transfers between devices: 87.5 us -> 95.8 us
  starting transfers between devices: 143 us -> 137 us
  blocking collectives: 17.6 us -> 22.4 us
    ppermute x12, starting transfers between devices: 30.8 us -> 17 us  [swap(): return lax.ppermute(x, 'core', [(0, 1), (1, 0)])]
    all_to_all x2 -> x1, waiting for transfers between devices: 19.9 us -> 6.48 us  [spread(): lax.all_to_all(x.reshape(3, 8, sub, w), ROW, 1, 0, tiled=True)]
    ppermute x9, starting transfers between devices: 20.2 us -> 10.5 us  [step(): lax.ppermute(x, ROW, [(2 * i + c, 2 * ((i + 1 - 2 * c) % 4) + c) for i in...]
    ppermute x0 -> x6, starting transfers between devices: none -> 8.8 us  [the longest x3 5.15 us: deal_cols(): out.append(lax.ppermute(part, 'z', [(i, (i + k) % 4) for i in range(4)]))]
    ppermute x36, waiting for transfers between devices: 37 us -> 45.6 us  [step(): lax.ppermute(x, ('core', axis), [(4 * c + i, 4 * c + (i + 1 - 2 * c) % 4)...]
    ppermute x36, starting transfers between devices: 71.7 us -> 80.2 us  [step(): lax.ppermute(x, ('core', axis), [(4 * c + i, 4 * c + (i + 1 - 2 * c) % 4)...]
    ppermute x9, waiting for transfers between devices: 15.3 us -> 22.8 us  [step(): lax.ppermute(x, ROW, [(2 * i + c, 2 * ((i + 1 - 2 * c) % 4) + c) for i in...]
    all_to_all x2 -> x1, starting transfers between devices: 10.9 us -> 5.23 us  [spread(): lax.all_to_all(x.reshape(3, 8, sub, w), ROW, 1, 0, tiled=True)]
  transfers between devices with their start and end apart: 61 -> 66, of which waited for: 20 -> 25; matrix products, arithmetic and copies ran while one was open for 1% -> 2% of each run, Pallas kernels for 9% -> 9%
where the time goes in v3:
time: 306 us; the launch traced here: 305 us
  starting transfers between devices  137 us (45%)
  waiting for transfers between devices  95.8 us (31%)
  Pallas kernels  40.8 us (13%)
  blocking collectives  22.4 us (7%)
  local copies, waits for them, and re-layouts  7.58 us (2%)
    ppermute x36, starting transfers between devices, step(): lax.ppermute(x, ('core', axis), [(4 * c + i, 4 * c + (i + 1 - 2 * c) % 4)...  80.2 us
    ppermute x36, waiting for transfers between devices, step(): lax.ppermute(x, ('core', axis), [(4 * c + i, 4 * c + (i + 1 - 2 * c) % 4)...  45.6 us
    ppermute x9, waiting for transfers between devices, step(): lax.ppermute(x, ROW, [(2 * i + c, 2 * ((i + 1 - 2 * c) % 4) + c) for i in...  22.8 us
    all_to_all x1, blocking collectives, spread(): lax.all_to_all(x.reshape(3, 8, sub, w), ROW, 1, 0, tiled=True)  22.4 us
    ppermute x12, starting transfers between devices, swap(): return lax.ppermute(x, 'core', [(0, 1), (1, 0)])  17 us
    pallas_call x1, Pallas kernels, update_product(): pl.pallas_call(update_kernel, out_shape=(out, jax.ShapeDtypeStruct((w, m)...  14.9 us
    pallas_call x1, Pallas kernels, child_product(): pl.pallas_call(child_kernel, out_shape=jax.ShapeDtypeStruct((h, w), F32),...  14 us
    all_to_all x1, waiting for transfers between devices, per_device(): back = lax.all_to_all(full.reshape(8, 3, sub, w), ROW, 0, 0, tiled=True)  13.6 us
  transfers between devices with their start and end apart: 66, of which 25 were waited for; matrix products, arithmetic and copies ran while one was open for 2% of the time, Pallas kernels for 9%

profile of v3, /device:TPU:1, one launch (start us, length us, event | category | flops | bytes accessed | tf_op | source)
XLA Modules:
  0.0 305.1 jit_solution(382769111734224108)
XLA Ops:
  2.0 22.4 %all_to_all.35 = f32[3,8,32,384]{3,2,0,1:T(8,128)S(1)} all-to-all(f32[3,8,32,384]{3,2,0,1:T(8,128)S(1)} %copy.7), channel_id=1, replica_groups=mesh['y'=4,'core'=2,'z'=4,'x'=4] {'y','core'}, dimensions={1} | all-to-all | bytes 2359296 | tf_op jit(solution)/shard_map/all_to_all | solution.py:250
  25.0 3.8 %collective-permute-start.3 = (f32[192,384]{1,0:T(8,128)S(1)}, f32[192,384]{1,0:T(8,128)S(1)}, u32[]{:S(2)}, u32[]{:S(2)}) collective-permute-start(f32[192,384]{1,0:T(8,128)S(1)} %bitcast.97), channel_id=1, source_target_pairs={{0,4},{16,28},{4,8},{20,16},{8,12},{24,20},{12,0},{28,24},{1,5},{1... | collective-permute-start | bytes 884744 | tf_op jit(solution)/shard_map/ppermute | solution.py:31
  28.8 2.5 collective-permute-start
  32.5 3.4 %collective-permute-start.4 = (f32[192,384]{1,0:T(8,128)S(1)}, f32[192,384]{1,0:T(8,128)S(1)}, u32[]{:S(2)}, u32[]{:S(2)}) collective-permute-start(f32[192,384]{1,0:T(8,128)S(1)} %collective-permute-done.3), channel_id=1, source_target_pairs={{0,4},{16,28},{4,8},{20,16},{8,12},{24,20},{12,0},{28,24},{1,5},{1... | collective-permute-start | bytes 884744 | tf_op jit(solution)/shard_map/ppermute | solution.py:31
  35.9 2.2 collective-permute-start.1
  38.1 1.5 collective-permute-done.4
  39.6 3.4 %collective-permute-start.5 = (f32[192,384]{1,0:T(8,128)S(1)}, f32[192,384]{1,0:T(8,128)S(1)}, u32[]{:S(2)}, u32[]{:S(2)}) collective-permute-start(f32[192,384]{1,0:T(8,128)S(1)} %collective-permute-done.4), channel_id=1, source_target_pairs={{0,4},{16,28},{4,8},{20,16},{8,12},{24,20},{12,0},{28,24},{1,5},{1... | collective-permute-start | bytes 884744 | tf_op jit(solution)/shard_map/ppermute | solution.py:31
  43.0 1.9 collective-permute-start.2
  46.7 2.0 collective-permute-start.7
  49.0 2.9 collective-permute-start.6
  53.1 5.2 %all-to-all-start.1 = ((f32[3,8,32,384]{3,2,0,1:T(8,128)}), f32[3,8,32,384]{3,2,0,1:T(8,128)S(1)}, u32[]{:S(2)}, u32[]{:S(2)}) async-start(f32[3,8,32,384]{3,2,0,1:T(8,128)} %copy.8), calls=%async_computation.1 | async-start | bytes 2359296 | tf_op jit(solution)/shard_map/all_to_all | solution.py:250
  58.3 2.3 collective-permute-done.30.refs_9_
  60.5 2.1 collective-permute-start.31
  62.6 2.7 collective-permute-start.12
  65.4 3.0 collective-permute-start.11
  68.4 6.5 %all-to-all-done.1 = f32[3,8,32,384]{3,2,0,1:T(8,128)S(1)} async-done(((f32[3,8,32,384]{3,2,0,1:T(8,128)}), f32[3,8,32,384]{3,2,0,1:T(8,128)S(1)}, u32[]{:S(2)}, u32[]{:S(2)}) %all-to-all-start.1) | async-done | bytes 1179680 | tf_op jit(solution)/shard_map/all_to_all | solution.py:250
  76.6 1.4 collective-permute-start.9
  78.0 8.6 %collective-permute-done.31.refs_10_ = f32[768,384]{1,0:T(8,128)} collective-permute-done((f32[768,384]{1,0:T(8,128)}, f32[768,384]{1,0:T(8,128)}, u32[]{:S(2)}, u32[]{:S(2)}) %collective-permute-start.31) | collective-permute-done | bytes 1179680 | tf_op jit(solution)/shard_map/ppermute | solution.py:30
  86.6 1.6 collective-permute-start.33
  90.0 2.8 collective-permute-done.10
  92.9 1.8 collective-permute-start.13
  94.7 1.8 collective-permute-start.14
  96.5 1.5 collective-permute-start.15
  98.6 2.3 collective-permute-done.14
  101.8 2.8 collective-permute-start.22
  104.6 3.3 %collective-permute-done.22 = f32[24,1536]{1,0:T(8,128)S(1)} collective-permute-done((f32[24,1536]{1,0:T(8,128)S(1)}, f32[24,1536]{1,0:T(8,128)S(1)}, u32[]{:S(2)}, u32[]{:S(2)}) %collective-permute-start.22) | collective-permute-done | bytes 147488 | tf_op jit(solution)/shard_map/ppermute | solution.py:31
  107.9 2.3 collective-permute-start.23
  110.1 2.1 collective-permute-done.23
  112.2 3.1 %collective-permute-start.24 = (f32[24,1536]{1,0:T(8,128)S(1)}, f32[24,1536]{1,0:T(8,128)S(1)}, u32[]{:S(2)}, u32[]{:S(2)}) collective-permute-start(f32[24,1536]{1,0:T(8,128)S(1)} %collective-permute-done.23), channel_id=1, source_target_pairs={{0,4},{16,28},{4,8},{20,16},{8,12},{24,20},{12,0},{28,24},{1,5},{1... | collective-permute-start | bytes 442376 | tf_op jit(solution)/shard_map/ppermute | solution.py:31
  115.3 6.8 %collective-permute-start.34 = (f32[768,384]{1,0:T(8,128)}, f32[768,384]{1,0:T(8,128)}, u32[]{:S(2)}, u32[]{:S(2)}) collective-permute-start(f32[768,384]{1,0:T(8,128)} %collective-permute-done.30.refs_9_), channel_id=1, source_target_pairs={{0,16},{16,0},{1,17},{17,1},{2,18},{18,2},{3,19},{19,3},{4,20},{20... | collective-permute-start | bytes 3538952 | tf_op jit(solution)/shard_map/ppermute | solution.py:35
  122.7 3.0 collective-permute-start.28
  125.8 3.1 %collective-permute-start.16 = (f32[24,1536]{1,0:T(8,128)S(1)}, f32[24,1536]{1,0:T(8,128)S(1)}, u32[]{:S(2)}, u32[]{:S(2)}) collective-permute-start(f32[24,1536]{1,0:T(8,128)S(1)} %get-tuple-element.21), channel_id=1, source_target_pairs={{0,1},{16,19},{1,2},{17,16},{2,3},{18,17},{3,0},{19,18},{4,5},{20,... | collective-permute-start | bytes 442376 | tf_op jit(solution)/shard_map/ppermute | solution.py:31
  129.1 8.7 %collective-permute-done.29.refs_7_ = f32[4,192,384]{2,1,0:T(8,128)} collective-permute-done((f32[4,192,384]{2,1,0:T(8,128)}, f32[4,192,384]{2,1,0:T(8,128)}, u32[]{:S(2)}, u32[]{:S(2)}) %collective-permute-start.29) | collective-permute-done | bytes 1179680 | tf_op jit(solution)/shard_map/ppermute | solution.py:31
  139.1 14.9 %update.1 = (f32[384,384]{1,0:T(8,128)S(1)}, f32[384,384]{1,0:T(8,128)S(1)}) custom-call(s32[40]{0:T(128)S(1)} %stack.234.at, f32[4,192,384]{2,1,0:T(8,128)S(1)} %pad_maximum_fusion.refs_0_, f32[4,192,384]{2,1,0:T(8,128)} %collective-permute-done.6.refs_1_, f32[4,192,384]{2,1,0:T(8,128)} %collective-permute-done.11.refs_2_, ...), custom_call_target="tpu_custom_call" | custom-call | flops 5435817984 | bytes 18874368 | tf_op jit(solution)/shard_map/update/pallas_call | solution.py:140
  154.0 8.6 %collective-permute-start.44 = (f32[384,384]{1,0:T(8,128)S(1)}, f32[384,384]{1,0:T(8,128)S(1)}, u32[]{:S(2)}, u32[]{:S(2)}) collective-permute-start(f32[384,384]{1,0:T(8,128)S(1)} %get-tuple-element.25), channel_id=1, source_target_pairs={{0,0},{1,1},{2,16},{3,17},{4,32},{5,33},{6,48},{7,49},{8,64},{9,65... | collective-permute-start | bytes 1769480 | tf_op jit(solution)/shard_map/ppermute | solution.py:331
  162.7 10.4 %collective-permute-done.17 = f32[24,1536]{1,0:T(8,128)S(1)} collective-permute-done((f32[24,1536]{1,0:T(8,128)S(1)}, f32[24,1536]{1,0:T(8,128)S(1)}, u32[]{:S(2)}, u32[]{:S(2)}) %collective-permute-start.17) | collective-permute-done | bytes 147488 | tf_op jit(solution)/shard_map/ppermute | solution.py:31
  174.2 3.2 %collective-permute-done.18 = f32[24,1536]{1,0:T(8,128)S(1)} collective-permute-done((f32[24,1536]{1,0:T(8,128)S(1)}, f32[24,1536]{1,0:T(8,128)S(1)}, u32[]{:S(2)}, u32[]{:S(2)}) %collective-permute-start.18) | collective-permute-done | bytes 147488 | tf_op jit(solution)/shard_map/ppermute | solution.py:31
  177.4 8.6 %collective-permute-start.19 = (f32[4,24,1536]{2,1,0:T(8,128)S(1)}, f32[4,24,1536]{2,1,0:T(8,128)S(1)}, u32[]{:S(2)}, u32[]{:S(2)}) collective-permute-start(f32[4,24,1536]{2,1,0:T(8,128)S(1)} %pad_maximum_fusion.7.refs_0_), channel_id=1, source_target_pairs={{0,4},{16,28},{4,8},{20,16},{8,12},{24,20},{12,0},{28,24},{1,5},{1... | collective-permute-start | bytes 1769480 | tf_op jit(solution)/shard_map/ppermute | solution.py:31
  187.8 9.3 %collective-permute-start.45 = (f32[192,384]{1,0:T(8,128)S(1)}, f32[192,384]{1,0:T(8,128)S(1)}, u32[]{:S(2)}, u32[]{:S(2)}) collective-permute-start(f32[192,384]{1,0:T(8,128)S(1)} %get-tuple-element.29), channel_id=1, source_target_pairs={{0,1},{16,19},{1,2},{17,16},{2,3},{18,17},{3,0},{19,18},{4,5},{20,... | collective-permute-start | bytes 884744 | tf_op jit(solution)/shard_map/ppermute | solution.py:31
  197.2 1.7 collective-permute-start.20
  198.9 2.9 collective-permute-start.52
  201.8 2.5 collective-permute-start.46
  204.3 5.1 %collective-permute-done.52 = f32[192,384]{1,0:T(8,128)S(1)} collective-permute-done((f32[192,384]{1,0:T(8,128)S(1)}, f32[192,384]{1,0:T(8,128)S(1)}, u32[]{:S(2)}, u32[]{:S(2)}) %collective-permute-start.52) | collective-permute-done | bytes 294944 | tf_op jit(solution)/shard_map/ppermute | solution.py:31
  209.4 2.6 collective-permute-start.53
  212.0 1.4 collective-permute-start.47
  213.5 2.1 collective-permute-done.53
  215.8 2.1 collective-permute-done.47
  217.9 2.6 collective-permute-start.54
  220.7 3.5 %collective-permute-done.27.refs_7_ = f32[4,24,1536]{2,1,0:T(8,128)S(1)} collective-permute-done((f32[4,24,1536]{2,1,0:T(8,128)S(1)}, f32[4,24,1536]{2,1,0:T(8,128)S(1)}, u32[]{:S(2)}, u32[]{:S(2)}) %collective-permute-start.27) | collective-permute-done | bytes 589856 | tf_op jit(solution)/shard_map/ppermute | solution.py:31
  224.2 1.5 collective-permute-start.41
  225.7 3.5 %collective-permute-start.43 = (f32[12,32,384]{2,1,0:T(8,128)S(1)}, f32[12,32,384]{2,1,0:T(8,128)S(1)}, u32[]{:S(2)}, u32[]{:S(2)}) collective-permute-start(f32[12,32,384]{2,1,0:T(8,128)S(1)} %collective-permute-done.39.refs_11_), channel_id=1, source_target_pairs={{0,16},{16,0},{1,17},{17,1},{2,18},{18,2},{3,19},{19,3},{4,20},{20... | collective-permute-start | bytes 1769480 | tf_op jit(solution)/shard_map/ppermute | solution.py:35
  229.2 1.6 collective-permute-done.43.refs_15_
  230.8 8.3 %cross.1.refs_8_ = f32[384,384]{1,0:T(8,128)S(1)} custom-call(s32[40]{0:T(128)S(1)} %stack.234.at, f32[4,24,1536]{2,1,0:T(8,128)S(1)} %pad_maximum_fusion.7.refs_0_, f32[4,24,1536]{2,1,0:T(8,128)S(1)} %collective-permute-done.19.refs_1_, f32[4,24,1536]{2,1,0:T(8,128)S(1)} %collective-permute-done.20.refs_2_, ...), custom_call_target="tpu_custom_call" | custom-call | flops 2717908992 | bytes 9437184 | tf_op jit(solution)/shard_map/cross/pallas_call | solution.py:189
  240.5 1.8 collective-permute-start.49
  243.3 5.2 %collective-permute-done.57.refs_9_ = f32[384,384]{1,0:T(8,128)S(1)} collective-permute-done((f32[384,384]{1,0:T(8,128)S(1)}, f32[384,384]{1,0:T(8,128)S(1)}, u32[]{:S(2)}, u32[]{:S(2)}) %collective-permute-start.57) | collective-permute-done | bytes 589856 | tf_op jit(solution)/shard_map/ppermute | solution.py:30
  248.5 2.2 collective-permute-start.58
  250.9 6.7 %collective-permute-done.58.refs_10_ = f32[384,384]{1,0:T(8,128)} collective-permute-done((f32[384,384]{1,0:T(8,128)S(1)}, f32[384,384]{1,0:T(8,128)}, u32[]{:S(2)}, u32[]{:S(2)}) %collective-permute-start.58) | collective-permute-done | bytes 589856 | tf_op jit(solution)/shard_map/ppermute | solution.py:30
  257.6 3.4 %collective-permute-start.59 = (f32[384,384]{1,0:T(8,128)}, f32[384,384]{1,0:T(8,128)}, u32[]{:S(2)}, u32[]{:S(2)}) collective-permute-start(f32[384,384]{1,0:T(8,128)} %collective-permute-done.58.refs_10_), channel_id=1, source_target_pairs={{0,32},{16,112},{32,64},{48,16},{64,96},{80,48},{96,0},{112,80},{1... | collective-permute-start | bytes 1769480 | tf_op jit(solution)/shard_map/ppermute | solution.py:30
  262.2 1.7 place_rows.1
  263.9 6.6 %all-to-all-start.2 = ((f32[8,3,32,384]{3,2,1,0:T(8,128)}), f32[8,3,32,384]{3,2,1,0:T(8,128)}, u32[]{:S(2)}, u32[]{:S(2)}) async-start(f32[8,3,32,384]{3,2,1,0:T(8,128)} %bitcast.69), calls=%async_computation.2 | async-start | bytes 2359296 | tf_op jit(solution)/shard_map/all_to_all | solution.py:341
  271.0 2.5 collective-permute-start.63
  273.5 13.6 %all-to-all-done.2 = f32[8,3,32,384]{3,2,1,0:T(8,128)} async-done(((f32[8,3,32,384]{3,2,1,0:T(8,128)}), f32[8,3,32,384]{3,2,1,0:T(8,128)}, u32[]{:S(2)}, u32[]{:S(2)}) %all-to-all-start.2) | async-done | bytes 1179680 | tf_op jit(solution)/shard_map/all_to_all | solution.py:341
  287.1 2.5 copy.9
  291.0 14.0 %child.1 = f32[768,384]{1,0:T(8,128)} custom-call(s32[40]{0:T(128)S(1)} %stack.234.at, f32[768,384]{1,0:T(8,128)S(1)} %copy-done.1, f32[4,192,384]{2,1,0:T(8,128)S(1)} %pad_maximum_fusion.2.refs_0_, f32[4,192,384]{2,1,0:T(8,128)S(1)} %copy-done.5, f32[4,192,384]{2,1,0:T(8,128)} %collective-permute-done.49.refs_2_, ...), custom_call_target="tpu_custom_call" | custom-call | flops 5435817984 | bytes 14155776 | tf_op jit(solution)/shard_map/child/pallas_call | solution.py:230
  (107 shorter events, 22.9 us)
Async XLA Ops:
  25.0 7.5 %collective-permute-start.3 = (f32[192,384]{1,0:T(8,128)S(1)}, f32[192,384]{1,0:T(8,128)S(1)}, u32[]{:S(2)}, u32[]{:S(2)}) collective-permute-start(f32[192,384]{1,0:T(8,128)S(1)} %bitcast.97), channel_id=1, source_target_pairs={{0,4},{16,28},{4,8},{20,16},{8,12},{24,20},{12,0},{28,24},{1,5},{1... | collective-permute-start | bytes 884744 | tf_op jit(solution)/shard_map/ppermute | solution.py:31
  28.8 7.1 %collective-permute-start = (f32[192,384]{1,0:T(8,128)S(1)}, f32[192,384]{1,0:T(8,128)S(1)}, u32[]{:S(2)}, u32[]{:S(2)}) collective-permute-start(f32[192,384]{1,0:T(8,128)S(1)} %bitcast.95), channel_id=1, source_target_pairs={{0,1},{16,19},{1,2},{17,16},{2,3},{18,17},{3,0},{19,18},{4,5},{20,... | collective-permute-start | bytes 884744 | tf_op jit(solution)/shard_map/ppermute | solution.py:31
  32.5 7.1 %collective-permute-start.4 = (f32[192,384]{1,0:T(8,128)S(1)}, f32[192,384]{1,0:T(8,128)S(1)}, u32[]{:S(2)}, u32[]{:S(2)}) collective-permute-start(f32[192,384]{1,0:T(8,128)S(1)} %collective-permute-done.3), channel_id=1, source_target_pairs={{0,4},{16,28},{4,8},{20,16},{8,12},{24,20},{12,0},{28,24},{1,5},{1... | collective-permute-start | bytes 884744 | tf_op jit(solution)/shard_map/ppermute | solution.py:31
  35.9 7.1 %collective-permute-start.1 = (f32[192,384]{1,0:T(8,128)S(1)}, f32[192,384]{1,0:T(8,128)S(1)}, u32[]{:S(2)}, u32[]{:S(2)}) collective-permute-start(f32[192,384]{1,0:T(8,128)S(1)} %collective-permute-done), channel_id=1, source_target_pairs={{0,1},{16,19},{1,2},{17,16},{2,3},{18,17},{3,0},{19,18},{4,5},{20,... | collective-permute-start | bytes 884744 | tf_op jit(solution)/shard_map/ppermute | solution.py:31
  39.6 7.1 %collective-permute-start.5 = (f32[192,384]{1,0:T(8,128)S(1)}, f32[192,384]{1,0:T(8,128)S(1)}, u32[]{:S(2)}, u32[]{:S(2)}) collective-permute-start(f32[192,384]{1,0:T(8,128)S(1)} %collective-permute-done.4), channel_id=1, source_target_pairs={{0,4},{16,28},{4,8},{20,16},{8,12},{24,20},{12,0},{28,24},{1,5},{1... | collective-permute-start | bytes 884744 | tf_op jit(solution)/shard_map/ppermute | solution.py:31
  43.0 6.0 %collective-permute-start.2 = (f32[192,384]{1,0:T(8,128)S(1)}, f32[192,384]{1,0:T(8,128)S(1)}, u32[]{:S(2)}, u32[]{:S(2)}) collective-permute-start(f32[192,384]{1,0:T(8,128)S(1)} %collective-permute-done.1), channel_id=1, source_target_pairs={{0,1},{16,19},{1,2},{17,16},{2,3},{18,17},{3,0},{19,18},{4,5},{20,... | collective-permute-start | bytes 884744 | tf_op jit(solution)/shard_map/ppermute | solution.py:31
  44.9 15.7 %collective-permute-start.30 = (f32[768,384]{1,0:T(8,128)}, f32[768,384]{1,0:T(8,128)}, u32[]{:S(2)}, u32[]{:S(2)}) collective-permute-start(f32[768,384]{1,0:T(8,128)} %refs_8_.1), channel_id=1, source_target_pairs={{0,32},{16,112},{32,64},{48,16},{64,96},{80,48},{96,0},{112,80},{1... | collective-permute-start | bytes 3538952 | tf_op jit(solution)/shard_map/ppermute | solution.py:30
  46.7 15.9 %collective-permute-start.7 = (f32[4,192,384]{2,1,0:T(8,128)S(1)}, f32[4,192,384]{2,1,0:T(8,128)}, u32[]{:S(2)}, u32[]{:S(2)}) collective-permute-start(f32[4,192,384]{2,1,0:T(8,128)S(1)} %pad_maximum_fusion.1.refs_4_), channel_id=1, source_target_pairs={{0,1},{16,19},{1,2},{17,16},{2,3},{18,17},{3,0},{19,18},{4,5},{20,... | collective-permute-start | bytes 3538952 | tf_op jit(solution)/shard_map/ppermute | solution.py:31
  49.0 16.3 %collective-permute-start.6 = (f32[4,192,384]{2,1,0:T(8,128)S(1)}, f32[4,192,384]{2,1,0:T(8,128)}, u32[]{:S(2)}, u32[]{:S(2)}) collective-permute-start(f32[4,192,384]{2,1,0:T(8,128)S(1)} %pad_maximum_fusion.refs_0_), channel_id=1, source_target_pairs={{0,4},{16,28},{4,8},{20,16},{8,12},{24,20},{12,0},{28,24},{1,5},{1... | collective-permute-start | bytes 3538952 | tf_op jit(solution)/shard_map/ppermute | solution.py:31
  53.1 21.8 %all-to-all-start.1 = ((f32[3,8,32,384]{3,2,0,1:T(8,128)}), f32[3,8,32,384]{3,2,0,1:T(8,128)S(1)}, u32[]{:S(2)}, u32[]{:S(2)}) async-start(f32[3,8,32,384]{3,2,0,1:T(8,128)} %copy.8), calls=%async_computation.1 | async-start | bytes 2359296 | tf_op jit(solution)/shard_map/all_to_all | solution.py:250
  60.5 26.0 %collective-permute-start.31 = (f32[768,384]{1,0:T(8,128)}, f32[768,384]{1,0:T(8,128)}, u32[]{:S(2)}, u32[]{:S(2)}) collective-permute-start(f32[768,384]{1,0:T(8,128)} %collective-permute-done.30.refs_9_), channel_id=1, source_target_pairs={{0,32},{16,112},{32,64},{48,16},{64,96},{80,48},{96,0},{112,80},{1... | collective-permute-start | bytes 3538952 | tf_op jit(solution)/shard_map/ppermute | solution.py:30
  62.6 30.2 %collective-permute-start.12 = (f32[4,192,384]{2,1,0:T(8,128)}, f32[4,192,384]{2,1,0:T(8,128)}, u32[]{:S(2)}, u32[]{:S(2)}) collective-permute-start(f32[4,192,384]{2,1,0:T(8,128)} %collective-permute-done.7.refs_5_), channel_id=1, source_target_pairs={{0,1},{16,19},{1,2},{17,16},{2,3},{18,17},{3,0},{19,18},{4,5},{20,... | collective-permute-start | bytes 3538952 | tf_op jit(solution)/shard_map/ppermute | solution.py:31
  65.4 27.5 %collective-permute-start.11 = (f32[4,192,384]{2,1,0:T(8,128)}, f32[4,192,384]{2,1,0:T(8,128)}, u32[]{:S(2)}, u32[]{:S(2)}) collective-permute-start(f32[4,192,384]{2,1,0:T(8,128)} %collective-permute-done.6.refs_1_), channel_id=1, source_target_pairs={{0,4},{16,28},{4,8},{20,16},{8,12},{24,20},{12,0},{28,24},{1,5},{1... | collective-permute-start | bytes 3538952 | tf_op jit(solution)/shard_map/ppermute | solution.py:31
  75.6 12.6 %collective-permute-start.8 = (f32[4,24,384]{2,1,0:T(8,128)S(1)}, f32[4,24,384]{2,1,0:T(8,128)S(1)}, u32[]{:S(2)}, u32[]{:S(2)}) collective-permute-start(f32[4,24,384]{2,1,0:T(8,128)S(1)} %get-tuple-element.37), channel_id=1, source_target_pairs={{0,1},{1,2},{2,3},{3,0},{4,5},{5,6},{6,7},{7,4},{8,9},{9,10},{10,1... | collective-permute-start | bytes 442376 | tf_op jit(solution)/shard_map/ppermute | solution.py:72
  76.6 12.2 %collective-permute-start.9 = (f32[4,24,384]{2,1,0:T(8,128)S(1)}, f32[4,24,384]{2,1,0:T(8,128)S(1)}, u32[]{:S(2)}, u32[]{:S(2)}) collective-permute-start(f32[4,24,384]{2,1,0:T(8,128)S(1)} %get-tuple-element.36), channel_id=1, source_target_pairs={{0,2},{1,3},{2,0},{3,1},{4,6},{5,7},{6,4},{7,5},{8,10},{9,11},{10,... | collective-permute-start | bytes 442376 | tf_op jit(solution)/shard_map/ppermute | solution.py:72
  86.6 35.6 %collective-permute-start.33 = (f32[768,384]{1,0:T(8,128)}, f32[768,384]{1,0:T(8,128)}, u32[]{:S(2)}, u32[]{:S(2)}) collective-permute-start(f32[768,384]{1,0:T(8,128)} %refs_8_.1), channel_id=1, source_target_pairs={{0,16},{16,0},{1,17},{17,1},{2,18},{18,2},{3,19},{19,3},{4,20},{20... | collective-permute-start | bytes 3538952 | tf_op jit(solution)/shard_map/ppermute | solution.py:35
  88.2 34.0 %collective-permute-start.32 = (f32[768,384]{1,0:T(8,128)}, f32[768,384]{1,0:T(8,128)}, u32[]{:S(2)}, u32[]{:S(2)}) collective-permute-start(f32[768,384]{1,0:T(8,128)} %collective-permute-done.31.refs_10_), channel_id=1, source_target_pairs={{0,32},{16,112},{32,64},{48,16},{64,96},{80,48},{96,0},{112,80},{1... | collective-permute-start | bytes 3538952 | tf_op jit(solution)/shard_map/ppermute | solution.py:30
  92.9 5.7 %collective-permute-start.13 = (f32[4,24,384]{2,1,0:T(8,128)S(1)}, f32[4,24,384]{2,1,0:T(8,128)S(1)}, u32[]{:S(2)}, u32[]{:S(2)}) collective-permute-start(f32[4,24,384]{2,1,0:T(8,128)S(1)} %get-tuple-element.33), channel_id=1, source_target_pairs={{0,4},{4,8},{8,12},{12,0},{1,5},{5,9},{9,13},{13,1},{2,6},{6,10},{... | collective-permute-start | bytes 442376 | tf_op jit(solution)/shard_map/ppermute | solution.py:78
  94.7 6.1 %collective-permute-start.14 = (f32[4,24,384]{2,1,0:T(8,128)S(1)}, f32[4,24,384]{2,1,0:T(8,128)S(1)}, u32[]{:S(2)}, u32[]{:S(2)}) collective-permute-start(f32[4,24,384]{2,1,0:T(8,128)S(1)} %get-tuple-element.32), channel_id=1, source_target_pairs={{0,8},{4,12},{8,0},{12,4},{1,9},{5,13},{9,1},{13,5},{2,10},{6,14},... | collective-permute-start | bytes 442376 | tf_op jit(solution)/shard_map/ppermute | solution.py:78
  96.5 4.4 %collective-permute-start.15 = (f32[4,24,384]{2,1,0:T(8,128)S(1)}, f32[4,24,384]{2,1,0:T(8,128)S(1)}, u32[]{:S(2)}, u32[]{:S(2)}) collective-permute-start(f32[4,24,384]{2,1,0:T(8,128)S(1)} %get-tuple-element.31), channel_id=1, source_target_pairs={{0,12},{4,0},{8,4},{12,8},{1,13},{5,1},{9,5},{13,9},{2,14},{6,2},{... | collective-permute-start | bytes 442376 | tf_op jit(solution)/shard_map/ppermute | solution.py:78
  101.8 6.1 %collective-permute-start.22 = (f32[24,1536]{1,0:T(8,128)S(1)}, f32[24,1536]{1,0:T(8,128)S(1)}, u32[]{:S(2)}, u32[]{:S(2)}) collective-permute-start(f32[24,1536]{1,0:T(8,128)S(1)} %get-tuple-element.22), channel_id=1, source_target_pairs={{0,4},{16,28},{4,8},{20,16},{8,12},{24,20},{12,0},{28,24},{1,5},{1... | collective-permute-start | bytes 442376 | tf_op jit(solution)/shard_map/ppermute | solution.py:31
  107.9 4.4 %collective-permute-start.23 = (f32[24,1536]{1,0:T(8,128)S(1)}, f32[24,1536]{1,0:T(8,128)S(1)}, u32[]{:S(2)}, u32[]{:S(2)}) collective-permute-start(f32[24,1536]{1,0:T(8,128)S(1)} %collective-permute-done.22), channel_id=1, source_target_pairs={{0,4},{16,28},{4,8},{20,16},{8,12},{24,20},{12,0},{28,24},{1,5},{1... | collective-permute-start | bytes 442376 | tf_op jit(solution)/shard_map/ppermute | solution.py:31
  112.2 10.5 %collective-permute-start.24 = (f32[24,1536]{1,0:T(8,128)S(1)}, f32[24,1536]{1,0:T(8,128)S(1)}, u32[]{:S(2)}, u32[]{:S(2)}) collective-permute-start(f32[24,1536]{1,0:T(8,128)S(1)} %collective-permute-done.23), channel_id=1, source_target_pairs={{0,4},{16,28},{4,8},{20,16},{8,12},{24,20},{12,0},{28,24},{1,5},{1... | collective-permute-start | bytes 442376 | tf_op jit(solution)/shard_map/ppermute | solution.py:31
  115.3 10.5 %collective-permute-start.34 = (f32[768,384]{1,0:T(8,128)}, f32[768,384]{1,0:T(8,128)}, u32[]{:S(2)}, u32[]{:S(2)}) collective-permute-start(f32[768,384]{1,0:T(8,128)} %collective-permute-done.30.refs_9_), channel_id=1, source_target_pairs={{0,16},{16,0},{1,17},{17,1},{2,18},{18,2},{3,19},{19,3},{4,20},{20... | collective-permute-start | bytes 3538952 | tf_op jit(solution)/shard_map/ppermute | solution.py:35
  122.1 6.9 %collective-permute-start.35 = (f32[768,384]{1,0:T(8,128)}, f32[768,384]{1,0:T(8,128)}, u32[]{:S(2)}, u32[]{:S(2)}) collective-permute-start(f32[768,384]{1,0:T(8,128)} %collective-permute-done.31.refs_10_), channel_id=1, source_target_pairs={{0,16},{16,0},{1,17},{17,1},{2,18},{18,2},{3,19},{19,3},{4,20},{20... | collective-permute-start | bytes 3538952 | tf_op jit(solution)/shard_map/ppermute | solution.py:35
  122.1 15.7 %collective-permute-start.29 = (f32[4,192,384]{2,1,0:T(8,128)}, f32[4,192,384]{2,1,0:T(8,128)}, u32[]{:S(2)}, u32[]{:S(2)}) collective-permute-start(f32[4,192,384]{2,1,0:T(8,128)} %collective-permute-done.12.refs_6_), channel_id=1, source_target_pairs={{0,1},{16,19},{1,2},{17,16},{2,3},{18,17},{3,0},{19,18},{4,5},{20,... | collective-permute-start | bytes 3538952 | tf_op jit(solution)/shard_map/ppermute | solution.py:31
  122.2 6.9 %collective-permute-start.36 = (f32[768,384]{1,0:T(8,128)}, f32[768,384]{1,0:T(8,128)}, u32[]{:S(2)}, u32[]{:S(2)}) collective-permute-start(f32[768,384]{1,0:T(8,128)} %collective-permute-done.32.refs_11_), channel_id=1, source_target_pairs={{0,16},{16,0},{1,17},{17,1},{2,18},{18,2},{3,19},{19,3},{4,20},{20... | collective-permute-start | bytes 3538952 | tf_op jit(solution)/shard_map/ppermute | solution.py:35
  122.7 16.4 %collective-permute-start.28 = (f32[4,192,384]{2,1,0:T(8,128)}, f32[4,192,384]{2,1,0:T(8,128)}, u32[]{:S(2)}, u32[]{:S(2)}) collective-permute-start(f32[4,192,384]{2,1,0:T(8,128)} %collective-permute-done.11.refs_2_), channel_id=1, source_target_pairs={{0,4},{16,28},{4,8},{20,16},{8,12},{24,20},{12,0},{28,24},{1,5},{1... | collective-permute-start | bytes 3538952 | tf_op jit(solution)/shard_map/ppermute | solution.py:31
  125.8 36.7 %collective-permute-start.16 = (f32[24,1536]{1,0:T(8,128)S(1)}, f32[24,1536]{1,0:T(8,128)S(1)}, u32[]{:S(2)}, u32[]{:S(2)}) collective-permute-start(f32[24,1536]{1,0:T(8,128)S(1)} %get-tuple-element.21), channel_id=1, source_target_pairs={{0,1},{16,19},{1,2},{17,16},{2,3},{18,17},{3,0},{19,18},{4,5},{20,... | collective-permute-start | bytes 442376 | tf_op jit(solution)/shard_map/ppermute | solution.py:31
  129.0 57.1 %collective-permute-start.25 = (f32[4,24,1536]{2,1,0:T(8,128)S(1)}, f32[4,24,1536]{2,1,0:T(8,128)S(1)}, u32[]{:S(2)}, u32[]{:S(2)}) collective-permute-start(f32[4,24,1536]{2,1,0:T(8,128)S(1)} %pad_maximum_fusion.8.refs_4_), channel_id=1, source_target_pairs={{0,1},{16,19},{1,2},{17,16},{2,3},{18,17},{3,0},{19,18},{4,5},{20,... | collective-permute-start | bytes 1769480 | tf_op jit(solution)/shard_map/ppermute | solution.py:31
  154.0 33.0 %collective-permute-start.44 = (f32[384,384]{1,0:T(8,128)S(1)}, f32[384,384]{1,0:T(8,128)S(1)}, u32[]{:S(2)}, u32[]{:S(2)}) collective-permute-start(f32[384,384]{1,0:T(8,128)S(1)} %get-tuple-element.25), channel_id=1, source_target_pairs={{0,0},{1,1},{2,16},{3,17},{4,32},{5,33},{6,48},{7,49},{8,64},{9,65... | collective-permute-start | bytes 1769480 | tf_op jit(solution)/shard_map/ppermute | solution.py:331
  162.6 10.5 %collective-permute-start.17 = (f32[24,1536]{1,0:T(8,128)S(1)}, f32[24,1536]{1,0:T(8,128)S(1)}, u32[]{:S(2)}, u32[]{:S(2)}) collective-permute-start(f32[24,1536]{1,0:T(8,128)S(1)} %collective-permute-done.16), channel_id=1, source_target_pairs={{0,1},{16,19},{1,2},{17,16},{2,3},{18,17},{3,0},{19,18},{4,5},{20,... | collective-permute-start | bytes 442376 | tf_op jit(solution)/shard_map/ppermute | solution.py:31
  173.1 4.3 %collective-permute-start.18 = (f32[24,1536]{1,0:T(8,128)S(1)}, f32[24,1536]{1,0:T(8,128)S(1)}, u32[]{:S(2)}, u32[]{:S(2)}) collective-permute-start(f32[24,1536]{1,0:T(8,128)S(1)} %collective-permute-done.17), channel_id=1, source_target_pairs={{0,1},{16,19},{1,2},{17,16},{2,3},{18,17},{3,0},{19,18},{4,5},{20,... | collective-permute-start | bytes 442376 | tf_op jit(solution)/shard_map/ppermute | solution.py:31
  177.4 19.8 %collective-permute-start.19 = (f32[4,24,1536]{2,1,0:T(8,128)S(1)}, f32[4,24,1536]{2,1,0:T(8,128)S(1)}, u32[]{:S(2)}, u32[]{:S(2)}) collective-permute-start(f32[4,24,1536]{2,1,0:T(8,128)S(1)} %pad_maximum_fusion.7.refs_0_), channel_id=1, source_target_pairs={{0,4},{16,28},{4,8},{20,16},{8,12},{24,20},{12,0},{28,24},{1,5},{1... | collective-permute-start | bytes 1769480 | tf_op jit(solution)/shard_map/ppermute | solution.py:31
  186.0 12.9 %collective-permute-start.37 = (f32[12,32,384]{2,1,0:T(8,128)S(1)}, f32[12,32,384]{2,1,0:T(8,128)S(1)}, u32[]{:S(2)}, u32[]{:S(2)}) collective-permute-start(f32[12,32,384]{2,1,0:T(8,128)S(1)} %bitcast.103), channel_id=1, source_target_pairs={{0,32},{16,112},{32,64},{48,16},{64,96},{80,48},{96,0},{112,80},{1... | collective-permute-start | bytes 1769480 | tf_op jit(solution)/shard_map/ppermute | solution.py:30
  186.0 18.2 %collective-permute-start.26 = (f32[4,24,1536]{2,1,0:T(8,128)S(1)}, f32[4,24,1536]{2,1,0:T(8,128)S(1)}, u32[]{:S(2)}, u32[]{:S(2)}) collective-permute-start(f32[4,24,1536]{2,1,0:T(8,128)S(1)} %collective-permute-done.25.refs_5_), channel_id=1, source_target_pairs={{0,1},{16,19},{1,2},{17,16},{2,3},{18,17},{3,0},{19,18},{4,5},{20,... | collective-permute-start | bytes 1769480 | tf_op jit(solution)/shard_map/ppermute | solution.py:31
  187.0 11.9 %collective-permute-start.51 = (f32[192,384]{1,0:T(8,128)S(1)}, f32[192,384]{1,0:T(8,128)S(1)}, u32[]{:S(2)}, u32[]{:S(2)}) collective-permute-start(f32[192,384]{1,0:T(8,128)S(1)} %get-tuple-element.28), channel_id=1, source_target_pairs={{0,4},{16,28},{4,8},{20,16},{8,12},{24,20},{12,0},{28,24},{1,5},{1... | collective-permute-start | bytes 884744 | tf_op jit(solution)/shard_map/ppermute | solution.py:31
  187.8 13.9 %collective-permute-start.45 = (f32[192,384]{1,0:T(8,128)S(1)}, f32[192,384]{1,0:T(8,128)S(1)}, u32[]{:S(2)}, u32[]{:S(2)}) collective-permute-start(f32[192,384]{1,0:T(8,128)S(1)} %get-tuple-element.29), channel_id=1, source_target_pairs={{0,1},{16,19},{1,2},{17,16},{2,3},{18,17},{3,0},{19,18},{4,5},{20,... | collective-permute-start | bytes 884744 | tf_op jit(solution)/shard_map/ppermute | solution.py:31
  197.2 16.3 %collective-permute-start.20 = (f32[4,24,1536]{2,1,0:T(8,128)S(1)}, f32[4,24,1536]{2,1,0:T(8,128)S(1)}, u32[]{:S(2)}, u32[]{:S(2)}) collective-permute-start(f32[4,24,1536]{2,1,0:T(8,128)S(1)} %collective-permute-done.19.refs_1_), channel_id=1, source_target_pairs={{0,4},{16,28},{4,8},{20,16},{8,12},{24,20},{12,0},{28,24},{1,5},{1... | collective-permute-start | bytes 1769480 | tf_op jit(solution)/shard_map/ppermute | solution.py:31
  198.9 14.6 %collective-permute-start.38 = (f32[12,32,384]{2,1,0:T(8,128)S(1)}, f32[12,32,384]{2,1,0:T(8,128)S(1)}, u32[]{:S(2)}, u32[]{:S(2)}) collective-permute-start(f32[12,32,384]{2,1,0:T(8,128)S(1)} %collective-permute-done.37.refs_9_), channel_id=1, source_target_pairs={{0,32},{16,112},{32,64},{48,16},{64,96},{80,48},{96,0},{112,80},{1... | collective-permute-start | bytes 1769480 | tf_op jit(solution)/shard_map/ppermute | solution.py:30
  198.9 10.5 %collective-permute-start.52 = (f32[192,384]{1,0:T(8,128)S(1)}, f32[192,384]{1,0:T(8,128)S(1)}, u32[]{:S(2)}, u32[]{:S(2)}) collective-permute-start(f32[192,384]{1,0:T(8,128)S(1)} %collective-permute-done.51), channel_id=1, source_target_pairs={{0,4},{16,28},{4,8},{20,16},{8,12},{24,20},{12,0},{28,24},{1,5},{1... | collective-permute-start | bytes 884744 | tf_op jit(solution)/shard_map/ppermute | solution.py:31
  201.8 10.2 %collective-permute-start.46 = (f32[192,384]{1,0:T(8,128)S(1)}, f32[192,384]{1,0:T(8,128)S(1)}, u32[]{:S(2)}, u32[]{:S(2)}) collective-permute-start(f32[192,384]{1,0:T(8,128)S(1)} %collective-permute-done.45), channel_id=1, source_target_pairs={{0,1},{16,19},{1,2},{17,16},{2,3},{18,17},{3,0},{19,18},{4,5},{20,... | collective-permute-start | bytes 884744 | tf_op jit(solution)/shard_map/ppermute | solution.py:31
  204.3 16.4 %collective-permute-start.40 = (f32[12,32,384]{2,1,0:T(8,128)S(1)}, f32[12,32,384]{2,1,0:T(8,128)S(1)}, u32[]{:S(2)}, u32[]{:S(2)}) collective-permute-start(f32[12,32,384]{2,1,0:T(8,128)S(1)} %bitcast.104), channel_id=1, source_target_pairs={{0,16},{16,0},{1,17},{17,1},{2,18},{18,2},{3,19},{19,3},{4,20},{20... | collective-permute-start | bytes 1769480 | tf_op jit(solution)/shard_map/ppermute | solution.py:35
  209.4 6.3 %collective-permute-start.53 = (f32[192,384]{1,0:T(8,128)S(1)}, f32[192,384]{1,0:T(8,128)S(1)}, u32[]{:S(2)}, u32[]{:S(2)}) collective-permute-start(f32[192,384]{1,0:T(8,128)S(1)} %collective-permute-done.52), channel_id=1, source_target_pairs={{0,4},{16,28},{4,8},{20,16},{8,12},{24,20},{12,0},{28,24},{1,5},{1... | collective-permute-start | bytes 884744 | tf_op jit(solution)/shard_map/ppermute | solution.py:31
  212.0 5.9 %collective-permute-start.47 = (f32[192,384]{1,0:T(8,128)S(1)}, f32[192,384]{1,0:T(8,128)S(1)}, u32[]{:S(2)}, u32[]{:S(2)}) collective-permute-start(f32[192,384]{1,0:T(8,128)S(1)} %collective-permute-done.46), channel_id=1, source_target_pairs={{0,1},{16,19},{1,2},{17,16},{2,3},{18,17},{3,0},{19,18},{4,5},{20,... | collective-permute-start | bytes 884744 | tf_op jit(solution)/shard_map/ppermute | solution.py:31
  213.4 10.7 %collective-permute-start.27 = (f32[4,24,1536]{2,1,0:T(8,128)S(1)}, f32[4,24,1536]{2,1,0:T(8,128)S(1)}, u32[]{:S(2)}, u32[]{:S(2)}) collective-permute-start(f32[4,24,1536]{2,1,0:T(8,128)S(1)} %collective-permute-done.26.refs_6_), channel_id=1, source_target_pairs={{0,1},{16,19},{1,2},{17,16},{2,3},{18,17},{3,0},{19,18},{4,5},{20,... | collective-permute-start | bytes 1769480 | tf_op jit(solution)/shard_map/ppermute | solution.py:31
  213.5 12.1 %collective-permute-start.21 = (f32[4,24,1536]{2,1,0:T(8,128)S(1)}, f32[4,24,1536]{2,1,0:T(8,128)S(1)}, u32[]{:S(2)}, u32[]{:S(2)}) collective-permute-start(f32[4,24,1536]{2,1,0:T(8,128)S(1)} %collective-permute-done.20.refs_2_), channel_id=1, source_target_pairs={{0,4},{16,28},{4,8},{20,16},{8,12},{24,20},{12,0},{28,24},{1,5},{1... | collective-permute-start | bytes 1769480 | tf_op jit(solution)/shard_map/ppermute | solution.py:31
  215.7 10.0 %collective-permute-start.39 = (f32[12,32,384]{2,1,0:T(8,128)S(1)}, f32[12,32,384]{2,1,0:T(8,128)S(1)}, u32[]{:S(2)}, u32[]{:S(2)}) collective-permute-start(f32[12,32,384]{2,1,0:T(8,128)S(1)} %collective-permute-done.38.refs_10_), channel_id=1, source_target_pairs={{0,32},{16,112},{32,64},{48,16},{64,96},{80,48},{96,0},{112,80},{1... | collective-permute-start | bytes 1769480 | tf_op jit(solution)/shard_map/ppermute | solution.py:30
  217.9 22.5 %collective-permute-start.54 = (f32[4,192,384]{2,1,0:T(8,128)S(1)}, f32[4,192,384]{2,1,0:T(8,128)S(1)}, u32[]{:S(2)}, u32[]{:S(2)}) collective-permute-start(f32[4,192,384]{2,1,0:T(8,128)S(1)} %pad_maximum_fusion.3.refs_4_), channel_id=1, source_target_pairs={{0,1},{16,19},{1,2},{17,16},{2,3},{18,17},{3,0},{19,18},{4,5},{20,... | collective-permute-start | bytes 3538952 | tf_op jit(solution)/shard_map/ppermute | solution.py:31
  220.6 19.9 %collective-permute-start.48 = (f32[4,192,384]{2,1,0:T(8,128)S(1)}, f32[4,192,384]{2,1,0:T(8,128)S(1)}, u32[]{:S(2)}, u32[]{:S(2)}) collective-permute-start(f32[4,192,384]{2,1,0:T(8,128)S(1)} %pad_maximum_fusion.2.refs_0_), channel_id=1, source_target_pairs={{0,4},{16,28},{4,8},{20,16},{8,12},{24,20},{12,0},{28,24},{1,5},{1... | collective-permute-start | bytes 3538952 | tf_op jit(solution)/shard_map/ppermute | solution.py:31
  224.2 5.0 %collective-permute-start.41 = (f32[12,32,384]{2,1,0:T(8,128)S(1)}, f32[12,32,384]{2,1,0:T(8,128)S(1)}, u32[]{:S(2)}, u32[]{:S(2)}) collective-permute-start(f32[12,32,384]{2,1,0:T(8,128)S(1)} %collective-permute-done.37.refs_9_), channel_id=1, source_target_pairs={{0,16},{16,0},{1,17},{17,1},{2,18},{18,2},{3,19},{19,3},{4,20},{20... | collective-permute-start | bytes 1769480 | tf_op jit(solution)/shard_map/ppermute | solution.py:35
  225.7 5.1 %collective-permute-start.43 = (f32[12,32,384]{2,1,0:T(8,128)S(1)}, f32[12,32,384]{2,1,0:T(8,128)S(1)}, u32[]{:S(2)}, u32[]{:S(2)}) collective-permute-start(f32[12,32,384]{2,1,0:T(8,128)S(1)} %collective-permute-done.39.refs_11_), channel_id=1, source_target_pairs={{0,16},{16,0},{1,17},{17,1},{2,18},{18,2},{3,19},{19,3},{4,20},{20... | collective-permute-start | bytes 1769480 | tf_op jit(solution)/shard_map/ppermute | solution.py:35
  239.0 9.4 %collective-permute-start.57 = (f32[384,384]{1,0:T(8,128)S(1)}, f32[384,384]{1,0:T(8,128)S(1)}, u32[]{:S(2)}, u32[]{:S(2)}) collective-permute-start(f32[384,384]{1,0:T(8,128)S(1)} %cross.1.refs_8_), channel_id=1, source_target_pairs={{0,32},{16,112},{32,64},{48,16},{64,96},{80,48},{96,0},{112,80},{1... | collective-permute-start | bytes 1769480 | tf_op jit(solution)/shard_map/ppermute | solution.py:30
  240.3 20.7 %collective-permute-start.55 = (f32[4,192,384]{2,1,0:T(8,128)S(1)}, f32[4,192,384]{2,1,0:T(8,128)}, u32[]{:S(2)}, u32[]{:S(2)}) collective-permute-start(f32[4,192,384]{2,1,0:T(8,128)S(1)} %collective-permute-done.54.refs_5_), channel_id=1, source_target_pairs={{0,1},{16,19},{1,2},{17,16},{2,3},{18,17},{3,0},{19,18},{4,5},{20,... | collective-permute-start | bytes 3538952 | tf_op jit(solution)/shard_map/ppermute | solution.py:31
  240.5 20.7 %collective-permute-start.49 = (f32[4,192,384]{2,1,0:T(8,128)S(1)}, f32[4,192,384]{2,1,0:T(8,128)}, u32[]{:S(2)}, u32[]{:S(2)}) collective-permute-start(f32[4,192,384]{2,1,0:T(8,128)S(1)} %collective-permute-done.48.refs_1_), channel_id=1, source_target_pairs={{0,4},{16,28},{4,8},{20,16},{8,12},{24,20},{12,0},{28,24},{1,5},{1... | collective-permute-start | bytes 3538952 | tf_op jit(solution)/shard_map/ppermute | solution.py:31
  248.5 9.1 %collective-permute-start.58 = (f32[384,384]{1,0:T(8,128)S(1)}, f32[384,384]{1,0:T(8,128)}, u32[]{:S(2)}, u32[]{:S(2)}) collective-permute-start(f32[384,384]{1,0:T(8,128)S(1)} %collective-permute-done.57.refs_9_), channel_id=1, source_target_pairs={{0,32},{16,112},{32,64},{48,16},{64,96},{80,48},{96,0},{112,80},{1... | collective-permute-start | bytes 1769480 | tf_op jit(solution)/shard_map/ppermute | solution.py:30
  250.7 19.8 %collective-permute-start.60 = (f32[384,384]{1,0:T(8,128)S(1)}, f32[384,384]{1,0:T(8,128)}, u32[]{:S(2)}, u32[]{:S(2)}) collective-permute-start(f32[384,384]{1,0:T(8,128)S(1)} %cross.1.refs_8_), channel_id=1, source_target_pairs={{0,16},{16,0},{1,17},{17,1},{2,18},{18,2},{3,19},{19,3},{4,20},{20... | collective-permute-start | bytes 1769480 | tf_op jit(solution)/shard_map/ppermute | solution.py:35
  257.6 13.4 %collective-permute-start.59 = (f32[384,384]{1,0:T(8,128)}, f32[384,384]{1,0:T(8,128)}, u32[]{:S(2)}, u32[]{:S(2)}) collective-permute-start(f32[384,384]{1,0:T(8,128)} %collective-permute-done.58.refs_10_), channel_id=1, source_target_pairs={{0,32},{16,112},{32,64},{48,16},{64,96},{80,48},{96,0},{112,80},{1... | collective-permute-start | bytes 1769480 | tf_op jit(solution)/shard_map/ppermute | solution.py:30
  261.0 28.6 %collective-permute-start.56 = (f32[4,192,384]{2,1,0:T(8,128)}, f32[4,192,384]{2,1,0:T(8,128)}, u32[]{:S(2)}, u32[]{:S(2)}) collective-permute-start(f32[4,192,384]{2,1,0:T(8,128)} %collective-permute-done.55.refs_6_), channel_id=1, source_target_pairs={{0,1},{16,19},{1,2},{17,16},{2,3},{18,17},{3,0},{19,18},{4,5},{20,... | collective-permute-start | bytes 3538952 | tf_op jit(solution)/shard_map/ppermute | solution.py:31
  261.2 28.5 %collective-permute-start.50 = (f32[4,192,384]{2,1,0:T(8,128)}, f32[4,192,384]{2,1,0:T(8,128)}, u32[]{:S(2)}, u32[]{:S(2)}) collective-permute-start(f32[4,192,384]{2,1,0:T(8,128)} %collective-permute-done.49.refs_2_), channel_id=1, source_target_pairs={{0,4},{16,28},{4,8},{20,16},{8,12},{24,20},{12,0},{28,24},{1,5},{1... | collective-permute-start | bytes 3538952 | tf_op jit(solution)/shard_map/ppermute | solution.py:31
  263.9 23.2 %all-to-all-start.2 = ((f32[8,3,32,384]{3,2,1,0:T(8,128)}), f32[8,3,32,384]{3,2,1,0:T(8,128)}, u32[]{:S(2)}, u32[]{:S(2)}) async-start(f32[8,3,32,384]{3,2,1,0:T(8,128)} %bitcast.69), calls=%async_computation.2 | async-start | bytes 2359296 | tf_op jit(solution)/shard_map/all_to_all | solution.py:341
  270.5 19.1 %collective-permute-start.61 = (f32[384,384]{1,0:T(8,128)S(1)}, f32[384,384]{1,0:T(8,128)}, u32[]{:S(2)}, u32[]{:S(2)}) collective-permute-start(f32[384,384]{1,0:T(8,128)S(1)} %collective-permute-done.57.refs_9_), channel_id=1, source_target_pairs={{0,16},{16,0},{1,17},{17,1},{2,18},{18,2},{3,19},{19,3},{4,20},{20... | collective-permute-start | bytes 1769480 | tf_op jit(solution)/shard_map/ppermute | solution.py:35
  270.5 19.1 %collective-permute-start.62 = (f32[384,384]{1,0:T(8,128)}, f32[384,384]{1,0:T(8,128)}, u32[]{:S(2)}, u32[]{:S(2)}) collective-permute-start(f32[384,384]{1,0:T(8,128)} %collective-permute-done.58.refs_10_), channel_id=1, source_target_pairs={{0,16},{16,0},{1,17},{17,1},{2,18},{18,2},{3,19},{19,3},{4,20},{20... | collective-permute-start | bytes 1769480 | tf_op jit(solution)/shard_map/ppermute | solution.py:35
  271.0 18.6 %collective-permute-start.63 = (f32[384,384]{1,0:T(8,128)}, f32[384,384]{1,0:T(8,128)}, u32[]{:S(2)}, u32[]{:S(2)}) collective-permute-start(f32[384,384]{1,0:T(8,128)} %collective-permute-done.59.refs_11_), channel_id=1, source_target_pairs={{0,16},{16,0},{1,17},{17,1},{2,18},{18,2},{3,19},{19,3},{4,20},{20... | collective-permute-start | bytes 1769480 | tf_op jit(solution)/shard_map/ppermute | solution.py:35
  (9 other events, 63.9 us)

commit v4 on v1

v4 whole, which is shorter than its diff:
```python
import functools

import jax
import jax.numpy as jnp
import numpy as np
from jax import lax
from jax.experimental import pallas as pl
from jax.experimental.pallas import tpu as pltpu
from jax.sharding import Mesh, PartitionSpec as P

NB = 24
NANC = 12
ROW = ("y", "core")
COL = ("z", "x")
ALL = ("y", "core", "z", "x")
VMEM = pl.BlockSpec(memory_space=pltpu.VMEM)
SMEM = pl.BlockSpec(memory_space=pltpu.SMEM)
ANY = pl.BlockSpec(memory_space=pl.ANY)
F32 = jnp.float32


def params(mib):
    return pltpu.CompilerParams(vmem_limit_bytes=mib * 1024 * 1024)


def cost(m, k, n, in_bytes):
    return pl.CostEstimate(flops=6 * m * k * n, bytes_accessed=in_bytes, transcendentals=0)


def after(x, *others):
    return lax.optimization_barrier((x, *others))[0]


def step(x):
    return lax.ppermute(x, ROW, [(2 * i + c, 2 * ((i + 1 - 2 * c) % 4) + c) for i in range(4) for c in range(2)])


def swap(x):
    return lax.ppermute(x, "core", [(0, 1), (1, 0)])


def gather_rows(x):
    mine = [x]
    for _ in range(3):
        mine.append(step(mine[-1]))
    return mine + [swap(t) for t in mine]


def hop(x, along, by):
    pairs = []
    for core in range(2):
        for i in range(4):
            for j in range(4):
                to = (i, (j + by) % 4) if along == core else ((i + by) % 4, j)
                pairs.append((16 * core + 4 * i + j, 16 * core + 4 * to[0] + to[1]))
    return lax.ppermute(x, ("core",) + COL, pairs)


def gather_cols(x, axis, gates=((), (), ())):
    half = x.shape[axis] // 2
    up, down = hop(x, 0, 1), hop(x, 0, -1)
    top = hop(lax.slice_in_dim(after(up, *gates[0]), 0, half, axis=axis), 0, 1)
    low = hop(lax.slice_in_dim(after(down, *gates[0]), half, 2 * half, axis=axis), 0, -1)
    group = after(jnp.stack([x, up, down, jnp.concatenate([top, low], axis=axis)]), *gates[1])
    up, down = hop(group, 1, 1), hop(group, 1, -1)
    return (group, up, down), (hop(after(up, *gates[2])[:2], 1, 1), hop(after(down, *gates[2])[2:], 1, -1))


def places():
    y, core, z, x = (lax.axis_index(n) for n in ALL)
    s = 1 - 2 * core
    near = lambda i, k: lax.rem(i + k + 8, 4)
    rows = [2 * near(y, -s * k) + core for k in range(4)] + [2 * near(y, s * k) + 1 - core for k in range(4)]
    first, second = jnp.where(core == 0, x, z), jnp.where(core == 0, z, x)
    cols = []
    for k in (0, -1, 1, 2):
        for i in (0, -1, 1, 2):
            u, v = near(first, i), near(second, k)
            cols.append(jnp.where(core == 0, 4 * v + u, 4 * u + v))
    return jnp.stack(rows + cols).astype(jnp.int32)


def dot3(a, b):
    a_hi, b_hi = a.astype(jnp.bfloat16), b.astype(jnp.bfloat16)
    a_lo = (a - a_hi.astype(F32)).astype(jnp.bfloat16)
    b_lo = (b - b_hi.astype(F32)).astype(jnp.bfloat16)
    mul = lambda p, q: jnp.dot(p, q, preferred_element_type=F32)
    return mul(a_hi, b_hi) + (mul(a_hi, b_lo) + mul(a_lo, b_hi))


def pair_dot(at, tile, a_buf, slot, b_buf, per):
    def one(k):
        return a_buf[slot + k], b_buf[lax.div(at[tile + k], per)]

    def body(q):
        (a0, b0), (a1, b1) = one(q), one(3 - q)
        return dot3(jnp.concatenate([a0, a1], axis=1), jnp.concatenate([b0, b1], axis=0))

    return body


def near_kernel(per, at, *refs):
    groups, tiles, (acc, far), (a_buf, b_buf, a_sem, b_sem) = refs[:3], refs[3:11], refs[11:13], refs[13:]
    outs = acc.shape[0]
    many = tiles[0].shape[0]
    copies = [
        pltpu.make_async_copy(tiles[i], b_buf.at[pl.ds(at[i] * many, many)], b_sem.at[i]) for i in range(8)
    ]
    copies += [pltpu.make_async_copy(groups[i], a_buf.at[pl.ds(4 * i, 4)], a_sem.at[i]) for i in range(3)]
    for copy in copies:
        copy.start()
    acc[...] = jnp.zeros_like(acc)
    for copy in copies:
        copy.wait()
    for k in range(4):
        far[k] = b_buf[lax.div(at[20 + k], per)]

    def body(i, carry):
        g, q = lax.div(i, 2), lax.rem(i, 2)
        p = lax.rem(at[8 + 4 * g + q], outs)
        acc[p] += pair_dot(at, 8 + 4 * g, a_buf, 4 * g, b_buf, per)(q)
        return carry

    lax.fori_loop(0, 6, body, 0)


def near_product(at, groups, tiles, outs):
    m, w = groups[0].shape[1:]
    many, k, n = tiles[0].shape
    return pl.pallas_call(
        functools.partial(near_kernel, 16 // (8 * many)),
        out_shape=(jax.ShapeDtypeStruct((outs, m, n), F32), jax.ShapeDtypeStruct((4, k, n), F32)),
        in_specs=[SMEM] + [ANY] * 11,
        out_specs=(VMEM, VMEM),
        scratch_shapes=[
            pltpu.VMEM((12, m, w), F32),
            pltpu.VMEM((8 * many, k, n), F32),
            pltpu.SemaphoreType.DMA((3,)),
            pltpu.SemaphoreType.DMA((8,)),
        ],
        compiler_params=params(40),
        cost_estimate=cost(m, 12 * w, n, 4 * w * (12 * m + 8 * many * n)),
        name="near",
    )(at, *groups, *tiles)


def far_sum(at, acc, top, low, far, a_buf, sem):
    copies = [pltpu.make_async_copy(top, a_buf.at[pl.ds(0, 2)], sem.at[0])]
    copies += [pltpu.make_async_copy(low, a_buf.at[pl.ds(2, 2)], sem.at[1])]
    for copy in copies:
        copy.start()
    for copy in copies:
        copy.wait()
    for q in range(2):
        yield q, dot3(
            jnp.concatenate([a_buf[q], a_buf[3 - q]], axis=1), jnp.concatenate([far[q], far[3 - q]], axis=0)
        )


def update_kernel(at, acc, top, low, far, u, ut, a_buf, sem):
    total = acc[0]
    for _, part in far_sum(at, acc, top, low, far, a_buf, sem):
        total += part
    u[...] = total
    ut[...] = total.T


def update_product(at, acc, top, low, far):
    _, m, n = acc.shape
    return pl.pallas_call(
        update_kernel,
        out_shape=(jax.ShapeDtypeStruct((m, n), F32), jax.ShapeDtypeStruct((n, m), F32)),
        in_specs=[SMEM, VMEM, ANY, ANY, VMEM],
        out_specs=(VMEM, VMEM),
        scratch_shapes=[pltpu.VMEM((4,) + top.shape[1:], F32), pltpu.SemaphoreType.DMA((2,))],
        compiler_params=params(24),
        cost_estimate=cost(m, 4 * top.shape[2], n, 16 * m * n),
        name="update",
    )(at, acc, top, low, far)


def child_kernel(at, acc, top, low, far, base, child, a_buf, sem):
    w = acc.shape[1]
    for p in range(2):
        child[pl.ds(p * w, w)] = base[pl.ds(p * w, w)] - acc[p]
    for q, part in far_sum(at, acc, top, low, far, a_buf, sem):
        p = pl.multiple_of(lax.rem(at[20 + q], 2) * w, 8)
        child[pl.ds(p, w)] -= part


def child_product(at, acc, top, low, far, base):
    return pl.pallas_call(
        child_kernel,
        out_shape=jax.ShapeDtypeStruct(base.shape, F32),
        in_specs=[SMEM, VMEM, ANY, ANY, VMEM, VMEM],
        out_specs=VMEM,
        scratch_shapes=[pltpu.VMEM((4,) + top.shape[1:], F32), pltpu.SemaphoreType.DMA((2,))],
        compiler_params=params(24),
        cost_estimate=cost(acc.shape[1], 4 * top.shape[2], acc.shape[2], 24 * acc.shape[1] * acc.shape[2]),
        name="child",
    )(at, acc, top, low, far, base)


def cross_kernel(at, *refs):
    groups, (top, low), tiles, (sigma,), (s_buf, u_buf, s_sem, u_sem) = (
        refs[:3], refs[3:5], refs[5:13], refs[13:14], refs[14:]
    )
    pieces = [g.at[i] for g in groups for i in range(4)] + [g.at[i] for g in (top, low) for i in range(2)]
    copies = [pltpu.make_async_copy(pieces[i], s_buf.at[at[8 + i]], s_sem.at[i]) for i in range(16)]
    copies += [pltpu.make_async_copy(tiles[i], u_buf.at[:, at[i]], u_sem.at[i]) for i in range(8)]
    for copy in copies:
        copy.start()
    sigma[...] = jnp.zeros_like(sigma)
    for copy in copies:
        copy.wait()
    m, w = sigma.shape

    def body(k, carry):
        lhs = s_buf[:, :, pl.ds(pl.multiple_of(k * 768, 128), 768)].reshape(m, 768)
        rhs = u_buf[pl.ds(3 * k, 3)].reshape(768, w)
        sigma[...] -= dot3(lhs, rhs)
        return carry

    lax.fori_loop(0, 4, body, 0)


def cross_product(at, near, far, tiles):
    q, width = near[0].shape[1:]
    sub, w = tiles[0].shape[1:]
    return pl.pallas_call(
        cross_kernel,
        out_shape=jax.ShapeDtypeStruct((16 * q, w), F32),
        in_specs=[SMEM] + [ANY] * 13,
        out_specs=VMEM,
        scratch_shapes=[
            pltpu.VMEM((16, q, width), F32),
            pltpu.VMEM((NANC, 8, sub, w), F32),
            pltpu.SemaphoreType.DMA((16,)),
            pltpu.SemaphoreType.DMA((8,)),
        ],
        compiler_params=params(40),
        cost_estimate=cost(16 * q, width, w, 4 * width * (16 * q + w)),
        name="cross",
    )(at, *near, *far, *tiles)


def spread(x):
    h, w = x.shape
    sub = h // 24
    return lax.all_to_all(x.reshape(3, 8, sub, w), ROW, 1, 0, tiled=True).reshape(NB, sub, w)


def pick_rows_kernel(anc, x, out):
    for i in range(NANC):
        out[i] = x[anc[i]]


def pick_rows(ancestors, x):
    sub, w = x.shape[1:]
    return pl.pallas_call(
        pick_rows_kernel,
        out_shape=jax.ShapeDtypeStruct((NANC, sub, w), F32),
        in_specs=[SMEM, VMEM],
        out_specs=VMEM,
        compiler_params=params(8),
        name="pick_rows",
    )(ancestors, x).reshape(NANC * sub, w)


def pick_cols_kernel(anc, x, out):
    for i in range(NANC):
        for k in range(2):
            t = 2 * anc[i] + k
            off = pl.multiple_of(lax.rem(t, 3) * 128, 128)
            out[:, pl.ds(i * 256 + k * 128, 128)] = x[lax.div(t, 3), :, pl.ds(off, 128)]


def pick_cols(ancestors, x):
    return pl.pallas_call(
        pick_cols_kernel,
        out_shape=jax.ShapeDtypeStruct((x.shape[1], NANC * 256), F32),
        in_specs=[SMEM, VMEM],
        out_specs=VMEM,
        compiler_params=params(8),
        name="pick_cols",
    )(ancestors, x)


def place_kernel(anc, x, out):
    out[...] = jnp.zeros_like(out)
    for i in range(NANC):
        out[anc[i]] = x[i]


def place_rows(ancestors, x):
    sub, w = x.shape[1:]
    return pl.pallas_call(
        place_kernel,
        out_shape=jax.ShapeDtypeStruct((NB, sub, w), F32),
        in_specs=[SMEM, VMEM],
        out_specs=VMEM,
        compiler_params=params(8),
        name="place_rows",
    )(ancestors, x)


def per_device(sigma_top, factor_cross, factor_inverse, block_inverse, ancestors):
    h, w = sigma_top.shape
    sub = h // 24
    at = places()

    f = pick_rows(ancestors, spread(factor_cross))
    inverse_tiles = [t.reshape(2, w, w) for t in gather_rows(factor_inverse)]
    f_near, f_far = gather_cols(f, 0)

    s = pick_rows(ancestors, spread(after(sigma_top, f)))
    s_cols = lax.all_to_all(after(s, f_near[0]).reshape(16, -1, w), COL, 0, 0, tiled=True)
    s_near, s_far = gather_cols(after(pick_cols(ancestors, s_cols), f_near[1], f_near[2]), 1, (f_far, (), ()))

    acc, b_far = near_product(at, f_near, inverse_tiles, 1)
    u, ut = update_product(at, acc, *f_far, b_far)

    moved = lax.ppermute(ut, ALL, [(16 * r + c, 16 * (c // 2) + 2 * r + c % 2) for r in range(8) for c in range(16)])
    u_near, u_far = gather_cols(moved, 0)
    u_tiles = gather_rows(u.reshape(NANC, sub, w))

    sigma = cross_product(at, s_near, s_far, u_tiles)
    sigma_tiles = [t[None] for t in gather_rows(sigma)]
    acc, b_far = near_product(at, u_near, sigma_tiles, 2)
    sigma_child = child_product(at, acc, *u_far, b_far, block_inverse)

    full = place_rows(ancestors, sigma.reshape(NANC, sub, w))
    back = lax.all_to_all(full.reshape(8, 3, sub, w), ROW, 0, 0, tiled=True)
    sigma_cross = back.reshape(8, 3, sub, w).transpose(1, 0, 2, 3).reshape(h, w)
    return (sigma_cross, sigma_child)


def solution(mesh):
    fine = Mesh(np.asarray(mesh.devices).reshape(4, 2, 4, 4), ALL)
    tile = P(ROW, COL)
    return jax.shard_map(
        per_device,
        mesh=fine,
        in_specs=(tile, tile, tile, tile, P()),
        out_specs=(tile, tile),
        check_vma=False,
    )
```

time: 345 us -> 298 us (0.86)
  between operations: 89 us -> 1.24 us
  Pallas kernels: 0 us -> 47 us
  local copies, waits for them, and re-layouts: 56.3 us -> 16.5 us
  starting transfers between devices: 62.1 us -> 98.8 us
  matrix products: 30.6 us -> 0 us
  blocking collectives: 0 us -> 22.4 us
  waiting for transfers between devices: 102 us -> 108 us
    pallas_call x0 -> x9, Pallas kernels: none -> 47 us  [the longest x2 24.4 us: near_product(): pl.pallas_call(functools.partial(near_kernel, 16 // (8 * many)), out_shap...]
    dot_general x4 -> x0, matrix products: 30.6 us -> none  [dot(): lax.dot_general(a, b, (dims, ((), ())), precision=lax.Precision.HIGH, pre...]
    ppermute x25 -> x46, starting transfers between devices: 48.2 us -> 74.9 us  [the longest x24 33.9 us: hop(): return lax.ppermute(x, ('core',) + COL, pairs)]
    dynamic_update_slice x23 -> x0, local copies, waits for them, and re-layouts: 26.2 us -> none  [the longest x8 15.4 us: per_device(): strip = lax.dynamic_update_slice(strip, t, (r * h, 0))]
    all_to_all x0 -> x1, blocking collectives: none -> 22.4 us  [spread(): lax.all_to_all(x.reshape(3, 8, sub, w), ROW, 1, 0, tiled=True)]
    ppermute x25 -> x46, waiting for transfers between devices: 75.6 us -> 91.6 us  [the longest x24 48 us: hop(): return lax.ppermute(x, ('core',) + COL, pairs)]
    all_to_all x2 -> x1, waiting for transfers between devices: 15.4 us -> 0.01 us  [spread(): lax.all_to_all(x.reshape(3, 8, sub, w), ROW, 1, 0, tiled=True)]
    unnamed x72 -> x8, local copies, waits for them, and re-layouts: 14.6 us -> 0.02 us
  transfers between devices with their start and end apart: 31 -> 49, of which waited for: 10 -> 16; matrix products, arithmetic and copies ran while one was open for 20% -> 6% of each run, Pallas kernels for 0% -> 14%
where the time goes in v4:
time: 298 us; the launch traced here: 297 us
  waiting for transfers between devices  108 us (36%)
  starting transfers between devices  98.8 us (33%)
  Pallas kernels  47 us (16%)
  blocking collectives  22.4 us (8%)
  local copies, waits for them, and re-layouts  16.5 us (6%)
  other arithmetic  3.1 us (1%)
    ppermute x24, waiting for transfers between devices, hop(): return lax.ppermute(x, ('core',) + COL, pairs)  48 us
    ppermute x24, starting transfers between devices, hop(): return lax.ppermute(x, ('core',) + COL, pairs)  33.9 us
    ppermute x9, waiting for transfers between devices, step(): lax.ppermute(x, ROW, [(2 * i + c, 2 * ((i + 1 - 2 * c) % 4) + c) for i in...  29.6 us
    pallas_call x2, Pallas kernels, near_product(): pl.pallas_call(functools.partial(near_kernel, 16 // (8 * many)), out_shap...  24.4 us
    all_to_all x1, blocking collectives, spread(): lax.all_to_all(x.reshape(3, 8, sub, w), ROW, 1, 0, tiled=True)  22.4 us
    ppermute x12, starting transfers between devices, swap(): return lax.ppermute(x, 'core', [(0, 1), (1, 0)])  21.9 us
    ppermute x9, starting transfers between devices, step(): lax.ppermute(x, ROW, [(2 * i + c, 2 * ((i + 1 - 2 * c) % 4) + c) for i in...  17.2 us
    ppermute x1, waiting for transfers between devices, per_device(): lax.ppermute(ut, ALL, [(16 * r + c, 16 * (c // 2) + 2 * r + c % 2) for r...  14 us
  transfers between devices with their start and end apart: 49, of which 16 were waited for; matrix products, arithmetic and copies ran while one was open for 6% of the time, Pallas kernels for 14%

profile of v4, /device:TPU:1, one launch (start us, length us, event | category | flops | bytes accessed | tf_op | source)
XLA Modules:
  0.0 297.1 jit_solution(5805167639733981598)
XLA Ops:
  0.6 1.3 copy.7
  2.0 22.4 %all_to_all.40 = f32[3,8,32,384]{3,2,0,1:T(8,128)S(1)} all-to-all(f32[3,8,32,384]{3,2,0,1:T(8,128)S(1)} %copy.7), channel_id=1, replica_groups=mesh['y'=4,'core'=2,'z'=4,'x'=4] {'y','core'}, dimensions={1} | all-to-all | bytes 2359296 | tf_op jit(solution)/shard_map/all_to_all | solution.py:250
  24.4 0.6 pick_rows.2
  25.0 3.8 %collective-permute-start.1 = (f32[384,384]{1,0:T(8,128)S(1)}, f32[384,384]{1,0:T(8,128)S(1)}, u32[]{:S(2)}, u32[]{:S(2)}) collective-permute-start(f32[384,384]{1,0:T(8,128)S(1)} %bitcast.77), channel_id=1, source_target_pairs={{0,3},{1,0},{2,1},{3,2},{4,7},{5,4},{6,5},{7,6},{8,11},{9,8},{10,9... | collective-permute-start | bytes 1769480 | tf_op jit(solution)/shard_map/ppermute | solution.py:56
  28.8 6.8 %collective-permute-done.1 = f32[384,384]{1,0:T(8,128)S(1)} collective-permute-done((f32[384,384]{1,0:T(8,128)S(1)}, f32[384,384]{1,0:T(8,128)S(1)}, u32[]{:S(2)}, u32[]{:S(2)}) %collective-permute-start.1) | collective-permute-done | bytes 589856 | tf_op jit(solution)/shard_map/ppermute | solution.py:56
  35.7 3.5 %collective-permute-start.3 = (f32[192,384]{1,0:T(8,128)S(1)}, f32[192,384]{1,0:T(8,128)S(1)}, u32[]{:S(2)}, u32[]{:S(2)}) collective-permute-start(f32[192,384]{1,0:T(8,128)S(1)} %slice.49), channel_id=1, source_target_pairs={{0,3},{1,0},{2,1},{3,2},{4,7},{5,4},{6,5},{7,6},{8,11},{9,8},{10,9... | collective-permute-start | bytes 884744 | tf_op jit(solution)/shard_map/ppermute | solution.py:56
  39.3 1.0 collective-permute-start.16
  40.2 2.6 collective-permute-done.3
  42.8 3.5 %collective-permute-done.2 = f32[192,384]{1,0:T(8,128)S(1)} collective-permute-done((f32[192,384]{1,0:T(8,128)S(1)}, f32[192,384]{1,0:T(8,128)S(1)}, u32[]{:S(2)}, u32[]{:S(2)}) %collective-permute-start.2) | collective-permute-done | bytes 294944 | tf_op jit(solution)/shard_map/ppermute | solution.py:56
  46.4 1.6 pad_maximum_fusion.refs_0_
  48.0 2.5 collective-permute-start.5
  50.5 4.3 %collective-permute-done.16 = f32[768,384]{1,0:T(8,128)S(1)} collective-permute-done((f32[768,384]{1,0:T(8,128)S(1)}, f32[768,384]{1,0:T(8,128)S(1)}, u32[]{:S(2)}, u32[]{:S(2)}) %collective-permute-start.16) | collective-permute-done | bytes 1179680 | tf_op jit(solution)/shard_map/ppermute | solution.py:35
  54.8 1.7 collective-permute-start.17
  56.5 1.1 copy.8
  57.6 5.5 %all-to-all-start.1 = ((f32[3,8,32,384]{3,2,0,1:T(8,128)}), f32[3,8,32,384]{3,2,0,1:T(8,128)S(1)}, u32[]{:S(2)}, u32[]{:S(2)}) async-start(f32[3,8,32,384]{3,2,0,1:T(8,128)} %copy.8), calls=%async_computation.1 | async-start | bytes 2359296 | tf_op jit(solution)/shard_map/all_to_all | solution.py:250
  63.1 13.7 %collective-permute-done.17 = f32[768,384]{1,0:T(8,128)} collective-permute-done((f32[768,384]{1,0:T(8,128)S(1)}, f32[768,384]{1,0:T(8,128)}, u32[]{:S(2)}, u32[]{:S(2)}) %collective-permute-start.17) | collective-permute-done | bytes 1179680 | tf_op jit(solution)/shard_map/ppermute | solution.py:35
  76.8 3.7 %collective-permute-start.18 = (f32[768,384]{1,0:T(8,128)}, f32[768,384]{1,0:T(8,128)}, u32[]{:S(2)}, u32[]{:S(2)}) collective-permute-start(f32[768,384]{1,0:T(8,128)} %collective-permute-done.17), channel_id=1, source_target_pairs={{0,32},{16,112},{32,64},{48,16},{64,96},{80,48},{96,0},{112,80},{1... | collective-permute-start | bytes 3538952 | tf_op jit(solution)/shard_map/ppermute | solution.py:35
  80.4 2.4 slice.51
  82.8 2.9 collective-permute-start.9
  85.7 1.4 pick_rows.3
  87.1 7.4 %all-to-all-start.2 = ((f32[16,24,384]{2,1,0:T(8,128)}), f32[16,24,384]{2,1,0:T(8,128)S(1)}, u32[]{:S(2)}, u32[]{:S(2)}) async-start(f32[16,24,384]{2,1,0:T(8,128)} %bitcast.38), calls=%async_computation.2 | async-start | bytes 1179648 | tf_op jit(solution)/shard_map/all_to_all | solution.py:317
  94.5 2.4 slice.50
  96.9 1.4 collective-permute-start.8
  98.2 7.2 %all-to-all-done.2.x = f32[16,24,384]{2,1,0:T(8,128)S(1)} async-done(((f32[16,24,384]{2,1,0:T(8,128)}), f32[16,24,384]{2,1,0:T(8,128)S(1)}, u32[]{:S(2)}, u32[]{:S(2)}) %all-to-all-start.2) | async-done | bytes 589856 | tf_op jit(solution)/shard_map/all_to_all | solution.py:317
  105.5 1.4 pick_cols.1
  107.3 5.3 %collective-permute-start.19 = (f32[768,384]{1,0:T(8,128)S(1)}, f32[768,384]{1,0:T(8,128)S(1)}, u32[]{:S(2)}, u32[]{:S(2)}) collective-permute-start(f32[768,384]{1,0:T(8,128)S(1)} %copy-done), channel_id=1, source_target_pairs={{0,16},{16,0},{1,17},{17,1},{2,18},{18,2},{3,19},{19,3},{4,20},{20... | collective-permute-start | bytes 3538952 | tf_op jit(solution)/shard_map/ppermute | solution.py:39
  113.0 6.0 %collective-permute-start.21 = (f32[768,384]{1,0:T(8,128)}, f32[768,384]{1,0:T(8,128)}, u32[]{:S(2)}, u32[]{:S(2)}) collective-permute-start(f32[768,384]{1,0:T(8,128)} %collective-permute-done.17), channel_id=1, source_target_pairs={{0,16},{16,0},{1,17},{17,1},{2,18},{18,2},{3,19},{19,3},{4,20},{20... | collective-permute-start | bytes 3538952 | tf_op jit(solution)/shard_map/ppermute | solution.py:39
  119.3 7.2 %collective-permute-done.6 = f32[24,3072]{1,0:T(8,128)} collective-permute-done((f32[24,3072]{1,0:T(8,128)}, f32[24,3072]{1,0:T(8,128)}, u32[]{:S(2)}, u32[]{:S(2)}) %collective-permute-start.6) | collective-permute-done | bytes 294944 | tf_op jit(solution)/shard_map/ppermute | solution.py:56
  126.5 0.9 slice.40
  127.4 0.9 slice.41
  128.7 1.3 collective-permute-start.10
  129.9 12.9 %near.2 = (f32[1,384,384]{2,1,0:T(8,128)S(1)}, f32[4,384,384]{2,1,0:T(8,128)S(1)}) custom-call(s32[24]{0:T(128)S(1)} %stack.141.at, f32[4,384,384]{2,1,0:T(8,128)} %pad_maximum_fusion.refs_0_, f32[4,384,384]{2,1,0:T(8,128)} %collective-permute-done.4.refs_1_, f32[4,384,384]{2,1,0:T(8,128)} %collective-permute-done.5.refs_2_, f32[2,384,384]{2,1,0:T(8,128)S(1)} %bitcast.80, ...), custom_call_target="tpu_custom_call" | custom-call | flops 4076863488 | bytes 16515072 | tf_op jit(solution)/shard_map/near/pallas_call | solution.py:130
  142.9 4.4 %update.1 = (f32[384,384]{1,0:T(8,128)S(1)}, f32[384,384]{1,0:T(8,128)S(1)}) custom-call(s32[24]{0:T(128)S(1)} %stack.141.at, f32[1,384,384]{2,1,0:T(8,128)S(1)} %get-tuple-element.18.acc, f32[2,384,384]{2,1,0:T(8,128)} %collective-permute-done.8.top, f32[2,384,384]{2,1,0:T(8,128)} %collective-permute-done.9.low, f32[4,384,384]{2,1,0:T(8,128)S(1)} %get-tuple-element.19.far), custom_call_target="tpu_custom_call" | custom-call | flops 1358954496 | bytes 2359296 | tf_op jit(solution)/shard_map/update/pallas_call | solution.py:170
  147.3 3.8 %collective-permute-start.23 = (f32[12,32,384]{2,1,0:T(8,128)S(1)}, f32[12,32,384]{2,1,0:T(8,128)S(1)}, u32[]{:S(2)}, u32[]{:S(2)}) collective-permute-start(f32[12,32,384]{2,1,0:T(8,128)S(1)} %bitcast.83), channel_id=1, source_target_pairs={{0,32},{16,112},{32,64},{48,16},{64,96},{80,48},{96,0},{112,80},{1... | collective-permute-start | bytes 1769480 | tf_op jit(solution)/shard_map/ppermute | solution.py:35
  151.1 1.9 collective-permute-start.30
  153.1 1.3 pad_maximum_fusion.2.refs_0_
  154.4 0.7 collective-permute-start.13
  155.1 0.8 collective-permute-start.12
  155.9 14.0 %collective-permute-done.30 = f32[384,384]{1,0:T(8,128)S(1)} collective-permute-done((f32[384,384]{1,0:T(8,128)S(1)}, f32[384,384]{1,0:T(8,128)S(1)}, u32[]{:S(2)}, u32[]{:S(2)}) %collective-permute-start.30) | collective-permute-done | bytes 589856 | tf_op jit(solution)/shard_map/ppermute | solution.py:323
  169.9 6.9 %collective-permute-start.32 = (f32[384,384]{1,0:T(8,128)S(1)}, f32[384,384]{1,0:T(8,128)S(1)}, u32[]{:S(2)}, u32[]{:S(2)}) collective-permute-start(f32[384,384]{1,0:T(8,128)S(1)} %collective-permute-done.30), channel_id=1, source_target_pairs={{0,3},{1,0},{2,1},{3,2},{4,7},{5,4},{6,5},{7,6},{8,11},{9,8},{10,9... | collective-permute-start | bytes 1769480 | tf_op jit(solution)/shard_map/ppermute | solution.py:56
  176.8 14.1 %collective-permute-done.32 = f32[384,384]{1,0:T(8,128)S(1)} collective-permute-done((f32[384,384]{1,0:T(8,128)S(1)}, f32[384,384]{1,0:T(8,128)S(1)}, u32[]{:S(2)}, u32[]{:S(2)}) %collective-permute-start.32) | collective-permute-done | bytes 589856 | tf_op jit(solution)/shard_map/ppermute | solution.py:56
  190.9 3.5 %collective-permute-start.34 = (f32[192,384]{1,0:T(8,128)S(1)}, f32[192,384]{1,0:T(8,128)S(1)}, u32[]{:S(2)}, u32[]{:S(2)}) collective-permute-start(f32[192,384]{1,0:T(8,128)S(1)} %slice.55), channel_id=1, source_target_pairs={{0,3},{1,0},{2,1},{3,2},{4,7},{5,4},{6,5},{7,6},{8,11},{9,8},{10,9... | collective-permute-start | bytes 884744 | tf_op jit(solution)/shard_map/ppermute | solution.py:56
  194.4 3.3 %collective-permute-start.26 = (f32[12,32,384]{2,1,0:T(8,128)S(1)}, f32[12,32,384]{2,1,0:T(8,128)S(1)}, u32[]{:S(2)}, u32[]{:S(2)}) collective-permute-start(f32[12,32,384]{2,1,0:T(8,128)S(1)} %bitcast.84), channel_id=1, source_target_pairs={{0,16},{16,0},{1,17},{17,1},{2,18},{18,2},{3,19},{19,3},{4,20},{20... | collective-permute-start | bytes 1769480 | tf_op jit(solution)/shard_map/ppermute | solution.py:39
  197.7 3.0 %collective-permute-start.25 = (f32[12,32,384]{2,1,0:T(8,128)S(1)}, f32[12,32,384]{2,1,0:T(8,128)S(1)}, u32[]{:S(2)}, u32[]{:S(2)}) collective-permute-start(f32[12,32,384]{2,1,0:T(8,128)S(1)} %collective-permute-done.24.refs_7_), channel_id=1, source_target_pairs={{0,32},{16,112},{32,64},{48,16},{64,96},{80,48},{96,0},{112,80},{1... | collective-permute-start | bytes 1769480 | tf_op jit(solution)/shard_map/ppermute | solution.py:35
  201.5 6.4 %collective-permute-done.33 = f32[192,384]{1,0:T(8,128)S(1)} collective-permute-done((f32[192,384]{1,0:T(8,128)S(1)}, f32[192,384]{1,0:T(8,128)S(1)}, u32[]{:S(2)}, u32[]{:S(2)}) %collective-permute-start.33) | collective-permute-done | bytes 294944 | tf_op jit(solution)/shard_map/ppermute | solution.py:56
  207.9 1.1 collective-permute-start.15
  209.7 2.8 collective-permute-start.36
  212.5 4.6 %collective-permute-done.15.refs_4_ = f32[2,24,3072]{2,1,0:T(8,128)S(1)} collective-permute-done((f32[2,24,3072]{2,1,0:T(8,128)S(1)}, f32[2,24,3072]{2,1,0:T(8,128)S(1)}, u32[]{:S(2)}, u32[]{:S(2)}) %collective-permute-start.15) | collective-permute-done | bytes 589856 | tf_op jit(solution)/shard_map/ppermute | solution.py:56
  217.0 2.4 collective-permute-done.14.refs_3_
  219.5 7.7 %cross.1 = f32[384,384]{1,0:T(8,128)} custom-call(s32[24]{0:T(128)S(1)} %stack.141.at, f32[4,24,3072]{2,1,0:T(8,128)S(1)} %pad_maximum_fusion.2.refs_0_, f32[4,24,3072]{2,1,0:T(8,128)S(1)} %collective-permute-done.12.refs_1_, f32[4,24,3072]{2,1,0:T(8,128)S(1)} %collective-permute-done.13.refs_2_, f32[2,24,3072]{2,1,0:T(8,128)S(1)} %collective-permute-done.14.refs_3_, ...), custom_call_target="tpu_custom_call" | custom-call | flops 2717908992 | bytes 9437184 | tf_op jit(solution)/shard_map/cross/pallas_call | solution.py:230
  227.3 9.3 %collective-permute-done.37 = f32[384,384]{1,0:T(8,128)} collective-permute-done((f32[384,384]{1,0:T(8,128)}, f32[384,384]{1,0:T(8,128)}, u32[]{:S(2)}, u32[]{:S(2)}) %collective-permute-start.37) | collective-permute-done | bytes 589856 | tf_op jit(solution)/shard_map/ppermute | solution.py:35
  236.6 1.2 collective-permute-start.38
  237.8 5.6 %collective-permute-start.40 = (f32[384,384]{1,0:T(8,128)}, f32[384,384]{1,0:T(8,128)}, u32[]{:S(2)}, u32[]{:S(2)}) collective-permute-start(f32[384,384]{1,0:T(8,128)} %cross.1), channel_id=1, source_target_pairs={{0,16},{16,0},{1,17},{17,1},{2,18},{18,2},{3,19},{19,3},{4,20},{20... | collective-permute-start | bytes 1769480 | tf_op jit(solution)/shard_map/ppermute | solution.py:39
  243.4 2.3 collective-permute-done.38
  245.6 2.7 collective-permute-start.39
  248.4 2.2 place_rows.1
  250.6 10.9 %all-to-all-start.3 = ((f32[8,3,32,384]{3,2,1,0:T(8,128)}), f32[8,3,32,384]{3,2,1,0:T(8,128)}, u32[]{:S(2)}, u32[]{:S(2)}) async-start(f32[8,3,32,384]{3,2,1,0:T(8,128)} %bitcast.53), calls=%async_computation.3 | async-start | bytes 2359296 | tf_op jit(solution)/shard_map/all_to_all | solution.py:333
  261.5 2.4 slice.57
  263.9 2.4 slice.56
  266.3 1.5 collective-permute-start.44
  268.9 9.2 %all-to-all-done.3 = f32[8,3,32,384]{3,2,1,0:T(8,128)} async-done(((f32[8,3,32,384]{3,2,1,0:T(8,128)}), f32[8,3,32,384]{3,2,1,0:T(8,128)}, u32[]{:S(2)}, u32[]{:S(2)}) %all-to-all-start.3) | async-done | bytes 1179680 | tf_op jit(solution)/shard_map/all_to_all | solution.py:333
  278.1 2.4 copy.9
  280.5 11.4 %near.3 = (f32[2,384,384]{2,1,0:T(8,128)S(1)}, f32[4,384,384]{2,1,0:T(8,128)S(1)}) custom-call(s32[24]{0:T(128)S(1)} %stack.141.at, f32[4,384,384]{2,1,0:T(8,128)S(1)} %pad_maximum_fusion.1.refs_0_, f32[4,384,384]{2,1,0:T(8,128)} %collective-permute-done.35.refs_1_, f32[4,384,384]{2,1,0:T(8,128)} %collective-permute-done.36.refs_2_, ...), custom_call_target="tpu_custom_call" | custom-call | flops 4076863488 | bytes 11796480 | tf_op jit(solution)/shard_map/near/pallas_call | solution.py:130
  292.0 5.0 %child.1 = f32[768,384]{1,0:T(8,128)} custom-call(s32[24]{0:T(128)S(1)} %stack.141.at, f32[2,384,384]{2,1,0:T(8,128)S(1)} %get-tuple-element.22.acc, f32[2,384,384]{2,1,0:T(8,128)} %collective-permute-done.44.top, f32[2,384,384]{2,1,0:T(8,128)S(1)} %collective-permute-done.45.low, f32[4,384,384]{2,1,0:T(8,128)S(1)} %get-tuple-element.23.far, ...), custom_call_target="tpu_custom_call" | custom-call | flops 1358954496 | bytes 3538944 | tf_op jit(solution)/shard_map/child/pallas_call | solution.py:192
  (74 shorter events, 4.2 us)
Async XLA Ops:
  2.0 22.4 %copy-start.2 = (s32[12]{0:T(128)S(1)}, s32[12]{0:T(128)}, u32[]{:S(2)}) copy-start(s32[12]{0:T(128)} %anc.7) | copy-start | bytes 148
  24.4 14.9 %copy-start = (f32[768,384]{1,0:T(8,128)S(1)}, f32[768,384]{1,0:T(8,128)}, u32[]{:S(2)}) copy-start(f32[768,384]{1,0:T(8,128)} %param.7) | copy-start | bytes 3538948
  25.0 10.7 %collective-permute-start.1 = (f32[384,384]{1,0:T(8,128)S(1)}, f32[384,384]{1,0:T(8,128)S(1)}, u32[]{:S(2)}, u32[]{:S(2)}) collective-permute-start(f32[384,384]{1,0:T(8,128)S(1)} %bitcast.77), channel_id=1, source_target_pairs={{0,3},{1,0},{2,1},{3,2},{4,7},{5,4},{6,5},{7,6},{8,11},{9,8},{10,9... | collective-permute-start | bytes 1769480 | tf_op jit(solution)/shard_map/ppermute | solution.py:56
  28.8 10.3 %collective-permute-start = (f32[384,384]{1,0:T(8,128)S(1)}, f32[384,384]{1,0:T(8,128)S(1)}, u32[]{:S(2)}, u32[]{:S(2)}) collective-permute-start(f32[384,384]{1,0:T(8,128)S(1)} %bitcast.78), channel_id=1, source_target_pairs={{0,1},{1,2},{2,3},{3,0},{4,5},{5,6},{6,7},{7,4},{8,9},{9,10},{10,1... | collective-permute-start | bytes 1769480 | tf_op jit(solution)/shard_map/ppermute | solution.py:56
  35.7 7.1 %collective-permute-start.3 = (f32[192,384]{1,0:T(8,128)S(1)}, f32[192,384]{1,0:T(8,128)S(1)}, u32[]{:S(2)}, u32[]{:S(2)}) collective-permute-start(f32[192,384]{1,0:T(8,128)S(1)} %slice.49), channel_id=1, source_target_pairs={{0,3},{1,0},{2,1},{3,2},{4,7},{5,4},{6,5},{7,6},{8,11},{9,8},{10,9... | collective-permute-start | bytes 884744 | tf_op jit(solution)/shard_map/ppermute | solution.py:56
  39.2 7.1 %collective-permute-start.2 = (f32[192,384]{1,0:T(8,128)S(1)}, f32[192,384]{1,0:T(8,128)S(1)}, u32[]{:S(2)}, u32[]{:S(2)}) collective-permute-start(f32[192,384]{1,0:T(8,128)S(1)} %slice.48), channel_id=1, source_target_pairs={{0,1},{1,2},{2,3},{3,0},{4,5},{5,6},{6,7},{7,4},{8,9},{9,10},{10,1... | collective-permute-start | bytes 884744 | tf_op jit(solution)/shard_map/ppermute | solution.py:56
  39.3 15.5 %collective-permute-start.16 = (f32[768,384]{1,0:T(8,128)S(1)}, f32[768,384]{1,0:T(8,128)S(1)}, u32[]{:S(2)}, u32[]{:S(2)}) collective-permute-start(f32[768,384]{1,0:T(8,128)S(1)} %copy-done), channel_id=1, source_target_pairs={{0,32},{16,112},{32,64},{48,16},{64,96},{80,48},{96,0},{112,80},{1... | collective-permute-start | bytes 3538952 | tf_op jit(solution)/shard_map/ppermute | solution.py:35
  46.4 10.1 %copy-start.3 = (f32[768,384]{1,0:T(8,128)S(1)}, f32[768,384]{1,0:T(8,128)}, u32[]{:S(2)}) copy-start(f32[768,384]{1,0:T(8,128)} %param.5) | copy-start | bytes 3538948
  48.0 32.4 %collective-permute-start.5 = (f32[4,384,384]{2,1,0:T(8,128)}, f32[4,384,384]{2,1,0:T(8,128)}, u32[]{:S(2)}, u32[]{:S(2)}) collective-permute-start(f32[4,384,384]{2,1,0:T(8,128)} %pad_maximum_fusion.refs_0_), channel_id=1, source_target_pairs={{0,12},{1,13},{2,14},{3,15},{4,0},{5,1},{6,2},{7,3},{8,4},{9,5},{1... | collective-permute-start | bytes 7077896 | tf_op jit(solution)/shard_map/ppermute | solution.py:56
  50.5 44.1 %collective-permute-start.4 = (f32[4,384,384]{2,1,0:T(8,128)}, f32[4,384,384]{2,1,0:T(8,128)}, u32[]{:S(2)}, u32[]{:S(2)}) collective-permute-start(f32[4,384,384]{2,1,0:T(8,128)} %pad_maximum_fusion.refs_0_), channel_id=1, source_target_pairs={{0,4},{1,5},{2,6},{3,7},{4,8},{5,9},{6,10},{7,11},{8,12},{9,13},{1... | collective-permute-start | bytes 7077896 | tf_op jit(solution)/shard_map/ppermute | solution.py:56
  54.8 21.9 %collective-permute-start.17 = (f32[768,384]{1,0:T(8,128)S(1)}, f32[768,384]{1,0:T(8,128)}, u32[]{:S(2)}, u32[]{:S(2)}) collective-permute-start(f32[768,384]{1,0:T(8,128)S(1)} %collective-permute-done.16), channel_id=1, source_target_pairs={{0,32},{16,112},{32,64},{48,16},{64,96},{80,48},{96,0},{112,80},{1... | collective-permute-start | bytes 3538952 | tf_op jit(solution)/shard_map/ppermute | solution.py:35
  57.6 28.1 %all-to-all-start.1 = ((f32[3,8,32,384]{3,2,0,1:T(8,128)}), f32[3,8,32,384]{3,2,0,1:T(8,128)S(1)}, u32[]{:S(2)}, u32[]{:S(2)}) async-start(f32[3,8,32,384]{3,2,0,1:T(8,128)} %copy.8), calls=%async_computation.1 | async-start | bytes 2359296 | tf_op jit(solution)/shard_map/all_to_all | solution.py:250
  76.8 35.9 %collective-permute-start.18 = (f32[768,384]{1,0:T(8,128)}, f32[768,384]{1,0:T(8,128)}, u32[]{:S(2)}, u32[]{:S(2)}) collective-permute-start(f32[768,384]{1,0:T(8,128)} %collective-permute-done.17), channel_id=1, source_target_pairs={{0,32},{16,112},{32,64},{48,16},{64,96},{80,48},{96,0},{112,80},{1... | collective-permute-start | bytes 3538952 | tf_op jit(solution)/shard_map/ppermute | solution.py:35
  82.8 36.3 %collective-permute-start.9 = (f32[2,384,384]{2,1,0:T(8,128)}, f32[2,384,384]{2,1,0:T(8,128)}, u32[]{:S(2)}, u32[]{:S(2)}) collective-permute-start(f32[2,384,384]{2,1,0:T(8,128)} %slice.51), channel_id=1, source_target_pairs={{0,12},{1,13},{2,14},{3,15},{4,0},{5,1},{6,2},{7,3},{8,4},{9,5},{1... | collective-permute-start | bytes 3538952 | tf_op jit(solution)/shard_map/ppermute | solution.py:56
  87.1 18.4 %all-to-all-start.2 = ((f32[16,24,384]{2,1,0:T(8,128)}), f32[16,24,384]{2,1,0:T(8,128)S(1)}, u32[]{:S(2)}, u32[]{:S(2)}) async-start(f32[16,24,384]{2,1,0:T(8,128)} %bitcast.38), calls=%async_computation.2 | async-start | bytes 1179648 | tf_op jit(solution)/shard_map/all_to_all | solution.py:317
  96.9 22.2 %collective-permute-start.8 = (f32[2,384,384]{2,1,0:T(8,128)}, f32[2,384,384]{2,1,0:T(8,128)}, u32[]{:S(2)}, u32[]{:S(2)}) collective-permute-start(f32[2,384,384]{2,1,0:T(8,128)} %slice.50), channel_id=1, source_target_pairs={{0,4},{1,5},{2,6},{3,7},{4,8},{5,9},{6,10},{7,11},{8,12},{9,13},{1... | collective-permute-start | bytes 3538952 | tf_op jit(solution)/shard_map/ppermute | solution.py:56
  106.8 6.2 %collective-permute-start.7 = (f32[24,3072]{1,0:T(8,128)}, f32[24,3072]{1,0:T(8,128)}, u32[]{:S(2)}, u32[]{:S(2)}) collective-permute-start(f32[24,3072]{1,0:T(8,128)} %pick_cols.1), channel_id=1, source_target_pairs={{0,3},{1,0},{2,1},{3,2},{4,7},{5,4},{6,5},{7,6},{8,11},{9,8},{10,9... | collective-permute-start | bytes 884744 | tf_op jit(solution)/shard_map/ppermute | solution.py:56
  107.3 21.4 %collective-permute-start.19 = (f32[768,384]{1,0:T(8,128)S(1)}, f32[768,384]{1,0:T(8,128)S(1)}, u32[]{:S(2)}, u32[]{:S(2)}) collective-permute-start(f32[768,384]{1,0:T(8,128)S(1)} %copy-done), channel_id=1, source_target_pairs={{0,16},{16,0},{1,17},{17,1},{2,18},{18,2},{3,19},{19,3},{4,20},{20... | collective-permute-start | bytes 3538952 | tf_op jit(solution)/shard_map/ppermute | solution.py:39
  112.6 17.3 %collective-permute-start.20 = (f32[768,384]{1,0:T(8,128)S(1)}, f32[768,384]{1,0:T(8,128)}, u32[]{:S(2)}, u32[]{:S(2)}) collective-permute-start(f32[768,384]{1,0:T(8,128)S(1)} %collective-permute-done.16), channel_id=1, source_target_pairs={{0,16},{16,0},{1,17},{17,1},{2,18},{18,2},{3,19},{19,3},{4,20},{20... | collective-permute-start | bytes 3538952 | tf_op jit(solution)/shard_map/ppermute | solution.py:39
  113.0 16.9 %collective-permute-start.21 = (f32[768,384]{1,0:T(8,128)}, f32[768,384]{1,0:T(8,128)}, u32[]{:S(2)}, u32[]{:S(2)}) collective-permute-start(f32[768,384]{1,0:T(8,128)} %collective-permute-done.17), channel_id=1, source_target_pairs={{0,16},{16,0},{1,17},{17,1},{2,18},{18,2},{3,19},{19,3},{4,20},{20... | collective-permute-start | bytes 3538952 | tf_op jit(solution)/shard_map/ppermute | solution.py:39
  119.1 10.9 %collective-permute-start.22 = (f32[768,384]{1,0:T(8,128)}, f32[768,384]{1,0:T(8,128)}, u32[]{:S(2)}, u32[]{:S(2)}) collective-permute-start(f32[768,384]{1,0:T(8,128)} %collective-permute-done.18), channel_id=1, source_target_pairs={{0,16},{16,0},{1,17},{17,1},{2,18},{18,2},{3,19},{19,3},{4,20},{20... | collective-permute-start | bytes 3538952 | tf_op jit(solution)/shard_map/ppermute | solution.py:39
  119.1 7.5 %collective-permute-start.6 = (f32[24,3072]{1,0:T(8,128)}, f32[24,3072]{1,0:T(8,128)}, u32[]{:S(2)}, u32[]{:S(2)}) collective-permute-start(f32[24,3072]{1,0:T(8,128)} %pick_cols.1), channel_id=1, source_target_pairs={{0,1},{1,2},{2,3},{3,0},{4,5},{5,6},{6,7},{7,4},{8,9},{9,10},{10,1... | collective-permute-start | bytes 884744 | tf_op jit(solution)/shard_map/ppermute | solution.py:56
  128.4 24.7 %collective-permute-start.11 = (f32[24,1536]{1,0:T(8,128)S(1)}, f32[24,1536]{1,0:T(8,128)S(1)}, u32[]{:S(2)}, u32[]{:S(2)}) collective-permute-start(f32[24,1536]{1,0:T(8,128)S(1)} %slice.41), channel_id=1, source_target_pairs={{0,3},{1,0},{2,1},{3,2},{4,7},{5,4},{6,5},{7,6},{8,11},{9,8},{10,9... | collective-permute-start | bytes 442376 | tf_op jit(solution)/shard_map/ppermute | solution.py:56
  128.7 24.4 %collective-permute-start.10 = (f32[24,1536]{1,0:T(8,128)S(1)}, f32[24,1536]{1,0:T(8,128)S(1)}, u32[]{:S(2)}, u32[]{:S(2)}) collective-permute-start(f32[24,1536]{1,0:T(8,128)S(1)} %slice.40), channel_id=1, source_target_pairs={{0,1},{1,2},{2,3},{3,0},{4,5},{5,6},{6,7},{7,4},{8,9},{9,10},{10,1... | collective-permute-start | bytes 442376 | tf_op jit(solution)/shard_map/ppermute | solution.py:56
  147.3 29.5 %collective-permute-start.23 = (f32[12,32,384]{2,1,0:T(8,128)S(1)}, f32[12,32,384]{2,1,0:T(8,128)S(1)}, u32[]{:S(2)}, u32[]{:S(2)}) collective-permute-start(f32[12,32,384]{2,1,0:T(8,128)S(1)} %bitcast.83), channel_id=1, source_target_pairs={{0,32},{16,112},{32,64},{48,16},{64,96},{80,48},{96,0},{112,80},{1... | collective-permute-start | bytes 1769480 | tf_op jit(solution)/shard_map/ppermute | solution.py:35
  151.1 18.7 %collective-permute-start.30 = (f32[384,384]{1,0:T(8,128)S(1)}, f32[384,384]{1,0:T(8,128)S(1)}, u32[]{:S(2)}, u32[]{:S(2)}) collective-permute-start(f32[384,384]{1,0:T(8,128)S(1)} %get-tuple-element.21), channel_id=1, source_target_pairs={{0,0},{1,1},{2,16},{3,17},{4,32},{5,33},{6,48},{7,49},{8,64},{9,65... | collective-permute-start | bytes 1769480 | tf_op jit(solution)/shard_map/ppermute | solution.py:323
  154.4 46.4 %collective-permute-start.13 = (f32[4,24,3072]{2,1,0:T(8,128)S(1)}, f32[4,24,3072]{2,1,0:T(8,128)S(1)}, u32[]{:S(2)}, u32[]{:S(2)}) collective-permute-start(f32[4,24,3072]{2,1,0:T(8,128)S(1)} %pad_maximum_fusion.2.refs_0_), channel_id=1, source_target_pairs={{0,12},{1,13},{2,14},{3,15},{4,0},{5,1},{6,2},{7,3},{8,4},{9,5},{1... | collective-permute-start | bytes 3538952 | tf_op jit(solution)/shard_map/ppermute | solution.py:56
  155.1 45.7 %collective-permute-start.12 = (f32[4,24,3072]{2,1,0:T(8,128)S(1)}, f32[4,24,3072]{2,1,0:T(8,128)S(1)}, u32[]{:S(2)}, u32[]{:S(2)}) collective-permute-start(f32[4,24,3072]{2,1,0:T(8,128)S(1)} %pad_maximum_fusion.2.refs_0_), channel_id=1, source_target_pairs={{0,4},{1,5},{2,6},{3,7},{4,8},{5,9},{6,10},{7,11},{8,12},{9,13},{1... | collective-permute-start | bytes 3538952 | tf_op jit(solution)/shard_map/ppermute | solution.py:56
  169.9 21.0 %collective-permute-start.32 = (f32[384,384]{1,0:T(8,128)S(1)}, f32[384,384]{1,0:T(8,128)S(1)}, u32[]{:S(2)}, u32[]{:S(2)}) collective-permute-start(f32[384,384]{1,0:T(8,128)S(1)} %collective-permute-done.30), channel_id=1, source_target_pairs={{0,3},{1,0},{2,1},{3,2},{4,7},{5,4},{6,5},{7,6},{8,11},{9,8},{10,9... | collective-permute-start | bytes 1769480 | tf_op jit(solution)/shard_map/ppermute | solution.py:56
  176.8 17.6 %collective-permute-start.24 = (f32[12,32,384]{2,1,0:T(8,128)S(1)}, f32[12,32,384]{2,1,0:T(8,128)S(1)}, u32[]{:S(2)}, u32[]{:S(2)}) collective-permute-start(f32[12,32,384]{2,1,0:T(8,128)S(1)} %collective-permute-done.23.refs_6_), channel_id=1, source_target_pairs={{0,32},{16,112},{32,64},{48,16},{64,96},{80,48},{96,0},{112,80},{1... | collective-permute-start | bytes 1769480 | tf_op jit(solution)/shard_map/ppermute | solution.py:35
  176.8 20.9 %collective-permute-start.31 = (f32[384,384]{1,0:T(8,128)S(1)}, f32[384,384]{1,0:T(8,128)S(1)}, u32[]{:S(2)}, u32[]{:S(2)}) collective-permute-start(f32[384,384]{1,0:T(8,128)S(1)} %collective-permute-done.30), channel_id=1, source_target_pairs={{0,1},{1,2},{2,3},{3,0},{4,5},{5,6},{6,7},{7,4},{8,9},{9,10},{10,1... | collective-permute-start | bytes 1769480 | tf_op jit(solution)/shard_map/ppermute | solution.py:56
  190.9 10.1 %collective-permute-start.34 = (f32[192,384]{1,0:T(8,128)S(1)}, f32[192,384]{1,0:T(8,128)S(1)}, u32[]{:S(2)}, u32[]{:S(2)}) collective-permute-start(f32[192,384]{1,0:T(8,128)S(1)} %slice.55), channel_id=1, source_target_pairs={{0,3},{1,0},{2,1},{3,2},{4,7},{5,4},{6,5},{7,6},{8,11},{9,8},{10,9... | collective-permute-start | bytes 884744 | tf_op jit(solution)/shard_map/ppermute | solution.py:56
  194.4 14.7 %collective-permute-start.26 = (f32[12,32,384]{2,1,0:T(8,128)S(1)}, f32[12,32,384]{2,1,0:T(8,128)S(1)}, u32[]{:S(2)}, u32[]{:S(2)}) collective-permute-start(f32[12,32,384]{2,1,0:T(8,128)S(1)} %bitcast.84), channel_id=1, source_target_pairs={{0,16},{16,0},{1,17},{17,1},{2,18},{18,2},{3,19},{19,3},{4,20},{20... | collective-permute-start | bytes 1769480 | tf_op jit(solution)/shard_map/ppermute | solution.py:39
  197.7 11.8 %collective-permute-start.25 = (f32[12,32,384]{2,1,0:T(8,128)S(1)}, f32[12,32,384]{2,1,0:T(8,128)S(1)}, u32[]{:S(2)}, u32[]{:S(2)}) collective-permute-start(f32[12,32,384]{2,1,0:T(8,128)S(1)} %collective-permute-done.24.refs_7_), channel_id=1, source_target_pairs={{0,32},{16,112},{32,64},{48,16},{64,96},{80,48},{96,0},{112,80},{1... | collective-permute-start | bytes 1769480 | tf_op jit(solution)/shard_map/ppermute | solution.py:35
  200.8 7.1 %collective-permute-start.33 = (f32[192,384]{1,0:T(8,128)S(1)}, f32[192,384]{1,0:T(8,128)S(1)}, u32[]{:S(2)}, u32[]{:S(2)}) collective-permute-start(f32[192,384]{1,0:T(8,128)S(1)} %slice.54), channel_id=1, source_target_pairs={{0,1},{1,2},{2,3},{3,0},{4,5},{5,6},{6,7},{7,4},{8,9},{9,10},{10,1... | collective-permute-start | bytes 884744 | tf_op jit(solution)/shard_map/ppermute | solution.py:56
  200.8 8.8 %collective-permute-start.27 = (f32[12,32,384]{2,1,0:T(8,128)S(1)}, f32[12,32,384]{2,1,0:T(8,128)S(1)}, u32[]{:S(2)}, u32[]{:S(2)}) collective-permute-start(f32[12,32,384]{2,1,0:T(8,128)S(1)} %collective-permute-done.23.refs_6_), channel_id=1, source_target_pairs={{0,16},{16,0},{1,17},{17,1},{2,18},{18,2},{3,19},{19,3},{4,20},{20... | collective-permute-start | bytes 1769480 | tf_op jit(solution)/shard_map/ppermute | solution.py:39
  201.0 11.5 %collective-permute-start.28 = (f32[12,32,384]{2,1,0:T(8,128)S(1)}, f32[12,32,384]{2,1,0:T(8,128)S(1)}, u32[]{:S(2)}, u32[]{:S(2)}) collective-permute-start(f32[12,32,384]{2,1,0:T(8,128)S(1)} %collective-permute-done.24.refs_7_), channel_id=1, source_target_pairs={{0,16},{16,0},{1,17},{17,1},{2,18},{18,2},{3,19},{19,3},{4,20},{20... | collective-permute-start | bytes 1769480 | tf_op jit(solution)/shard_map/ppermute | solution.py:39
  207.9 9.1 %collective-permute-start.15 = (f32[2,24,3072]{2,1,0:T(8,128)S(1)}, f32[2,24,3072]{2,1,0:T(8,128)S(1)}, u32[]{:S(2)}, u32[]{:S(2)}) collective-permute-start(f32[2,24,3072]{2,1,0:T(8,128)S(1)} %slice.53), channel_id=1, source_target_pairs={{0,12},{1,13},{2,14},{3,15},{4,0},{5,1},{6,2},{7,3},{8,4},{9,5},{1... | collective-permute-start | bytes 1769480 | tf_op jit(solution)/shard_map/ppermute | solution.py:56
  209.0 10.4 %collective-permute-start.14 = (f32[2,24,3072]{2,1,0:T(8,128)S(1)}, f32[2,24,3072]{2,1,0:T(8,128)S(1)}, u32[]{:S(2)}, u32[]{:S(2)}) collective-permute-start(f32[2,24,3072]{2,1,0:T(8,128)S(1)} %slice.52), channel_id=1, source_target_pairs={{0,4},{1,5},{2,6},{3,7},{4,8},{5,9},{6,10},{7,11},{8,12},{9,13},{1... | collective-permute-start | bytes 1769480 | tf_op jit(solution)/shard_map/ppermute | solution.py:56
  209.5 10.0 %collective-permute-start.29 = (f32[12,32,384]{2,1,0:T(8,128)S(1)}, f32[12,32,384]{2,1,0:T(8,128)S(1)}, u32[]{:S(2)}, u32[]{:S(2)}) collective-permute-start(f32[12,32,384]{2,1,0:T(8,128)S(1)} %collective-permute-done.25.refs_8_), channel_id=1, source_target_pairs={{0,16},{16,0},{1,17},{17,1},{2,18},{18,2},{3,19},{19,3},{4,20},{20... | collective-permute-start | bytes 1769480 | tf_op jit(solution)/shard_map/ppermute | solution.py:39
  209.7 51.8 %collective-permute-start.36 = (f32[4,384,384]{2,1,0:T(8,128)S(1)}, f32[4,384,384]{2,1,0:T(8,128)}, u32[]{:S(2)}, u32[]{:S(2)}) collective-permute-start(f32[4,384,384]{2,1,0:T(8,128)S(1)} %pad_maximum_fusion.1.refs_0_), channel_id=1, source_target_pairs={{0,12},{1,13},{2,14},{3,15},{4,0},{5,1},{6,2},{7,3},{8,4},{9,5},{1... | collective-permute-start | bytes 7077896 | tf_op jit(solution)/shard_map/ppermute | solution.py:56
  212.5 51.5 %collective-permute-start.35 = (f32[4,384,384]{2,1,0:T(8,128)S(1)}, f32[4,384,384]{2,1,0:T(8,128)}, u32[]{:S(2)}, u32[]{:S(2)}) collective-permute-start(f32[4,384,384]{2,1,0:T(8,128)S(1)} %pad_maximum_fusion.1.refs_0_), channel_id=1, source_target_pairs={{0,4},{1,5},{2,6},{3,7},{4,8},{5,9},{6,10},{7,11},{8,12},{9,13},{1... | collective-permute-start | bytes 7077896 | tf_op jit(solution)/shard_map/ppermute | solution.py:56
  227.2 9.4 %collective-permute-start.37 = (f32[384,384]{1,0:T(8,128)}, f32[384,384]{1,0:T(8,128)}, u32[]{:S(2)}, u32[]{:S(2)}) collective-permute-start(f32[384,384]{1,0:T(8,128)} %cross.1), channel_id=1, source_target_pairs={{0,32},{16,112},{32,64},{48,16},{64,96},{80,48},{96,0},{112,80},{1... | collective-permute-start | bytes 1769480 | tf_op jit(solution)/shard_map/ppermute | solution.py:35
  236.6 9.0 %collective-permute-start.38 = (f32[384,384]{1,0:T(8,128)}, f32[384,384]{1,0:T(8,128)}, u32[]{:S(2)}, u32[]{:S(2)}) collective-permute-start(f32[384,384]{1,0:T(8,128)} %collective-permute-done.37), channel_id=1, source_target_pairs={{0,32},{16,112},{32,64},{48,16},{64,96},{80,48},{96,0},{112,80},{1... | collective-permute-start | bytes 1769480 | tf_op jit(solution)/shard_map/ppermute | solution.py:35
  237.8 30.5 %collective-permute-start.40 = (f32[384,384]{1,0:T(8,128)}, f32[384,384]{1,0:T(8,128)}, u32[]{:S(2)}, u32[]{:S(2)}) collective-permute-start(f32[384,384]{1,0:T(8,128)} %cross.1), channel_id=1, source_target_pairs={{0,16},{16,0},{1,17},{17,1},{2,18},{18,2},{3,19},{19,3},{4,20},{20... | collective-permute-start | bytes 1769480 | tf_op jit(solution)/shard_map/ppermute | solution.py:39
  245.6 22.7 %collective-permute-start.39 = (f32[384,384]{1,0:T(8,128)}, f32[384,384]{1,0:T(8,128)}, u32[]{:S(2)}, u32[]{:S(2)}) collective-permute-start(f32[384,384]{1,0:T(8,128)} %collective-permute-done.38), channel_id=1, source_target_pairs={{0,32},{16,112},{32,64},{48,16},{64,96},{80,48},{96,0},{112,80},{1... | collective-permute-start | bytes 1769480 | tf_op jit(solution)/shard_map/ppermute | solution.py:35
  250.6 27.5 %all-to-all-start.3 = ((f32[8,3,32,384]{3,2,1,0:T(8,128)}), f32[8,3,32,384]{3,2,1,0:T(8,128)}, u32[]{:S(2)}, u32[]{:S(2)}) async-start(f32[8,3,32,384]{3,2,1,0:T(8,128)} %bitcast.53), calls=%async_computation.3 | async-start | bytes 2359296 | tf_op jit(solution)/shard_map/all_to_all | solution.py:333
  263.9 28.0 %collective-permute-start.45 = (f32[2,384,384]{2,1,0:T(8,128)}, f32[2,384,384]{2,1,0:T(8,128)S(1)}, u32[]{:S(2)}, u32[]{:S(2)}) collective-permute-start(f32[2,384,384]{2,1,0:T(8,128)} %slice.57), channel_id=1, source_target_pairs={{0,12},{1,13},{2,14},{3,15},{4,0},{5,1},{6,2},{7,3},{8,4},{9,5},{1... | collective-permute-start | bytes 3538952 | tf_op jit(solution)/shard_map/ppermute | solution.py:56
  266.3 25.6 %collective-permute-start.44 = (f32[2,384,384]{2,1,0:T(8,128)}, f32[2,384,384]{2,1,0:T(8,128)}, u32[]{:S(2)}, u32[]{:S(2)}) collective-permute-start(f32[2,384,384]{2,1,0:T(8,128)} %slice.56), channel_id=1, source_target_pairs={{0,4},{1,5},{2,6},{3,7},{4,8},{5,9},{6,10},{7,11},{8,12},{9,13},{1... | collective-permute-start | bytes 3538952 | tf_op jit(solution)/shard_map/ppermute | solution.py:56
  267.8 12.7 %collective-permute-start.41 = (f32[384,384]{1,0:T(8,128)}, f32[384,384]{1,0:T(8,128)}, u32[]{:S(2)}, u32[]{:S(2)}) collective-permute-start(f32[384,384]{1,0:T(8,128)} %collective-permute-done.37), channel_id=1, source_target_pairs={{0,16},{16,0},{1,17},{17,1},{2,18},{18,2},{3,19},{19,3},{4,20},{20... | collective-permute-start | bytes 1769480 | tf_op jit(solution)/shard_map/ppermute | solution.py:39
  268.4 12.1 %collective-permute-start.42 = (f32[384,384]{1,0:T(8,128)}, f32[384,384]{1,0:T(8,128)}, u32[]{:S(2)}, u32[]{:S(2)}) collective-permute-start(f32[384,384]{1,0:T(8,128)} %collective-permute-done.38), channel_id=1, source_target_pairs={{0,16},{16,0},{1,17},{17,1},{2,18},{18,2},{3,19},{19,3},{4,20},{20... | collective-permute-start | bytes 1769480 | tf_op jit(solution)/shard_map/ppermute | solution.py:39
  268.4 12.1 %collective-permute-start.43 = (f32[384,384]{1,0:T(8,128)}, f32[384,384]{1,0:T(8,128)}, u32[]{:S(2)}, u32[]{:S(2)}) collective-permute-start(f32[384,384]{1,0:T(8,128)} %collective-permute-done.39), channel_id=1, source_target_pairs={{0,16},{16,0},{1,17},{17,1},{2,18},{18,2},{3,19},{19,3},{4,20},{20... | collective-permute-start | bytes 1769480 | tf_op jit(solution)/shard_map/ppermute | solution.py:39
  280.5 11.5 %copy-start.1 = (f32[768,384]{1,0:T(8,128)S(1)}, f32[768,384]{1,0:T(8,128)}, u32[]{:S(2)}) copy-start(f32[768,384]{1,0:T(8,128)} %base.1) | copy-start | bytes 3538948

commit v5 on v4

--- a/solution.py
+++ b/solution.py
@@ -100,20 +100,15 @@
 
 
 def near_kernel(per, at, *refs):
-    groups, tiles, (acc, far), (a_buf, b_buf, a_sem, b_sem) = refs[:3], refs[3:11], refs[11:13], refs[13:]
+    groups, tiles, acc, (a_buf, b_buf, a_sem, b_sem) = refs[:3], refs[3], refs[4], refs[5:]
     outs = acc.shape[0]
-    many = tiles[0].shape[0]
-    copies = [
-        pltpu.make_async_copy(tiles[i], b_buf.at[pl.ds(at[i] * many, many)], b_sem.at[i]) for i in range(8)
-    ]
+    copies = [pltpu.make_async_copy(tiles, b_buf, b_sem)]
     copies += [pltpu.make_async_copy(groups[i], a_buf.at[pl.ds(4 * i, 4)], a_sem.at[i]) for i in range(3)]
     for copy in copies:
         copy.start()
     acc[...] = jnp.zeros_like(acc)
     for copy in copies:
         copy.wait()
-    for k in range(4):
-        far[k] = b_buf[lax.div(at[20 + k], per)]
 
     def body(i, carry):
         g, q = lax.div(i, 2), lax.rem(i, 2)
@@ -126,97 +121,102 @@
 
 def near_product(at, groups, tiles, outs):
     m, w = groups[0].shape[1:]
-    many, k, n = tiles[0].shape
-    return pl.pallas_call(
-        functools.partial(near_kernel, 16 // (8 * many)),
-        out_shape=(jax.ShapeDtypeStruct((outs, m, n), F32), jax.ShapeDtypeStruct((4, k, n), F32)),
-        in_specs=[SMEM] + [ANY] * 11,
-        out_specs=(VMEM, VMEM),
+    many, _, n = tiles.shape
+    return pl.pallas_call(
+        functools.partial(near_kernel, 16 // many),
+        out_shape=jax.ShapeDtypeStruct((outs, m, n), F32),
+        in_specs=[SMEM] + [ANY] * 4,
+        out_specs=VMEM,
         scratch_shapes=[
             pltpu.VMEM((12, m, w), F32),
-            pltpu.VMEM((8 * many, k, n), F32),
+            pltpu.VMEM(tiles.shape, F32),
             pltpu.SemaphoreType.DMA((3,)),
-            pltpu.SemaphoreType.DMA((8,)),
+            pltpu.SemaphoreType.DMA,
         ],
         compiler_params=params(40),
-        cost_estimate=cost(m, 12 * w, n, 4 * w * (12 * m + 8 * many * n)),
+        cost_estimate=cost(20 * m, 12 * w, n, 20 * 4 * w * (12 * m + many * n)),
         name="near",
-    )(at, *groups, *tiles)
-
-
-def far_sum(at, acc, top, low, far, a_buf, sem):
+    )(at, *groups, tiles)
+
+
+def far_sum(at, top, low, tiles, a_buf, b_buf, sem, per):
     copies = [pltpu.make_async_copy(top, a_buf.at[pl.ds(0, 2)], sem.at[0])]
     copies += [pltpu.make_async_copy(low, a_buf.at[pl.ds(2, 2)], sem.at[1])]
+    copies += [pltpu.make_async_copy(tiles.at[lax.div(at[20 + k], per)], b_buf.at[k], sem.at[2 + k]) for k in range(4)]
     for copy in copies:
         copy.start()
     for copy in copies:
         copy.wait()
     for q in range(2):
         yield q, dot3(
-            jnp.concatenate([a_buf[q], a_buf[3 - q]], axis=1), jnp.concatenate([far[q], far[3 - q]], axis=0)
+            jnp.concatenate([a_buf[q], a_buf[3 - q]], axis=1), jnp.concatenate([b_buf[q], b_buf[3 - q]], axis=0)
         )
 
 
-def update_kernel(at, acc, top, low, far, u, ut, a_buf, sem):
+def far_scratch(top, tiles):
+    return [
+        pltpu.VMEM((4,) + top.shape[1:], F32),
+        pltpu.VMEM((4,) + tiles.shape[1:], F32),
+        pltpu.SemaphoreType.DMA((6,)),
+    ]
+
+
+def update_kernel(at, acc, top, low, tiles, u, ut, a_buf, b_buf, sem):
     total = acc[0]
-    for _, part in far_sum(at, acc, top, low, far, a_buf, sem):
+    for _, part in far_sum(at, top, low, tiles, a_buf, b_buf, sem, 1):
         total += part
     u[...] = total
     ut[...] = total.T
 
 
-def update_product(at, acc, top, low, far):
+def update_product(at, acc, top, low, tiles):
     _, m, n = acc.shape
     return pl.pallas_call(
         update_kernel,
         out_shape=(jax.ShapeDtypeStruct((m, n), F32), jax.ShapeDtypeStruct((n, m), F32)),
-        in_specs=[SMEM, VMEM, ANY, ANY, VMEM],
+        in_specs=[SMEM, VMEM, ANY, ANY, ANY],
         out_specs=(VMEM, VMEM),
-        scratch_shapes=[pltpu.VMEM((4,) + top.shape[1:], F32), pltpu.SemaphoreType.DMA((2,))],
+        scratch_shapes=far_scratch(top, tiles),
         compiler_params=params(24),
         cost_estimate=cost(m, 4 * top.shape[2], n, 16 * m * n),
         name="update",
-    )(at, acc, top, low, far)
-
-
-def child_kernel(at, acc, top, low, far, base, child, a_buf, sem):
+    )(at, acc, top, low, tiles)
+
+
+def child_kernel(at, acc, top, low, tiles, base, child, a_buf, b_buf, sem):
     w = acc.shape[1]
     for p in range(2):
         child[pl.ds(p * w, w)] = base[pl.ds(p * w, w)] - acc[p]
-    for q, part in far_sum(at, acc, top, low, far, a_buf, sem):
+    for q, part in far_sum(at, top, low, tiles, a_buf, b_buf, sem, 2):
         p = pl.multiple_of(lax.rem(at[20 + q], 2) * w, 8)
         child[pl.ds(p, w)] -= part
 
 
-def child_product(at, acc, top, low, far, base):
+def child_product(at, acc, top, low, tiles, base):
     return pl.pallas_call(
         child_kernel,
         out_shape=jax.ShapeDtypeStruct(base.shape, F32),
-        in_specs=[SMEM, VMEM, ANY, ANY, VMEM, VMEM],
-        out_specs=VMEM,
-        scratch_shapes=[pltpu.VMEM((4,) + top.shape[1:], F32), pltpu.SemaphoreType.DMA((2,))],
+        in_specs=[SMEM, VMEM, ANY, ANY, ANY, VMEM],
+        out_specs=VMEM,
+        scratch_shapes=far_scratch(top, tiles),
         compiler_params=params(24),
         cost_estimate=cost(acc.shape[1], 4 * top.shape[2], acc.shape[2], 24 * acc.shape[1] * acc.shape[2]),
         name="child",
-    )(at, acc, top, low, far, base)
-
-
-def cross_kernel(at, *refs):
-    groups, (top, low), tiles, (sigma,), (s_buf, u_buf, s_sem, u_sem) = (
-        refs[:3], refs[3:5], refs[5:13], refs[13:14], refs[14:]
-    )
-    pieces = [g.at[i] for g in groups for i in range(4)] + [g.at[i] for g in (top, low) for i in range(2)]
-    copies = [pltpu.make_async_copy(pieces[i], s_buf.at[at[8 + i]], s_sem.at[i]) for i in range(16)]
-    copies += [pltpu.make_async_copy(tiles[i], u_buf.at[:, at[i]], u_sem.at[i]) for i in range(8)]
+    )(at, acc, top, low, tiles, base)
+
+
+def cross_kernel(at, s, *refs):
+    tiles, (sigma, u_buf, u_sem) = refs[:8], refs[8:]
+    copies = [pltpu.make_async_copy(tiles[i], u_buf.at[:, at[i]], u_sem.at[i]) for i in range(8)]
     for copy in copies:
         copy.start()
     sigma[...] = jnp.zeros_like(sigma)
     for copy in copies:
         copy.wait()
-    m, w = sigma.shape
+    w = sigma.shape[1]
 
     def body(k, carry):
-        lhs = s_buf[:, :, pl.ds(pl.multiple_of(k * 768, 128), 768)].reshape(m, 768)
+        lhs = s[:, pl.ds(pl.multiple_of(k * 768, 128), 768)]
         rhs = u_buf[pl.ds(3 * k, 3)].reshape(768, w)
         sigma[...] -= dot3(lhs, rhs)
         return carry
@@ -224,24 +224,19 @@
     lax.fori_loop(0, 4, body, 0)
 
 
-def cross_product(at, near, far, tiles):
-    q, width = near[0].shape[1:]
+def cross_product(at, s, tiles):
+    m, width = s.shape
     sub, w = tiles[0].shape[1:]
     return pl.pallas_call(
         cross_kernel,
-        out_shape=jax.ShapeDtypeStruct((16 * q, w), F32),
-        in_specs=[SMEM] + [ANY] * 13,
-        out_specs=VMEM,
-        scratch_shapes=[
-            pltpu.VMEM((16, q, width), F32),
-            pltpu.VMEM((NANC, 8, sub, w), F32),
-            pltpu.SemaphoreType.DMA((16,)),
-            pltpu.SemaphoreType.DMA((8,)),
-        ],
+        out_shape=jax.ShapeDtypeStruct((m, w), F32),
+        in_specs=[SMEM, VMEM] + [ANY] * 8,
+        out_specs=VMEM,
+        scratch_shapes=[pltpu.VMEM((NANC, 8, sub, w), F32), pltpu.SemaphoreType.DMA((8,))],
         compiler_params=params(40),
-        cost_estimate=cost(16 * q, width, w, 4 * width * (16 * q + w)),
+        cost_estimate=cost(m, width, w, 4 * width * (m + w)),
         name="cross",
-    )(at, *near, *far, *tiles)
+    )(at, s, *tiles)
 
 
 def spread(x):
@@ -310,24 +305,24 @@
     at = places()
 
     f = pick_rows(ancestors, spread(factor_cross))
-    inverse_tiles = [t.reshape(2, w, w) for t in gather_rows(factor_inverse)]
+    inverse = lax.all_gather(after(factor_inverse, f), ROW, axis=0, tiled=True).reshape(16, w, w)
     f_near, f_far = gather_cols(f, 0)
 
     s = pick_rows(ancestors, spread(after(sigma_top, f)))
-    s_cols = lax.all_to_all(after(s, f_near[0]).reshape(16, -1, w), COL, 0, 0, tiled=True)
-    s_near, s_far = gather_cols(after(pick_cols(ancestors, s_cols), f_near[1], f_near[2]), 1, (f_far, (), ()))
-
-    acc, b_far = near_product(at, f_near, inverse_tiles, 1)
-    u, ut = update_product(at, acc, *f_far, b_far)
+    s = lax.all_to_all(after(s, f_near[0]).reshape(16, -1, w), COL, 0, 0, tiled=True)
+    s_all = lax.all_gather(pick_cols(ancestors, s), COL, axis=0, tiled=True)
+
+    acc = near_product(at, f_near, inverse, 1)
+    u, ut = update_product(at, acc, *f_far, inverse)
 
     moved = lax.ppermute(ut, ALL, [(16 * r + c, 16 * (c // 2) + 2 * r + c % 2) for r in range(8) for c in range(16)])
     u_near, u_far = gather_cols(moved, 0)
     u_tiles = gather_rows(u.reshape(NANC, sub, w))
 
-    sigma = cross_product(at, s_near, s_far, u_tiles)
-    sigma_tiles = [t[None] for t in gather_rows(sigma)]
-    acc, b_far = near_product(at, u_near, sigma_tiles, 2)
-    sigma_child = child_product(at, acc, *u_far, b_far, block_inverse)
+    sigma = cross_product(at, after(s_all, u_near[0]), u_tiles)
+    sigma_all = lax.all_gather(sigma, ROW, axis=0, tiled=True).reshape(8, w, w)
+    acc = near_product(at, u_near, sigma_all, 2)
+    sigma_child = child_product(at, acc, *u_far, sigma_all, block_inverse)
 
     full = place_rows(ancestors, sigma.reshape(NANC, sub, w))
     back = lax.all_to_all(full.reshape(8, 3, sub, w), ROW, 0, 0, tiled=True)

time: 298 us -> 284 us (0.953)
  blocking collectives: 22.4 us -> 94.8 us
  starting transfers between devices: 98.8 us -> 39.2 us
  waiting for transfers between devices: 108 us -> 72.2 us
  between operations: 1.24 us -> 14.1 us
  Pallas kernels: 47 us -> 43 us
    all_to_all x0 -> x1, blocking collectives: none -> 38 us  [per_device(): back = lax.all_to_all(full.reshape(8, 3, sub, w), ROW, 0, 0, tiled=True)]
    all_to_all x1 -> x2, blocking collectives: 22.4 us -> 56.8 us  [spread(): lax.all_to_all(x.reshape(3, 8, sub, w), ROW, 1, 0, tiled=True)]
    ppermute x9 -> x3, waiting for transfers between devices: 29.6 us -> 8.4 us  [step(): lax.ppermute(x, ROW, [(2 * i + c, 2 * ((i + 1 - 2 * c) % 4) + c) for i in...]
    ppermute x12 -> x4, starting transfers between devices: 21.9 us -> 1.02 us  [swap(): return lax.ppermute(x, 'core', [(0, 1), (1, 0)])]
    all_to_all x2 -> x0, starting transfers between devices: 16.4 us -> none  [the longest x1 10.9 us: per_device(): back = lax.all_to_all(full.reshape(8, 3, sub, w), ROW, 0, 0, tiled=True)]
    ppermute x9 -> x3, starting transfers between devices: 17.2 us -> 2.03 us  [step(): lax.ppermute(x, ROW, [(2 * i + c, 2 * ((i + 1 - 2 * c) % 4) + c) for i in...]
    ppermute x24 -> x16, waiting for transfers between devices: 48 us -> 36.4 us  [hop(): return lax.ppermute(x, ('core',) + COL, pairs)]
    unnamed x8 -> x24, local copies, waits for them, and re-layouts: 0.02 us -> 9.43 us
  transfers between devices with their start and end apart: 49 -> 28, of which waited for: 16 -> 13; matrix products, arithmetic and copies ran while one was open for 6% -> 3% of each run, Pallas kernels for 14% -> 10%
where the time goes in v5:
time: 284 us; the launch traced here: 283 us
  blocking collectives  94.8 us (33%)
  waiting for transfers between devices  72.2 us (25%)
  Pallas kernels  43 us (15%)
  starting transfers between devices  39.2 us (14%)
  local copies, waits for them, and re-layouts  19.2 us (7%)
  between operations  14.1 us (5%)
    all_to_all x2, blocking collectives, spread(): lax.all_to_all(x.reshape(3, 8, sub, w), ROW, 1, 0, tiled=True)  56.8 us
    all_to_all x1, blocking collectives, per_device(): back = lax.all_to_all(full.reshape(8, 3, sub, w), ROW, 0, 0, tiled=True)  38 us
    ppermute x16, waiting for transfers between devices, hop(): return lax.ppermute(x, ('core',) + COL, pairs)  36.4 us
    ppermute x16, starting transfers between devices, hop(): return lax.ppermute(x, ('core',) + COL, pairs)  24.8 us
    pallas_call x2, Pallas kernels, near_product(): pl.pallas_call(functools.partial(near_kernel, 16 // many), out_shape=jax....  20.8 us
    ppermute x1, waiting for transfers between devices, per_device(): lax.ppermute(ut, ALL, [(16 * r + c, 16 * (c // 2) + 2 * r + c % 2) for r...  14.6 us
    all_to_all x1, waiting for transfers between devices, per_device(): lax.all_to_all(after(s, f_near[0]).reshape(16, -1, w), COL, 0, 0, tiled=T...  10.6 us
    unnamed x24, local copies, waits for them, and re-layouts  9.43 us
  transfers between devices with their start and end apart: 28, of which 13 were waited for; matrix products, arithmetic and copies ran while one was open for 3% of the time, Pallas kernels for 10%

profile of v5, /device:TPU:1, one launch (start us, length us, event | category | flops | bytes accessed | tf_op | source)
XLA Modules:
  0.0 283.0 jit_solution(12492046301106203385)
XLA Ops:
  7.2 0.0 all-gather.6.cloned.1.call-start
  7.2 1.4 copy.7
  8.6 22.4 %all_to_all.40 = f32[3,8,32,384]{3,2,0,1:T(8,128)S(1)} all-to-all(f32[3,8,32,384]{3,2,0,1:T(8,128)S(1)} %copy.7), channel_id=1, replica_groups=mesh['y'=4,'core'=2,'z'=4,'x'=4] {'y','core'}, dimensions={1} | all-to-all | bytes 2359296 | tf_op jit(solution)/shard_map/all_to_all | solution.py:245
  31.0 0.6 pick_rows.2
  31.6 1.7 collective-permute-start
  33.3 2.2 collective-permute-start.1
  35.5 7.5 %collective-permute-done = f32[384,384]{1,0:T(8,128)S(1)} collective-permute-done((f32[384,384]{1,0:T(8,128)S(1)}, f32[384,384]{1,0:T(8,128)S(1)}, u32[]{:S(2)}, u32[]{:S(2)}) %collective-permute-start) | collective-permute-done | bytes 589856 | tf_op jit(solution)/shard_map/ppermute | solution.py:56
  43.0 0.1 collective-permute-start.2
  43.1 2.7 collective-permute-start.3
  45.9 4.4 %collective-permute-done.2 = f32[192,384]{1,0:T(8,128)S(1)} collective-permute-done((f32[192,384]{1,0:T(8,128)S(1)}, f32[192,384]{1,0:T(8,128)S(1)}, u32[]{:S(2)}, u32[]{:S(2)}) %collective-permute-start.2) | collective-permute-done | bytes 294944 | tf_op jit(solution)/shard_map/ppermute | solution.py:56
  50.3 0.2 pad_maximum_fusion.refs_0_
  50.6 1.0 collective-permute-start.4
  51.6 1.8 collective-permute-start.5
  53.3 0.1 copy.8
  53.4 34.4 %all_to_all.41 = f32[3,8,32,384]{3,2,0,1:T(8,128)S(1)} all-to-all(f32[3,8,32,384]{3,2,0,1:T(8,128)S(1)} %copy.8), channel_id=1, replica_groups=mesh['y'=4,'core'=2,'z'=4,'x'=4] {'y','core'}, dimensions={1} | all-to-all | bytes 2359296 | tf_op jit(solution)/shard_map/all_to_all | solution.py:245
  87.8 1.4 pick_rows.3
  89.2 5.8 %all-to-all-start.2 = ((f32[16,24,384]{2,1,0:T(8,128)}), f32[16,24,384]{2,1,0:T(8,128)S(1)}, u32[]{:S(2)}, u32[]{:S(2)}) async-start(f32[16,24,384]{2,1,0:T(8,128)} %bitcast.38), calls=%async_computation.2 | async-start | bytes 1179648 | tf_op jit(solution)/shard_map/all_to_all | solution.py:312
  95.0 0.0 all-gather.4.cloned.1.call-start
  95.1 0.1 stack.126.at
  95.3 10.6 %all-to-all-done.2.x = f32[16,24,384]{2,1,0:T(8,128)S(1)} async-done(((f32[16,24,384]{2,1,0:T(8,128)}), f32[16,24,384]{2,1,0:T(8,128)S(1)}, u32[]{:S(2)}, u32[]{:S(2)}) %all-to-all-start.2) | async-done | bytes 589856 | tf_op jit(solution)/shard_map/all_to_all | solution.py:312
  105.9 1.4 pick_cols.1
  107.3 0.0 all-gather.8.cloned.1.call-start
  107.3 2.4 slice.34
  109.7 0.4 collective-permute-start.6
  110.0 2.4 slice.35
  112.4 2.3 collective-permute-start.7
  114.7 12.6 %near.2.acc = f32[1,384,384]{2,1,0:T(8,128)S(1)} custom-call(s32[24]{0:T(128)S(1)} %stack.126.at, f32[4,384,384]{2,1,0:T(8,128)S(1)} %pad_maximum_fusion.refs_0_, f32[4,384,384]{2,1,0:T(8,128)} %collective-permute-done.4.refs_1_, f32[4,384,384]{2,1,0:T(8,128)} %collective-permute-done.5.refs_2_, f32[16,384,384]{2,1,0:T(8,128)} %bitcast.56), custom_call_target="tpu_custom_call" | custom-call | flops 81537269760 | bytes 330301440 | tf_op jit(solution)/shard_map/near/pallas_call | solution.py:125
  127.4 3.9 %collective-permute-done.6.top = f32[2,384,384]{2,1,0:T(8,128)} collective-permute-done((f32[2,384,384]{2,1,0:T(8,128)}, f32[2,384,384]{2,1,0:T(8,128)}, u32[]{:S(2)}, u32[]{:S(2)}) %collective-permute-start.6) | collective-permute-done | bytes 1179680 | tf_op jit(solution)/shard_map/ppermute | solution.py:56
  131.3 1.6 collective-permute-done.7.low
  132.9 4.4 %update.1 = (f32[384,384]{1,0:T(8,128)S(1)}, f32[384,384]{1,0:T(8,128)S(1)}) custom-call(s32[24]{0:T(128)S(1)} %stack.126.at, f32[1,384,384]{2,1,0:T(8,128)S(1)} %near.2.acc, f32[2,384,384]{2,1,0:T(8,128)} %collective-permute-done.6.top, f32[2,384,384]{2,1,0:T(8,128)} %collective-permute-done.7.low, f32[16,384,384]{2,1,0:T(8,128)S(1)} %bitcast.59), custom_call_target="tpu_custom_call" | custom-call | flops 1358954496 | bytes 2359296 | tf_op jit(solution)/shard_map/update/pallas_call | solution.py:174
  137.3 0.9 collective-permute-start.13
  138.2 5.5 %collective-permute-start.8 = (f32[384,384]{1,0:T(8,128)S(1)}, f32[384,384]{1,0:T(8,128)S(1)}, u32[]{:S(2)}, u32[]{:S(2)}) collective-permute-start(f32[384,384]{1,0:T(8,128)S(1)} %get-tuple-element.11), channel_id=1, source_target_pairs={{0,0},{1,1},{2,16},{3,17},{4,32},{5,33},{6,48},{7,49},{8,64},{9,65... | collective-permute-start | bytes 1769480 | tf_op jit(solution)/shard_map/ppermute | solution.py:318
  143.7 4.5 %collective-permute-done.13.refs_1_ = f32[12,32,384]{2,1,0:T(8,128)} collective-permute-done((f32[12,32,384]{2,1,0:T(8,128)S(1)}, f32[12,32,384]{2,1,0:T(8,128)}, u32[]{:S(2)}, u32[]{:S(2)}) %collective-permute-start.13) | collective-permute-done | bytes 589856 | tf_op jit(solution)/shard_map/ppermute | solution.py:35
  148.2 1.1 collective-permute-start.14
  149.3 14.6 %collective-permute-done.8 = f32[384,384]{1,0:T(8,128)S(1)} collective-permute-done((f32[384,384]{1,0:T(8,128)S(1)}, f32[384,384]{1,0:T(8,128)S(1)}, u32[]{:S(2)}, u32[]{:S(2)}) %collective-permute-start.8) | collective-permute-done | bytes 589856 | tf_op jit(solution)/shard_map/ppermute | solution.py:318
  163.9 4.9 %collective-permute-start.10 = (f32[384,384]{1,0:T(8,128)S(1)}, f32[384,384]{1,0:T(8,128)S(1)}, u32[]{:S(2)}, u32[]{:S(2)}) collective-permute-start(f32[384,384]{1,0:T(8,128)S(1)} %collective-permute-done.8), channel_id=1, source_target_pairs={{0,3},{1,0},{2,1},{3,2},{4,7},{5,4},{6,5},{7,6},{8,11},{9,8},{10,9... | collective-permute-start | bytes 1769480 | tf_op jit(solution)/shard_map/ppermute | solution.py:56
  168.8 3.9 %collective-permute-done.14.refs_2_ = f32[12,32,384]{2,1,0:T(8,128)} collective-permute-done((f32[12,32,384]{2,1,0:T(8,128)}, f32[12,32,384]{2,1,0:T(8,128)}, u32[]{:S(2)}, u32[]{:S(2)}) %collective-permute-start.14) | collective-permute-done | bytes 589856 | tf_op jit(solution)/shard_map/ppermute | solution.py:35
  172.7 15.2 %collective-permute-done.9 = f32[384,384]{1,0:T(8,128)S(1)} collective-permute-done((f32[384,384]{1,0:T(8,128)S(1)}, f32[384,384]{1,0:T(8,128)S(1)}, u32[]{:S(2)}, u32[]{:S(2)}) %collective-permute-start.9) | collective-permute-done | bytes 589856 | tf_op jit(solution)/shard_map/ppermute | solution.py:56
  187.9 2.0 collective-permute-start.11
  189.9 0.8 collective-permute-start.12
  190.8 0.5 collective-permute-start.17
  191.3 3.5 %collective-permute-done.11 = f32[192,384]{1,0:T(8,128)S(1)} collective-permute-done((f32[192,384]{1,0:T(8,128)S(1)}, f32[192,384]{1,0:T(8,128)S(1)}, u32[]{:S(2)}, u32[]{:S(2)}) %collective-permute-start.11) | collective-permute-done | bytes 294944 | tf_op jit(solution)/shard_map/ppermute | solution.py:56
  194.8 0.5 collective-permute-start.19
  195.3 0.3 collective-permute-done.12
  195.6 0.2 pad_maximum_fusion.1.refs_0_
  195.8 1.3 collective-permute-done.18.refs_6_
  197.1 0.8 collective-permute-done.19.refs_7_
  198.0 2.3 copy-done.7
  200.3 8.1 %cross.1 = f32[384,384]{1,0:T(8,128)} custom-call(s32[24]{0:T(128)S(1)} %stack.126.at, f32[384,3072]{1,0:T(8,128)S(1)} %copy-done.7, f32[12,32,384]{2,1,0:T(8,128)S(1)} %bitcast.70, f32[12,32,384]{2,1,0:T(8,128)} %collective-permute-done.13.refs_1_, f32[12,32,384]{2,1,0:T(8,128)} %collective-permute-done.14.refs_2_, ...), custom_call_target="tpu_custom_call" | custom-call | flops 2717908992 | bytes 9437184 | tf_op jit(solution)/shard_map/cross/pallas_call | solution.py:230
  208.4 1.5 collective-permute-start.20
  209.9 1.4 collective-permute-start.21
  211.3 1.2 place_rows.1
  212.5 38.0 %all_to_all.42 = f32[8,3,32,384]{3,2,1,0:T(8,128)S(1)} all-to-all(f32[8,3,32,384]{3,2,1,0:T(8,128)S(1)} %bitcast.64), channel_id=1, replica_groups=mesh['y'=4,'core'=2,'z'=4,'x'=4] {'y','core'}, dimensions={0} | all-to-all | bytes 2359296 | tf_op jit(solution)/shard_map/all_to_all | solution.py:328
  250.5 1.1 copy.9
  251.6 1.1 slice.38
  252.7 0.6 copy-done.2
  253.4 1.2 slice.39
  254.6 0.7 copy-done.4
  255.3 2.0 collective-permute-start.23
  257.3 2.3 copy-done
  259.7 1.7 copy-done.3
  261.3 1.7 copy-done.5
  263.0 8.2 %near.3.acc = f32[2,384,384]{2,1,0:T(8,128)S(1)} custom-call(s32[24]{0:T(128)S(1)} %stack.126.at, f32[4,384,384]{2,1,0:T(8,128)S(1)} %pad_maximum_fusion.1.refs_0_, f32[4,384,384]{2,1,0:T(8,128)S(1)} %copy-done.3, f32[4,384,384]{2,1,0:T(8,128)S(1)} %copy-done.5, f32[8,384,384]{2,1,0:T(8,128)S(1)} %bitcast.60), custom_call_target="tpu_custom_call" | custom-call | flops 81537269760 | bytes 235929600 | tf_op jit(solution)/shard_map/near/pallas_call | solution.py:125
  271.2 5.2 %child.1 = f32[768,384]{1,0:T(8,128)} custom-call(s32[24]{0:T(128)S(1)} %stack.126.at, f32[2,384,384]{2,1,0:T(8,128)S(1)} %near.3.acc, f32[2,384,384]{2,1,0:T(8,128)S(1)} %collective-permute-done.22.top, f32[2,384,384]{2,1,0:T(8,128)} %collective-permute-done.23.low, f32[8,384,384]{2,1,0:T(8,128)S(1)} %bitcast.61, f32[768,384]{1,0:T(8,128)S(1)} %copy-done.1), custom_call_target="tpu_custom_call" | custom-call | flops 1358954496 | bytes 3538944 | tf_op jit(solution)/shard_map/child/pallas_call | solution.py:196
  (48 shorter events, 0.3 us)
Async XLA Ops:
  7.2 107.6 %all-gather.6.cloned.1.call-start = ((), (), s32[]{:S(2)}) async-start(), calls=%async_computation.5 | async-start | bytes 10616832 | tf_op jit(solution)/shard_map/all_gather | solution.py:308
  7.2 23.8 %copy-start.6 = (s32[12]{0:T(128)S(1)}, s32[12]{0:T(128)}, u32[]{:S(2)}) copy-start(s32[12]{0:T(128)} %anc.7) | copy-start | bytes 148
  31.6 11.4 %collective-permute-start = (f32[384,384]{1,0:T(8,128)S(1)}, f32[384,384]{1,0:T(8,128)S(1)}, u32[]{:S(2)}, u32[]{:S(2)}) collective-permute-start(f32[384,384]{1,0:T(8,128)S(1)} %bitcast.65), channel_id=1, source_target_pairs={{0,1},{1,2},{2,3},{3,0},{4,5},{5,6},{6,7},{7,4},{8,9},{9,10},{10,1... | collective-permute-start | bytes 1769480 | tf_op jit(solution)/shard_map/ppermute | solution.py:56
  33.3 9.8 %collective-permute-start.1 = (f32[384,384]{1,0:T(8,128)S(1)}, f32[384,384]{1,0:T(8,128)S(1)}, u32[]{:S(2)}, u32[]{:S(2)}) collective-permute-start(f32[384,384]{1,0:T(8,128)S(1)} %bitcast.66), channel_id=1, source_target_pairs={{0,3},{1,0},{2,1},{3,2},{4,7},{5,4},{6,5},{7,6},{8,11},{9,8},{10,9... | collective-permute-start | bytes 1769480 | tf_op jit(solution)/shard_map/ppermute | solution.py:56
  43.0 7.3 %collective-permute-start.2 = (f32[192,384]{1,0:T(8,128)S(1)}, f32[192,384]{1,0:T(8,128)S(1)}, u32[]{:S(2)}, u32[]{:S(2)}) collective-permute-start(f32[192,384]{1,0:T(8,128)S(1)} %slice.32), channel_id=1, source_target_pairs={{0,1},{1,2},{2,3},{3,0},{4,5},{5,6},{6,7},{7,4},{8,9},{9,10},{10,1... | collective-permute-start | bytes 884744 | tf_op jit(solution)/shard_map/ppermute | solution.py:56
  43.1 7.1 %collective-permute-start.3 = (f32[192,384]{1,0:T(8,128)S(1)}, f32[192,384]{1,0:T(8,128)S(1)}, u32[]{:S(2)}, u32[]{:S(2)}) collective-permute-start(f32[192,384]{1,0:T(8,128)S(1)} %slice.33), channel_id=1, source_target_pairs={{0,3},{1,0},{2,1},{3,2},{4,7},{5,4},{6,5},{7,6},{8,11},{9,8},{10,9... | collective-permute-start | bytes 884744 | tf_op jit(solution)/shard_map/ppermute | solution.py:56
  50.3 3.0 %copy-start.8 = (f32[768,384]{1,0:T(8,128)S(1)}, f32[768,384]{1,0:T(8,128)}, u32[]{:S(2)}) copy-start(f32[768,384]{1,0:T(8,128)} %param.5) | copy-start | bytes 3538948
  50.6 56.7 %collective-permute-start.4 = (f32[4,384,384]{2,1,0:T(8,128)S(1)}, f32[4,384,384]{2,1,0:T(8,128)}, u32[]{:S(2)}, u32[]{:S(2)}) collective-permute-start(f32[4,384,384]{2,1,0:T(8,128)S(1)} %pad_maximum_fusion.refs_0_), channel_id=1, source_target_pairs={{0,4},{1,5},{2,6},{3,7},{4,8},{5,9},{6,10},{7,11},{8,12},{9,13},{1... | collective-permute-start | bytes 7077896 | tf_op jit(solution)/shard_map/ppermute | solution.py:56
  51.6 58.5 %collective-permute-start.5 = (f32[4,384,384]{2,1,0:T(8,128)S(1)}, f32[4,384,384]{2,1,0:T(8,128)}, u32[]{:S(2)}, u32[]{:S(2)}) collective-permute-start(f32[4,384,384]{2,1,0:T(8,128)S(1)} %pad_maximum_fusion.refs_0_), channel_id=1, source_target_pairs={{0,12},{1,13},{2,14},{3,15},{4,0},{5,1},{6,2},{7,3},{8,4},{9,5},{1... | collective-permute-start | bytes 7077896 | tf_op jit(solution)/shard_map/ppermute | solution.py:56
  89.2 16.7 %all-to-all-start.2 = ((f32[16,24,384]{2,1,0:T(8,128)}), f32[16,24,384]{2,1,0:T(8,128)S(1)}, u32[]{:S(2)}, u32[]{:S(2)}) async-start(f32[16,24,384]{2,1,0:T(8,128)} %bitcast.38), calls=%async_computation.2 | async-start | bytes 1179648 | tf_op jit(solution)/shard_map/all_to_all | solution.py:312
  95.0 100.8 %all-gather.4.cloned.1.call-start = ((), (), s32[]{:S(2)}) async-start(), calls=%async_computation.4 | async-start | bytes 5013504 | tf_op jit(solution)/shard_map/all_gather | solution.py:313
  107.3 150.1 %all-gather.8.cloned.1.call-start = ((), (), s32[]{:S(2)}) async-start(), calls=%async_computation.6 | async-start | bytes 5308416 | tf_op jit(solution)/shard_map/all_gather | solution.py:323
  109.7 21.6 %collective-permute-start.6 = (f32[2,384,384]{2,1,0:T(8,128)}, f32[2,384,384]{2,1,0:T(8,128)}, u32[]{:S(2)}, u32[]{:S(2)}) collective-permute-start(f32[2,384,384]{2,1,0:T(8,128)} %slice.34), channel_id=1, source_target_pairs={{0,4},{1,5},{2,6},{3,7},{4,8},{5,9},{6,10},{7,11},{8,12},{9,13},{1... | collective-permute-start | bytes 3538952 | tf_op jit(solution)/shard_map/ppermute | solution.py:56
  112.4 20.5 %collective-permute-start.7 = (f32[2,384,384]{2,1,0:T(8,128)}, f32[2,384,384]{2,1,0:T(8,128)}, u32[]{:S(2)}, u32[]{:S(2)}) collective-permute-start(f32[2,384,384]{2,1,0:T(8,128)} %slice.35), channel_id=1, source_target_pairs={{0,12},{1,13},{2,14},{3,15},{4,0},{5,1},{6,2},{7,3},{8,4},{9,5},{1... | collective-permute-start | bytes 3538952 | tf_op jit(solution)/shard_map/ppermute | solution.py:56
  114.7 18.2 %slice-start = ((s8[9437184]{0:T(1024)(128)(4,1)}), s8[4194304]{0:T(1024)(128)(4,1)S(1)}, s32[]{:S(2)}) async-start(s8[9437184]{0:T(1024)(128)(4,1)} %bitcast.57), calls=%async_computation.7 | async-start | bytes 8388608
  114.7 18.2 %slice-start.1 = ((s8[9437184]{0:T(1024)(128)(4,1)}), s8[4194304]{0:T(1024)(128)(4,1)S(1)}, s32[]{:S(2)}) async-start(s8[9437184]{0:T(1024)(128)(4,1)} %bitcast.57), calls=%async_computation.8 | async-start | bytes 8388608
  114.7 18.2 %slice-start.2 = ((s8[9437184]{0:T(1024)(128)(4,1)}), s8[1048576]{0:T(1024)(128)(4,1)S(1)}, s32[]{:S(2)}) async-start(s8[9437184]{0:T(1024)(128)(4,1)} %bitcast.57), calls=%async_computation.9 | async-start | bytes 2097152
  137.3 10.9 %collective-permute-start.13 = (f32[12,32,384]{2,1,0:T(8,128)S(1)}, f32[12,32,384]{2,1,0:T(8,128)}, u32[]{:S(2)}, u32[]{:S(2)}) collective-permute-start(f32[12,32,384]{2,1,0:T(8,128)S(1)} %bitcast.68), channel_id=1, source_target_pairs={{0,32},{16,112},{32,64},{48,16},{64,96},{80,48},{96,0},{112,80},{1... | collective-permute-start | bytes 1769480 | tf_op jit(solution)/shard_map/ppermute | solution.py:35
  138.2 25.7 %collective-permute-start.8 = (f32[384,384]{1,0:T(8,128)S(1)}, f32[384,384]{1,0:T(8,128)S(1)}, u32[]{:S(2)}, u32[]{:S(2)}) collective-permute-start(f32[384,384]{1,0:T(8,128)S(1)} %get-tuple-element.11), channel_id=1, source_target_pairs={{0,0},{1,1},{2,16},{3,17},{4,32},{5,33},{6,48},{7,49},{8,64},{9,65... | collective-permute-start | bytes 1769480 | tf_op jit(solution)/shard_map/ppermute | solution.py:318
  148.2 24.5 %collective-permute-start.14 = (f32[12,32,384]{2,1,0:T(8,128)}, f32[12,32,384]{2,1,0:T(8,128)}, u32[]{:S(2)}, u32[]{:S(2)}) collective-permute-start(f32[12,32,384]{2,1,0:T(8,128)} %collective-permute-done.13.refs_1_), channel_id=1, source_target_pairs={{0,32},{16,112},{32,64},{48,16},{64,96},{80,48},{96,0},{112,80},{1... | collective-permute-start | bytes 1769480 | tf_op jit(solution)/shard_map/ppermute | solution.py:35
  163.9 24.0 %collective-permute-start.9 = (f32[384,384]{1,0:T(8,128)S(1)}, f32[384,384]{1,0:T(8,128)S(1)}, u32[]{:S(2)}, u32[]{:S(2)}) collective-permute-start(f32[384,384]{1,0:T(8,128)S(1)} %collective-permute-done.8), channel_id=1, source_target_pairs={{0,1},{1,2},{2,3},{3,0},{4,5},{5,6},{6,7},{7,4},{8,9},{9,10},{10,1... | collective-permute-start | bytes 1769480 | tf_op jit(solution)/shard_map/ppermute | solution.py:56
  163.9 26.0 %collective-permute-start.10 = (f32[384,384]{1,0:T(8,128)S(1)}, f32[384,384]{1,0:T(8,128)S(1)}, u32[]{:S(2)}, u32[]{:S(2)}) collective-permute-start(f32[384,384]{1,0:T(8,128)S(1)} %collective-permute-done.8), channel_id=1, source_target_pairs={{0,3},{1,0},{2,1},{3,2},{4,7},{5,4},{6,5},{7,6},{8,11},{9,8},{10,9... | collective-permute-start | bytes 1769480 | tf_op jit(solution)/shard_map/ppermute | solution.py:56
  172.7 22.1 %collective-permute-start.15 = (f32[12,32,384]{2,1,0:T(8,128)}, f32[12,32,384]{2,1,0:T(8,128)}, u32[]{:S(2)}, u32[]{:S(2)}) collective-permute-start(f32[12,32,384]{2,1,0:T(8,128)} %collective-permute-done.14.refs_2_), channel_id=1, source_target_pairs={{0,32},{16,112},{32,64},{48,16},{64,96},{80,48},{96,0},{112,80},{1... | collective-permute-start | bytes 1769480 | tf_op jit(solution)/shard_map/ppermute | solution.py:35
  187.9 6.9 %collective-permute-start.11 = (f32[192,384]{1,0:T(8,128)S(1)}, f32[192,384]{1,0:T(8,128)S(1)}, u32[]{:S(2)}, u32[]{:S(2)}) collective-permute-start(f32[192,384]{1,0:T(8,128)S(1)} %slice.36), channel_id=1, source_target_pairs={{0,1},{1,2},{2,3},{3,0},{4,5},{5,6},{6,7},{7,4},{8,9},{9,10},{10,1... | collective-permute-start | bytes 884744 | tf_op jit(solution)/shard_map/ppermute | solution.py:56
  189.9 5.6 %collective-permute-start.12 = (f32[192,384]{1,0:T(8,128)S(1)}, f32[192,384]{1,0:T(8,128)S(1)}, u32[]{:S(2)}, u32[]{:S(2)}) collective-permute-start(f32[192,384]{1,0:T(8,128)S(1)} %slice.37), channel_id=1, source_target_pairs={{0,3},{1,0},{2,1},{3,2},{4,7},{5,4},{6,5},{7,6},{8,11},{9,8},{10,9... | collective-permute-start | bytes 884744 | tf_op jit(solution)/shard_map/ppermute | solution.py:56
  190.8 5.0 %collective-permute-start.16 = (f32[12,32,384]{2,1,0:T(8,128)S(1)}, f32[12,32,384]{2,1,0:T(8,128)}, u32[]{:S(2)}, u32[]{:S(2)}) collective-permute-start(f32[12,32,384]{2,1,0:T(8,128)S(1)} %bitcast.69), channel_id=1, source_target_pairs={{0,16},{16,0},{1,17},{17,1},{2,18},{18,2},{3,19},{19,3},{4,20},{20... | collective-permute-start | bytes 1769480 | tf_op jit(solution)/shard_map/ppermute | solution.py:39
  190.8 5.0 %collective-permute-start.17 = (f32[12,32,384]{2,1,0:T(8,128)}, f32[12,32,384]{2,1,0:T(8,128)}, u32[]{:S(2)}, u32[]{:S(2)}) collective-permute-start(f32[12,32,384]{2,1,0:T(8,128)} %collective-permute-done.13.refs_1_), channel_id=1, source_target_pairs={{0,16},{16,0},{1,17},{17,1},{2,18},{18,2},{3,19},{19,3},{4,20},{20... | collective-permute-start | bytes 1769480 | tf_op jit(solution)/shard_map/ppermute | solution.py:39
  194.8 2.3 collective-permute-start.18
  194.8 3.2 %collective-permute-start.19 = (f32[12,32,384]{2,1,0:T(8,128)}, f32[12,32,384]{2,1,0:T(8,128)}, u32[]{:S(2)}, u32[]{:S(2)}) collective-permute-start(f32[12,32,384]{2,1,0:T(8,128)} %collective-permute-done.15.refs_3_), channel_id=1, source_target_pairs={{0,16},{16,0},{1,17},{17,1},{2,18},{18,2},{3,19},{19,3},{4,20},{20... | collective-permute-start | bytes 1769480 | tf_op jit(solution)/shard_map/ppermute | solution.py:39
  198.0 2.3 copy-start.7
  208.4 43.2 %collective-permute-start.20 = (f32[4,384,384]{2,1,0:T(8,128)S(1)}, f32[4,384,384]{2,1,0:T(8,128)S(1)}, u32[]{:S(2)}, u32[]{:S(2)}) collective-permute-start(f32[4,384,384]{2,1,0:T(8,128)S(1)} %pad_maximum_fusion.1.refs_0_), channel_id=1, source_target_pairs={{0,4},{1,5},{2,6},{3,7},{4,8},{5,9},{6,10},{7,11},{8,12},{9,13},{1... | collective-permute-start | bytes 7077896 | tf_op jit(solution)/shard_map/ppermute | solution.py:56
  209.9 42.8 %collective-permute-start.21 = (f32[4,384,384]{2,1,0:T(8,128)S(1)}, f32[4,384,384]{2,1,0:T(8,128)S(1)}, u32[]{:S(2)}, u32[]{:S(2)}) collective-permute-start(f32[4,384,384]{2,1,0:T(8,128)S(1)} %pad_maximum_fusion.1.refs_0_), channel_id=1, source_target_pairs={{0,12},{1,13},{2,14},{3,15},{4,0},{5,1},{6,2},{7,3},{8,4},{9,5},{1... | collective-permute-start | bytes 7077896 | tf_op jit(solution)/shard_map/ppermute | solution.py:56
  251.6 1.8 copy-start.2
  252.7 18.4 %collective-permute-start.22 = (f32[2,384,384]{2,1,0:T(8,128)}, f32[2,384,384]{2,1,0:T(8,128)S(1)}, u32[]{:S(2)}, u32[]{:S(2)}) collective-permute-start(f32[2,384,384]{2,1,0:T(8,128)} %slice.38), channel_id=1, source_target_pairs={{0,4},{1,5},{2,6},{3,7},{4,8},{5,9},{6,10},{7,11},{8,12},{9,13},{1... | collective-permute-start | bytes 3538952 | tf_op jit(solution)/shard_map/ppermute | solution.py:56
  253.4 1.9 copy-start.4
  255.3 15.9 %collective-permute-start.23 = (f32[2,384,384]{2,1,0:T(8,128)}, f32[2,384,384]{2,1,0:T(8,128)}, u32[]{:S(2)}, u32[]{:S(2)}) collective-permute-start(f32[2,384,384]{2,1,0:T(8,128)} %slice.39), channel_id=1, source_target_pairs={{0,12},{1,13},{2,14},{3,15},{4,0},{5,1},{6,2},{7,3},{8,4},{9,5},{1... | collective-permute-start | bytes 3538952 | tf_op jit(solution)/shard_map/ppermute | solution.py:56
  257.3 2.3 copy-start
  259.7 1.7 copy-start.3
  261.3 1.7 copy-start.5
  263.0 8.2 %copy-start.1 = (f32[768,384]{1,0:T(8,128)S(1)}, f32[768,384]{1,0:T(8,128)}, u32[]{:S(2)}) copy-start(f32[768,384]{1,0:T(8,128)} %base.1) | copy-start | bytes 3538948
Sparse Core Ops, SparseCore 0:
  31.7 67.7 all-gather.5
  107.4 79.0 all-gather.3
  208.5 48.0 all-gather.7

commit v6 on v5

--- a/solution.py
+++ b/solution.py
@@ -10,6 +10,7 @@
 
 NB = 24
 NANC = 12
+W1, W2 = 12, 12
 ROW = ("y", "core")
 COL = ("z", "x")
 ALL = ("y", "core", "z", "x")
@@ -88,38 +89,41 @@
     return mul(a_hi, b_hi) + (mul(a_hi, b_lo) + mul(a_lo, b_hi))
 
 
-def pair_dot(at, tile, a_buf, slot, b_buf, per):
-    def one(k):
-        return a_buf[slot + k], b_buf[lax.div(at[tile + k], per)]
-
-    def body(q):
-        (a0, b0), (a1, b1) = one(q), one(3 - q)
-        return dot3(jnp.concatenate([a0, a1], axis=1), jnp.concatenate([b0, b1], axis=0))
-
-    return body
-
-
 def near_kernel(per, at, *refs):
     groups, tiles, acc, (a_buf, b_buf, a_sem, b_sem) = refs[:3], refs[3], refs[4], refs[5:]
     outs = acc.shape[0]
-    copies = [pltpu.make_async_copy(tiles, b_buf, b_sem)]
-    copies += [pltpu.make_async_copy(groups[i], a_buf.at[pl.ds(4 * i, 4)], a_sem.at[i]) for i in range(3)]
-    for copy in copies:
-        copy.start()
+
+    def group_copy(g, source):
+        return pltpu.make_async_copy(source, a_buf.at[pl.ds(4 * g, 4)], a_sem.at[g])
+
+    def tile_copy(k):
+        return pltpu.make_async_copy(tiles.at[lax.div(at[8 + k], per)], b_buf.at[k], b_sem.at[k])
+
+    for g in range(3):
+        group_copy(g, groups[g]).start()
+        for k in (0, 3, 1, 2):
+            tile_copy(4 * g + k).start()
     acc[...] = jnp.zeros_like(acc)
-    for copy in copies:
-        copy.wait()
 
     def body(i, carry):
         g, q = lax.div(i, 2), lax.rem(i, 2)
-        p = lax.rem(at[8 + 4 * g + q], outs)
-        acc[p] += pair_dot(at, 8 + 4 * g, a_buf, 4 * g, b_buf, per)(q)
+
+        @pl.when(q == 0)
+        def _():
+            group_copy(g, groups[0]).wait()
+
+        k0, k1 = 4 * g + q, 4 * g + 3 - q
+        tile_copy(k0).wait()
+        tile_copy(k1).wait()
+        acc[lax.rem(at[8 + k0], outs)] += dot3(
+            jnp.concatenate([a_buf[k0], a_buf[k1]], axis=1), jnp.concatenate([b_buf[k0], b_buf[k1]], axis=0)
+        )
         return carry
 
     lax.fori_loop(0, 6, body, 0)
 
 
-def near_product(at, groups, tiles, outs):
+def near_product(at, groups, tiles, outs, weight):
     m, w = groups[0].shape[1:]
     many, _, n = tiles.shape
     return pl.pallas_call(
@@ -129,12 +133,12 @@
         out_specs=VMEM,
         scratch_shapes=[
             pltpu.VMEM((12, m, w), F32),
-            pltpu.VMEM(tiles.shape, F32),
+            pltpu.VMEM((12,) + tiles.shape[1:], F32),
             pltpu.SemaphoreType.DMA((3,)),
-            pltpu.SemaphoreType.DMA,
+            pltpu.SemaphoreType.DMA((12,)),
         ],
         compiler_params=params(40),
-        cost_estimate=cost(20 * m, 12 * w, n, 20 * 4 * w * (12 * m + many * n)),
+        cost_estimate=cost(weight * m, 12 * w, n, weight * 4 * w * (12 * m + many * n)),
         name="near",
     )(at, *groups, tiles)
 
@@ -281,22 +285,30 @@
     )(ancestors, x)
 
 
-def place_kernel(anc, x, out):
+def place_kernel(anc, first, x, out, sem):
     out[...] = jnp.zeros_like(out)
-    for i in range(NANC):
-        out[anc[i]] = x[i]
-
-
-def place_rows(ancestors, x):
-    sub, w = x.shape[1:]
+    for b in range(out.shape[0]):
+        for i in range(NANC):
+
+            @pl.when(anc[i] == first[0] + b)
+            def _():
+                copy = pltpu.make_async_copy(x.at[:, i], out.at[b], sem)
+                copy.start()
+                copy.wait()
+
+
+def place_rows(ancestors, x, h):
+    _, _, sub, w = x.shape
+    first = (3 * lax.axis_index(ROW)).astype(jnp.int32).reshape(1)
     return pl.pallas_call(
         place_kernel,
-        out_shape=jax.ShapeDtypeStruct((NB, sub, w), F32),
-        in_specs=[SMEM, VMEM],
-        out_specs=VMEM,
+        out_shape=jax.ShapeDtypeStruct((3, 8, sub, w), F32),
+        in_specs=[SMEM, SMEM, ANY],
+        out_specs=VMEM,
+        scratch_shapes=[pltpu.SemaphoreType.DMA],
         compiler_params=params(8),
         name="place_rows",
-    )(ancestors, x)
+    )(ancestors, first, x).reshape(h, w)
 
 
 def per_device(sigma_top, factor_cross, factor_inverse, block_inverse, ancestors):
@@ -312,7 +324,7 @@
     s = lax.all_to_all(after(s, f_near[0]).reshape(16, -1, w), COL, 0, 0, tiled=True)
     s_all = lax.all_gather(pick_cols(ancestors, s), COL, axis=0, tiled=True)
 
-    acc = near_product(at, f_near, inverse, 1)
+    acc = near_product(at, f_near, inverse, 1, W1)
     u, ut = update_product(at, acc, *f_far, inverse)
 
     moved = lax.ppermute(ut, ALL, [(16 * r + c, 16 * (c // 2) + 2 * r + c % 2) for r in range(8) for c in range(16)])
@@ -321,12 +333,10 @@
 
     sigma = cross_product(at, after(s_all, u_near[0]), u_tiles)
     sigma_all = lax.all_gather(sigma, ROW, axis=0, tiled=True).reshape(8, w, w)
-    acc = near_product(at, u_near, sigma_all, 2)
+    acc = near_product(at, u_near, sigma_all, 2, W2)
     sigma_child = child_product(at, acc, *u_far, sigma_all, block_inverse)
 
-    full = place_rows(ancestors, sigma.reshape(NANC, sub, w))
-    back = lax.all_to_all(full.reshape(8, 3, sub, w), ROW, 0, 0, tiled=True)
-    sigma_cross = back.reshape(8, 3, sub, w).transpose(1, 0, 2, 3).reshape(h, w)
+    sigma_cross = place_rows(ancestors, sigma_all.reshape(8, NANC, sub, w), h)
     return (sigma_cross, sigma_child)
 
 

time: 284 us -> 268 us (0.944); the launches traced: 283 us -> 262 us
  blocking collectives: 94.8 us -> 46.3 us
  starting transfers between devices: 39.2 us -> 58 us
  waiting for transfers between devices: 72.2 us -> 84.4 us
    all_to_all x2 -> x1, blocking collectives: 56.8 us -> 22.5 us  [spread(): lax.all_to_all(x.reshape(3, 8, sub, w), ROW, 1, 0, tiled=True)]
    ppermute x4, starting transfers between devices: 1.02 us -> 23.5 us  [swap(): return lax.ppermute(x, 'core', [(0, 1), (1, 0)])]
    ppermute x3, waiting for transfers between devices: 8.4 us -> 24.9 us  [step(): lax.ppermute(x, ROW, [(2 * i + c, 2 * ((i + 1 - 2 * c) % 4) + c) for i in...]
    ppermute x1, waiting for transfers between devices: 14.6 us -> 0.01 us  [per_device(): lax.ppermute(ut, ALL, [(16 * r + c, 16 * (c // 2) + 2 * r + c % 2) for r...]
    all_to_all x1, blocking collectives: 38 us -> 23.8 us  [per_device(): lax.all_to_all(after(s, f_near[0]).reshape(16, -1, w), COL, 0, 0, tiled=T...]
    ppermute x16, waiting for transfers between devices: 36.4 us -> 45 us  [hop(): return lax.ppermute(x, ('core',) + COL, pairs)]
    unnamed x24 -> x20, local copies, waits for them, and re-layouts: 9.43 us -> 6.52 us
  transfers between devices with their start and end apart: 28 -> 28, of which waited for: 13 -> 11; matrix products, arithmetic and copies ran while one was open for 3% -> 4% of each run, Pallas kernels for 10% -> 10%
where the time goes in v6:
time: 268 us; the launch traced here: 262 us
  waiting for transfers between devices  84.4 us (31%)
  starting transfers between devices  58 us (22%)
  blocking collectives  46.3 us (17%)
  Pallas kernels  40.4 us (15%)
  local copies, waits for them, and re-layouts  17.4 us (6%)
  between operations  14.1 us (5%)
    ppermute x16, waiting for transfers between devices, hop(): return lax.ppermute(x, ('core',) + COL, pairs)  45 us
    ppermute x3, waiting for transfers between devices, step(): lax.ppermute(x, ROW, [(2 * i + c, 2 * ((i + 1 - 2 * c) % 4) + c) for i in...  24.9 us
    ppermute x16, starting transfers between devices, hop(): return lax.ppermute(x, ('core',) + COL, pairs)  23.9 us
    all_to_all x1, blocking collectives, per_device(): lax.all_to_all(after(s, f_near[0]).reshape(16, -1, w), COL, 0, 0, tiled=T...  23.8 us
    ppermute x4, starting transfers between devices, swap(): return lax.ppermute(x, 'core', [(0, 1), (1, 0)])  23.5 us
    all_to_all x1, blocking collectives, spread(): lax.all_to_all(x.reshape(3, 8, sub, w), ROW, 1, 0, tiled=True)  22.5 us
    pallas_call x2, Pallas kernels, near_product(): pl.pallas_call(functools.partial(near_kernel, 16 // many), out_shape=jax....  18.9 us
    all_to_all x1, waiting for transfers between devices, spread(): lax.all_to_all(x.reshape(3, 8, sub, w), ROW, 1, 0, tiled=True)  11.9 us
  transfers between devices with their start and end apart: 28, of which 11 were waited for; matrix products, arithmetic and copies ran while one was open for 4% of the time, Pallas kernels for 10%

profile of v6, /device:TPU:1, one launch (start us, length us, event | category | flops | bytes accessed | tf_op | source)
XLA Modules:
  0.0 262.4 jit_solution(13973968273972271316)
XLA Ops:
  7.2 0.0 all-gather.6.cloned.1.call-start
  7.2 1.4 copy.7
  8.6 0.0 copy-start.6
  8.6 22.5 %all_to_all.35 = f32[3,8,32,384]{3,2,0,1:T(8,128)S(1)} all-to-all(f32[3,8,32,384]{3,2,0,1:T(8,128)S(1)} %copy.7), channel_id=1, replica_groups=mesh['y'=4,'core'=2,'z'=4,'x'=4] {'y','core'}, dimensions={1} | all-to-all | bytes 2359296 | tf_op jit(solution)/shard_map/all_to_all | solution.py:249
  31.1 0.6 pick_rows.2
  31.7 0.0 all-gather.6.cloned.1.call-update
  31.8 1.7 collective-permute-start
  33.5 2.2 collective-permute-start.1
  35.7 1.1 copy.8
  36.8 3.7 %all-to-all-start.1 = ((f32[3,8,32,384]{3,2,0,1:T(8,128)}), f32[3,8,32,384]{3,2,0,1:T(8,128)S(1)}, u32[]{:S(2)}, u32[]{:S(2)}) async-start(f32[3,8,32,384]{3,2,0,1:T(8,128)} %copy.8), calls=%async_computation.1 | async-start | bytes 2359296 | tf_op jit(solution)/shard_map/all_to_all | solution.py:249
  40.5 2.7 %collective-permute-done = f32[384,384]{1,0:T(8,128)S(1)} collective-permute-done((f32[384,384]{1,0:T(8,128)S(1)}, f32[384,384]{1,0:T(8,128)S(1)}, u32[]{:S(2)}, u32[]{:S(2)}) %collective-permute-start) | collective-permute-done | bytes 589856 | tf_op jit(solution)/shard_map/ppermute | solution.py:57
  43.2 0.1 collective-permute-start.2
  43.3 2.7 %collective-permute-start.3 = (f32[192,384]{1,0:T(8,128)S(1)}, f32[192,384]{1,0:T(8,128)S(1)}, u32[]{:S(2)}, u32[]{:S(2)}) collective-permute-start(f32[192,384]{1,0:T(8,128)S(1)} %slice.33), channel_id=1, source_target_pairs={{0,3},{1,0},{2,1},{3,2},{4,7},{5,4},{6,5},{7,6},{8,11},{9,8},{10,9... | collective-permute-start | bytes 884744 | tf_op jit(solution)/shard_map/ppermute | solution.py:57
  46.0 4.4 %collective-permute-done.2 = f32[192,384]{1,0:T(8,128)S(1)} collective-permute-done((f32[192,384]{1,0:T(8,128)S(1)}, f32[192,384]{1,0:T(8,128)S(1)}, u32[]{:S(2)}, u32[]{:S(2)}) %collective-permute-start.2) | collective-permute-done | bytes 294944 | tf_op jit(solution)/shard_map/ppermute | solution.py:57
  50.4 0.0 collective-permute-done.3
  50.5 1.5 pad_maximum_fusion.refs_0_
  52.0 0.9 collective-permute-start.4
  52.9 1.8 collective-permute-start.5
  54.7 11.9 %all-to-all-done.1 = f32[3,8,32,384]{3,2,0,1:T(8,128)S(1)} async-done(((f32[3,8,32,384]{3,2,0,1:T(8,128)}), f32[3,8,32,384]{3,2,0,1:T(8,128)S(1)}, u32[]{:S(2)}, u32[]{:S(2)}) %all-to-all-start.1) | async-done | bytes 1179680 | tf_op jit(solution)/shard_map/all_to_all | solution.py:249
  66.6 0.6 pick_rows.3
  67.2 23.8 %all_to_all.36.x = f32[16,24,384]{2,1,0:T(8,128)S(1)} all-to-all(f32[16,24,384]{2,1,0:T(8,128)S(1)} %bitcast.67), channel_id=1, replica_groups=mesh['y'=4,'core'=2,'z'=4,'x'=4] {'z','x'}, dimensions={0} | all-to-all | bytes 1179648 | tf_op jit(solution)/shard_map/all_to_all | solution.py:324
  90.9 1.4 pick_cols.1
  92.3 0.0 all-gather.4.cloned.1.call-update
  92.3 0.0 all-gather.8.cloned.1.call-start
  92.5 0.1 stack.126.at
  92.6 1.2 slice.34
  93.8 0.9 collective-permute-start.6
  94.7 0.0 collective-permute-done.5.refs_2_
  94.8 2.4 slice.35
  97.1 1.8 collective-permute-start.7
  98.9 1.8 copy-done.3
  100.7 9.9 %near.2.acc = f32[1,384,384]{2,1,0:T(8,128)S(1)} custom-call(s32[24]{0:T(128)S(1)} %stack.126.at, f32[4,384,384]{2,1,0:T(8,128)} %pad_maximum_fusion.refs_0_, f32[4,384,384]{2,1,0:T(8,128)S(1)} %copy-done.3, f32[4,384,384]{2,1,0:T(8,128)} %collective-permute-done.5.refs_2_, f32[16,384,384]{2,1,0:T(8,128)} %bitcast.58), custom_call_target="tpu_custom_call" | custom-call | flops 48922361856 | bytes 198180864 | tf_op jit(solution)/shard_map/near/pallas_call | solution.py:129
  110.6 3.8 %collective-permute-done.7.low = f32[2,384,384]{2,1,0:T(8,128)S(1)} collective-permute-done((f32[2,384,384]{2,1,0:T(8,128)}, f32[2,384,384]{2,1,0:T(8,128)S(1)}, u32[]{:S(2)}, u32[]{:S(2)}) %collective-permute-start.7) | collective-permute-done | bytes 1179680 | tf_op jit(solution)/shard_map/ppermute | solution.py:57
  114.4 3.7 %update.1 = (f32[384,384]{1,0:T(8,128)S(1)}, f32[384,384]{1,0:T(8,128)S(1)}) custom-call(s32[24]{0:T(128)S(1)} %stack.126.at, f32[1,384,384]{2,1,0:T(8,128)S(1)} %near.2.acc, f32[2,384,384]{2,1,0:T(8,128)S(1)} %collective-permute-done.6.top, f32[2,384,384]{2,1,0:T(8,128)S(1)} %collective-permute-done.7.low, f32[16,384,384]{2,1,0:T(8,128)S(1)} %bitcast.61), custom_call_target="tpu_custom_call" | custom-call | flops 1358954496 | bytes 2359296 | tf_op jit(solution)/shard_map/update/pallas_call | solution.py:178
  118.1 0.6 collective-permute-start.13
  118.7 6.2 %collective-permute-start.8 = (f32[384,384]{1,0:T(8,128)S(1)}, f32[384,384]{1,0:T(8,128)S(1)}, u32[]{:S(2)}, u32[]{:S(2)}) collective-permute-start(f32[384,384]{1,0:T(8,128)S(1)} %get-tuple-element.11), channel_id=1, source_target_pairs={{0,0},{1,1},{2,16},{3,17},{4,32},{5,33},{6,48},{7,49},{8,64},{9,65... | collective-permute-start | bytes 1769480 | tf_op jit(solution)/shard_map/ppermute | solution.py:330
  124.9 14.3 %collective-permute-done.13.refs_1_ = f32[12,32,384]{2,1,0:T(8,128)S(1)} collective-permute-done((f32[12,32,384]{2,1,0:T(8,128)S(1)}, f32[12,32,384]{2,1,0:T(8,128)S(1)}, u32[]{:S(2)}, u32[]{:S(2)}) %collective-permute-start.13) | collective-permute-done | bytes 589856 | tf_op jit(solution)/shard_map/ppermute | solution.py:36
  139.2 3.5 %collective-permute-start.10 = (f32[384,384]{1,0:T(8,128)S(1)}, f32[384,384]{1,0:T(8,128)S(1)}, u32[]{:S(2)}, u32[]{:S(2)}) collective-permute-start(f32[384,384]{1,0:T(8,128)S(1)} %collective-permute-done.8), channel_id=1, source_target_pairs={{0,3},{1,0},{2,1},{3,2},{4,7},{5,4},{6,5},{7,6},{8,11},{9,8},{10,9... | collective-permute-start | bytes 1769480 | tf_op jit(solution)/shard_map/ppermute | solution.py:57
  142.8 10.7 %collective-permute-done.14.refs_2_ = f32[12,32,384]{2,1,0:T(8,128)} collective-permute-done((f32[12,32,384]{2,1,0:T(8,128)S(1)}, f32[12,32,384]{2,1,0:T(8,128)}, u32[]{:S(2)}, u32[]{:S(2)}) %collective-permute-start.14) | collective-permute-done | bytes 589856 | tf_op jit(solution)/shard_map/ppermute | solution.py:36
  153.4 7.5 %collective-permute-done.9 = f32[384,384]{1,0:T(8,128)S(1)} collective-permute-done((f32[384,384]{1,0:T(8,128)S(1)}, f32[384,384]{1,0:T(8,128)S(1)}, u32[]{:S(2)}, u32[]{:S(2)}) %collective-permute-start.9) | collective-permute-done | bytes 589856 | tf_op jit(solution)/shard_map/ppermute | solution.py:57
  160.9 2.4 collective-permute-start.11
  163.3 0.4 collective-permute-start.12
  163.8 18.9 %collective-permute-start.16 = (f32[12,32,384]{2,1,0:T(8,128)S(1)}, f32[12,32,384]{2,1,0:T(8,128)}, u32[]{:S(2)}, u32[]{:S(2)}) collective-permute-start(f32[12,32,384]{2,1,0:T(8,128)S(1)} %bitcast.69), channel_id=1, source_target_pairs={{0,16},{16,0},{1,17},{17,1},{2,18},{18,2},{3,19},{19,3},{4,20},{20... | collective-permute-start | bytes 1769480 | tf_op jit(solution)/shard_map/ppermute | solution.py:40
  182.7 4.6 %collective-permute-start.18 = (f32[12,32,384]{2,1,0:T(8,128)}, f32[12,32,384]{2,1,0:T(8,128)}, u32[]{:S(2)}, u32[]{:S(2)}) collective-permute-start(f32[12,32,384]{2,1,0:T(8,128)} %collective-permute-done.14.refs_2_), channel_id=1, source_target_pairs={{0,16},{16,0},{1,17},{17,1},{2,18},{18,2},{3,19},{19,3},{4,20},{20... | collective-permute-start | bytes 1769480 | tf_op jit(solution)/shard_map/ppermute | solution.py:40
  187.3 0.0 collective-permute-start.19
  187.3 0.2 pad_maximum_fusion.1.refs_0_
  187.5 0.0 all-gather.4.cloned.1.call-done.s
  187.5 1.7 collective-permute-done.18.refs_6_
  189.2 0.8 collective-permute-done.19.refs_7_
  190.1 2.3 copy-done.5
  192.4 8.0 %cross.1 = f32[384,384]{1,0:T(8,128)} custom-call(s32[24]{0:T(128)S(1)} %stack.126.at, f32[384,3072]{1,0:T(8,128)S(1)} %copy-done.5, f32[12,32,384]{2,1,0:T(8,128)S(1)} %bitcast.70, f32[12,32,384]{2,1,0:T(8,128)S(1)} %collective-permute-done.13.refs_1_, f32[12,32,384]{2,1,0:T(8,128)} %collective-permute-done.14.refs_2_, ...), custom_call_target="tpu_custom_call" | custom-call | flops 2717908992 | bytes 9437184 | tf_op jit(solution)/shard_map/cross/pallas_call | solution.py:234
  200.4 0.0 all-gather.8.cloned.1.call-update
  200.4 0.1 collective-permute-start.20
  200.5 2.7 %collective-permute-start.21 = (f32[4,384,384]{2,1,0:T(8,128)S(1)}, f32[4,384,384]{2,1,0:T(8,128)}, u32[]{:S(2)}, u32[]{:S(2)}) collective-permute-start(f32[4,384,384]{2,1,0:T(8,128)S(1)} %pad_maximum_fusion.1.refs_0_), channel_id=1, source_target_pairs={{0,12},{1,13},{2,14},{3,15},{4,0},{5,1},{6,2},{7,3},{8,4},{9,5},{1... | collective-permute-start | bytes 7077896 | tf_op jit(solution)/shard_map/ppermute | solution.py:57
  203.2 26.6 %collective-permute-done.20.refs_1_ = f32[4,384,384]{2,1,0:T(8,128)} collective-permute-done((f32[4,384,384]{2,1,0:T(8,128)S(1)}, f32[4,384,384]{2,1,0:T(8,128)}, u32[]{:S(2)}, u32[]{:S(2)}) %collective-permute-start.20) | collective-permute-done | bytes 2359328 | tf_op jit(solution)/shard_map/ppermute | solution.py:57
  229.8 2.4 slice.38
  232.2 2.4 slice.39
  234.5 2.7 %collective-permute-start.23 = (f32[2,384,384]{2,1,0:T(8,128)}, f32[2,384,384]{2,1,0:T(8,128)}, u32[]{:S(2)}, u32[]{:S(2)}) collective-permute-start(f32[2,384,384]{2,1,0:T(8,128)} %slice.39), channel_id=1, source_target_pairs={{0,12},{1,13},{2,14},{3,15},{4,0},{5,1},{6,2},{7,3},{8,4},{9,5},{1... | collective-permute-start | bytes 3538952 | tf_op jit(solution)/shard_map/ppermute | solution.py:57
  237.2 2.3 copy-done
  239.5 9.1 %near.3.acc = f32[2,384,384]{2,1,0:T(8,128)S(1)} custom-call(s32[24]{0:T(128)S(1)} %stack.126.at, f32[4,384,384]{2,1,0:T(8,128)S(1)} %pad_maximum_fusion.1.refs_0_, f32[4,384,384]{2,1,0:T(8,128)} %collective-permute-done.20.refs_1_, f32[4,384,384]{2,1,0:T(8,128)} %collective-permute-done.21.refs_2_, f32[8,384,384]{2,1,0:T(8,128)S(1)} %bitcast.55), custom_call_target="tpu_custom_call" | custom-call | flops 48922361856 | bytes 141557760 | tf_op jit(solution)/shard_map/near/pallas_call | solution.py:129
  248.6 0.0 copy-start.1
  248.6 2.0 place_rows.1
  250.6 0.1 collective-permute-done.23.low
  250.7 5.2 %child.1 = f32[768,384]{1,0:T(8,128)} custom-call(s32[24]{0:T(128)S(1)} %stack.126.at, f32[2,384,384]{2,1,0:T(8,128)S(1)} %near.3.acc, f32[2,384,384]{2,1,0:T(8,128)S(1)} %collective-permute-done.22.top, f32[2,384,384]{2,1,0:T(8,128)} %collective-permute-done.23.low, f32[8,384,384]{2,1,0:T(8,128)S(1)} %bitcast.57, f32[768,384]{1,0:T(8,128)S(1)} %copy-done.1), custom_call_target="tpu_custom_call" | custom-call | flops 1358954496 | bytes 3538944 | tf_op jit(solution)/shard_map/child/pallas_call | solution.py:200
  (42 shorter events, 0.2 us)
Async XLA Ops:
  7.2 91.7 %all-gather.6.cloned.1.call-start = ((), (), s32[]{:S(2)}) async-start(), calls=%async_computation.4 | async-start | bytes 10616832 | tf_op jit(solution)/shard_map/all_gather | solution.py:320
  7.2 23.9 %copy-start.4 = (s32[12]{0:T(128)S(1)}, s32[12]{0:T(128)}, u32[]{:S(2)}) copy-start(s32[12]{0:T(128)} %anc.7) | copy-start | bytes 148
  8.6 27.1 %copy-start.6 = (f32[768,384]{1,0:T(8,128)S(1)}, f32[768,384]{1,0:T(8,128)}, u32[]{:S(2)}) copy-start(f32[768,384]{1,0:T(8,128)} %param.5) | copy-start | bytes 3538948
  31.8 11.4 %collective-permute-start = (f32[384,384]{1,0:T(8,128)S(1)}, f32[384,384]{1,0:T(8,128)S(1)}, u32[]{:S(2)}, u32[]{:S(2)}) collective-permute-start(f32[384,384]{1,0:T(8,128)S(1)} %bitcast.64), channel_id=1, source_target_pairs={{0,1},{1,2},{2,3},{3,0},{4,5},{5,6},{6,7},{7,4},{8,9},{9,10},{10,1... | collective-permute-start | bytes 1769480 | tf_op jit(solution)/shard_map/ppermute | solution.py:57
  33.5 9.8 %collective-permute-start.1 = (f32[384,384]{1,0:T(8,128)S(1)}, f32[384,384]{1,0:T(8,128)S(1)}, u32[]{:S(2)}, u32[]{:S(2)}) collective-permute-start(f32[384,384]{1,0:T(8,128)S(1)} %bitcast.65), channel_id=1, source_target_pairs={{0,3},{1,0},{2,1},{3,2},{4,7},{5,4},{6,5},{7,6},{8,11},{9,8},{10,9... | collective-permute-start | bytes 1769480 | tf_op jit(solution)/shard_map/ppermute | solution.py:57
  36.8 29.8 %all-to-all-start.1 = ((f32[3,8,32,384]{3,2,0,1:T(8,128)}), f32[3,8,32,384]{3,2,0,1:T(8,128)S(1)}, u32[]{:S(2)}, u32[]{:S(2)}) async-start(f32[3,8,32,384]{3,2,0,1:T(8,128)} %copy.8), calls=%async_computation.1 | async-start | bytes 2359296 | tf_op jit(solution)/shard_map/all_to_all | solution.py:249
  40.5 147.0 %all-gather.4.cloned.1.call-start = ((), (), s32[]{:S(2)}) async-start(), calls=%async_computation.3 | async-start | bytes 5013504 | tf_op jit(solution)/shard_map/all_gather | solution.py:325
  43.2 7.3 %collective-permute-start.2 = (f32[192,384]{1,0:T(8,128)S(1)}, f32[192,384]{1,0:T(8,128)S(1)}, u32[]{:S(2)}, u32[]{:S(2)}) collective-permute-start(f32[192,384]{1,0:T(8,128)S(1)} %slice.32), channel_id=1, source_target_pairs={{0,1},{1,2},{2,3},{3,0},{4,5},{5,6},{6,7},{7,4},{8,9},{9,10},{10,1... | collective-permute-start | bytes 884744 | tf_op jit(solution)/shard_map/ppermute | solution.py:57
  43.3 7.1 %collective-permute-start.3 = (f32[192,384]{1,0:T(8,128)S(1)}, f32[192,384]{1,0:T(8,128)S(1)}, u32[]{:S(2)}, u32[]{:S(2)}) collective-permute-start(f32[192,384]{1,0:T(8,128)S(1)} %slice.33), channel_id=1, source_target_pairs={{0,3},{1,0},{2,1},{3,2},{4,7},{5,4},{6,5},{7,6},{8,11},{9,8},{10,9... | collective-permute-start | bytes 884744 | tf_op jit(solution)/shard_map/ppermute | solution.py:57
  52.0 40.6 %collective-permute-start.4 = (f32[4,384,384]{2,1,0:T(8,128)}, f32[4,384,384]{2,1,0:T(8,128)S(1)}, u32[]{:S(2)}, u32[]{:S(2)}) collective-permute-start(f32[4,384,384]{2,1,0:T(8,128)} %pad_maximum_fusion.refs_0_), channel_id=1, source_target_pairs={{0,4},{1,5},{2,6},{3,7},{4,8},{5,9},{6,10},{7,11},{8,12},{9,13},{1... | collective-permute-start | bytes 7077896 | tf_op jit(solution)/shard_map/ppermute | solution.py:57
  52.9 41.8 %collective-permute-start.5 = (f32[4,384,384]{2,1,0:T(8,128)}, f32[4,384,384]{2,1,0:T(8,128)}, u32[]{:S(2)}, u32[]{:S(2)}) collective-permute-start(f32[4,384,384]{2,1,0:T(8,128)} %pad_maximum_fusion.refs_0_), channel_id=1, source_target_pairs={{0,12},{1,13},{2,14},{3,15},{4,0},{5,1},{6,2},{7,3},{8,4},{9,5},{1... | collective-permute-start | bytes 7077896 | tf_op jit(solution)/shard_map/ppermute | solution.py:57
  92.3 144.8 %all-gather.8.cloned.1.call-start = ((), (), s32[]{:S(2)}) async-start(), calls=%async_computation.5 | async-start | bytes 5308416 | tf_op jit(solution)/shard_map/all_gather | solution.py:335
  92.6 2.1 copy-start.2
  93.8 16.8 %collective-permute-start.6 = (f32[2,384,384]{2,1,0:T(8,128)}, f32[2,384,384]{2,1,0:T(8,128)S(1)}, u32[]{:S(2)}, u32[]{:S(2)}) collective-permute-start(f32[2,384,384]{2,1,0:T(8,128)} %slice.34), channel_id=1, source_target_pairs={{0,4},{1,5},{2,6},{3,7},{4,8},{5,9},{6,10},{7,11},{8,12},{9,13},{1... | collective-permute-start | bytes 3538952 | tf_op jit(solution)/shard_map/ppermute | solution.py:57
  97.1 17.2 %collective-permute-start.7 = (f32[2,384,384]{2,1,0:T(8,128)}, f32[2,384,384]{2,1,0:T(8,128)S(1)}, u32[]{:S(2)}, u32[]{:S(2)}) collective-permute-start(f32[2,384,384]{2,1,0:T(8,128)} %slice.35), channel_id=1, source_target_pairs={{0,12},{1,13},{2,14},{3,15},{4,0},{5,1},{6,2},{7,3},{8,4},{9,5},{1... | collective-permute-start | bytes 3538952 | tf_op jit(solution)/shard_map/ppermute | solution.py:57
  98.9 15.5 %slice-start = ((s8[9437184]{0:T(1024)(128)(4,1)}), s8[4194304]{0:T(1024)(128)(4,1)S(1)}, s32[]{:S(2)}) async-start(s8[9437184]{0:T(1024)(128)(4,1)} %bitcast.59), calls=%async_computation.6 | async-start | bytes 8388608
  98.9 1.8 copy-start.3
  100.7 13.6 %slice-start.1 = ((s8[9437184]{0:T(1024)(128)(4,1)}), s8[4194304]{0:T(1024)(128)(4,1)S(1)}, s32[]{:S(2)}) async-start(s8[9437184]{0:T(1024)(128)(4,1)} %bitcast.59), calls=%async_computation.7 | async-start | bytes 8388608
  100.7 13.6 %slice-start.2 = ((s8[9437184]{0:T(1024)(128)(4,1)}), s8[1048576]{0:T(1024)(128)(4,1)S(1)}, s32[]{:S(2)}) async-start(s8[9437184]{0:T(1024)(128)(4,1)} %bitcast.59), calls=%async_computation.8 | async-start | bytes 2097152
  118.1 21.1 %collective-permute-start.13 = (f32[12,32,384]{2,1,0:T(8,128)S(1)}, f32[12,32,384]{2,1,0:T(8,128)S(1)}, u32[]{:S(2)}, u32[]{:S(2)}) collective-permute-start(f32[12,32,384]{2,1,0:T(8,128)S(1)} %bitcast.68), channel_id=1, source_target_pairs={{0,32},{16,112},{32,64},{48,16},{64,96},{80,48},{96,0},{112,80},{1... | collective-permute-start | bytes 1769480 | tf_op jit(solution)/shard_map/ppermute | solution.py:36
  118.7 20.5 %collective-permute-start.8 = (f32[384,384]{1,0:T(8,128)S(1)}, f32[384,384]{1,0:T(8,128)S(1)}, u32[]{:S(2)}, u32[]{:S(2)}) collective-permute-start(f32[384,384]{1,0:T(8,128)S(1)} %get-tuple-element.11), channel_id=1, source_target_pairs={{0,0},{1,1},{2,16},{3,17},{4,32},{5,33},{6,48},{7,49},{8,64},{9,65... | collective-permute-start | bytes 1769480 | tf_op jit(solution)/shard_map/ppermute | solution.py:330
  139.2 14.2 %collective-permute-start.14 = (f32[12,32,384]{2,1,0:T(8,128)S(1)}, f32[12,32,384]{2,1,0:T(8,128)}, u32[]{:S(2)}, u32[]{:S(2)}) collective-permute-start(f32[12,32,384]{2,1,0:T(8,128)S(1)} %collective-permute-done.13.refs_1_), channel_id=1, source_target_pairs={{0,32},{16,112},{32,64},{48,16},{64,96},{80,48},{96,0},{112,80},{1... | collective-permute-start | bytes 1769480 | tf_op jit(solution)/shard_map/ppermute | solution.py:36
  139.2 21.7 %collective-permute-start.9 = (f32[384,384]{1,0:T(8,128)S(1)}, f32[384,384]{1,0:T(8,128)S(1)}, u32[]{:S(2)}, u32[]{:S(2)}) collective-permute-start(f32[384,384]{1,0:T(8,128)S(1)} %collective-permute-done.8), channel_id=1, source_target_pairs={{0,1},{1,2},{2,3},{3,0},{4,5},{5,6},{6,7},{7,4},{8,9},{9,10},{10,1... | collective-permute-start | bytes 1769480 | tf_op jit(solution)/shard_map/ppermute | solution.py:57
  139.2 24.1 %collective-permute-start.10 = (f32[384,384]{1,0:T(8,128)S(1)}, f32[384,384]{1,0:T(8,128)S(1)}, u32[]{:S(2)}, u32[]{:S(2)}) collective-permute-start(f32[384,384]{1,0:T(8,128)S(1)} %collective-permute-done.8), channel_id=1, source_target_pairs={{0,3},{1,0},{2,1},{3,2},{4,7},{5,4},{6,5},{7,6},{8,11},{9,8},{10,9... | collective-permute-start | bytes 1769480 | tf_op jit(solution)/shard_map/ppermute | solution.py:57
  153.4 33.8 %collective-permute-start.15 = (f32[12,32,384]{2,1,0:T(8,128)}, f32[12,32,384]{2,1,0:T(8,128)}, u32[]{:S(2)}, u32[]{:S(2)}) collective-permute-start(f32[12,32,384]{2,1,0:T(8,128)} %collective-permute-done.14.refs_2_), channel_id=1, source_target_pairs={{0,32},{16,112},{32,64},{48,16},{64,96},{80,48},{96,0},{112,80},{1... | collective-permute-start | bytes 1769480 | tf_op jit(solution)/shard_map/ppermute | solution.py:36
  160.9 21.7 %collective-permute-start.11 = (f32[192,384]{1,0:T(8,128)S(1)}, f32[192,384]{1,0:T(8,128)S(1)}, u32[]{:S(2)}, u32[]{:S(2)}) collective-permute-start(f32[192,384]{1,0:T(8,128)S(1)} %slice.36), channel_id=1, source_target_pairs={{0,1},{1,2},{2,3},{3,0},{4,5},{5,6},{6,7},{7,4},{8,9},{9,10},{10,1... | collective-permute-start | bytes 884744 | tf_op jit(solution)/shard_map/ppermute | solution.py:57
  163.3 23.9 %collective-permute-start.12 = (f32[192,384]{1,0:T(8,128)S(1)}, f32[192,384]{1,0:T(8,128)S(1)}, u32[]{:S(2)}, u32[]{:S(2)}) collective-permute-start(f32[192,384]{1,0:T(8,128)S(1)} %slice.37), channel_id=1, source_target_pairs={{0,3},{1,0},{2,1},{3,2},{4,7},{5,4},{6,5},{7,6},{8,11},{9,8},{10,9... | collective-permute-start | bytes 884744 | tf_op jit(solution)/shard_map/ppermute | solution.py:57
  163.8 23.7 %collective-permute-start.16 = (f32[12,32,384]{2,1,0:T(8,128)S(1)}, f32[12,32,384]{2,1,0:T(8,128)}, u32[]{:S(2)}, u32[]{:S(2)}) collective-permute-start(f32[12,32,384]{2,1,0:T(8,128)S(1)} %bitcast.69), channel_id=1, source_target_pairs={{0,16},{16,0},{1,17},{17,1},{2,18},{18,2},{3,19},{19,3},{4,20},{20... | collective-permute-start | bytes 1769480 | tf_op jit(solution)/shard_map/ppermute | solution.py:40
  182.6 4.9 %collective-permute-start.17 = (f32[12,32,384]{2,1,0:T(8,128)S(1)}, f32[12,32,384]{2,1,0:T(8,128)}, u32[]{:S(2)}, u32[]{:S(2)}) collective-permute-start(f32[12,32,384]{2,1,0:T(8,128)S(1)} %collective-permute-done.13.refs_1_), channel_id=1, source_target_pairs={{0,16},{16,0},{1,17},{17,1},{2,18},{18,2},{3,19},{19,3},{4,20},{20... | collective-permute-start | bytes 1769480 | tf_op jit(solution)/shard_map/ppermute | solution.py:40
  182.7 6.6 %collective-permute-start.18 = (f32[12,32,384]{2,1,0:T(8,128)}, f32[12,32,384]{2,1,0:T(8,128)}, u32[]{:S(2)}, u32[]{:S(2)}) collective-permute-start(f32[12,32,384]{2,1,0:T(8,128)} %collective-permute-done.14.refs_2_), channel_id=1, source_target_pairs={{0,16},{16,0},{1,17},{17,1},{2,18},{18,2},{3,19},{19,3},{4,20},{20... | collective-permute-start | bytes 1769480 | tf_op jit(solution)/shard_map/ppermute | solution.py:40
  187.3 2.8 %collective-permute-start.19 = (f32[12,32,384]{2,1,0:T(8,128)}, f32[12,32,384]{2,1,0:T(8,128)}, u32[]{:S(2)}, u32[]{:S(2)}) collective-permute-start(f32[12,32,384]{2,1,0:T(8,128)} %collective-permute-done.15.refs_3_), channel_id=1, source_target_pairs={{0,16},{16,0},{1,17},{17,1},{2,18},{18,2},{3,19},{19,3},{4,20},{20... | collective-permute-start | bytes 1769480 | tf_op jit(solution)/shard_map/ppermute | solution.py:40
  190.1 2.3 copy-start.5
  200.4 29.4 %collective-permute-start.20 = (f32[4,384,384]{2,1,0:T(8,128)S(1)}, f32[4,384,384]{2,1,0:T(8,128)}, u32[]{:S(2)}, u32[]{:S(2)}) collective-permute-start(f32[4,384,384]{2,1,0:T(8,128)S(1)} %pad_maximum_fusion.1.refs_0_), channel_id=1, source_target_pairs={{0,4},{1,5},{2,6},{3,7},{4,8},{5,9},{6,10},{7,11},{8,12},{9,13},{1... | collective-permute-start | bytes 7077896 | tf_op jit(solution)/shard_map/ppermute | solution.py:57
  200.5 31.7 %collective-permute-start.21 = (f32[4,384,384]{2,1,0:T(8,128)S(1)}, f32[4,384,384]{2,1,0:T(8,128)}, u32[]{:S(2)}, u32[]{:S(2)}) collective-permute-start(f32[4,384,384]{2,1,0:T(8,128)S(1)} %pad_maximum_fusion.1.refs_0_), channel_id=1, source_target_pairs={{0,12},{1,13},{2,14},{3,15},{4,0},{5,1},{6,2},{7,3},{8,4},{9,5},{1... | collective-permute-start | bytes 7077896 | tf_op jit(solution)/shard_map/ppermute | solution.py:57
  232.1 18.4 %collective-permute-start.22 = (f32[2,384,384]{2,1,0:T(8,128)}, f32[2,384,384]{2,1,0:T(8,128)S(1)}, u32[]{:S(2)}, u32[]{:S(2)}) collective-permute-start(f32[2,384,384]{2,1,0:T(8,128)} %slice.38), channel_id=1, source_target_pairs={{0,4},{1,5},{2,6},{3,7},{4,8},{5,9},{6,10},{7,11},{8,12},{9,13},{1... | collective-permute-start | bytes 3538952 | tf_op jit(solution)/shard_map/ppermute | solution.py:57
  234.5 16.1 %collective-permute-start.23 = (f32[2,384,384]{2,1,0:T(8,128)}, f32[2,384,384]{2,1,0:T(8,128)}, u32[]{:S(2)}, u32[]{:S(2)}) collective-permute-start(f32[2,384,384]{2,1,0:T(8,128)} %slice.39), channel_id=1, source_target_pairs={{0,12},{1,13},{2,14},{3,15},{4,0},{5,1},{6,2},{7,3},{8,4},{9,5},{1... | collective-permute-start | bytes 3538952 | tf_op jit(solution)/shard_map/ppermute | solution.py:57
  237.2 2.3 copy-start
  248.6 2.1 copy-start.1
Sparse Core Ops, SparseCore 0:
  31.9 65.2 all-gather.5
  99.3 83.6 all-gather.3
  200.5 34.4 all-gather.7

commit v7 on v6

--- a/solution.py
+++ b/solution.py
@@ -10,7 +10,7 @@
 
 NB = 24
 NANC = 12
-W1, W2 = 12, 12
+W1, W2 = 14, 12
 ROW = ("y", "core")
 COL = ("z", "x")
 ALL = ("y", "core", "z", "x")
@@ -40,10 +40,10 @@
     return lax.ppermute(x, "core", [(0, 1), (1, 0)])
 
 
-def gather_rows(x):
+def gather_rows(x, gate=()):
     mine = [x]
-    for _ in range(3):
-        mine.append(step(mine[-1]))
+    for k in range(3):
+        mine.append(step(after(mine[-1], *gate) if k == 1 else mine[-1]))
     return mine + [swap(t) for t in mine]
 
 
@@ -57,14 +57,16 @@
     return lax.ppermute(x, ("core",) + COL, pairs)
 
 
-def gather_cols(x, axis, gates=((), (), ())):
-    half = x.shape[axis] // 2
+def gather_cols(x, gate=()):
+    half = x.shape[0] // 2
     up, down = hop(x, 0, 1), hop(x, 0, -1)
-    top = hop(lax.slice_in_dim(after(up, *gates[0]), 0, half, axis=axis), 0, 1)
-    low = hop(lax.slice_in_dim(after(down, *gates[0]), half, 2 * half, axis=axis), 0, -1)
-    group = after(jnp.stack([x, up, down, jnp.concatenate([top, low], axis=axis)]), *gates[1])
-    up, down = hop(group, 1, 1), hop(group, 1, -1)
-    return (group, up, down), (hop(after(up, *gates[2])[:2], 1, 1), hop(after(down, *gates[2])[2:], 1, -1))
+    up, down = lax.optimization_barrier((up, down, *gate))[:2]
+    top, low = hop(up[:half], 0, 1), hop(down[half:], 0, -1)
+    one, two = jnp.stack([x, up]), jnp.stack([down, jnp.concatenate([top, low])])
+    one, two = lax.optimization_barrier((one, two))
+    up_one, down_one = hop(one, 1, 1), hop(one, 1, -1)
+    up_two, down_two = hop(two, 1, 1), hop(two, 1, -1)
+    return (one, two, up_one, up_two, down_one, down_two), (hop(up_one, 1, 1), hop(down_two, 1, -1)), down
 
 
 def places():
@@ -89,20 +91,65 @@
     return mul(a_hi, b_hi) + (mul(a_hi, b_lo) + mul(a_lo, b_hi))
 
 
-def near_kernel(per, at, *refs):
-    groups, tiles, acc, (a_buf, b_buf, a_sem, b_sem) = refs[:3], refs[3], refs[4], refs[5:]
+def pair_copy(a_buf, a_sem, i, source):
+    return pltpu.make_async_copy(source, a_buf.at[pl.ds(2 * i, 2)], a_sem.at[i])
+
+
+def near_rows_kernel(at, *refs):
+    pairs, tiles, (acc, far), (a_buf, b_buf, a_sem, b_sem) = refs[:6], refs[6:14], refs[14:16], refs[16:]
+    copies = [pltpu.make_async_copy(tiles[i], b_buf.at[pl.ds(2 * at[i], 2)], b_sem.at[i]) for i in range(8)]
+    copies += [pair_copy(a_buf, a_sem, i, pairs[i]) for i in range(6)]
+    for copy in copies:
+        copy.start()
+    acc[...] = jnp.zeros_like(acc)
+    for copy in copies:
+        copy.wait()
+
+    def body(i, carry):
+        k0 = 4 * lax.div(i, 2) + lax.rem(i, 2)
+        k1 = k0 + 3 - 2 * lax.rem(i, 2)
+        acc[0] += dot3(
+            jnp.concatenate([a_buf[k0], a_buf[k1]], axis=1),
+            jnp.concatenate([b_buf[at[8 + k0]], b_buf[at[8 + k1]]], axis=0),
+        )
+        return carry
+
+    lax.fori_loop(0, 6, body, 0)
+    for k in range(4):
+        far[k] = b_buf[at[20 + k]]
+
+
+def near_rows_product(at, pairs, tiles):
+    m, w = pairs[0].shape[1:]
+    _, k, n = tiles[0].shape
+    return pl.pallas_call(
+        near_rows_kernel,
+        out_shape=(jax.ShapeDtypeStruct((1, m, n), F32), jax.ShapeDtypeStruct((4, k, n), F32)),
+        in_specs=[SMEM] + [ANY] * 14,
+        out_specs=(VMEM, VMEM),
+        scratch_shapes=[
+            pltpu.VMEM((12, m, w), F32),
+            pltpu.VMEM((16, k, n), F32),
+            pltpu.SemaphoreType.DMA((6,)),
+            pltpu.SemaphoreType.DMA((8,)),
+        ],
+        compiler_params=params(40),
+        cost_estimate=cost(W1 * m, 12 * w, n, W1 * 4 * w * (12 * m + 16 * n)),
+        name="near_rows",
+    )(at, *pairs, *tiles)
+
+
+def near_kernel(at, *refs):
+    pairs, tiles, acc, (a_buf, b_buf, a_sem, b_sem) = refs[:6], refs[6], refs[7], refs[8:]
     outs = acc.shape[0]
 
-    def group_copy(g, source):
-        return pltpu.make_async_copy(source, a_buf.at[pl.ds(4 * g, 4)], a_sem.at[g])
-
     def tile_copy(k):
-        return pltpu.make_async_copy(tiles.at[lax.div(at[8 + k], per)], b_buf.at[k], b_sem.at[k])
-
-    for g in range(3):
-        group_copy(g, groups[g]).start()
-        for k in (0, 3, 1, 2):
-            tile_copy(4 * g + k).start()
+        return pltpu.make_async_copy(tiles.at[lax.div(at[8 + k], 2)], b_buf.at[k], b_sem.at[k])
+
+    for i in range(6):
+        pair_copy(a_buf, a_sem, i, pairs[i]).start()
+        tile_copy(2 * i).start()
+        tile_copy(2 * i + 1).start()
     acc[...] = jnp.zeros_like(acc)
 
     def body(i, carry):
@@ -110,7 +157,8 @@
 
         @pl.when(q == 0)
         def _():
-            group_copy(g, groups[0]).wait()
+            for k in range(2):
+                pair_copy(a_buf, a_sem, 2 * g + k, pairs[0]).wait()
 
         k0, k1 = 4 * g + q, 4 * g + 3 - q
         tile_copy(k0).wait()
@@ -123,30 +171,31 @@
     lax.fori_loop(0, 6, body, 0)
 
 
-def near_product(at, groups, tiles, outs, weight):
-    m, w = groups[0].shape[1:]
+def near_product(at, pairs, tiles):
+    m, w = pairs[0].shape[1:]
     many, _, n = tiles.shape
     return pl.pallas_call(
-        functools.partial(near_kernel, 16 // many),
-        out_shape=jax.ShapeDtypeStruct((outs, m, n), F32),
-        in_specs=[SMEM] + [ANY] * 4,
+        near_kernel,
+        out_shape=jax.ShapeDtypeStruct((2, m, n), F32),
+        in_specs=[SMEM] + [ANY] * 7,
         out_specs=VMEM,
         scratch_shapes=[
             pltpu.VMEM((12, m, w), F32),
             pltpu.VMEM((12,) + tiles.shape[1:], F32),
-            pltpu.SemaphoreType.DMA((3,)),
+            pltpu.SemaphoreType.DMA((6,)),
             pltpu.SemaphoreType.DMA((12,)),
         ],
         compiler_params=params(40),
-        cost_estimate=cost(weight * m, 12 * w, n, weight * 4 * w * (12 * m + many * n)),
+        cost_estimate=cost(W2 * m, 12 * w, n, W2 * 4 * w * (12 * m + many * n)),
         name="near",
-    )(at, *groups, tiles)
+    )(at, *pairs, tiles)
 
 
 def far_sum(at, top, low, tiles, a_buf, b_buf, sem, per):
     copies = [pltpu.make_async_copy(top, a_buf.at[pl.ds(0, 2)], sem.at[0])]
     copies += [pltpu.make_async_copy(low, a_buf.at[pl.ds(2, 2)], sem.at[1])]
-    copies += [pltpu.make_async_copy(tiles.at[lax.div(at[20 + k], per)], b_buf.at[k], sem.at[2 + k]) for k in range(4)]
+    index = lambda k: lax.div(at[20 + k], per) if per else k
+    copies += [pltpu.make_async_copy(tiles.at[index(k)], b_buf.at[k], sem.at[2 + k]) for k in range(4)]
     for copy in copies:
         copy.start()
     for copy in copies:
@@ -167,7 +216,7 @@
 
 def update_kernel(at, acc, top, low, tiles, u, ut, a_buf, b_buf, sem):
     total = acc[0]
-    for _, part in far_sum(at, top, low, tiles, a_buf, b_buf, sem, 1):
+    for _, part in far_sum(at, top, low, tiles, a_buf, b_buf, sem, 0):
         total += part
     u[...] = total
     ut[...] = total.T
@@ -209,9 +258,8 @@
     )(at, acc, top, low, tiles, base)
 
 
-def cross_kernel(at, s, *refs):
-    tiles, (sigma, u_buf, u_sem) = refs[:8], refs[8:]
-    copies = [pltpu.make_async_copy(tiles[i], u_buf.at[:, at[i]], u_sem.at[i]) for i in range(8)]
+def cross_kernel(s, u, sigma, u_buf, u_sem):
+    copies = [pltpu.make_async_copy(u.at[i], u_buf.at[:, i], u_sem.at[i]) for i in range(8)]
     for copy in copies:
         copy.start()
     sigma[...] = jnp.zeros_like(sigma)
@@ -228,19 +276,19 @@
     lax.fori_loop(0, 4, body, 0)
 
 
-def cross_product(at, s, tiles):
+def cross_product(s, u):
     m, width = s.shape
-    sub, w = tiles[0].shape[1:]
+    _, _, sub, w = u.shape
     return pl.pallas_call(
         cross_kernel,
         out_shape=jax.ShapeDtypeStruct((m, w), F32),
-        in_specs=[SMEM, VMEM] + [ANY] * 8,
+        in_specs=[VMEM, ANY],
         out_specs=VMEM,
         scratch_shapes=[pltpu.VMEM((NANC, 8, sub, w), F32), pltpu.SemaphoreType.DMA((8,))],
         compiler_params=params(40),
         cost_estimate=cost(m, width, w, 4 * width * (m + w)),
         name="cross",
-    )(at, s, *tiles)
+    )(s, u)
 
 
 def spread(x):
@@ -249,21 +297,25 @@
     return lax.all_to_all(x.reshape(3, 8, sub, w), ROW, 1, 0, tiled=True).reshape(NB, sub, w)
 
 
-def pick_rows_kernel(anc, x, out):
+def pick_rows_kernel(anc, x, a, b):
+    w = a.shape[2]
     for i in range(NANC):
-        out[i] = x[anc[i]]
+        a[i] = x[anc[i], :, :w]
+        b[i] = x[anc[i], :, w:]
 
 
 def pick_rows(ancestors, x):
-    sub, w = x.shape[1:]
-    return pl.pallas_call(
+    sub, w = x.shape[1], x.shape[2] // 2
+    out = jax.ShapeDtypeStruct((NANC, sub, w), F32)
+    a, b = pl.pallas_call(
         pick_rows_kernel,
-        out_shape=jax.ShapeDtypeStruct((NANC, sub, w), F32),
+        out_shape=(out, out),
         in_specs=[SMEM, VMEM],
-        out_specs=VMEM,
-        compiler_params=params(8),
+        out_specs=(VMEM, VMEM),
+        compiler_params=params(12),
         name="pick_rows",
-    )(ancestors, x).reshape(NANC * sub, w)
+    )(ancestors, x)
+    return a.reshape(NANC * sub, w), b.reshape(NANC * sub, w)
 
 
 def pick_cols_kernel(anc, x, out):
@@ -316,24 +368,23 @@
     sub = h // 24
     at = places()
 
-    f = pick_rows(ancestors, spread(factor_cross))
-    inverse = lax.all_gather(after(factor_inverse, f), ROW, axis=0, tiled=True).reshape(16, w, w)
-    f_near, f_far = gather_cols(f, 0)
-
-    s = pick_rows(ancestors, spread(after(sigma_top, f)))
-    s = lax.all_to_all(after(s, f_near[0]).reshape(16, -1, w), COL, 0, 0, tiled=True)
-    s_all = lax.all_gather(pick_cols(ancestors, s), COL, axis=0, tiled=True)
-
-    acc = near_product(at, f_near, inverse, 1, W1)
-    u, ut = update_product(at, acc, *f_far, inverse)
+    both = jnp.concatenate([factor_cross, sigma_top], axis=1)
+    f, s = pick_rows(ancestors, spread(both))
+    s = pick_cols(ancestors, lax.all_to_all(s.reshape(16, -1, w), COL, 0, 0, tiled=True))
+    s_all = lax.all_gather(s, COL, axis=0, tiled=True)
+    f_near, f_far, f_down = gather_cols(f, (s,))
+    inverse_tiles = [t.reshape(2, w, w) for t in gather_rows(after(factor_inverse, f), (f_down,))]
+
+    acc, far = near_rows_product(at, f_near, inverse_tiles)
+    u, ut = update_product(at, acc, *f_far, far)
 
     moved = lax.ppermute(ut, ALL, [(16 * r + c, 16 * (c // 2) + 2 * r + c % 2) for r in range(8) for c in range(16)])
-    u_near, u_far = gather_cols(moved, 0)
-    u_tiles = gather_rows(u.reshape(NANC, sub, w))
-
-    sigma = cross_product(at, after(s_all, u_near[0]), u_tiles)
+    u_near, u_far, _ = gather_cols(moved)
+    u_all = lax.all_gather(after(u, s_all), ROW, axis=0, tiled=True).reshape(8, NANC, sub, w)
+
+    sigma = cross_product(s_all, after(u_all, u_near[1]))
     sigma_all = lax.all_gather(sigma, ROW, axis=0, tiled=True).reshape(8, w, w)
-    acc = near_product(at, u_near, sigma_all, 2, W2)
+    acc = near_product(at, u_near, sigma_all)
     sigma_child = child_product(at, acc, *u_far, sigma_all, block_inverse)
 
     sigma_cross = place_rows(ancestors, sigma_all.reshape(8, NANC, sub, w), h)

time: 268 us -> 299 us (1.12); the launches traced: 262 us -> 299 us
  waiting for transfers between devices: 84.4 us -> 122 us
  starting transfers between devices: 58 us -> 47.5 us
  blocking collectives: 46.3 us -> 51.8 us
    ppermute x16 -> x20, waiting for transfers between devices: 45 us -> 81.8 us  [hop(): return lax.ppermute(x, ('core',) + COL, pairs)]
    ppermute x3, waiting for transfers between devices: 24.9 us -> 0.48 us  [step(): lax.ppermute(x, ROW, [(2 * i + c, 2 * ((i + 1 - 2 * c) % 4) + c) for i in...]
    all_gather x1, waiting for transfers between devices: 0.01 us -> 18.4 us  [per_device(): sigma_all = lax.all_gather(sigma, ROW, axis=0, tiled=True).reshape(8, w, w)]
    ppermute x4, starting transfers between devices: 23.5 us -> 7.13 us  [swap(): return lax.ppermute(x, 'core', [(0, 1), (1, 0)])]
    all_to_all x1, blocking collectives: 22.5 us -> 35.1 us  [spread(): lax.all_to_all(x.reshape(3, 8, sub, w), ROW, 1, 0, tiled=True)]
    ppermute x1, waiting for transfers between devices: 0.01 us -> 12.4 us  [per_device(): lax.ppermute(ut, ALL, [(16 * r + c, 16 * (c // 2) + 2 * r + c % 2) for r...]
    all_to_all x1 -> x0, waiting for transfers between devices: 11.9 us -> none  [spread(): lax.all_to_all(x.reshape(3, 8, sub, w), ROW, 1, 0, tiled=True)]
    all_gather x2, waiting for transfers between devices: 0.02 us -> 8.78 us  [the longest x1 8.76 us: per_device(): lax.all_gather(after(u, s_all), ROW, axis=0, tiled=True)]
  transfers between devices with their start and end apart: 28 -> 31, of which waited for: 11 -> 14; matrix products, arithmetic and copies ran while one was open for 4% -> 2% of each run, Pallas kernels for 10% -> 10%
where the time goes in v7:
time: 299 us
  waiting for transfers between devices  122 us (41%)
  blocking collectives  51.8 us (17%)
  starting transfers between devices  47.5 us (16%)
  Pallas kernels  42.4 us (14%)
  local copies, waits for them, and re-layouts  16.5 us (6%)
  between operations  14 us (5%)
  other arithmetic  4.49 us (2%)
    ppermute x20, waiting for transfers between devices, hop(): return lax.ppermute(x, ('core',) + COL, pairs)  81.8 us
    all_to_all x1, blocking collectives, spread(): lax.all_to_all(x.reshape(3, 8, sub, w), ROW, 1, 0, tiled=True)  35.1 us
    ppermute x20, starting transfers between devices, hop(): return lax.ppermute(x, ('core',) + COL, pairs)  30 us
    all_gather x1, waiting for transfers between devices, per_device(): sigma_all = lax.all_gather(sigma, ROW, axis=0, tiled=True).reshape(8, w, w)  18.4 us
    all_to_all x1, blocking collectives, per_device(): lax.all_to_all(s.reshape(16, -1, w), COL, 0, 0, tiled=True)  16.7 us
    unnamed x26, local copies, waits for them, and re-layouts  14.2 us
    pallas_call x1, Pallas kernels, near_rows_product(): pl.pallas_call(near_rows_kernel, out_shape=(jax.ShapeDtypeStruct((1, m, n...  13.2 us
    ppermute x1, waiting for transfers between devices, per_device(): lax.ppermute(ut, ALL, [(16 * r + c, 16 * (c // 2) + 2 * r + c % 2) for r...  12.4 us
  transfers between devices with their start and end apart: 31, of which 14 were waited for; matrix products, arithmetic and copies ran while one was open for 2% of the time, Pallas kernels for 10%

profile of v7, /device:TPU:1, one launch (start us, length us, event | category | flops | bytes accessed | tf_op | source)
XLA Modules:
  0.0 298.6 jit_solution(15171368693643609477)
XLA Ops:
  7.2 1.8 pad_maximum_fusion
  9.0 0.2 copy.7
  9.3 35.1 %all_to_all.20 = f32[3,8,32,768]{3,2,0,1:T(8,128)S(1)} all-to-all(f32[3,8,32,768]{3,2,0,1:T(8,128)S(1)} %copy.7), channel_id=1, replica_groups=mesh['y'=4,'core'=2,'z'=4,'x'=4] {'y','core'}, dimensions={1} | all-to-all | bytes 4718592 | tf_op jit(solution)/shard_map/all_to_all | solution.py:297
  44.4 0.6 pick_rows.1
  45.0 0.6 copy-done.6
  45.6 0.8 collective-permute-start.8
  46.5 1.6 collective-permute-start
  48.1 2.1 collective-permute-start.1
  50.2 16.7 %all_to_all.21.x = f32[16,24,384]{2,1,0:T(8,128)S(1)} all-to-all(f32[16,24,384]{2,1,0:T(8,128)S(1)} %bitcast.59), channel_id=1, replica_groups=mesh['y'=4,'core'=2,'z'=4,'x'=4] {'z','x'}, dimensions={0} | all-to-all | bytes 1179648 | tf_op jit(solution)/shard_map/all_to_all | solution.py:373
  66.9 1.4 pick_cols.1
  68.3 1.1 collective-permute-start.9
  69.5 1.0 slice.13
  70.5 0.8 collective-permute-start.3
  71.3 1.0 slice.12
  72.3 0.8 collective-permute-start.2
  73.1 2.1 collective-permute-start.11
  75.1 1.2 pad_maximum_fusion.1.refs_0_
  76.3 0.2 collective-permute-done.3
  76.5 3.0 %collective-permute-done.2 = f32[192,384]{1,0:T(8,128)S(1)} collective-permute-done((f32[192,384]{1,0:T(8,128)S(1)}, f32[192,384]{1,0:T(8,128)S(1)}, u32[]{:S(2)}, u32[]{:S(2)}) %collective-permute-start.2) | collective-permute-done | bytes 294944 | tf_op jit(solution)/shard_map/ppermute | solution.py:57
  79.6 1.2 pad_maximum_fusion.2.refs_1_
  80.8 0.5 collective-permute-start.4
  81.4 2.2 collective-permute-start.7
  83.6 0.5 collective-permute-done.9
  84.1 1.9 collective-permute-start.10
  86.0 0.5 collective-permute-start.5
  86.5 1.0 copy-done.7
  87.5 2.2 collective-permute-start.6
  89.7 12.0 %collective-permute-done.4.refs_2_ = f32[2,384,384]{2,1,0:T(8,128)S(1)} collective-permute-done((f32[2,384,384]{2,1,0:T(8,128)S(1)}, f32[2,384,384]{2,1,0:T(8,128)S(1)}, u32[]{:S(2)}, u32[]{:S(2)}) %collective-permute-start.4) | collective-permute-done | bytes 1179680 | tf_op jit(solution)/shard_map/ppermute | solution.py:57
  101.7 3.1 %collective-permute-start.12 = (f32[768,384]{1,0:T(8,128)}, f32[768,384]{1,0:T(8,128)}, u32[]{:S(2)}, u32[]{:S(2)}) collective-permute-start(f32[768,384]{1,0:T(8,128)} %collective-permute-done.8), channel_id=1, source_target_pairs={{0,16},{16,0},{1,17},{17,1},{2,18},{18,2},{3,19},{19,3},{4,20},{20... | collective-permute-start | bytes 3538952 | tf_op jit(solution)/shard_map/ppermute | solution.py:40
  104.8 1.0 collective-permute-start.13
  105.8 1.0 collective-permute-start.14
  106.8 0.1 stack.132.at
  106.9 23.8 %collective-permute-done.5.refs_3_ = f32[2,384,384]{2,1,0:T(8,128)} collective-permute-done((f32[2,384,384]{2,1,0:T(8,128)S(1)}, f32[2,384,384]{2,1,0:T(8,128)}, u32[]{:S(2)}, u32[]{:S(2)}) %collective-permute-start.5) | collective-permute-done | bytes 1179680 | tf_op jit(solution)/shard_map/ppermute | solution.py:57
  130.7 0.8 collective-permute-done.6.refs_4_
  131.5 3.5 %collective-permute-start.16 = (f32[2,384,384]{2,1,0:T(8,128)}, f32[2,384,384]{2,1,0:T(8,128)S(1)}, u32[]{:S(2)}, u32[]{:S(2)}) collective-permute-start(f32[2,384,384]{2,1,0:T(8,128)} %copy-done.11), channel_id=1, source_target_pairs={{0,12},{1,13},{2,14},{3,15},{4,0},{5,1},{6,2},{7,3},{8,4},{9,5},{1... | collective-permute-start | bytes 3538952 | tf_op jit(solution)/shard_map/ppermute | solution.py:57
  135.0 1.3 copy-done.8
  136.3 1.3 copy-done.10
  137.6 1.3 copy-done.12
  138.8 13.2 %near_rows.1 = (f32[1,384,384]{2,1,0:T(8,128)S(1)}, f32[4,384,384]{2,1,0:T(8,128)}) custom-call(s32[24]{0:T(128)S(1)} %stack.132.at, f32[2,384,384]{2,1,0:T(8,128)S(1)} %pad_maximum_fusion.1.refs_0_, f32[2,384,384]{2,1,0:T(8,128)S(1)} %pad_maximum_fusion.2.refs_1_, f32[2,384,384]{2,1,0:T(8,128)S(1)} %copy-done.10, ...), custom_call_target="tpu_custom_call" | custom-call | flops 57076088832 | bytes 231211008 | tf_op jit(solution)/shard_map/near_rows/pallas_call | solution.py:125
  152.1 1.7 copy-done.1
  153.8 4.4 %update.1 = (f32[384,384]{1,0:T(8,128)}, f32[384,384]{1,0:T(8,128)S(1)}) custom-call(s32[24]{0:T(128)S(1)} %stack.132.at, f32[1,384,384]{2,1,0:T(8,128)S(1)} %get-tuple-element.28.acc, f32[2,384,384]{2,1,0:T(8,128)S(1)} %collective-permute-done.15.top, f32[2,384,384]{2,1,0:T(8,128)S(1)} %collective-permute-done.16.low, f32[4,384,384]{2,1,0:T(8,128)S(1)} %copy-done.1), custom_call_target="tpu_custom_call" | custom-call | flops 1358954496 | bytes 2359296 | tf_op jit(solution)/shard_map/update/pallas_call | solution.py:227
  158.3 6.4 %collective-permute-start.17 = (f32[384,384]{1,0:T(8,128)S(1)}, f32[384,384]{1,0:T(8,128)S(1)}, u32[]{:S(2)}, u32[]{:S(2)}) collective-permute-start(f32[384,384]{1,0:T(8,128)S(1)} %get-tuple-element.32), channel_id=1, source_target_pairs={{0,0},{1,1},{2,16},{3,17},{4,32},{5,33},{6,48},{7,49},{8,64},{9,65... | collective-permute-start | bytes 1769480 | tf_op jit(solution)/shard_map/ppermute | solution.py:381
  164.7 12.4 %collective-permute-done.17 = f32[384,384]{1,0:T(8,128)S(1)} collective-permute-done((f32[384,384]{1,0:T(8,128)S(1)}, f32[384,384]{1,0:T(8,128)S(1)}, u32[]{:S(2)}, u32[]{:S(2)}) %collective-permute-start.17) | collective-permute-done | bytes 589856 | tf_op jit(solution)/shard_map/ppermute | solution.py:381
  177.1 0.9 collective-permute-start.18
  178.0 3.9 %collective-permute-start.19 = (f32[384,384]{1,0:T(8,128)S(1)}, f32[384,384]{1,0:T(8,128)S(1)}, u32[]{:S(2)}, u32[]{:S(2)}) collective-permute-start(f32[384,384]{1,0:T(8,128)S(1)} %collective-permute-done.17), channel_id=1, source_target_pairs={{0,3},{1,0},{2,1},{3,2},{4,7},{5,4},{6,5},{7,6},{8,11},{9,8},{10,9... | collective-permute-start | bytes 1769480 | tf_op jit(solution)/shard_map/ppermute | solution.py:57
  181.9 15.3 %collective-permute-done.18 = f32[384,384]{1,0:T(8,128)S(1)} collective-permute-done((f32[384,384]{1,0:T(8,128)S(1)}, f32[384,384]{1,0:T(8,128)S(1)}, u32[]{:S(2)}, u32[]{:S(2)}) %collective-permute-start.18) | collective-permute-done | bytes 589856 | tf_op jit(solution)/shard_map/ppermute | solution.py:57
  197.2 2.3 collective-permute-start.20
  199.6 0.5 collective-permute-start.21
  200.1 4.3 %collective-permute-done.20 = f32[192,384]{1,0:T(8,128)S(1)} collective-permute-done((f32[192,384]{1,0:T(8,128)S(1)}, f32[192,384]{1,0:T(8,128)S(1)}, u32[]{:S(2)}, u32[]{:S(2)}) %collective-permute-start.20) | collective-permute-done | bytes 294944 | tf_op jit(solution)/shard_map/ppermute | solution.py:57
  204.5 1.1 collective-permute-done.21
  205.7 8.8 %all-gather.6.cloned.1.call-done = f32[3072,384]{1,0:T(8,128)} async-done(((f32[384,384]{1,0:T(8,128)}), f32[3072,384]{1,0:T(8,128)}) %all-gather.6.cloned.1.call-update) | async-done | bytes 4718608 | tf_op jit(solution)/shard_map/all_gather | solution.py:383
  214.5 2.3 copy-done.4
  216.9 2.3 copy-done.5
  219.2 5.8 %cross.1 = f32[384,384]{1,0:T(8,128)} custom-call(f32[384,3072]{1,0:T(8,128)S(1)} %copy-done.4, f32[8,12,32,384]{3,2,1,0:T(8,128)S(1)} %bitcast.63), custom_call_target="tpu_custom_call" | custom-call | flops 2717908992 | bytes 9437184 | tf_op jit(solution)/shard_map/cross/pallas_call | solution.py:282
  225.2 2.7 collective-permute-start.25
  227.8 2.7 collective-permute-start.24
  230.5 11.0 %collective-permute-done.22.refs_2_ = f32[2,384,384]{2,1,0:T(8,128)} collective-permute-done((f32[2,384,384]{2,1,0:T(8,128)S(1)}, f32[2,384,384]{2,1,0:T(8,128)}, u32[]{:S(2)}, u32[]{:S(2)}) %collective-permute-start.22) | collective-permute-done | bytes 1179680 | tf_op jit(solution)/shard_map/ppermute | solution.py:57
  241.5 2.7 collective-permute-start.27
  244.2 10.3 %collective-permute-done.23.refs_3_ = f32[2,384,384]{2,1,0:T(8,128)} collective-permute-done((f32[2,384,384]{2,1,0:T(8,128)S(1)}, f32[2,384,384]{2,1,0:T(8,128)}, u32[]{:S(2)}, u32[]{:S(2)}) %collective-permute-start.23) | collective-permute-done | bytes 1179680 | tf_op jit(solution)/shard_map/ppermute | solution.py:57
  254.4 18.4 %all-gather.8.cloned.1.call-done = f32[3072,384]{1,0:T(8,128)} async-done(((f32[384,384]{1,0:T(8,128)}), f32[3072,384]{1,0:T(8,128)}) %all-gather.8.cloned.1.call-update) | async-done | bytes 4718608 | tf_op jit(solution)/shard_map/all_gather | solution.py:386
  272.8 2.3 copy-done
  275.1 9.6 %near.1.acc = f32[2,384,384]{2,1,0:T(8,128)S(1)} custom-call(s32[24]{0:T(128)S(1)} %stack.132.at, f32[2,384,384]{2,1,0:T(8,128)S(1)} %pad_maximum_fusion.3.refs_0_, f32[2,384,384]{2,1,0:T(8,128)S(1)} %pad_maximum_fusion.4.refs_1_, f32[2,384,384]{2,1,0:T(8,128)} %collective-permute-done.22.refs_2_, f32[2,384,384]{2,1,0:T(8,128)} %collective-permute-done.23.refs_3_, ...), custom_call_target="tpu_custom_call" | custom-call | flops 48922361856 | bytes 141557760 | tf_op jit(solution)/shard_map/near/pallas_call | solution.py:177
  284.8 2.0 place_rows.1
  286.8 5.3 %child.1 = f32[768,384]{1,0:T(8,128)} custom-call(s32[24]{0:T(128)S(1)} %stack.132.at, f32[2,384,384]{2,1,0:T(8,128)S(1)} %near.1.acc, f32[2,384,384]{2,1,0:T(8,128)S(1)} %collective-permute-done.26.top, f32[2,384,384]{2,1,0:T(8,128)} %collective-permute-done.27.low, f32[8,384,384]{2,1,0:T(8,128)S(1)} %bitcast.57, f32[768,384]{1,0:T(8,128)S(1)} %copy-done.2), custom_call_target="tpu_custom_call" | custom-call | flops 1358954496 | bytes 3538944 | tf_op jit(solution)/shard_map/child/pallas_call | solution.py:249
  (50 shorter events, 0.6 us)
Async XLA Ops:
  7.2 151.0 %all-gather.4.cloned.1.call-start = ((), (), s32[]{:S(2)}) async-start(), calls=%async_computation.2 | async-start | bytes 5013504 | tf_op jit(solution)/shard_map/all_gather | solution.py:374
  9.2 35.1 %copy-start.3 = (s32[12]{0:T(128)S(1)}, s32[12]{0:T(128)}, u32[]{:S(2)}) copy-start(s32[12]{0:T(128)} %anc.5) | copy-start | bytes 148
  44.4 1.3 copy-start.6
  45.6 22.7 %collective-permute-start.8 = (f32[768,384]{1,0:T(8,128)S(1)}, f32[768,384]{1,0:T(8,128)}, u32[]{:S(2)}, u32[]{:S(2)}) collective-permute-start(f32[768,384]{1,0:T(8,128)S(1)} %copy-done.6), channel_id=1, source_target_pairs={{0,32},{16,112},{32,64},{48,16},{64,96},{80,48},{96,0},{112,80},{1... | collective-permute-start | bytes 3538952 | tf_op jit(solution)/shard_map/ppermute | solution.py:36
  46.5 21.8 %collective-permute-start = (f32[384,384]{1,0:T(8,128)S(1)}, f32[384,384]{1,0:T(8,128)}, u32[]{:S(2)}, u32[]{:S(2)}) collective-permute-start(f32[384,384]{1,0:T(8,128)S(1)} %bitcast.60), channel_id=1, source_target_pairs={{0,1},{1,2},{2,3},{3,0},{4,5},{5,6},{6,7},{7,4},{8,9},{9,10},{10,1... | collective-permute-start | bytes 1769480 | tf_op jit(solution)/shard_map/ppermute | solution.py:57
  48.1 20.2 %collective-permute-start.1 = (f32[384,384]{1,0:T(8,128)S(1)}, f32[384,384]{1,0:T(8,128)}, u32[]{:S(2)}, u32[]{:S(2)}) collective-permute-start(f32[384,384]{1,0:T(8,128)S(1)} %bitcast.61), channel_id=1, source_target_pairs={{0,3},{1,0},{2,1},{3,2},{4,7},{5,4},{6,5},{7,6},{8,11},{9,8},{10,9... | collective-permute-start | bytes 1769480 | tf_op jit(solution)/shard_map/ppermute | solution.py:57
  68.3 15.7 %collective-permute-start.9 = (f32[768,384]{1,0:T(8,128)}, f32[768,384]{1,0:T(8,128)}, u32[]{:S(2)}, u32[]{:S(2)}) collective-permute-start(f32[768,384]{1,0:T(8,128)} %collective-permute-done.8), channel_id=1, source_target_pairs={{0,32},{16,112},{32,64},{48,16},{64,96},{80,48},{96,0},{112,80},{1... | collective-permute-start | bytes 3538952 | tf_op jit(solution)/shard_map/ppermute | solution.py:36
  69.4 145.1 %all-gather.6.cloned.1.call-start = ((), (), s32[]{:S(2)}) async-start(), calls=%async_computation.3 | async-start | bytes 5308416 | tf_op jit(solution)/shard_map/all_gather | solution.py:383
  70.5 6.0 %collective-permute-start.3 = (f32[192,384]{1,0:T(8,128)S(1)}, f32[192,384]{1,0:T(8,128)S(1)}, u32[]{:S(2)}, u32[]{:S(2)}) collective-permute-start(f32[192,384]{1,0:T(8,128)S(1)} %slice.13), channel_id=1, source_target_pairs={{0,3},{1,0},{2,1},{3,2},{4,7},{5,4},{6,5},{7,6},{8,11},{9,8},{10,9... | collective-permute-start | bytes 884744 | tf_op jit(solution)/shard_map/ppermute | solution.py:57
  72.3 7.3 %collective-permute-start.2 = (f32[192,384]{1,0:T(8,128)S(1)}, f32[192,384]{1,0:T(8,128)S(1)}, u32[]{:S(2)}, u32[]{:S(2)}) collective-permute-start(f32[192,384]{1,0:T(8,128)S(1)} %slice.12), channel_id=1, source_target_pairs={{0,1},{1,2},{2,3},{3,0},{4,5},{5,6},{6,7},{7,4},{8,9},{9,10},{10,1... | collective-permute-start | bytes 884744 | tf_op jit(solution)/shard_map/ppermute | solution.py:57
  73.1 13.4 %collective-permute-start.11 = (f32[768,384]{1,0:T(8,128)S(1)}, f32[768,384]{1,0:T(8,128)S(1)}, u32[]{:S(2)}, u32[]{:S(2)}) collective-permute-start(f32[768,384]{1,0:T(8,128)S(1)} %copy-done.6), channel_id=1, source_target_pairs={{0,16},{16,0},{1,17},{17,1},{2,18},{18,2},{3,19},{19,3},{4,20},{20... | collective-permute-start | bytes 3538952 | tf_op jit(solution)/shard_map/ppermute | solution.py:40
  80.8 20.9 %collective-permute-start.4 = (f32[2,384,384]{2,1,0:T(8,128)S(1)}, f32[2,384,384]{2,1,0:T(8,128)S(1)}, u32[]{:S(2)}, u32[]{:S(2)}) collective-permute-start(f32[2,384,384]{2,1,0:T(8,128)S(1)} %pad_maximum_fusion.1.refs_0_), channel_id=1, source_target_pairs={{0,4},{1,5},{2,6},{3,7},{4,8},{5,9},{6,10},{7,11},{8,12},{9,13},{1... | collective-permute-start | bytes 3538952 | tf_op jit(solution)/shard_map/ppermute | solution.py:57
  81.4 23.4 %collective-permute-start.7 = (f32[2,384,384]{2,1,0:T(8,128)S(1)}, f32[2,384,384]{2,1,0:T(8,128)S(1)}, u32[]{:S(2)}, u32[]{:S(2)}) collective-permute-start(f32[2,384,384]{2,1,0:T(8,128)S(1)} %pad_maximum_fusion.2.refs_1_), channel_id=1, source_target_pairs={{0,12},{1,13},{2,14},{3,15},{4,0},{5,1},{6,2},{7,3},{8,4},{9,5},{1... | collective-permute-start | bytes 3538952 | tf_op jit(solution)/shard_map/ppermute | solution.py:57
  84.1 21.7 %collective-permute-start.10 = (f32[768,384]{1,0:T(8,128)}, f32[768,384]{1,0:T(8,128)}, u32[]{:S(2)}, u32[]{:S(2)}) collective-permute-start(f32[768,384]{1,0:T(8,128)} %collective-permute-done.9), channel_id=1, source_target_pairs={{0,32},{16,112},{32,64},{48,16},{64,96},{80,48},{96,0},{112,80},{1... | collective-permute-start | bytes 3538952 | tf_op jit(solution)/shard_map/ppermute | solution.py:36
  86.0 44.7 %collective-permute-start.5 = (f32[2,384,384]{2,1,0:T(8,128)S(1)}, f32[2,384,384]{2,1,0:T(8,128)}, u32[]{:S(2)}, u32[]{:S(2)}) collective-permute-start(f32[2,384,384]{2,1,0:T(8,128)S(1)} %pad_maximum_fusion.2.refs_1_), channel_id=1, source_target_pairs={{0,4},{1,5},{2,6},{3,7},{4,8},{5,9},{6,10},{7,11},{8,12},{9,13},{1... | collective-permute-start | bytes 3538952 | tf_op jit(solution)/shard_map/ppermute | solution.py:57
  86.5 1.0 copy-start.7
  87.5 44.0 %collective-permute-start.6 = (f32[2,384,384]{2,1,0:T(8,128)S(1)}, f32[2,384,384]{2,1,0:T(8,128)}, u32[]{:S(2)}, u32[]{:S(2)}) collective-permute-start(f32[2,384,384]{2,1,0:T(8,128)S(1)} %pad_maximum_fusion.1.refs_0_), channel_id=1, source_target_pairs={{0,12},{1,13},{2,14},{3,15},{4,0},{5,1},{6,2},{7,3},{8,4},{9,5},{1... | collective-permute-start | bytes 3538952 | tf_op jit(solution)/shard_map/ppermute | solution.py:57
  101.7 3.1 %copy-start.9 = (f32[2,384,384]{2,1,0:T(8,128)}, f32[2,384,384]{2,1,0:T(8,128)S(1)}, u32[]{:S(2)}) copy-start(f32[2,384,384]{2,1,0:T(8,128)S(1)} %collective-permute-done.4.refs_2_) | copy-start | bytes 3538948
  101.7 33.3 %collective-permute-start.12 = (f32[768,384]{1,0:T(8,128)}, f32[768,384]{1,0:T(8,128)}, u32[]{:S(2)}, u32[]{:S(2)}) collective-permute-start(f32[768,384]{1,0:T(8,128)} %collective-permute-done.8), channel_id=1, source_target_pairs={{0,16},{16,0},{1,17},{17,1},{2,18},{18,2},{3,19},{19,3},{4,20},{20... | collective-permute-start | bytes 3538952 | tf_op jit(solution)/shard_map/ppermute | solution.py:40
  104.8 1.0 copy-start.11
  104.8 30.2 %collective-permute-start.13 = (f32[768,384]{1,0:T(8,128)}, f32[768,384]{1,0:T(8,128)}, u32[]{:S(2)}, u32[]{:S(2)}) collective-permute-start(f32[768,384]{1,0:T(8,128)} %collective-permute-done.9), channel_id=1, source_target_pairs={{0,16},{16,0},{1,17},{17,1},{2,18},{18,2},{3,19},{19,3},{4,20},{20... | collective-permute-start | bytes 3538952 | tf_op jit(solution)/shard_map/ppermute | solution.py:40
  105.8 29.2 %collective-permute-start.14 = (f32[768,384]{1,0:T(8,128)}, f32[768,384]{1,0:T(8,128)}, u32[]{:S(2)}, u32[]{:S(2)}) collective-permute-start(f32[768,384]{1,0:T(8,128)} %collective-permute-done.10), channel_id=1, source_target_pairs={{0,16},{16,0},{1,17},{17,1},{2,18},{18,2},{3,19},{19,3},{4,20},{20... | collective-permute-start | bytes 3538952 | tf_op jit(solution)/shard_map/ppermute | solution.py:40
  130.7 21.4 %collective-permute-start.15 = (f32[2,384,384]{2,1,0:T(8,128)}, f32[2,384,384]{2,1,0:T(8,128)S(1)}, u32[]{:S(2)}, u32[]{:S(2)}) collective-permute-start(f32[2,384,384]{2,1,0:T(8,128)} %copy-done.9), channel_id=1, source_target_pairs={{0,4},{1,5},{2,6},{3,7},{4,8},{5,9},{6,10},{7,11},{8,12},{9,13},{1... | collective-permute-start | bytes 3538952 | tf_op jit(solution)/shard_map/ppermute | solution.py:57
  131.5 20.6 %collective-permute-start.16 = (f32[2,384,384]{2,1,0:T(8,128)}, f32[2,384,384]{2,1,0:T(8,128)S(1)}, u32[]{:S(2)}, u32[]{:S(2)}) collective-permute-start(f32[2,384,384]{2,1,0:T(8,128)} %copy-done.11), channel_id=1, source_target_pairs={{0,12},{1,13},{2,14},{3,15},{4,0},{5,1},{6,2},{7,3},{8,4},{9,5},{1... | collective-permute-start | bytes 3538952 | tf_op jit(solution)/shard_map/ppermute | solution.py:57
  135.0 1.3 copy-start.8
  136.3 1.3 copy-start.10
  137.6 1.3 copy-start.12
  152.1 1.7 copy-start.1
  158.2 114.6 %all-gather.8.cloned.1.call-start = ((), (), s32[]{:S(2)}) async-start(), calls=%async_computation.4 | async-start | bytes 5308416 | tf_op jit(solution)/shard_map/all_gather | solution.py:386
  158.3 18.8 %collective-permute-start.17 = (f32[384,384]{1,0:T(8,128)S(1)}, f32[384,384]{1,0:T(8,128)S(1)}, u32[]{:S(2)}, u32[]{:S(2)}) collective-permute-start(f32[384,384]{1,0:T(8,128)S(1)} %get-tuple-element.32), channel_id=1, source_target_pairs={{0,0},{1,1},{2,16},{3,17},{4,32},{5,33},{6,48},{7,49},{8,64},{9,65... | collective-permute-start | bytes 1769480 | tf_op jit(solution)/shard_map/ppermute | solution.py:381
  177.1 20.1 %collective-permute-start.18 = (f32[384,384]{1,0:T(8,128)S(1)}, f32[384,384]{1,0:T(8,128)S(1)}, u32[]{:S(2)}, u32[]{:S(2)}) collective-permute-start(f32[384,384]{1,0:T(8,128)S(1)} %collective-permute-done.17), channel_id=1, source_target_pairs={{0,1},{1,2},{2,3},{3,0},{4,5},{5,6},{6,7},{7,4},{8,9},{9,10},{10,1... | collective-permute-start | bytes 1769480 | tf_op jit(solution)/shard_map/ppermute | solution.py:57
  178.0 19.2 %collective-permute-start.19 = (f32[384,384]{1,0:T(8,128)S(1)}, f32[384,384]{1,0:T(8,128)S(1)}, u32[]{:S(2)}, u32[]{:S(2)}) collective-permute-start(f32[384,384]{1,0:T(8,128)S(1)} %collective-permute-done.17), channel_id=1, source_target_pairs={{0,3},{1,0},{2,1},{3,2},{4,7},{5,4},{6,5},{7,6},{8,11},{9,8},{10,9... | collective-permute-start | bytes 1769480 | tf_op jit(solution)/shard_map/ppermute | solution.py:57
  197.2 7.3 %collective-permute-start.20 = (f32[192,384]{1,0:T(8,128)S(1)}, f32[192,384]{1,0:T(8,128)S(1)}, u32[]{:S(2)}, u32[]{:S(2)}) collective-permute-start(f32[192,384]{1,0:T(8,128)S(1)} %slice.14), channel_id=1, source_target_pairs={{0,1},{1,2},{2,3},{3,0},{4,5},{5,6},{6,7},{7,4},{8,9},{9,10},{10,1... | collective-permute-start | bytes 884744 | tf_op jit(solution)/shard_map/ppermute | solution.py:57
  199.6 6.0 %collective-permute-start.21 = (f32[192,384]{1,0:T(8,128)S(1)}, f32[192,384]{1,0:T(8,128)S(1)}, u32[]{:S(2)}, u32[]{:S(2)}) collective-permute-start(f32[192,384]{1,0:T(8,128)S(1)} %slice.15), channel_id=1, source_target_pairs={{0,3},{1,0},{2,1},{3,2},{4,7},{5,4},{6,5},{7,6},{8,11},{9,8},{10,9... | collective-permute-start | bytes 884744 | tf_op jit(solution)/shard_map/ppermute | solution.py:57
  214.5 2.3 copy-start.4
  216.8 2.3 copy-start.5
  225.1 16.4 %collective-permute-start.22 = (f32[2,384,384]{2,1,0:T(8,128)S(1)}, f32[2,384,384]{2,1,0:T(8,128)}, u32[]{:S(2)}, u32[]{:S(2)}) collective-permute-start(f32[2,384,384]{2,1,0:T(8,128)S(1)} %pad_maximum_fusion.3.refs_0_), channel_id=1, source_target_pairs={{0,4},{1,5},{2,6},{3,7},{4,8},{5,9},{6,10},{7,11},{8,12},{9,13},{1... | collective-permute-start | bytes 3538952 | tf_op jit(solution)/shard_map/ppermute | solution.py:57
  225.2 16.4 %collective-permute-start.25 = (f32[2,384,384]{2,1,0:T(8,128)S(1)}, f32[2,384,384]{2,1,0:T(8,128)}, u32[]{:S(2)}, u32[]{:S(2)}) collective-permute-start(f32[2,384,384]{2,1,0:T(8,128)S(1)} %pad_maximum_fusion.4.refs_1_), channel_id=1, source_target_pairs={{0,12},{1,13},{2,14},{3,15},{4,0},{5,1},{6,2},{7,3},{8,4},{9,5},{1... | collective-permute-start | bytes 3538952 | tf_op jit(solution)/shard_map/ppermute | solution.py:57
  227.8 26.6 %collective-permute-start.23 = (f32[2,384,384]{2,1,0:T(8,128)S(1)}, f32[2,384,384]{2,1,0:T(8,128)}, u32[]{:S(2)}, u32[]{:S(2)}) collective-permute-start(f32[2,384,384]{2,1,0:T(8,128)S(1)} %pad_maximum_fusion.4.refs_1_), channel_id=1, source_target_pairs={{0,4},{1,5},{2,6},{3,7},{4,8},{5,9},{6,10},{7,11},{8,12},{9,13},{1... | collective-permute-start | bytes 3538952 | tf_op jit(solution)/shard_map/ppermute | solution.py:57
  227.8 26.6 %collective-permute-start.24 = (f32[2,384,384]{2,1,0:T(8,128)S(1)}, f32[2,384,384]{2,1,0:T(8,128)}, u32[]{:S(2)}, u32[]{:S(2)}) collective-permute-start(f32[2,384,384]{2,1,0:T(8,128)S(1)} %pad_maximum_fusion.3.refs_0_), channel_id=1, source_target_pairs={{0,12},{1,13},{2,14},{3,15},{4,0},{5,1},{6,2},{7,3},{8,4},{9,5},{1... | collective-permute-start | bytes 3538952 | tf_op jit(solution)/shard_map/ppermute | solution.py:57
  241.5 45.3 %collective-permute-start.26 = (f32[2,384,384]{2,1,0:T(8,128)}, f32[2,384,384]{2,1,0:T(8,128)S(1)}, u32[]{:S(2)}, u32[]{:S(2)}) collective-permute-start(f32[2,384,384]{2,1,0:T(8,128)} %collective-permute-done.22.refs_2_), channel_id=1, source_target_pairs={{0,4},{1,5},{2,6},{3,7},{4,8},{5,9},{6,10},{7,11},{8,12},{9,13},{1... | collective-permute-start | bytes 3538952 | tf_op jit(solution)/shard_map/ppermute | solution.py:57
  241.5 45.3 %collective-permute-start.27 = (f32[2,384,384]{2,1,0:T(8,128)}, f32[2,384,384]{2,1,0:T(8,128)}, u32[]{:S(2)}, u32[]{:S(2)}) collective-permute-start(f32[2,384,384]{2,1,0:T(8,128)} %collective-permute-done.25.refs_5_), channel_id=1, source_target_pairs={{0,12},{1,13},{2,14},{3,15},{4,0},{5,1},{6,2},{7,3},{8,4},{9,5},{1... | collective-permute-start | bytes 3538952 | tf_op jit(solution)/shard_map/ppermute | solution.py:57
  272.8 2.3 copy-start
  284.8 2.0 copy-start.2
Sparse Core Ops, SparseCore 0:
  69.6 65.5 all-gather.3
  158.4 56.1 all-gather.5
  225.2 47.5 all-gather.7

commit v8 on v6

--- a/solution.py
+++ b/solution.py
@@ -10,7 +10,7 @@
 
 NB = 24
 NANC = 12
-W1, W2 = 12, 12
+W1, W2 = 18, 12
 ROW = ("y", "core")
 COL = ("z", "x")
 ALL = ("y", "core", "z", "x")
@@ -57,14 +57,15 @@
     return lax.ppermute(x, ("core",) + COL, pairs)
 
 
-def gather_cols(x, axis, gates=((), (), ())):
-    half = x.shape[axis] // 2
+def gather_cols(x):
+    half = x.shape[0] // 2
     up, down = hop(x, 0, 1), hop(x, 0, -1)
-    top = hop(lax.slice_in_dim(after(up, *gates[0]), 0, half, axis=axis), 0, 1)
-    low = hop(lax.slice_in_dim(after(down, *gates[0]), half, 2 * half, axis=axis), 0, -1)
-    group = after(jnp.stack([x, up, down, jnp.concatenate([top, low], axis=axis)]), *gates[1])
-    up, down = hop(group, 1, 1), hop(group, 1, -1)
-    return (group, up, down), (hop(after(up, *gates[2])[:2], 1, 1), hop(after(down, *gates[2])[2:], 1, -1))
+    top, low = hop(up[:half], 0, 1), hop(down[half:], 0, -1)
+    one, two = jnp.stack([x, up]), jnp.stack([down, jnp.concatenate([top, low])])
+    one, two = lax.optimization_barrier((one, two))
+    up_one, down_two = hop(one, 1, 1), hop(two, 1, -1)
+    up_two, down_one = hop(two, 1, 1), hop(one, 1, -1)
+    return (one, two, up_one, up_two, down_one, down_two), (hop(up_one, 1, 1), hop(down_two, 1, -1))
 
 
 def places():
@@ -90,19 +91,19 @@
 
 
 def near_kernel(per, at, *refs):
-    groups, tiles, acc, (a_buf, b_buf, a_sem, b_sem) = refs[:3], refs[3], refs[4], refs[5:]
+    pairs, tiles, acc, (a_buf, b_buf, a_sem, b_sem) = refs[:6], refs[6], refs[7], refs[8:]
     outs = acc.shape[0]
 
-    def group_copy(g, source):
-        return pltpu.make_async_copy(source, a_buf.at[pl.ds(4 * g, 4)], a_sem.at[g])
+    def pair_copy(i, source):
+        return pltpu.make_async_copy(source, a_buf.at[pl.ds(2 * i, 2)], a_sem.at[i])
 
     def tile_copy(k):
         return pltpu.make_async_copy(tiles.at[lax.div(at[8 + k], per)], b_buf.at[k], b_sem.at[k])
 
-    for g in range(3):
-        group_copy(g, groups[g]).start()
-        for k in (0, 3, 1, 2):
-            tile_copy(4 * g + k).start()
+    for i in range(6):
+        pair_copy(i, pairs[i]).start()
+        tile_copy(2 * i).start()
+        tile_copy(2 * i + 1).start()
     acc[...] = jnp.zeros_like(acc)
 
     def body(i, carry):
@@ -110,7 +111,8 @@
 
         @pl.when(q == 0)
         def _():
-            group_copy(g, groups[0]).wait()
+            for k in range(2):
+                pair_copy(2 * g + k, pairs[0]).wait()
 
         k0, k1 = 4 * g + q, 4 * g + 3 - q
         tile_copy(k0).wait()
@@ -123,24 +125,24 @@
     lax.fori_loop(0, 6, body, 0)
 
 
-def near_product(at, groups, tiles, outs, weight):
-    m, w = groups[0].shape[1:]
+def near_product(at, pairs, tiles, outs, weight):
+    m, w = pairs[0].shape[1:]
     many, _, n = tiles.shape
     return pl.pallas_call(
         functools.partial(near_kernel, 16 // many),
         out_shape=jax.ShapeDtypeStruct((outs, m, n), F32),
-        in_specs=[SMEM] + [ANY] * 4,
+        in_specs=[SMEM] + [ANY] * 7,
         out_specs=VMEM,
         scratch_shapes=[
             pltpu.VMEM((12, m, w), F32),
             pltpu.VMEM((12,) + tiles.shape[1:], F32),
-            pltpu.SemaphoreType.DMA((3,)),
+            pltpu.SemaphoreType.DMA((6,)),
             pltpu.SemaphoreType.DMA((12,)),
         ],
         compiler_params=params(40),
         cost_estimate=cost(weight * m, 12 * w, n, weight * 4 * w * (12 * m + many * n)),
         name="near",
-    )(at, *groups, tiles)
+    )(at, *pairs, tiles)
 
 
 def far_sum(at, top, low, tiles, a_buf, b_buf, sem, per):
@@ -210,22 +212,23 @@
 
 
 def cross_kernel(at, s, *refs):
-    tiles, (sigma, u_buf, u_sem) = refs[:8], refs[8:]
+    tiles, (sigma, s_buf, u_buf, s_sem, u_sem) = refs[:8], refs[8:]
+    m, w = sigma.shape
+
+    def s_copy(k):
+        return pltpu.make_async_copy(s.at[:, pl.ds(768 * k, 768)], s_buf.at[k], s_sem.at[k])
+
     copies = [pltpu.make_async_copy(tiles[i], u_buf.at[:, at[i]], u_sem.at[i]) for i in range(8)]
     for copy in copies:
         copy.start()
+    for k in range(4):
+        s_copy(k).start()
     sigma[...] = jnp.zeros_like(sigma)
     for copy in copies:
         copy.wait()
-    w = sigma.shape[1]
-
-    def body(k, carry):
-        lhs = s[:, pl.ds(pl.multiple_of(k * 768, 128), 768)]
-        rhs = u_buf[pl.ds(3 * k, 3)].reshape(768, w)
-        sigma[...] -= dot3(lhs, rhs)
-        return carry
-
-    lax.fori_loop(0, 4, body, 0)
+    for k in range(4):
+        s_copy(k).wait()
+        sigma[...] -= dot3(s_buf[k], u_buf[pl.ds(3 * k, 3)].reshape(768, w))
 
 
 def cross_product(at, s, tiles):
@@ -234,9 +237,14 @@
     return pl.pallas_call(
         cross_kernel,
         out_shape=jax.ShapeDtypeStruct((m, w), F32),
-        in_specs=[SMEM, VMEM] + [ANY] * 8,
-        out_specs=VMEM,
-        scratch_shapes=[pltpu.VMEM((NANC, 8, sub, w), F32), pltpu.SemaphoreType.DMA((8,))],
+        in_specs=[SMEM] + [ANY] * 9,
+        out_specs=VMEM,
+        scratch_shapes=[
+            pltpu.VMEM((4, m, 768), F32),
+            pltpu.VMEM((NANC, 8, sub, w), F32),
+            pltpu.SemaphoreType.DMA((4,)),
+            pltpu.SemaphoreType.DMA((8,)),
+        ],
         compiler_params=params(40),
         cost_estimate=cost(m, width, w, 4 * width * (m + w)),
         name="cross",
@@ -317,8 +325,8 @@
     at = places()
 
     f = pick_rows(ancestors, spread(factor_cross))
-    inverse = lax.all_gather(after(factor_inverse, f), ROW, axis=0, tiled=True).reshape(16, w, w)
-    f_near, f_far = gather_cols(f, 0)
+    inverse = lax.all_gather(factor_inverse, ROW, axis=0, tiled=True).reshape(16, w, w)
+    f_near, f_far = gather_cols(f)
 
     s = pick_rows(ancestors, spread(after(sigma_top, f)))
     s = lax.all_to_all(after(s, f_near[0]).reshape(16, -1, w), COL, 0, 0, tiled=True)
@@ -328,11 +336,11 @@
     u, ut = update_product(at, acc, *f_far, inverse)
 
     moved = lax.ppermute(ut, ALL, [(16 * r + c, 16 * (c // 2) + 2 * r + c % 2) for r in range(8) for c in range(16)])
-    u_near, u_far = gather_cols(moved, 0)
+    u_near, u_far = gather_cols(moved)
     u_tiles = gather_rows(u.reshape(NANC, sub, w))
 
     sigma = cross_product(at, after(s_all, u_near[0]), u_tiles)
-    sigma_all = lax.all_gather(sigma, ROW, axis=0, tiled=True).reshape(8, w, w)
+    sigma_all = lax.all_gather(after(sigma, u_near[2]), ROW, axis=0, tiled=True).reshape(8, w, w)
     acc = near_product(at, u_near, sigma_all, 2, W2)
     sigma_child = child_product(at, acc, *u_far, sigma_all, block_inverse)
 

time: 268 us -> 268 us (level); the launches traced: 262 us -> 267 us
  waiting for transfers between devices: 84.4 us -> 112 us
  blocking collectives: 46.3 us -> 26 us
  local copies, waits for them, and re-layouts: 17.4 us -> 8.06 us
  starting transfers between devices: 58 us -> 61.9 us
    ppermute x3, waiting for transfers between devices: 24.9 us -> 0.01 us  [step(): lax.ppermute(x, ROW, [(2 * i + c, 2 * ((i + 1 - 2 * c) % 4) + c) for i in...]
    all_to_all x1 -> x0, blocking collectives: 23.8 us -> none  [per_device(): lax.all_to_all(after(s, f_near[0]).reshape(16, -1, w), COL, 0, 0, tiled=T...]
    ppermute x1, waiting for transfers between devices: 0.01 us -> 18.8 us  [per_device(): lax.ppermute(ut, ALL, [(16 * r + c, 16 * (c // 2) + 2 * r + c % 2) for r...]
    ppermute x4, starting transfers between devices: 23.5 us -> 7.69 us  [swap(): return lax.ppermute(x, 'core', [(0, 1), (1, 0)])]
    ppermute x16 -> x20, waiting for transfers between devices: 45 us -> 56.7 us  [hop(): return lax.ppermute(x, ('core',) + COL, pairs)]
    all_to_all x0 -> x1, waiting for transfers between devices: none -> 10.9 us  [per_device(): lax.all_to_all(after(s, f_near[0]).reshape(16, -1, w), COL, 0, 0, tiled=T...]
    all_to_all x0 -> x1, starting transfers between devices: none -> 7.55 us  [per_device(): lax.all_to_all(after(s, f_near[0]).reshape(16, -1, w), COL, 0, 0, tiled=T...]
    ppermute x3, starting transfers between devices: 0.59 us -> 7.43 us  [step(): lax.ppermute(x, ROW, [(2 * i + c, 2 * ((i + 1 - 2 * c) % 4) + c) for i in...]
  transfers between devices with their start and end apart: 28 -> 33, of which waited for: 11 -> 13; matrix products, arithmetic and copies ran while one was open for 4% -> 2% of each run, Pallas kernels for 10% -> 14%
where the time goes in v8:
time: 268 us; the launch traced here: 267 us
  waiting for transfers between devices  112 us (42%)
  starting transfers between devices  61.9 us (23%)
  Pallas kernels  42.1 us (16%)
  blocking collectives  26 us (10%)
  between operations  14.1 us (5%)
  local copies, waits for them, and re-layouts  8.06 us (3%)
  other arithmetic  3.56 us (1%)
    ppermute x20, waiting for transfers between devices, hop(): return lax.ppermute(x, ('core',) + COL, pairs)  56.7 us
    ppermute x20, starting transfers between devices, hop(): return lax.ppermute(x, ('core',) + COL, pairs)  30 us
    all_to_all x1, blocking collectives, spread(): lax.all_to_all(x.reshape(3, 8, sub, w), ROW, 1, 0, tiled=True)  26 us
    pallas_call x2, Pallas kernels, near_product(): pl.pallas_call(functools.partial(near_kernel, 16 // many), out_shape=jax....  19.9 us
    ppermute x1, waiting for transfers between devices, per_device(): lax.ppermute(ut, ALL, [(16 * r + c, 16 * (c // 2) + 2 * r + c % 2) for r...  18.8 us
    all_to_all x1, waiting for transfers between devices, spread(): lax.all_to_all(x.reshape(3, 8, sub, w), ROW, 1, 0, tiled=True)  17.4 us
    all_to_all x1, waiting for transfers between devices, per_device(): lax.all_to_all(after(s, f_near[0]).reshape(16, -1, w), COL, 0, 0, tiled=T...  10.9 us
    pallas_call x1, Pallas kernels, cross_product(): pl.pallas_call(cross_kernel, out_shape=jax.ShapeDtypeStruct((m, w), F32),...  7.87 us
  transfers between devices with their start and end apart: 33, of which 13 were waited for; matrix products, arithmetic and copies ran while one was open for 2% of the time, Pallas kernels for 14%

profile of v8, /device:TPU:1, one launch (start us, length us, event | category | flops | bytes accessed | tf_op | source)
XLA Modules:
  0.0 267.3 jit_solution(14330456810218257005)
XLA Ops:
  7.2 0.7 all-gather.6.cloned.1.call-update
  7.9 0.5 copy-done.5
  8.4 0.1 copy.7
  8.5 26.0 %all_to_all.35 = f32[3,8,32,384]{3,2,0,1:T(8,128)S(1)} all-to-all(f32[3,8,32,384]{3,2,0,1:T(8,128)S(1)} %copy.7), channel_id=1, replica_groups=mesh['y'=4,'core'=2,'z'=4,'x'=4] {'y','core'}, dimensions={1} | all-to-all | bytes 2359296 | tf_op jit(solution)/shard_map/all_to_all | solution.py:257
  34.6 0.6 pick_rows.2
  35.2 2.1 collective-permute-start
  37.2 2.8 %collective-permute-start.1 = (f32[384,384]{1,0:T(8,128)S(1)}, f32[384,384]{1,0:T(8,128)S(1)}, u32[]{:S(2)}, u32[]{:S(2)}) collective-permute-start(f32[384,384]{1,0:T(8,128)S(1)} %bitcast.65), channel_id=1, source_target_pairs={{0,3},{1,0},{2,1},{3,2},{4,7},{5,4},{6,5},{7,6},{8,11},{9,8},{10,9... | collective-permute-start | bytes 1769480 | tf_op jit(solution)/shard_map/ppermute | solution.py:57
  40.1 7.6 %collective-permute-done = f32[384,384]{1,0:T(8,128)S(1)} collective-permute-done((f32[384,384]{1,0:T(8,128)S(1)}, f32[384,384]{1,0:T(8,128)S(1)}, u32[]{:S(2)}, u32[]{:S(2)}) %collective-permute-start) | collective-permute-done | bytes 589856 | tf_op jit(solution)/shard_map/ppermute | solution.py:57
  47.7 0.8 slice.16
  48.4 0.7 slice.17
  49.2 2.7 %collective-permute-start.3 = (f32[192,384]{1,0:T(8,128)}, f32[192,384]{1,0:T(8,128)}, u32[]{:S(2)}, u32[]{:S(2)}) collective-permute-start(f32[192,384]{1,0:T(8,128)} %slice.17), channel_id=1, source_target_pairs={{0,3},{1,0},{2,1},{3,2},{4,7},{5,4},{6,5},{7,6},{8,11},{9,8},{10,9... | collective-permute-start | bytes 884744 | tf_op jit(solution)/shard_map/ppermute | solution.py:57
  51.9 1.1 copy.8
  53.0 3.9 %all-to-all-start.1 = ((f32[3,8,32,384]{3,2,0,1:T(8,128)}), f32[3,8,32,384]{3,2,0,1:T(8,128)S(1)}, u32[]{:S(2)}, u32[]{:S(2)}) async-start(f32[3,8,32,384]{3,2,0,1:T(8,128)} %copy.8), calls=%async_computation.1 | async-start | bytes 2359296 | tf_op jit(solution)/shard_map/all_to_all | solution.py:257
  56.8 1.2 pad_maximum_fusion.refs_0_
  58.0 1.1 maximum_bitcast_fusion
  59.1 1.1 pad_maximum_fusion.1.refs_1_
  60.2 0.9 collective-permute-start.4
  61.1 1.8 collective-permute-start.7
  62.9 1.1 collective-permute-start.6
  64.0 0.4 collective-permute-start.5
  64.4 17.4 %all-to-all-done.1 = f32[3,8,32,384]{3,2,0,1:T(8,128)S(1)} async-done(((f32[3,8,32,384]{3,2,0,1:T(8,128)}), f32[3,8,32,384]{3,2,0,1:T(8,128)S(1)}, u32[]{:S(2)}, u32[]{:S(2)}) %all-to-all-start.1) | async-done | bytes 1179680 | tf_op jit(solution)/shard_map/all_to_all | solution.py:257
  81.8 1.4 pick_rows.3
  83.2 7.6 %all-to-all-start.2 = ((f32[16,24,384]{2,1,0:T(8,128)}), f32[16,24,384]{2,1,0:T(8,128)S(1)}, u32[]{:S(2)}, u32[]{:S(2)}) async-start(f32[16,24,384]{2,1,0:T(8,128)} %bitcast.39), calls=%async_computation.2 | async-start | bytes 1179648 | tf_op jit(solution)/shard_map/all_to_all | solution.py:332
  90.8 0.0 all-gather.4.cloned.1.call-start
  90.9 0.1 stack.132.at
  91.0 10.9 %all-to-all-done.2.x = f32[16,24,384]{2,1,0:T(8,128)S(1)} async-done(((f32[16,24,384]{2,1,0:T(8,128)}), f32[16,24,384]{2,1,0:T(8,128)S(1)}, u32[]{:S(2)}, u32[]{:S(2)}) %all-to-all-start.2) | async-done | bytes 589856 | tf_op jit(solution)/shard_map/all_to_all | solution.py:332
  101.9 1.4 pick_cols.1
  103.3 0.0 all-gather.8.cloned.1.call-start
  103.4 0.4 collective-permute-start.8
  103.8 2.4 collective-permute-start.9
  106.2 10.5 %near.2.acc = f32[1,384,384]{2,1,0:T(8,128)S(1)} custom-call(s32[24]{0:T(128)S(1)} %stack.132.at, f32[2,384,384]{2,1,0:T(8,128)S(1)} %pad_maximum_fusion.refs_0_, f32[2,384,384]{2,1,0:T(8,128)} %pad_maximum_fusion.1.refs_1_, f32[2,384,384]{2,1,0:T(8,128)} %collective-permute-done.4.refs_2_, f32[2,384,384]{2,1,0:T(8,128)} %collective-permute-done.5.refs_3_, ...), custom_call_target="tpu_custom_call" | custom-call | flops 73383542784 | bytes 297271296 | tf_op jit(solution)/shard_map/near/pallas_call | solution.py:131
  116.7 8.0 %collective-permute-done.8.top = f32[2,384,384]{2,1,0:T(8,128)S(1)} collective-permute-done((f32[2,384,384]{2,1,0:T(8,128)}, f32[2,384,384]{2,1,0:T(8,128)S(1)}, u32[]{:S(2)}, u32[]{:S(2)}) %collective-permute-start.8) | collective-permute-done | bytes 1179680 | tf_op jit(solution)/shard_map/ppermute | solution.py:57
  124.7 3.7 %update.1 = (f32[384,384]{1,0:T(8,128)S(1)}, f32[384,384]{1,0:T(8,128)S(1)}) custom-call(s32[24]{0:T(128)S(1)} %stack.132.at, f32[1,384,384]{2,1,0:T(8,128)S(1)} %near.2.acc, f32[2,384,384]{2,1,0:T(8,128)S(1)} %collective-permute-done.8.top, f32[2,384,384]{2,1,0:T(8,128)S(1)} %collective-permute-done.9.low, f32[16,384,384]{2,1,0:T(8,128)S(1)} %bitcast.61), custom_call_target="tpu_custom_call" | custom-call | flops 1358954496 | bytes 2359296 | tf_op jit(solution)/shard_map/update/pallas_call | solution.py:180
  128.5 5.3 %collective-permute-start.10 = (f32[384,384]{1,0:T(8,128)S(1)}, f32[384,384]{1,0:T(8,128)S(1)}, u32[]{:S(2)}, u32[]{:S(2)}) collective-permute-start(f32[384,384]{1,0:T(8,128)S(1)} %get-tuple-element.16), channel_id=1, source_target_pairs={{0,0},{1,1},{2,16},{3,17},{4,32},{5,33},{6,48},{7,49},{8,64},{9,65... | collective-permute-start | bytes 1769480 | tf_op jit(solution)/shard_map/ppermute | solution.py:338
  133.8 5.3 %collective-permute-start.15 = (f32[12,32,384]{2,1,0:T(8,128)S(1)}, f32[12,32,384]{2,1,0:T(8,128)S(1)}, u32[]{:S(2)}, u32[]{:S(2)}) collective-permute-start(f32[12,32,384]{2,1,0:T(8,128)S(1)} %bitcast.67), channel_id=1, source_target_pairs={{0,32},{16,112},{32,64},{48,16},{64,96},{80,48},{96,0},{112,80},{1... | collective-permute-start | bytes 1769480 | tf_op jit(solution)/shard_map/ppermute | solution.py:36
  139.1 18.8 %collective-permute-done.10 = f32[384,384]{1,0:T(8,128)S(1)} collective-permute-done((f32[384,384]{1,0:T(8,128)S(1)}, f32[384,384]{1,0:T(8,128)S(1)}, u32[]{:S(2)}, u32[]{:S(2)}) %collective-permute-start.10) | collective-permute-done | bytes 589856 | tf_op jit(solution)/shard_map/ppermute | solution.py:338
  157.9 2.7 %collective-permute-start.12 = (f32[384,384]{1,0:T(8,128)S(1)}, f32[384,384]{1,0:T(8,128)S(1)}, u32[]{:S(2)}, u32[]{:S(2)}) collective-permute-start(f32[384,384]{1,0:T(8,128)S(1)} %collective-permute-done.10), channel_id=1, source_target_pairs={{0,3},{1,0},{2,1},{3,2},{4,7},{5,4},{6,5},{7,6},{8,11},{9,8},{10,9... | collective-permute-start | bytes 1769480 | tf_op jit(solution)/shard_map/ppermute | solution.py:57
  160.6 1.0 collective-permute-start.16
  161.6 17.0 %collective-permute-done.11 = f32[384,384]{1,0:T(8,128)S(1)} collective-permute-done((f32[384,384]{1,0:T(8,128)S(1)}, f32[384,384]{1,0:T(8,128)S(1)}, u32[]{:S(2)}, u32[]{:S(2)}) %collective-permute-start.11) | collective-permute-done | bytes 589856 | tf_op jit(solution)/shard_map/ppermute | solution.py:57
  178.6 2.4 collective-permute-start.13
  181.0 0.4 collective-permute-start.14
  181.4 1.1 collective-permute-start.17
  182.6 0.1 pad_maximum_fusion.2.refs_0_
  182.7 4.3 %collective-permute-done.13 = f32[192,384]{1,0:T(8,128)S(1)} collective-permute-done((f32[192,384]{1,0:T(8,128)S(1)}, f32[192,384]{1,0:T(8,128)S(1)}, u32[]{:S(2)}, u32[]{:S(2)}) %collective-permute-start.13) | collective-permute-done | bytes 294944 | tf_op jit(solution)/shard_map/ppermute | solution.py:57
  187.0 0.1 pad_maximum_fusion.3.refs_1_
  187.1 1.6 collective-permute-start.22
  188.8 4.3 %collective-permute-start.18 = (f32[12,32,384]{2,1,0:T(8,128)S(1)}, f32[12,32,384]{2,1,0:T(8,128)}, u32[]{:S(2)}, u32[]{:S(2)}) collective-permute-start(f32[12,32,384]{2,1,0:T(8,128)S(1)} %bitcast.68), channel_id=1, source_target_pairs={{0,16},{16,0},{1,17},{17,1},{2,18},{18,2},{3,19},{19,3},{4,20},{20... | collective-permute-start | bytes 1769480 | tf_op jit(solution)/shard_map/ppermute | solution.py:40
  193.1 0.5 collective-permute-start.20
  193.6 2.9 %collective-permute-start.21 = (f32[12,32,384]{2,1,0:T(8,128)}, f32[12,32,384]{2,1,0:T(8,128)}, u32[]{:S(2)}, u32[]{:S(2)}) collective-permute-start(f32[12,32,384]{2,1,0:T(8,128)} %collective-permute-done.17.refs_3_), channel_id=1, source_target_pairs={{0,16},{16,0},{1,17},{17,1},{2,18},{18,2},{3,19},{19,3},{4,20},{20... | collective-permute-start | bytes 1769480 | tf_op jit(solution)/shard_map/ppermute | solution.py:40
  196.4 0.1 collective-permute-done.19.refs_5_
  196.5 0.2 collective-permute-done.20.refs_6_
  196.7 1.7 collective-permute-done.21.refs_7_
  198.4 2.3 copy-done.3
  200.8 7.9 %cross.1 = f32[384,384]{1,0:T(8,128)} custom-call(s32[24]{0:T(128)S(1)} %stack.132.at, f32[384,3072]{1,0:T(8,128)S(1)} %copy-done.3, f32[12,32,384]{2,1,0:T(8,128)S(1)} %bitcast.69, f32[12,32,384]{2,1,0:T(8,128)S(1)} %collective-permute-done.15.refs_1_, f32[12,32,384]{2,1,0:T(8,128)} %collective-permute-done.16.refs_2_, ...), custom_call_target="tpu_custom_call" | custom-call | flops 2717908992 | bytes 9437184 | tf_op jit(solution)/shard_map/cross/pallas_call | solution.py:237
  208.7 2.3 collective-permute-start.25
  211.0 2.7 %collective-permute-start.24 = (f32[2,384,384]{2,1,0:T(8,128)S(1)}, f32[2,384,384]{2,1,0:T(8,128)}, u32[]{:S(2)}, u32[]{:S(2)}) collective-permute-start(f32[2,384,384]{2,1,0:T(8,128)S(1)} %pad_maximum_fusion.2.refs_0_), channel_id=1, source_target_pairs={{0,12},{1,13},{2,14},{3,15},{4,0},{5,1},{6,2},{7,3},{8,4},{9,5},{1... | collective-permute-start | bytes 3538952 | tf_op jit(solution)/shard_map/ppermute | solution.py:57
  213.6 10.6 %collective-permute-done.25.refs_5_ = f32[2,384,384]{2,1,0:T(8,128)} collective-permute-done((f32[2,384,384]{2,1,0:T(8,128)S(1)}, f32[2,384,384]{2,1,0:T(8,128)}, u32[]{:S(2)}, u32[]{:S(2)}) %collective-permute-start.25) | collective-permute-done | bytes 1179680 | tf_op jit(solution)/shard_map/ppermute | solution.py:57
  224.2 3.4 %collective-permute-start.27 = (f32[2,384,384]{2,1,0:T(8,128)}, f32[2,384,384]{2,1,0:T(8,128)}, u32[]{:S(2)}, u32[]{:S(2)}) collective-permute-start(f32[2,384,384]{2,1,0:T(8,128)} %collective-permute-done.25.refs_5_), channel_id=1, source_target_pairs={{0,12},{1,13},{2,14},{3,15},{4,0},{5,1},{6,2},{7,3},{8,4},{9,5},{1... | collective-permute-start | bytes 3538952 | tf_op jit(solution)/shard_map/ppermute | solution.py:57
  227.6 9.2 %collective-permute-done.24.refs_4_ = f32[2,384,384]{2,1,0:T(8,128)} collective-permute-done((f32[2,384,384]{2,1,0:T(8,128)S(1)}, f32[2,384,384]{2,1,0:T(8,128)}, u32[]{:S(2)}, u32[]{:S(2)}) %collective-permute-start.24) | collective-permute-done | bytes 1179680 | tf_op jit(solution)/shard_map/ppermute | solution.py:57
  236.8 4.9 %all-gather.8.cloned.1.call-done = f32[3072,384]{1,0:T(8,128)} async-done(((f32[384,384]{1,0:T(8,128)}), f32[3072,384]{1,0:T(8,128)}) %all-gather.8.cloned.1.call-update) | async-done | bytes 4718608 | tf_op jit(solution)/shard_map/all_gather | solution.py:343
  241.8 2.3 copy-done
  244.1 9.4 %near.3.acc = f32[2,384,384]{2,1,0:T(8,128)S(1)} custom-call(s32[24]{0:T(128)S(1)} %stack.132.at, f32[2,384,384]{2,1,0:T(8,128)S(1)} %pad_maximum_fusion.2.refs_0_, f32[2,384,384]{2,1,0:T(8,128)S(1)} %pad_maximum_fusion.3.refs_1_, f32[2,384,384]{2,1,0:T(8,128)} %collective-permute-done.22.refs_2_, f32[2,384,384]{2,1,0:T(8,128)} %collective-permute-done.23.refs_3_, ...), custom_call_target="tpu_custom_call" | custom-call | flops 48922361856 | bytes 141557760 | tf_op jit(solution)/shard_map/near/pallas_call | solution.py:131
  253.5 2.0 place_rows.1
  255.5 5.2 %child.1 = f32[768,384]{1,0:T(8,128)} custom-call(s32[24]{0:T(128)S(1)} %stack.132.at, f32[2,384,384]{2,1,0:T(8,128)S(1)} %near.3.acc, f32[2,384,384]{2,1,0:T(8,128)S(1)} %collective-permute-done.26.top, f32[2,384,384]{2,1,0:T(8,128)} %collective-permute-done.27.low, f32[8,384,384]{2,1,0:T(8,128)S(1)} %bitcast.57, f32[768,384]{1,0:T(8,128)S(1)} %copy-done.1), custom_call_target="tpu_custom_call" | custom-call | flops 1358954496 | bytes 3538944 | tf_op jit(solution)/shard_map/child/pallas_call | solution.py:202
  (49 shorter events, 0.3 us)
Async XLA Ops:
  7.2 1.3 copy-start.5
  7.2 99.0 %all-gather.6.cloned.1.call-start = ((), (), s32[]{:S(2)}) async-start(), calls=%async_computation.4 | async-start | bytes 10616832 | tf_op jit(solution)/shard_map/all_gather | solution.py:328
  8.5 26.1 %copy-start.2 = (s32[12]{0:T(128)S(1)}, s32[12]{0:T(128)}, u32[]{:S(2)}) copy-start(s32[12]{0:T(128)} %anc.7) | copy-start | bytes 148
  34.6 17.3 %copy-start.6 = (f32[768,384]{1,0:T(8,128)S(1)}, f32[768,384]{1,0:T(8,128)}, u32[]{:S(2)}) copy-start(f32[768,384]{1,0:T(8,128)} %param.5) | copy-start | bytes 3538948
  35.2 12.5 %collective-permute-start = (f32[384,384]{1,0:T(8,128)S(1)}, f32[384,384]{1,0:T(8,128)S(1)}, u32[]{:S(2)}, u32[]{:S(2)}) collective-permute-start(f32[384,384]{1,0:T(8,128)S(1)} %bitcast.64), channel_id=1, source_target_pairs={{0,1},{1,2},{2,3},{3,0},{4,5},{5,6},{6,7},{7,4},{8,9},{9,10},{10,1... | collective-permute-start | bytes 1769480 | tf_op jit(solution)/shard_map/ppermute | solution.py:57
  37.2 11.2 %collective-permute-start.1 = (f32[384,384]{1,0:T(8,128)S(1)}, f32[384,384]{1,0:T(8,128)S(1)}, u32[]{:S(2)}, u32[]{:S(2)}) collective-permute-start(f32[384,384]{1,0:T(8,128)S(1)} %bitcast.65), channel_id=1, source_target_pairs={{0,3},{1,0},{2,1},{3,2},{4,7},{5,4},{6,5},{7,6},{8,11},{9,8},{10,9... | collective-permute-start | bytes 1769480 | tf_op jit(solution)/shard_map/ppermute | solution.py:57
  47.7 9.2 %copy-start.4 = (f32[384,384]{1,0:T(8,128)}, f32[384,384]{1,0:T(8,128)S(1)}, u32[]{:S(2)}) copy-start(f32[384,384]{1,0:T(8,128)S(1)} %collective-permute-done) | copy-start | bytes 1769476
  48.4 9.6 %collective-permute-start.2 = (f32[192,384]{1,0:T(8,128)}, f32[192,384]{1,0:T(8,128)}, u32[]{:S(2)}, u32[]{:S(2)}) collective-permute-start(f32[192,384]{1,0:T(8,128)} %slice.16), channel_id=1, source_target_pairs={{0,1},{1,2},{2,3},{3,0},{4,5},{5,6},{6,7},{7,4},{8,9},{9,10},{10,1... | collective-permute-start | bytes 884744 | tf_op jit(solution)/shard_map/ppermute | solution.py:57
  49.2 8.8 %collective-permute-start.3 = (f32[192,384]{1,0:T(8,128)}, f32[192,384]{1,0:T(8,128)}, u32[]{:S(2)}, u32[]{:S(2)}) collective-permute-start(f32[192,384]{1,0:T(8,128)} %slice.17), channel_id=1, source_target_pairs={{0,3},{1,0},{2,1},{3,2},{4,7},{5,4},{6,5},{7,6},{8,11},{9,8},{10,9... | collective-permute-start | bytes 884744 | tf_op jit(solution)/shard_map/ppermute | solution.py:57
  53.0 28.8 %all-to-all-start.1 = ((f32[3,8,32,384]{3,2,0,1:T(8,128)}), f32[3,8,32,384]{3,2,0,1:T(8,128)S(1)}, u32[]{:S(2)}, u32[]{:S(2)}) async-start(f32[3,8,32,384]{3,2,0,1:T(8,128)} %copy.8), calls=%async_computation.1 | async-start | bytes 2359296 | tf_op jit(solution)/shard_map/all_to_all | solution.py:257
  60.2 43.2 %collective-permute-start.4 = (f32[2,384,384]{2,1,0:T(8,128)S(1)}, f32[2,384,384]{2,1,0:T(8,128)}, u32[]{:S(2)}, u32[]{:S(2)}) collective-permute-start(f32[2,384,384]{2,1,0:T(8,128)S(1)} %pad_maximum_fusion.refs_0_), channel_id=1, source_target_pairs={{0,4},{1,5},{2,6},{3,7},{4,8},{5,9},{6,10},{7,11},{8,12},{9,13},{1... | collective-permute-start | bytes 3538952 | tf_op jit(solution)/shard_map/ppermute | solution.py:57
  61.1 42.6 %collective-permute-start.7 = (f32[2,384,384]{2,1,0:T(8,128)}, f32[2,384,384]{2,1,0:T(8,128)}, u32[]{:S(2)}, u32[]{:S(2)}) collective-permute-start(f32[2,384,384]{2,1,0:T(8,128)} %pad_maximum_fusion.1.refs_1_), channel_id=1, source_target_pairs={{0,12},{1,13},{2,14},{3,15},{4,0},{5,1},{6,2},{7,3},{8,4},{9,5},{1... | collective-permute-start | bytes 3538952 | tf_op jit(solution)/shard_map/ppermute | solution.py:57
  62.9 43.3 %collective-permute-start.6 = (f32[2,384,384]{2,1,0:T(8,128)S(1)}, f32[2,384,384]{2,1,0:T(8,128)}, u32[]{:S(2)}, u32[]{:S(2)}) collective-permute-start(f32[2,384,384]{2,1,0:T(8,128)S(1)} %pad_maximum_fusion.refs_0_), channel_id=1, source_target_pairs={{0,12},{1,13},{2,14},{3,15},{4,0},{5,1},{6,2},{7,3},{8,4},{9,5},{1... | collective-permute-start | bytes 3538952 | tf_op jit(solution)/shard_map/ppermute | solution.py:57
  64.0 42.2 %collective-permute-start.5 = (f32[2,384,384]{2,1,0:T(8,128)}, f32[2,384,384]{2,1,0:T(8,128)}, u32[]{:S(2)}, u32[]{:S(2)}) collective-permute-start(f32[2,384,384]{2,1,0:T(8,128)} %pad_maximum_fusion.1.refs_1_), channel_id=1, source_target_pairs={{0,4},{1,5},{2,6},{3,7},{4,8},{5,9},{6,10},{7,11},{8,12},{9,13},{1... | collective-permute-start | bytes 3538952 | tf_op jit(solution)/shard_map/ppermute | solution.py:57
  83.2 18.7 %all-to-all-start.2 = ((f32[16,24,384]{2,1,0:T(8,128)}), f32[16,24,384]{2,1,0:T(8,128)S(1)}, u32[]{:S(2)}, u32[]{:S(2)}) async-start(f32[16,24,384]{2,1,0:T(8,128)} %bitcast.39), calls=%async_computation.2 | async-start | bytes 1179648 | tf_op jit(solution)/shard_map/all_to_all | solution.py:332
  90.8 105.7 %all-gather.4.cloned.1.call-start = ((), (), s32[]{:S(2)}) async-start(), calls=%async_computation.3 | async-start | bytes 5013504 | tf_op jit(solution)/shard_map/all_gather | solution.py:333
  103.3 138.4 %all-gather.8.cloned.1.call-start = ((), (), s32[]{:S(2)}) async-start(), calls=%async_computation.5 | async-start | bytes 5308416 | tf_op jit(solution)/shard_map/all_gather | solution.py:343
  103.4 21.3 %collective-permute-start.8 = (f32[2,384,384]{2,1,0:T(8,128)}, f32[2,384,384]{2,1,0:T(8,128)S(1)}, u32[]{:S(2)}, u32[]{:S(2)}) collective-permute-start(f32[2,384,384]{2,1,0:T(8,128)} %collective-permute-done.4.refs_2_), channel_id=1, source_target_pairs={{0,4},{1,5},{2,6},{3,7},{4,8},{5,9},{6,10},{7,11},{8,12},{9,13},{1... | collective-permute-start | bytes 3538952 | tf_op jit(solution)/shard_map/ppermute | solution.py:57
  103.8 20.9 %collective-permute-start.9 = (f32[2,384,384]{2,1,0:T(8,128)}, f32[2,384,384]{2,1,0:T(8,128)S(1)}, u32[]{:S(2)}, u32[]{:S(2)}) collective-permute-start(f32[2,384,384]{2,1,0:T(8,128)} %collective-permute-done.7.refs_5_), channel_id=1, source_target_pairs={{0,12},{1,13},{2,14},{3,15},{4,0},{5,1},{6,2},{7,3},{8,4},{9,5},{1... | collective-permute-start | bytes 3538952 | tf_op jit(solution)/shard_map/ppermute | solution.py:57
  106.2 18.5 %slice-start = ((s8[9437184]{0:T(1024)(128)(4,1)}), s8[4194304]{0:T(1024)(128)(4,1)S(1)}, s32[]{:S(2)}) async-start(s8[9437184]{0:T(1024)(128)(4,1)} %bitcast.59), calls=%async_computation.6 | async-start | bytes 8388608
  106.2 18.5 %slice-start.1 = ((s8[9437184]{0:T(1024)(128)(4,1)}), s8[4194304]{0:T(1024)(128)(4,1)S(1)}, s32[]{:S(2)}) async-start(s8[9437184]{0:T(1024)(128)(4,1)} %bitcast.59), calls=%async_computation.7 | async-start | bytes 8388608
  106.2 18.5 %slice-start.2 = ((s8[9437184]{0:T(1024)(128)(4,1)}), s8[1048576]{0:T(1024)(128)(4,1)S(1)}, s32[]{:S(2)}) async-start(s8[9437184]{0:T(1024)(128)(4,1)} %bitcast.59), calls=%async_computation.8 | async-start | bytes 2097152
  128.5 29.4 %collective-permute-start.10 = (f32[384,384]{1,0:T(8,128)S(1)}, f32[384,384]{1,0:T(8,128)S(1)}, u32[]{:S(2)}, u32[]{:S(2)}) collective-permute-start(f32[384,384]{1,0:T(8,128)S(1)} %get-tuple-element.16), channel_id=1, source_target_pairs={{0,0},{1,1},{2,16},{3,17},{4,32},{5,33},{6,48},{7,49},{8,64},{9,65... | collective-permute-start | bytes 1769480 | tf_op jit(solution)/shard_map/ppermute | solution.py:338
  133.8 26.8 %collective-permute-start.15 = (f32[12,32,384]{2,1,0:T(8,128)S(1)}, f32[12,32,384]{2,1,0:T(8,128)S(1)}, u32[]{:S(2)}, u32[]{:S(2)}) collective-permute-start(f32[12,32,384]{2,1,0:T(8,128)S(1)} %bitcast.67), channel_id=1, source_target_pairs={{0,32},{16,112},{32,64},{48,16},{64,96},{80,48},{96,0},{112,80},{1... | collective-permute-start | bytes 1769480 | tf_op jit(solution)/shard_map/ppermute | solution.py:36
  157.9 20.6 %collective-permute-start.11 = (f32[384,384]{1,0:T(8,128)S(1)}, f32[384,384]{1,0:T(8,128)S(1)}, u32[]{:S(2)}, u32[]{:S(2)}) collective-permute-start(f32[384,384]{1,0:T(8,128)S(1)} %collective-permute-done.10), channel_id=1, source_target_pairs={{0,1},{1,2},{2,3},{3,0},{4,5},{5,6},{6,7},{7,4},{8,9},{9,10},{10,1... | collective-permute-start | bytes 1769480 | tf_op jit(solution)/shard_map/ppermute | solution.py:57
  157.9 23.0 %collective-permute-start.12 = (f32[384,384]{1,0:T(8,128)S(1)}, f32[384,384]{1,0:T(8,128)S(1)}, u32[]{:S(2)}, u32[]{:S(2)}) collective-permute-start(f32[384,384]{1,0:T(8,128)S(1)} %collective-permute-done.10), channel_id=1, source_target_pairs={{0,3},{1,0},{2,1},{3,2},{4,7},{5,4},{6,5},{7,6},{8,11},{9,8},{10,9... | collective-permute-start | bytes 1769480 | tf_op jit(solution)/shard_map/ppermute | solution.py:57
  160.6 20.8 %collective-permute-start.16 = (f32[12,32,384]{2,1,0:T(8,128)S(1)}, f32[12,32,384]{2,1,0:T(8,128)}, u32[]{:S(2)}, u32[]{:S(2)}) collective-permute-start(f32[12,32,384]{2,1,0:T(8,128)S(1)} %collective-permute-done.15.refs_1_), channel_id=1, source_target_pairs={{0,32},{16,112},{32,64},{48,16},{64,96},{80,48},{96,0},{112,80},{1... | collective-permute-start | bytes 1769480 | tf_op jit(solution)/shard_map/ppermute | solution.py:36
  178.6 8.4 %collective-permute-start.13 = (f32[192,384]{1,0:T(8,128)S(1)}, f32[192,384]{1,0:T(8,128)S(1)}, u32[]{:S(2)}, u32[]{:S(2)}) collective-permute-start(f32[192,384]{1,0:T(8,128)S(1)} %slice.18), channel_id=1, source_target_pairs={{0,1},{1,2},{2,3},{3,0},{4,5},{5,6},{6,7},{7,4},{8,9},{9,10},{10,1... | collective-permute-start | bytes 884744 | tf_op jit(solution)/shard_map/ppermute | solution.py:57
  181.0 6.0 %collective-permute-start.14 = (f32[192,384]{1,0:T(8,128)S(1)}, f32[192,384]{1,0:T(8,128)S(1)}, u32[]{:S(2)}, u32[]{:S(2)}) collective-permute-start(f32[192,384]{1,0:T(8,128)S(1)} %slice.19), channel_id=1, source_target_pairs={{0,3},{1,0},{2,1},{3,2},{4,7},{5,4},{6,5},{7,6},{8,11},{9,8},{10,9... | collective-permute-start | bytes 884744 | tf_op jit(solution)/shard_map/ppermute | solution.py:57
  181.4 12.2 %collective-permute-start.17 = (f32[12,32,384]{2,1,0:T(8,128)}, f32[12,32,384]{2,1,0:T(8,128)}, u32[]{:S(2)}, u32[]{:S(2)}) collective-permute-start(f32[12,32,384]{2,1,0:T(8,128)} %collective-permute-done.16.refs_2_), channel_id=1, source_target_pairs={{0,32},{16,112},{32,64},{48,16},{64,96},{80,48},{96,0},{112,80},{1... | collective-permute-start | bytes 1769480 | tf_op jit(solution)/shard_map/ppermute | solution.py:36
  187.1 21.5 %collective-permute-start.22 = (f32[2,384,384]{2,1,0:T(8,128)S(1)}, f32[2,384,384]{2,1,0:T(8,128)}, u32[]{:S(2)}, u32[]{:S(2)}) collective-permute-start(f32[2,384,384]{2,1,0:T(8,128)S(1)} %pad_maximum_fusion.2.refs_0_), channel_id=1, source_target_pairs={{0,4},{1,5},{2,6},{3,7},{4,8},{5,9},{6,10},{7,11},{8,12},{9,13},{1... | collective-permute-start | bytes 3538952 | tf_op jit(solution)/shard_map/ppermute | solution.py:57
  188.8 7.7 %collective-permute-start.18 = (f32[12,32,384]{2,1,0:T(8,128)S(1)}, f32[12,32,384]{2,1,0:T(8,128)}, u32[]{:S(2)}, u32[]{:S(2)}) collective-permute-start(f32[12,32,384]{2,1,0:T(8,128)S(1)} %bitcast.68), channel_id=1, source_target_pairs={{0,16},{16,0},{1,17},{17,1},{2,18},{18,2},{3,19},{19,3},{4,20},{20... | collective-permute-start | bytes 1769480 | tf_op jit(solution)/shard_map/ppermute | solution.py:40
  193.1 3.4 %collective-permute-start.19 = (f32[12,32,384]{2,1,0:T(8,128)S(1)}, f32[12,32,384]{2,1,0:T(8,128)}, u32[]{:S(2)}, u32[]{:S(2)}) collective-permute-start(f32[12,32,384]{2,1,0:T(8,128)S(1)} %collective-permute-done.15.refs_1_), channel_id=1, source_target_pairs={{0,16},{16,0},{1,17},{17,1},{2,18},{18,2},{3,19},{19,3},{4,20},{20... | collective-permute-start | bytes 1769480 | tf_op jit(solution)/shard_map/ppermute | solution.py:40
  193.1 3.7 %collective-permute-start.20 = (f32[12,32,384]{2,1,0:T(8,128)}, f32[12,32,384]{2,1,0:T(8,128)}, u32[]{:S(2)}, u32[]{:S(2)}) collective-permute-start(f32[12,32,384]{2,1,0:T(8,128)} %collective-permute-done.16.refs_2_), channel_id=1, source_target_pairs={{0,16},{16,0},{1,17},{17,1},{2,18},{18,2},{3,19},{19,3},{4,20},{20... | collective-permute-start | bytes 1769480 | tf_op jit(solution)/shard_map/ppermute | solution.py:40
  193.6 4.8 %collective-permute-start.21 = (f32[12,32,384]{2,1,0:T(8,128)}, f32[12,32,384]{2,1,0:T(8,128)}, u32[]{:S(2)}, u32[]{:S(2)}) collective-permute-start(f32[12,32,384]{2,1,0:T(8,128)} %collective-permute-done.17.refs_3_), channel_id=1, source_target_pairs={{0,16},{16,0},{1,17},{17,1},{2,18},{18,2},{3,19},{19,3},{4,20},{20... | collective-permute-start | bytes 1769480 | tf_op jit(solution)/shard_map/ppermute | solution.py:40
  198.4 2.3 copy-start.3
  208.7 15.5 %collective-permute-start.25 = (f32[2,384,384]{2,1,0:T(8,128)S(1)}, f32[2,384,384]{2,1,0:T(8,128)}, u32[]{:S(2)}, u32[]{:S(2)}) collective-permute-start(f32[2,384,384]{2,1,0:T(8,128)S(1)} %pad_maximum_fusion.3.refs_1_), channel_id=1, source_target_pairs={{0,12},{1,13},{2,14},{3,15},{4,0},{5,1},{6,2},{7,3},{8,4},{9,5},{1... | collective-permute-start | bytes 3538952 | tf_op jit(solution)/shard_map/ppermute | solution.py:57
  211.0 16.7 %collective-permute-start.23 = (f32[2,384,384]{2,1,0:T(8,128)S(1)}, f32[2,384,384]{2,1,0:T(8,128)}, u32[]{:S(2)}, u32[]{:S(2)}) collective-permute-start(f32[2,384,384]{2,1,0:T(8,128)S(1)} %pad_maximum_fusion.3.refs_1_), channel_id=1, source_target_pairs={{0,4},{1,5},{2,6},{3,7},{4,8},{5,9},{6,10},{7,11},{8,12},{9,13},{1... | collective-permute-start | bytes 3538952 | tf_op jit(solution)/shard_map/ppermute | solution.py:57
  211.0 25.9 %collective-permute-start.24 = (f32[2,384,384]{2,1,0:T(8,128)S(1)}, f32[2,384,384]{2,1,0:T(8,128)}, u32[]{:S(2)}, u32[]{:S(2)}) collective-permute-start(f32[2,384,384]{2,1,0:T(8,128)S(1)} %pad_maximum_fusion.2.refs_0_), channel_id=1, source_target_pairs={{0,12},{1,13},{2,14},{3,15},{4,0},{5,1},{6,2},{7,3},{8,4},{9,5},{1... | collective-permute-start | bytes 3538952 | tf_op jit(solution)/shard_map/ppermute | solution.py:57
  213.6 41.9 %collective-permute-start.26 = (f32[2,384,384]{2,1,0:T(8,128)}, f32[2,384,384]{2,1,0:T(8,128)S(1)}, u32[]{:S(2)}, u32[]{:S(2)}) collective-permute-start(f32[2,384,384]{2,1,0:T(8,128)} %collective-permute-done.22.refs_2_), channel_id=1, source_target_pairs={{0,4},{1,5},{2,6},{3,7},{4,8},{5,9},{6,10},{7,11},{8,12},{9,13},{1... | collective-permute-start | bytes 3538952 | tf_op jit(solution)/shard_map/ppermute | solution.py:57
  224.2 31.3 %collective-permute-start.27 = (f32[2,384,384]{2,1,0:T(8,128)}, f32[2,384,384]{2,1,0:T(8,128)}, u32[]{:S(2)}, u32[]{:S(2)}) collective-permute-start(f32[2,384,384]{2,1,0:T(8,128)} %collective-permute-done.25.refs_5_), channel_id=1, source_target_pairs={{0,12},{1,13},{2,14},{3,15},{4,0},{5,1},{6,2},{7,3},{8,4},{9,5},{1... | collective-permute-start | bytes 3538952 | tf_op jit(solution)/shard_map/ppermute | solution.py:57
  241.8 2.3 copy-start
  253.5 2.0 copy-start.1
Sparse Core Ops, SparseCore 0:
  9.7 70.0 all-gather.5
  103.5 81.0 all-gather.3
  208.8 32.9 all-gather.7

commit v9 on v8

--- a/solution.py
+++ b/solution.py
@@ -10,7 +10,7 @@
 
 NB = 24
 NANC = 12
-W1, W2 = 18, 12
+W1, W2 = 14, 12
 ROW = ("y", "core")
 COL = ("z", "x")
 ALL = ("y", "core", "z", "x")

time: 268 us -> 290 us (1.082)
  waiting for transfers between devices: 112 us -> 125 us
  starting transfers between devices: 61.9 us -> 69.8 us
    ppermute x20, waiting for transfers between devices: 56.7 us -> 77.6 us  [hop(): return lax.ppermute(x, ('core',) + COL, pairs)]
    ppermute x1, waiting for transfers between devices: 18.8 us -> 6.37 us  [per_device(): lax.ppermute(ut, ALL, [(16 * r + c, 16 * (c // 2) + 2 * r + c % 2) for r...]
    ppermute x4, starting transfers between devices: 7.69 us -> 17.2 us  [swap(): return lax.ppermute(x, 'core', [(0, 1), (1, 0)])]
    ppermute x3, waiting for transfers between devices: 0.01 us -> 9.49 us  [step(): lax.ppermute(x, ROW, [(2 * i + c, 2 * ((i + 1 - 2 * c) % 4) + c) for i in...]
    all_to_all x1, waiting for transfers between devices: 10.9 us -> 6.84 us  [per_device(): lax.all_to_all(after(s, f_near[0]).reshape(16, -1, w), COL, 0, 0, tiled=T...]
    unnamed x20 -> x24, local copies, waits for them, and re-layouts: 5.24 us -> 6.51 us
  transfers between devices with their start and end apart: 33 -> 33, of which waited for: 13 -> 19; matrix products, arithmetic and copies ran while one was open for 2% -> 1% of each run, Pallas kernels for 14% -> 13%
where the time goes in v9:
time: 290 us; the launch traced here: 289 us
  waiting for transfers between devices  125 us (43%)
  starting transfers between devices  69.8 us (24%)
  Pallas kernels  43.7 us (15%)
  blocking collectives  26 us (9%)
  between operations  14.1 us (5%)
  local copies, waits for them, and re-layouts  7.87 us (3%)
    ppermute x20, waiting for transfers between devices, hop(): return lax.ppermute(x, ('core',) + COL, pairs)  77.6 us
    ppermute x20, starting transfers between devices, hop(): return lax.ppermute(x, ('core',) + COL, pairs)  31.3 us
    all_to_all x1, blocking collectives, spread(): lax.all_to_all(x.reshape(3, 8, sub, w), ROW, 1, 0, tiled=True)  26 us
    pallas_call x2, Pallas kernels, near_product(): pl.pallas_call(functools.partial(near_kernel, 16 // many), out_shape=jax....  20.6 us
    all_to_all x1, waiting for transfers between devices, spread(): lax.all_to_all(x.reshape(3, 8, sub, w), ROW, 1, 0, tiled=True)  17.6 us
    ppermute x4, starting transfers between devices, swap(): return lax.ppermute(x, 'core', [(0, 1), (1, 0)])  17.2 us
    ppermute x3, waiting for transfers between devices, step(): lax.ppermute(x, ROW, [(2 * i + c, 2 * ((i + 1 - 2 * c) % 4) + c) for i in...  9.49 us
    pallas_call x1, Pallas kernels, cross_product(): pl.pallas_call(cross_kernel, out_shape=jax.ShapeDtypeStruct((m, w), F32),...  8.12 us
  transfers between devices with their start and end apart: 33, of which 19 were waited for; matrix products, arithmetic and copies ran while one was open for 1% of the time, Pallas kernels for 13%

profile of v9, /device:TPU:1, one launch (start us, length us, event | category | flops | bytes accessed | tf_op | source)
XLA Modules:
  0.0 289.1 jit_solution(17856592983102398606)
XLA Ops:
  7.2 0.7 all-gather.6.cloned.1.call-update
  7.9 0.5 copy-done.7
  8.4 0.1 copy.7
  8.5 26.0 %all_to_all.35 = f32[3,8,32,384]{3,2,0,1:T(8,128)S(1)} all-to-all(f32[3,8,32,384]{3,2,0,1:T(8,128)S(1)} %copy.7), channel_id=1, replica_groups=mesh['y'=4,'core'=2,'z'=4,'x'=4] {'y','core'}, dimensions={1} | all-to-all | bytes 2359296 | tf_op jit(solution)/shard_map/all_to_all | solution.py:257
  34.6 0.6 pick_rows.2
  35.2 2.1 collective-permute-start
  37.2 2.8 collective-permute-start.1
  40.1 1.1 copy.8
  41.2 3.5 %all-to-all-start.1 = ((f32[3,8,32,384]{3,2,0,1:T(8,128)}), f32[3,8,32,384]{3,2,0,1:T(8,128)S(1)}, u32[]{:S(2)}, u32[]{:S(2)}) async-start(f32[3,8,32,384]{3,2,0,1:T(8,128)} %copy.8), calls=%async_computation.1 | async-start | bytes 2359296 | tf_op jit(solution)/shard_map/all_to_all | solution.py:257
  44.7 3.0 %collective-permute-done = f32[384,384]{1,0:T(8,128)S(1)} collective-permute-done((f32[384,384]{1,0:T(8,128)S(1)}, f32[384,384]{1,0:T(8,128)S(1)}, u32[]{:S(2)}, u32[]{:S(2)}) %collective-permute-start) | collective-permute-done | bytes 589856 | tf_op jit(solution)/shard_map/ppermute | solution.py:57
  47.8 2.7 collective-permute-start.3
  50.5 1.2 pad_maximum_fusion.refs_0_
  51.8 3.2 %collective-permute-done.2 = f32[192,384]{1,0:T(8,128)S(1)} collective-permute-done((f32[192,384]{1,0:T(8,128)S(1)}, f32[192,384]{1,0:T(8,128)S(1)}, u32[]{:S(2)}, u32[]{:S(2)}) %collective-permute-start.2) | collective-permute-done | bytes 294944 | tf_op jit(solution)/shard_map/ppermute | solution.py:57
  55.0 1.1 pad_maximum_fusion.1.refs_1_
  56.1 17.6 %all-to-all-done.1 = f32[3,8,32,384]{3,2,0,1:T(8,128)S(1)} async-done(((f32[3,8,32,384]{3,2,0,1:T(8,128)}), f32[3,8,32,384]{3,2,0,1:T(8,128)S(1)}, u32[]{:S(2)}, u32[]{:S(2)}) %all-to-all-start.1) | async-done | bytes 1179680 | tf_op jit(solution)/shard_map/all_to_all | solution.py:257
  73.6 1.4 pick_rows.3
  75.0 7.4 %all-to-all-start.2 = ((f32[16,24,384]{2,1,0:T(8,128)}), f32[16,24,384]{2,1,0:T(8,128)S(1)}, u32[]{:S(2)}, u32[]{:S(2)}) async-start(f32[16,24,384]{2,1,0:T(8,128)} %bitcast.39), calls=%async_computation.2 | async-start | bytes 1179648 | tf_op jit(solution)/shard_map/all_to_all | solution.py:332
  82.5 1.4 collective-permute-start.4
  84.0 1.3 collective-permute-start.7
  85.3 1.4 collective-permute-start.6
  86.6 0.1 collective-permute-start.5
  86.7 6.8 %all-to-all-done.2.x = f32[16,24,384]{2,1,0:T(8,128)S(1)} async-done(((f32[16,24,384]{2,1,0:T(8,128)}), f32[16,24,384]{2,1,0:T(8,128)S(1)}, u32[]{:S(2)}, u32[]{:S(2)}) %all-to-all-start.2) | async-done | bytes 589856 | tf_op jit(solution)/shard_map/all_to_all | solution.py:332
  93.6 1.4 pick_cols.1
  95.1 0.1 stack.132.at
  95.2 10.3 %collective-permute-done.4.refs_2_ = f32[2,384,384]{2,1,0:T(8,128)} collective-permute-done((f32[2,384,384]{2,1,0:T(8,128)S(1)}, f32[2,384,384]{2,1,0:T(8,128)}, u32[]{:S(2)}, u32[]{:S(2)}) %collective-permute-start.4) | collective-permute-done | bytes 1179680 | tf_op jit(solution)/shard_map/ppermute | solution.py:57
  105.6 2.7 collective-permute-start.9
  108.3 13.5 %collective-permute-done.6.refs_4_ = f32[2,384,384]{2,1,0:T(8,128)} collective-permute-done((f32[2,384,384]{2,1,0:T(8,128)S(1)}, f32[2,384,384]{2,1,0:T(8,128)}, u32[]{:S(2)}, u32[]{:S(2)}) %collective-permute-start.6) | collective-permute-done | bytes 1179680 | tf_op jit(solution)/shard_map/ppermute | solution.py:57
  121.8 1.2 collective-permute-done.5.refs_3_
  123.0 10.7 %near.2.acc = f32[1,384,384]{2,1,0:T(8,128)S(1)} custom-call(s32[24]{0:T(128)S(1)} %stack.132.at, f32[2,384,384]{2,1,0:T(8,128)S(1)} %pad_maximum_fusion.refs_0_, f32[2,384,384]{2,1,0:T(8,128)} %pad_maximum_fusion.1.refs_1_, f32[2,384,384]{2,1,0:T(8,128)} %collective-permute-done.4.refs_2_, f32[2,384,384]{2,1,0:T(8,128)} %collective-permute-done.5.refs_3_, ...), custom_call_target="tpu_custom_call" | custom-call | flops 57076088832 | bytes 231211008 | tf_op jit(solution)/shard_map/near/pallas_call | solution.py:131
  133.7 13.6 %collective-permute-done.8.top = f32[2,384,384]{2,1,0:T(8,128)S(1)} collective-permute-done((f32[2,384,384]{2,1,0:T(8,128)}, f32[2,384,384]{2,1,0:T(8,128)S(1)}, u32[]{:S(2)}, u32[]{:S(2)}) %collective-permute-start.8) | collective-permute-done | bytes 1179680 | tf_op jit(solution)/shard_map/ppermute | solution.py:57
  147.3 4.4 %update.1 = (f32[384,384]{1,0:T(8,128)}, f32[384,384]{1,0:T(8,128)S(1)}) custom-call(s32[24]{0:T(128)S(1)} %stack.132.at, f32[1,384,384]{2,1,0:T(8,128)S(1)} %near.2.acc, f32[2,384,384]{2,1,0:T(8,128)S(1)} %collective-permute-done.8.top, f32[2,384,384]{2,1,0:T(8,128)S(1)} %collective-permute-done.9.low, f32[16,384,384]{2,1,0:T(8,128)S(1)} %bitcast.61), custom_call_target="tpu_custom_call" | custom-call | flops 1358954496 | bytes 2359296 | tf_op jit(solution)/shard_map/update/pallas_call | solution.py:180
  151.8 5.1 %collective-permute-start.10 = (f32[384,384]{1,0:T(8,128)S(1)}, f32[384,384]{1,0:T(8,128)S(1)}, u32[]{:S(2)}, u32[]{:S(2)}) collective-permute-start(f32[384,384]{1,0:T(8,128)S(1)} %get-tuple-element.16), channel_id=1, source_target_pairs={{0,0},{1,1},{2,16},{3,17},{4,32},{5,33},{6,48},{7,49},{8,64},{9,65... | collective-permute-start | bytes 1769480 | tf_op jit(solution)/shard_map/ppermute | solution.py:338
  156.9 3.9 %collective-permute-start.15 = (f32[12,32,384]{2,1,0:T(8,128)}, f32[12,32,384]{2,1,0:T(8,128)}, u32[]{:S(2)}, u32[]{:S(2)}) collective-permute-start(f32[12,32,384]{2,1,0:T(8,128)} %bitcast.45.refs_0_), channel_id=1, source_target_pairs={{0,32},{16,112},{32,64},{48,16},{64,96},{80,48},{96,0},{112,80},{1... | collective-permute-start | bytes 1769480 | tf_op jit(solution)/shard_map/ppermute | solution.py:36
  160.8 6.4 %collective-permute-done.10 = f32[384,384]{1,0:T(8,128)S(1)} collective-permute-done((f32[384,384]{1,0:T(8,128)S(1)}, f32[384,384]{1,0:T(8,128)S(1)}, u32[]{:S(2)}, u32[]{:S(2)}) %collective-permute-start.10) | collective-permute-done | bytes 589856 | tf_op jit(solution)/shard_map/ppermute | solution.py:338
  167.2 4.5 %collective-permute-start.11 = (f32[384,384]{1,0:T(8,128)S(1)}, f32[384,384]{1,0:T(8,128)S(1)}, u32[]{:S(2)}, u32[]{:S(2)}) collective-permute-start(f32[384,384]{1,0:T(8,128)S(1)} %collective-permute-done.10), channel_id=1, source_target_pairs={{0,1},{1,2},{2,3},{3,0},{4,5},{5,6},{6,7},{7,4},{8,9},{9,10},{10,1... | collective-permute-start | bytes 1769480 | tf_op jit(solution)/shard_map/ppermute | solution.py:57
  171.7 4.9 %collective-permute-start.12 = (f32[384,384]{1,0:T(8,128)S(1)}, f32[384,384]{1,0:T(8,128)S(1)}, u32[]{:S(2)}, u32[]{:S(2)}) collective-permute-start(f32[384,384]{1,0:T(8,128)S(1)} %collective-permute-done.10), channel_id=1, source_target_pairs={{0,3},{1,0},{2,1},{3,2},{4,7},{5,4},{6,5},{7,6},{8,11},{9,8},{10,9... | collective-permute-start | bytes 1769480 | tf_op jit(solution)/shard_map/ppermute | solution.py:57
  176.6 8.7 %collective-permute-done.15.refs_1_ = f32[12,32,384]{2,1,0:T(8,128)} collective-permute-done((f32[12,32,384]{2,1,0:T(8,128)}, f32[12,32,384]{2,1,0:T(8,128)}, u32[]{:S(2)}, u32[]{:S(2)}) %collective-permute-start.15) | collective-permute-done | bytes 589856 | tf_op jit(solution)/shard_map/ppermute | solution.py:36
  185.3 5.4 %collective-permute-done.11 = f32[384,384]{1,0:T(8,128)S(1)} collective-permute-done((f32[384,384]{1,0:T(8,128)S(1)}, f32[384,384]{1,0:T(8,128)S(1)}, u32[]{:S(2)}, u32[]{:S(2)}) %collective-permute-start.11) | collective-permute-done | bytes 589856 | tf_op jit(solution)/shard_map/ppermute | solution.py:57
  190.7 2.3 collective-permute-start.13
  193.0 0.5 collective-permute-start.14
  193.6 0.8 collective-permute-done.16.refs_2_
  194.3 1.2 collective-permute-start.17
  195.6 2.0 collective-permute-done.13
  197.6 1.5 collective-permute-done.14
  199.1 0.1 pad_maximum_fusion.3.refs_1_
  199.2 0.3 collective-permute-start.22
  199.5 7.4 %collective-permute-start.18 = (f32[12,32,384]{2,1,0:T(8,128)}, f32[12,32,384]{2,1,0:T(8,128)}, u32[]{:S(2)}, u32[]{:S(2)}) collective-permute-start(f32[12,32,384]{2,1,0:T(8,128)} %bitcast.45.refs_0_), channel_id=1, source_target_pairs={{0,16},{16,0},{1,17},{17,1},{2,18},{18,2},{3,19},{19,3},{4,20},{20... | collective-permute-start | bytes 1769480 | tf_op jit(solution)/shard_map/ppermute | solution.py:40
  206.9 0.5 collective-permute-start.20
  207.4 9.3 %collective-permute-start.21 = (f32[12,32,384]{2,1,0:T(8,128)}, f32[12,32,384]{2,1,0:T(8,128)}, u32[]{:S(2)}, u32[]{:S(2)}) collective-permute-start(f32[12,32,384]{2,1,0:T(8,128)} %collective-permute-done.17.refs_3_), channel_id=1, source_target_pairs={{0,16},{16,0},{1,17},{17,1},{2,18},{18,2},{3,19},{19,3},{4,20},{20... | collective-permute-start | bytes 1769480 | tf_op jit(solution)/shard_map/ppermute | solution.py:40
  216.7 2.0 collective-permute-done.21.refs_7_
  218.7 2.3 copy-done.3
  221.0 8.1 %cross.1 = f32[384,384]{1,0:T(8,128)} custom-call(s32[24]{0:T(128)S(1)} %stack.132.at, f32[384,3072]{1,0:T(8,128)S(1)} %copy-done.3, f32[12,32,384]{2,1,0:T(8,128)} %bitcast.45.refs_0_, f32[12,32,384]{2,1,0:T(8,128)} %collective-permute-done.15.refs_1_, f32[12,32,384]{2,1,0:T(8,128)} %collective-permute-done.16.refs_2_, ...), custom_call_target="tpu_custom_call" | custom-call | flops 2717908992 | bytes 9437184 | tf_op jit(solution)/shard_map/cross/pallas_call | solution.py:237
  229.3 1.5 collective-permute-start.23
  230.7 1.3 collective-permute-start.24
  232.0 0.2 collective-permute-start.26
  232.2 12.5 %collective-permute-done.25.refs_5_ = f32[2,384,384]{2,1,0:T(8,128)} collective-permute-done((f32[2,384,384]{2,1,0:T(8,128)S(1)}, f32[2,384,384]{2,1,0:T(8,128)}, u32[]{:S(2)}, u32[]{:S(2)}) %collective-permute-start.25) | collective-permute-done | bytes 1179680 | tf_op jit(solution)/shard_map/ppermute | solution.py:57
  244.7 1.2 collective-permute-start.27
  246.0 11.3 %collective-permute-done.24.refs_4_ = f32[2,384,384]{2,1,0:T(8,128)} collective-permute-done((f32[2,384,384]{2,1,0:T(8,128)S(1)}, f32[2,384,384]{2,1,0:T(8,128)}, u32[]{:S(2)}, u32[]{:S(2)}) %collective-permute-start.24) | collective-permute-done | bytes 1179680 | tf_op jit(solution)/shard_map/ppermute | solution.py:57
  257.4 4.4 %all-gather.8.cloned.1.call-done = f32[3072,384]{1,0:T(8,128)} async-done(((f32[384,384]{1,0:T(8,128)}), f32[3072,384]{1,0:T(8,128)}) %all-gather.8.cloned.1.call-update) | async-done | bytes 4718608 | tf_op jit(solution)/shard_map/all_gather | solution.py:343
  261.8 2.3 copy-done
  264.1 1.3 copy-done.5
  265.4 9.9 %near.3.acc = f32[2,384,384]{2,1,0:T(8,128)S(1)} custom-call(s32[24]{0:T(128)S(1)} %stack.132.at, f32[2,384,384]{2,1,0:T(8,128)S(1)} %pad_maximum_fusion.2.refs_0_, f32[2,384,384]{2,1,0:T(8,128)S(1)} %pad_maximum_fusion.3.refs_1_, f32[2,384,384]{2,1,0:T(8,128)S(1)} %copy-done.5, f32[2,384,384]{2,1,0:T(8,128)} %collective-permute-done.23.refs_3_, ...), custom_call_target="tpu_custom_call" | custom-call | flops 48922361856 | bytes 141557760 | tf_op jit(solution)/shard_map/near/pallas_call | solution.py:131
  275.3 2.0 place_rows.1
  277.3 5.3 %child.1 = f32[768,384]{1,0:T(8,128)} custom-call(s32[24]{0:T(128)S(1)} %stack.132.at, f32[2,384,384]{2,1,0:T(8,128)S(1)} %near.3.acc, f32[2,384,384]{2,1,0:T(8,128)S(1)} %collective-permute-done.26.top, f32[2,384,384]{2,1,0:T(8,128)} %collective-permute-done.27.low, f32[8,384,384]{2,1,0:T(8,128)S(1)} %bitcast.57, f32[768,384]{1,0:T(8,128)S(1)} %copy-done.1), custom_call_target="tpu_custom_call" | custom-call | flops 1358954496 | bytes 3538944 | tf_op jit(solution)/shard_map/child/pallas_call | solution.py:202
  (53 shorter events, 0.7 us)
Async XLA Ops:
  7.2 1.3 copy-start.7
  7.2 115.8 %all-gather.6.cloned.1.call-start = ((), (), s32[]{:S(2)}) async-start(), calls=%async_computation.4 | async-start | bytes 10616832 | tf_op jit(solution)/shard_map/all_gather | solution.py:328
  8.5 26.1 %copy-start.2 = (s32[12]{0:T(128)S(1)}, s32[12]{0:T(128)}, u32[]{:S(2)}) copy-start(s32[12]{0:T(128)} %anc.7) | copy-start | bytes 148
  34.6 5.5 %copy-start.8 = (f32[768,384]{1,0:T(8,128)S(1)}, f32[768,384]{1,0:T(8,128)}, u32[]{:S(2)}) copy-start(f32[768,384]{1,0:T(8,128)} %param.5) | copy-start | bytes 3538948
  35.2 12.5 %collective-permute-start = (f32[384,384]{1,0:T(8,128)S(1)}, f32[384,384]{1,0:T(8,128)S(1)}, u32[]{:S(2)}, u32[]{:S(2)}) collective-permute-start(f32[384,384]{1,0:T(8,128)S(1)} %bitcast.64), channel_id=1, source_target_pairs={{0,1},{1,2},{2,3},{3,0},{4,5},{5,6},{6,7},{7,4},{8,9},{9,10},{10,1... | collective-permute-start | bytes 1769480 | tf_op jit(solution)/shard_map/ppermute | solution.py:57
  37.2 10.5 %collective-permute-start.1 = (f32[384,384]{1,0:T(8,128)S(1)}, f32[384,384]{1,0:T(8,128)S(1)}, u32[]{:S(2)}, u32[]{:S(2)}) collective-permute-start(f32[384,384]{1,0:T(8,128)S(1)} %bitcast.65), channel_id=1, source_target_pairs={{0,3},{1,0},{2,1},{3,2},{4,7},{5,4},{6,5},{7,6},{8,11},{9,8},{10,9... | collective-permute-start | bytes 1769480 | tf_op jit(solution)/shard_map/ppermute | solution.py:57
  41.2 32.5 %all-to-all-start.1 = ((f32[3,8,32,384]{3,2,0,1:T(8,128)}), f32[3,8,32,384]{3,2,0,1:T(8,128)S(1)}, u32[]{:S(2)}, u32[]{:S(2)}) async-start(f32[3,8,32,384]{3,2,0,1:T(8,128)} %copy.8), calls=%async_computation.1 | async-start | bytes 2359296 | tf_op jit(solution)/shard_map/all_to_all | solution.py:257
  47.7 2.9 copy-start.6
  47.7 7.3 %collective-permute-start.2 = (f32[192,384]{1,0:T(8,128)S(1)}, f32[192,384]{1,0:T(8,128)S(1)}, u32[]{:S(2)}, u32[]{:S(2)}) collective-permute-start(f32[192,384]{1,0:T(8,128)S(1)} %slice.16), channel_id=1, source_target_pairs={{0,1},{1,2},{2,3},{3,0},{4,5},{5,6},{6,7},{7,4},{8,9},{9,10},{10,1... | collective-permute-start | bytes 884744 | tf_op jit(solution)/shard_map/ppermute | solution.py:57
  47.8 7.1 %collective-permute-start.3 = (f32[192,384]{1,0:T(8,128)S(1)}, f32[192,384]{1,0:T(8,128)S(1)}, u32[]{:S(2)}, u32[]{:S(2)}) collective-permute-start(f32[192,384]{1,0:T(8,128)S(1)} %slice.17), channel_id=1, source_target_pairs={{0,3},{1,0},{2,1},{3,2},{4,7},{5,4},{6,5},{7,6},{8,11},{9,8},{10,9... | collective-permute-start | bytes 884744 | tf_op jit(solution)/shard_map/ppermute | solution.py:57
  75.0 18.5 %all-to-all-start.2 = ((f32[16,24,384]{2,1,0:T(8,128)}), f32[16,24,384]{2,1,0:T(8,128)S(1)}, u32[]{:S(2)}, u32[]{:S(2)}) async-start(f32[16,24,384]{2,1,0:T(8,128)} %bitcast.39), calls=%async_computation.2 | async-start | bytes 1179648 | tf_op jit(solution)/shard_map/all_to_all | solution.py:332
  82.5 134.2 %all-gather.4.cloned.1.call-start = ((), (), s32[]{:S(2)}) async-start(), calls=%async_computation.3 | async-start | bytes 5013504 | tf_op jit(solution)/shard_map/all_gather | solution.py:333
  82.5 23.0 %collective-permute-start.4 = (f32[2,384,384]{2,1,0:T(8,128)S(1)}, f32[2,384,384]{2,1,0:T(8,128)}, u32[]{:S(2)}, u32[]{:S(2)}) collective-permute-start(f32[2,384,384]{2,1,0:T(8,128)S(1)} %pad_maximum_fusion.refs_0_), channel_id=1, source_target_pairs={{0,4},{1,5},{2,6},{3,7},{4,8},{5,9},{6,10},{7,11},{8,12},{9,13},{1... | collective-permute-start | bytes 3538952 | tf_op jit(solution)/shard_map/ppermute | solution.py:57
  84.0 21.6 %collective-permute-start.7 = (f32[2,384,384]{2,1,0:T(8,128)}, f32[2,384,384]{2,1,0:T(8,128)}, u32[]{:S(2)}, u32[]{:S(2)}) collective-permute-start(f32[2,384,384]{2,1,0:T(8,128)} %pad_maximum_fusion.1.refs_1_), channel_id=1, source_target_pairs={{0,12},{1,13},{2,14},{3,15},{4,0},{5,1},{6,2},{7,3},{8,4},{9,5},{1... | collective-permute-start | bytes 3538952 | tf_op jit(solution)/shard_map/ppermute | solution.py:57
  85.3 36.5 %collective-permute-start.6 = (f32[2,384,384]{2,1,0:T(8,128)S(1)}, f32[2,384,384]{2,1,0:T(8,128)}, u32[]{:S(2)}, u32[]{:S(2)}) collective-permute-start(f32[2,384,384]{2,1,0:T(8,128)S(1)} %pad_maximum_fusion.refs_0_), channel_id=1, source_target_pairs={{0,12},{1,13},{2,14},{3,15},{4,0},{5,1},{6,2},{7,3},{8,4},{9,5},{1... | collective-permute-start | bytes 3538952 | tf_op jit(solution)/shard_map/ppermute | solution.py:57
  86.6 36.3 %collective-permute-start.5 = (f32[2,384,384]{2,1,0:T(8,128)}, f32[2,384,384]{2,1,0:T(8,128)}, u32[]{:S(2)}, u32[]{:S(2)}) collective-permute-start(f32[2,384,384]{2,1,0:T(8,128)} %pad_maximum_fusion.1.refs_1_), channel_id=1, source_target_pairs={{0,4},{1,5},{2,6},{3,7},{4,8},{5,9},{6,10},{7,11},{8,12},{9,13},{1... | collective-permute-start | bytes 3538952 | tf_op jit(solution)/shard_map/ppermute | solution.py:57
  95.0 166.8 %all-gather.8.cloned.1.call-start = ((), (), s32[]{:S(2)}) async-start(), calls=%async_computation.5 | async-start | bytes 5308416 | tf_op jit(solution)/shard_map/all_gather | solution.py:343
  105.6 41.7 %collective-permute-start.8 = (f32[2,384,384]{2,1,0:T(8,128)}, f32[2,384,384]{2,1,0:T(8,128)S(1)}, u32[]{:S(2)}, u32[]{:S(2)}) collective-permute-start(f32[2,384,384]{2,1,0:T(8,128)} %collective-permute-done.4.refs_2_), channel_id=1, source_target_pairs={{0,4},{1,5},{2,6},{3,7},{4,8},{5,9},{6,10},{7,11},{8,12},{9,13},{1... | collective-permute-start | bytes 3538952 | tf_op jit(solution)/shard_map/ppermute | solution.py:57
  105.6 41.7 %collective-permute-start.9 = (f32[2,384,384]{2,1,0:T(8,128)}, f32[2,384,384]{2,1,0:T(8,128)S(1)}, u32[]{:S(2)}, u32[]{:S(2)}) collective-permute-start(f32[2,384,384]{2,1,0:T(8,128)} %collective-permute-done.7.refs_5_), channel_id=1, source_target_pairs={{0,12},{1,13},{2,14},{3,15},{4,0},{5,1},{6,2},{7,3},{8,4},{9,5},{1... | collective-permute-start | bytes 3538952 | tf_op jit(solution)/shard_map/ppermute | solution.py:57
  123.0 24.4 %slice-start = ((s8[9437184]{0:T(1024)(128)(4,1)}), s8[4194304]{0:T(1024)(128)(4,1)S(1)}, s32[]{:S(2)}) async-start(s8[9437184]{0:T(1024)(128)(4,1)} %bitcast.59), calls=%async_computation.6 | async-start | bytes 8388608
  123.0 24.4 %slice-start.1 = ((s8[9437184]{0:T(1024)(128)(4,1)}), s8[4194304]{0:T(1024)(128)(4,1)S(1)}, s32[]{:S(2)}) async-start(s8[9437184]{0:T(1024)(128)(4,1)} %bitcast.59), calls=%async_computation.7 | async-start | bytes 8388608
  123.0 24.4 %slice-start.2 = ((s8[9437184]{0:T(1024)(128)(4,1)}), s8[1048576]{0:T(1024)(128)(4,1)S(1)}, s32[]{:S(2)}) async-start(s8[9437184]{0:T(1024)(128)(4,1)} %bitcast.59), calls=%async_computation.8 | async-start | bytes 2097152
  151.8 15.4 %collective-permute-start.10 = (f32[384,384]{1,0:T(8,128)S(1)}, f32[384,384]{1,0:T(8,128)S(1)}, u32[]{:S(2)}, u32[]{:S(2)}) collective-permute-start(f32[384,384]{1,0:T(8,128)S(1)} %get-tuple-element.16), channel_id=1, source_target_pairs={{0,0},{1,1},{2,16},{3,17},{4,32},{5,33},{6,48},{7,49},{8,64},{9,65... | collective-permute-start | bytes 1769480 | tf_op jit(solution)/shard_map/ppermute | solution.py:338
  156.9 28.4 %collective-permute-start.15 = (f32[12,32,384]{2,1,0:T(8,128)}, f32[12,32,384]{2,1,0:T(8,128)}, u32[]{:S(2)}, u32[]{:S(2)}) collective-permute-start(f32[12,32,384]{2,1,0:T(8,128)} %bitcast.45.refs_0_), channel_id=1, source_target_pairs={{0,32},{16,112},{32,64},{48,16},{64,96},{80,48},{96,0},{112,80},{1... | collective-permute-start | bytes 1769480 | tf_op jit(solution)/shard_map/ppermute | solution.py:36
  167.2 23.5 %collective-permute-start.11 = (f32[384,384]{1,0:T(8,128)S(1)}, f32[384,384]{1,0:T(8,128)S(1)}, u32[]{:S(2)}, u32[]{:S(2)}) collective-permute-start(f32[384,384]{1,0:T(8,128)S(1)} %collective-permute-done.10), channel_id=1, source_target_pairs={{0,1},{1,2},{2,3},{3,0},{4,5},{5,6},{6,7},{7,4},{8,9},{9,10},{10,1... | collective-permute-start | bytes 1769480 | tf_op jit(solution)/shard_map/ppermute | solution.py:57
  171.7 21.3 %collective-permute-start.12 = (f32[384,384]{1,0:T(8,128)S(1)}, f32[384,384]{1,0:T(8,128)S(1)}, u32[]{:S(2)}, u32[]{:S(2)}) collective-permute-start(f32[384,384]{1,0:T(8,128)S(1)} %collective-permute-done.10), channel_id=1, source_target_pairs={{0,3},{1,0},{2,1},{3,2},{4,7},{5,4},{6,5},{7,6},{8,11},{9,8},{10,9... | collective-permute-start | bytes 1769480 | tf_op jit(solution)/shard_map/ppermute | solution.py:57
  185.3 9.0 %collective-permute-start.16 = (f32[12,32,384]{2,1,0:T(8,128)}, f32[12,32,384]{2,1,0:T(8,128)}, u32[]{:S(2)}, u32[]{:S(2)}) collective-permute-start(f32[12,32,384]{2,1,0:T(8,128)} %collective-permute-done.15.refs_1_), channel_id=1, source_target_pairs={{0,32},{16,112},{32,64},{48,16},{64,96},{80,48},{96,0},{112,80},{1... | collective-permute-start | bytes 1769480 | tf_op jit(solution)/shard_map/ppermute | solution.py:36
  190.7 6.9 %collective-permute-start.13 = (f32[192,384]{1,0:T(8,128)S(1)}, f32[192,384]{1,0:T(8,128)S(1)}, u32[]{:S(2)}, u32[]{:S(2)}) collective-permute-start(f32[192,384]{1,0:T(8,128)S(1)} %slice.18), channel_id=1, source_target_pairs={{0,1},{1,2},{2,3},{3,0},{4,5},{5,6},{6,7},{7,4},{8,9},{9,10},{10,1... | collective-permute-start | bytes 884744 | tf_op jit(solution)/shard_map/ppermute | solution.py:57
  193.0 6.0 %collective-permute-start.14 = (f32[192,384]{1,0:T(8,128)S(1)}, f32[192,384]{1,0:T(8,128)S(1)}, u32[]{:S(2)}, u32[]{:S(2)}) collective-permute-start(f32[192,384]{1,0:T(8,128)S(1)} %slice.19), channel_id=1, source_target_pairs={{0,3},{1,0},{2,1},{3,2},{4,7},{5,4},{6,5},{7,6},{8,11},{9,8},{10,9... | collective-permute-start | bytes 884744 | tf_op jit(solution)/shard_map/ppermute | solution.py:57
  194.3 13.1 %collective-permute-start.17 = (f32[12,32,384]{2,1,0:T(8,128)}, f32[12,32,384]{2,1,0:T(8,128)}, u32[]{:S(2)}, u32[]{:S(2)}) collective-permute-start(f32[12,32,384]{2,1,0:T(8,128)} %collective-permute-done.16.refs_2_), channel_id=1, source_target_pairs={{0,32},{16,112},{32,64},{48,16},{64,96},{80,48},{96,0},{112,80},{1... | collective-permute-start | bytes 1769480 | tf_op jit(solution)/shard_map/ppermute | solution.py:36
  199.2 30.0 %collective-permute-start.22 = (f32[2,384,384]{2,1,0:T(8,128)S(1)}, f32[2,384,384]{2,1,0:T(8,128)S(1)}, u32[]{:S(2)}, u32[]{:S(2)}) collective-permute-start(f32[2,384,384]{2,1,0:T(8,128)S(1)} %pad_maximum_fusion.2.refs_0_), channel_id=1, source_target_pairs={{0,4},{1,5},{2,6},{3,7},{4,8},{5,9},{6,10},{7,11},{8,12},{9,13},{1... | collective-permute-start | bytes 3538952 | tf_op jit(solution)/shard_map/ppermute | solution.py:57
  199.5 17.3 %collective-permute-start.18 = (f32[12,32,384]{2,1,0:T(8,128)}, f32[12,32,384]{2,1,0:T(8,128)}, u32[]{:S(2)}, u32[]{:S(2)}) collective-permute-start(f32[12,32,384]{2,1,0:T(8,128)} %bitcast.45.refs_0_), channel_id=1, source_target_pairs={{0,16},{16,0},{1,17},{17,1},{2,18},{18,2},{3,19},{19,3},{4,20},{20... | collective-permute-start | bytes 1769480 | tf_op jit(solution)/shard_map/ppermute | solution.py:40
  206.9 9.8 %collective-permute-start.19 = (f32[12,32,384]{2,1,0:T(8,128)}, f32[12,32,384]{2,1,0:T(8,128)}, u32[]{:S(2)}, u32[]{:S(2)}) collective-permute-start(f32[12,32,384]{2,1,0:T(8,128)} %collective-permute-done.15.refs_1_), channel_id=1, source_target_pairs={{0,16},{16,0},{1,17},{17,1},{2,18},{18,2},{3,19},{19,3},{4,20},{20... | collective-permute-start | bytes 1769480 | tf_op jit(solution)/shard_map/ppermute | solution.py:40
  206.9 9.8 %collective-permute-start.20 = (f32[12,32,384]{2,1,0:T(8,128)}, f32[12,32,384]{2,1,0:T(8,128)}, u32[]{:S(2)}, u32[]{:S(2)}) collective-permute-start(f32[12,32,384]{2,1,0:T(8,128)} %collective-permute-done.16.refs_2_), channel_id=1, source_target_pairs={{0,16},{16,0},{1,17},{17,1},{2,18},{18,2},{3,19},{19,3},{4,20},{20... | collective-permute-start | bytes 1769480 | tf_op jit(solution)/shard_map/ppermute | solution.py:40
  207.4 11.3 %collective-permute-start.21 = (f32[12,32,384]{2,1,0:T(8,128)}, f32[12,32,384]{2,1,0:T(8,128)}, u32[]{:S(2)}, u32[]{:S(2)}) collective-permute-start(f32[12,32,384]{2,1,0:T(8,128)} %collective-permute-done.17.refs_3_), channel_id=1, source_target_pairs={{0,16},{16,0},{1,17},{17,1},{2,18},{18,2},{3,19},{19,3},{4,20},{20... | collective-permute-start | bytes 1769480 | tf_op jit(solution)/shard_map/ppermute | solution.py:40
  218.7 2.3 copy-start.3
  229.2 2.9 copy-start.4
  229.2 15.5 %collective-permute-start.25 = (f32[2,384,384]{2,1,0:T(8,128)S(1)}, f32[2,384,384]{2,1,0:T(8,128)}, u32[]{:S(2)}, u32[]{:S(2)}) collective-permute-start(f32[2,384,384]{2,1,0:T(8,128)S(1)} %pad_maximum_fusion.3.refs_1_), channel_id=1, source_target_pairs={{0,12},{1,13},{2,14},{3,15},{4,0},{5,1},{6,2},{7,3},{8,4},{9,5},{1... | collective-permute-start | bytes 3538952 | tf_op jit(solution)/shard_map/ppermute | solution.py:57
  229.3 16.7 %collective-permute-start.23 = (f32[2,384,384]{2,1,0:T(8,128)S(1)}, f32[2,384,384]{2,1,0:T(8,128)}, u32[]{:S(2)}, u32[]{:S(2)}) collective-permute-start(f32[2,384,384]{2,1,0:T(8,128)S(1)} %pad_maximum_fusion.3.refs_1_), channel_id=1, source_target_pairs={{0,4},{1,5},{2,6},{3,7},{4,8},{5,9},{6,10},{7,11},{8,12},{9,13},{1... | collective-permute-start | bytes 3538952 | tf_op jit(solution)/shard_map/ppermute | solution.py:57
  230.7 26.6 %collective-permute-start.24 = (f32[2,384,384]{2,1,0:T(8,128)S(1)}, f32[2,384,384]{2,1,0:T(8,128)}, u32[]{:S(2)}, u32[]{:S(2)}) collective-permute-start(f32[2,384,384]{2,1,0:T(8,128)S(1)} %pad_maximum_fusion.2.refs_0_), channel_id=1, source_target_pairs={{0,12},{1,13},{2,14},{3,15},{4,0},{5,1},{6,2},{7,3},{8,4},{9,5},{1... | collective-permute-start | bytes 3538952 | tf_op jit(solution)/shard_map/ppermute | solution.py:57
  232.0 45.2 %collective-permute-start.26 = (f32[2,384,384]{2,1,0:T(8,128)}, f32[2,384,384]{2,1,0:T(8,128)S(1)}, u32[]{:S(2)}, u32[]{:S(2)}) collective-permute-start(f32[2,384,384]{2,1,0:T(8,128)} %copy-done.4), channel_id=1, source_target_pairs={{0,4},{1,5},{2,6},{3,7},{4,8},{5,9},{6,10},{7,11},{8,12},{9,13},{1... | collective-permute-start | bytes 3538952 | tf_op jit(solution)/shard_map/ppermute | solution.py:57
  244.7 32.5 %collective-permute-start.27 = (f32[2,384,384]{2,1,0:T(8,128)}, f32[2,384,384]{2,1,0:T(8,128)}, u32[]{:S(2)}, u32[]{:S(2)}) collective-permute-start(f32[2,384,384]{2,1,0:T(8,128)} %collective-permute-done.25.refs_5_), channel_id=1, source_target_pairs={{0,12},{1,13},{2,14},{3,15},{4,0},{5,1},{6,2},{7,3},{8,4},{9,5},{1... | collective-permute-start | bytes 3538952 | tf_op jit(solution)/shard_map/ppermute | solution.py:57
  261.8 2.3 copy-start
  264.1 1.3 copy-start.5
  275.3 2.0 copy-start.1
Sparse Core Ops, SparseCore 0:
  9.7 73.7 all-gather.5
  95.1 60.6 all-gather.3
  229.3 32.4 all-gather.7

commit v10 on v9

--- a/solution.py
+++ b/solution.py
@@ -10,13 +10,14 @@
 
 NB = 24
 NANC = 12
-W1, W2 = 14, 12
+W1, W2 = 12, 12
 ROW = ("y", "core")
 COL = ("z", "x")
 ALL = ("y", "core", "z", "x")
 VMEM = pl.BlockSpec(memory_space=pltpu.VMEM)
 SMEM = pl.BlockSpec(memory_space=pltpu.SMEM)
 ANY = pl.BlockSpec(memory_space=pl.ANY)
+HBM = pl.BlockSpec(memory_space=pltpu.HBM)
 F32 = jnp.float32
 
 
@@ -57,10 +58,14 @@
     return lax.ppermute(x, ("core",) + COL, pairs)
 
 
-def gather_cols(x):
+def gather_cols(x, whole):
     half = x.shape[0] // 2
     up, down = hop(x, 0, 1), hop(x, 0, -1)
     top, low = hop(up[:half], 0, 1), hop(down[half:], 0, -1)
+    if whole:
+        group = jnp.stack([x, up, down, jnp.concatenate([top, low])])
+        up, down = hop(group, 1, 1), hop(group, 1, -1)
+        return (group, up, down), (hop(up[:2], 1, 1), hop(down[2:], 1, -1))
     one, two = jnp.stack([x, up]), jnp.stack([down, jnp.concatenate([top, low])])
     one, two = lax.optimization_barrier((one, two))
     up_one, down_two = hop(one, 1, 1), hop(two, 1, -1)
@@ -68,7 +73,14 @@
     return (one, two, up_one, up_two, down_one, down_two), (hop(up_one, 1, 1), hop(down_two, 1, -1))
 
 
-def places():
+def turn(x):
+    at = lambda y, core, z, x: ((2 * y + core) * 4 + z) * 4 + x
+    every = [(y, core, z, x) for y in range(4) for core in range(2) for z in range(4) for x in range(4)]
+    x = lax.ppermute(x, ALL, [(at(y, c, z, x), at(y, x // 2, (y + z) % 4, 2 * c + x % 2)) for y, c, z, x in every])
+    return lax.ppermute(x, ALL, [(at(y, c, z, x), at((z - y) % 4, c, z, x)) for y, c, z, x in every])
+
+
+def places(turned):
     y, core, z, x = (lax.axis_index(n) for n in ALL)
     s = 1 - 2 * core
     near = lambda i, k: lax.rem(i + k + 8, 4)
@@ -78,7 +90,8 @@
     for k in (0, -1, 1, 2):
         for i in (0, -1, 1, 2):
             u, v = near(first, i), near(second, k)
-            cols.append(jnp.where(core == 0, 4 * v + u, 4 * u + v))
+            at_z, at_x = jnp.where(core == 0, v, u), jnp.where(core == 0, u, v)
+            cols.append(4 * (lax.rem(at_z - y + 4, 4) if turned else at_z) + at_x)
     return jnp.stack(rows + cols).astype(jnp.int32)
 
 
@@ -90,20 +103,20 @@
     return mul(a_hi, b_hi) + (mul(a_hi, b_lo) + mul(a_lo, b_hi))
 
 
-def near_kernel(per, at, *refs):
-    pairs, tiles, acc, (a_buf, b_buf, a_sem, b_sem) = refs[:6], refs[6], refs[7], refs[8:]
-    outs = acc.shape[0]
-
-    def pair_copy(i, source):
-        return pltpu.make_async_copy(source, a_buf.at[pl.ds(2 * i, 2)], a_sem.at[i])
+def near_kernel(per, count, at, *refs):
+    pieces, tiles, acc, (a_buf, b_buf, a_sem, b_sem) = refs[:count], refs[count], refs[count + 1], refs[count + 2 :]
+    outs, many = acc.shape[0], 12 // count
+
+    def piece_copy(i, source):
+        return pltpu.make_async_copy(source, a_buf.at[pl.ds(many * i, many)], a_sem.at[i])
 
     def tile_copy(k):
         return pltpu.make_async_copy(tiles.at[lax.div(at[8 + k], per)], b_buf.at[k], b_sem.at[k])
 
-    for i in range(6):
-        pair_copy(i, pairs[i]).start()
-        tile_copy(2 * i).start()
-        tile_copy(2 * i + 1).start()
+    for i in range(count):
+        piece_copy(i, pieces[i]).start()
+        for k in range(many):
+            tile_copy(many * i + k).start()
     acc[...] = jnp.zeros_like(acc)
 
     def body(i, carry):
@@ -111,8 +124,8 @@
 
         @pl.when(q == 0)
         def _():
-            for k in range(2):
-                pair_copy(2 * g + k, pairs[0]).wait()
+            for k in range(count // 3):
+                piece_copy((count // 3) * g + k, pieces[0]).wait()
 
         k0, k1 = 4 * g + q, 4 * g + 3 - q
         tile_copy(k0).wait()
@@ -125,24 +138,24 @@
     lax.fori_loop(0, 6, body, 0)
 
 
-def near_product(at, pairs, tiles, outs, weight):
-    m, w = pairs[0].shape[1:]
+def near_product(at, pieces, tiles, outs, weight):
+    m, w = pieces[0].shape[1:]
     many, _, n = tiles.shape
     return pl.pallas_call(
-        functools.partial(near_kernel, 16 // many),
+        functools.partial(near_kernel, 16 // many, len(pieces)),
         out_shape=jax.ShapeDtypeStruct((outs, m, n), F32),
-        in_specs=[SMEM] + [ANY] * 7,
+        in_specs=[SMEM] + [ANY] * len(pieces) + [HBM],
         out_specs=VMEM,
         scratch_shapes=[
             pltpu.VMEM((12, m, w), F32),
             pltpu.VMEM((12,) + tiles.shape[1:], F32),
-            pltpu.SemaphoreType.DMA((6,)),
+            pltpu.SemaphoreType.DMA((len(pieces),)),
             pltpu.SemaphoreType.DMA((12,)),
         ],
         compiler_params=params(40),
         cost_estimate=cost(weight * m, 12 * w, n, weight * 4 * w * (12 * m + many * n)),
         name="near",
-    )(at, *pairs, tiles)
+    )(at, *pieces, tiles)
 
 
 def far_sum(at, top, low, tiles, a_buf, b_buf, sem, per):
@@ -180,7 +193,7 @@
     return pl.pallas_call(
         update_kernel,
         out_shape=(jax.ShapeDtypeStruct((m, n), F32), jax.ShapeDtypeStruct((n, m), F32)),
-        in_specs=[SMEM, VMEM, ANY, ANY, ANY],
+        in_specs=[SMEM, VMEM, ANY, ANY, HBM],
         out_specs=(VMEM, VMEM),
         scratch_shapes=far_scratch(top, tiles),
         compiler_params=params(24),
@@ -202,7 +215,7 @@
     return pl.pallas_call(
         child_kernel,
         out_shape=jax.ShapeDtypeStruct(base.shape, F32),
-        in_specs=[SMEM, VMEM, ANY, ANY, ANY, VMEM],
+        in_specs=[SMEM, VMEM, ANY, ANY, HBM, VMEM],
         out_specs=VMEM,
         scratch_shapes=far_scratch(top, tiles),
         compiler_params=params(24),
@@ -237,7 +250,7 @@
     return pl.pallas_call(
         cross_kernel,
         out_shape=jax.ShapeDtypeStruct((m, w), F32),
-        in_specs=[SMEM] + [ANY] * 9,
+        in_specs=[SMEM, HBM] + [ANY] * 8,
         out_specs=VMEM,
         scratch_shapes=[
             pltpu.VMEM((4, m, 768), F32),
@@ -322,11 +335,11 @@
 def per_device(sigma_top, factor_cross, factor_inverse, block_inverse, ancestors):
     h, w = sigma_top.shape
     sub = h // 24
-    at = places()
+    at, at_turned = places(False), places(True)
 
     f = pick_rows(ancestors, spread(factor_cross))
-    inverse = lax.all_gather(factor_inverse, ROW, axis=0, tiled=True).reshape(16, w, w)
-    f_near, f_far = gather_cols(f)
+    inverse = lax.all_gather(after(factor_inverse, f), ROW, axis=0, tiled=True).reshape(16, w, w)
+    f_near, f_far = gather_cols(f, True)
 
     s = pick_rows(ancestors, spread(after(sigma_top, f)))
     s = lax.all_to_all(after(s, f_near[0]).reshape(16, -1, w), COL, 0, 0, tiled=True)
@@ -335,14 +348,13 @@
     acc = near_product(at, f_near, inverse, 1, W1)
     u, ut = update_product(at, acc, *f_far, inverse)
 
-    moved = lax.ppermute(ut, ALL, [(16 * r + c, 16 * (c // 2) + 2 * r + c % 2) for r in range(8) for c in range(16)])
-    u_near, u_far = gather_cols(moved)
+    u_near, u_far = gather_cols(turn(ut), False)
     u_tiles = gather_rows(u.reshape(NANC, sub, w))
 
     sigma = cross_product(at, after(s_all, u_near[0]), u_tiles)
-    sigma_all = lax.all_gather(after(sigma, u_near[2]), ROW, axis=0, tiled=True).reshape(8, w, w)
-    acc = near_product(at, u_near, sigma_all, 2, W2)
-    sigma_child = child_product(at, acc, *u_far, sigma_all, block_inverse)
+    sigma_all = lax.all_gather(sigma, ROW, axis=0, tiled=True).reshape(8, w, w)
+    acc = near_product(at_turned, u_near, sigma_all, 2, W2)
+    sigma_child = child_product(at_turned, acc, *u_far, sigma_all, block_inverse)
 
     sigma_cross = place_rows(ancestors, sigma_all.reshape(8, NANC, sub, w), h)
     return (sigma_cross, sigma_child)

time: 290 us -> 255 us (0.88)
  waiting for transfers between devices: 125 us -> 85.4 us
  blocking collectives: 26 us -> 46.2 us
  starting transfers between devices: 69.8 us -> 53.2 us
  local copies, waits for them, and re-layouts: 7.87 us -> 12.5 us
  Pallas kernels: 43.7 us -> 40.8 us
    ppermute x20 -> x18, waiting for transfers between devices: 77.6 us -> 52 us  [hop(): return lax.ppermute(x, ('core',) + COL, pairs)]
    all_to_all x0 -> x1, blocking collectives: none -> 23.8 us  [per_device(): lax.all_to_all(after(s, f_near[0]).reshape(16, -1, w), COL, 0, 0, tiled=T...]
    ppermute x4, starting transfers between devices: 17.2 us -> 1.78 us  [swap(): return lax.ppermute(x, 'core', [(0, 1), (1, 0)])]
    all_to_all x1 -> x0, starting transfers between devices: 7.43 us -> none  [per_device(): lax.all_to_all(after(s, f_near[0]).reshape(16, -1, w), COL, 0, 0, tiled=T...]
    all_to_all x1 -> x0, waiting for transfers between devices: 6.84 us -> none  [per_device(): lax.all_to_all(after(s, f_near[0]).reshape(16, -1, w), COL, 0, 0, tiled=T...]
    all_to_all x1, waiting for transfers between devices: 17.6 us -> 11.9 us  [spread(): lax.all_to_all(x.reshape(3, 8, sub, w), ROW, 1, 0, tiled=True)]
    ppermute x3, starting transfers between devices: 5.1 us -> 10.4 us  [step(): lax.ppermute(x, ROW, [(2 * i + c, 2 * ((i + 1 - 2 * c) % 4) + c) for i in...]
    all_to_all x1, blocking collectives: 26 us -> 22.4 us  [spread(): lax.all_to_all(x.reshape(3, 8, sub, w), ROW, 1, 0, tiled=True)]
  transfers between devices with their start and end apart: 33 -> 31, of which waited for: 19 -> 15; matrix products, arithmetic and copies ran while one was open for 1% -> 2% of each run, Pallas kernels for 13% -> 11%
where the time goes in v10:
time: 255 us; the launch traced here: 254 us
  waiting for transfers between devices  85.4 us (33%)
  starting transfers between devices  53.2 us (21%)
  blocking collectives  46.2 us (18%)
  Pallas kernels  40.8 us (16%)
  between operations  14.3 us (6%)
  local copies, waits for them, and re-layouts  12.5 us (5%)
    ppermute x18, waiting for transfers between devices, hop(): return lax.ppermute(x, ('core',) + COL, pairs)  52 us
    ppermute x18, starting transfers between devices, hop(): return lax.ppermute(x, ('core',) + COL, pairs)  30.3 us
    all_to_all x1, blocking collectives, per_device(): lax.all_to_all(after(s, f_near[0]).reshape(16, -1, w), COL, 0, 0, tiled=T...  23.8 us
    all_to_all x1, blocking collectives, spread(): lax.all_to_all(x.reshape(3, 8, sub, w), ROW, 1, 0, tiled=True)  22.4 us
    pallas_call x2, Pallas kernels, near_product(): pl.pallas_call(functools.partial(near_kernel, 16 // many, len(pieces)), o...  19.4 us
    all_to_all x1, waiting for transfers between devices, spread(): lax.all_to_all(x.reshape(3, 8, sub, w), ROW, 1, 0, tiled=True)  11.9 us
    ppermute x3, starting transfers between devices, step(): lax.ppermute(x, ROW, [(2 * i + c, 2 * ((i + 1 - 2 * c) % 4) + c) for i in...  10.4 us
    ppermute x3, waiting for transfers between devices, step(): lax.ppermute(x, ROW, [(2 * i + c, 2 * ((i + 1 - 2 * c) % 4) + c) for i in...  10.2 us
  transfers between devices with their start and end apart: 31, of which 15 were waited for; matrix products, arithmetic and copies ran while one was open for 2% of the time, Pallas kernels for 11%

profile of v10, /device:TPU:1, one launch (start us, length us, event | category | flops | bytes accessed | tf_op | source)
XLA Modules:
  0.0 254.1 jit_solution(16889274433581930204)
XLA Ops:
  7.2 1.3 copy.7
  8.6 22.4 %all_to_all.35 = f32[3,8,32,384]{3,2,0,1:T(8,128)S(1)} all-to-all(f32[3,8,32,384]{3,2,0,1:T(8,128)S(1)} %copy.7), channel_id=1, replica_groups=mesh['y'=4,'core'=2,'z'=4,'x'=4] {'y','core'}, dimensions={1} | all-to-all | bytes 2359296 | tf_op jit(solution)/shard_map/all_to_all | solution.py:270
  31.0 0.6 pick_rows.2
  31.6 1.7 collective-permute-start
  33.3 2.2 collective-permute-start.1
  35.5 1.1 copy.8
  36.6 3.7 %all-to-all-start.1 = ((f32[3,8,32,384]{3,2,0,1:T(8,128)}), f32[3,8,32,384]{3,2,0,1:T(8,128)S(1)}, u32[]{:S(2)}, u32[]{:S(2)}) async-start(f32[3,8,32,384]{3,2,0,1:T(8,128)} %copy.8), calls=%async_computation.1 | async-start | bytes 2359296 | tf_op jit(solution)/shard_map/all_to_all | solution.py:270
  40.3 2.7 %collective-permute-done = f32[384,384]{1,0:T(8,128)S(1)} collective-permute-done((f32[384,384]{1,0:T(8,128)S(1)}, f32[384,384]{1,0:T(8,128)S(1)}, u32[]{:S(2)}, u32[]{:S(2)}) %collective-permute-start) | collective-permute-done | bytes 589856 | tf_op jit(solution)/shard_map/ppermute | solution.py:58
  43.1 2.7 %collective-permute-start.3 = (f32[192,384]{1,0:T(8,128)S(1)}, f32[192,384]{1,0:T(8,128)S(1)}, u32[]{:S(2)}, u32[]{:S(2)}) collective-permute-start(f32[192,384]{1,0:T(8,128)S(1)} %slice.25), channel_id=1, source_target_pairs={{0,3},{1,0},{2,1},{3,2},{4,7},{5,4},{6,5},{7,6},{8,11},{9,8},{10,9... | collective-permute-start | bytes 884744 | tf_op jit(solution)/shard_map/ppermute | solution.py:58
  45.9 4.4 %collective-permute-done.2 = f32[192,384]{1,0:T(8,128)S(1)} collective-permute-done((f32[192,384]{1,0:T(8,128)S(1)}, f32[192,384]{1,0:T(8,128)S(1)}, u32[]{:S(2)}, u32[]{:S(2)}) %collective-permute-start.2) | collective-permute-done | bytes 294944 | tf_op jit(solution)/shard_map/ppermute | solution.py:58
  50.3 1.5 pad_maximum_fusion.refs_0_
  51.9 0.9 collective-permute-start.4
  52.8 1.8 collective-permute-start.5
  54.5 11.9 %all-to-all-done.1 = f32[3,8,32,384]{3,2,0,1:T(8,128)S(1)} async-done(((f32[3,8,32,384]{3,2,0,1:T(8,128)}), f32[3,8,32,384]{3,2,0,1:T(8,128)S(1)}, u32[]{:S(2)}, u32[]{:S(2)}) %all-to-all-start.1) | async-done | bytes 1179680 | tf_op jit(solution)/shard_map/all_to_all | solution.py:270
  66.4 0.6 pick_rows.3
  67.0 23.8 %all_to_all.36.x = f32[16,24,384]{2,1,0:T(8,128)S(1)} all-to-all(f32[16,24,384]{2,1,0:T(8,128)S(1)} %bitcast.83), channel_id=1, replica_groups=mesh['y'=4,'core'=2,'z'=4,'x'=4] {'z','x'}, dimensions={0} | all-to-all | bytes 1179648 | tf_op jit(solution)/shard_map/all_to_all | solution.py:345
  90.8 1.4 pick_cols.1
  92.4 0.1 stack.188.at
  92.6 1.2 slice.26
  93.8 0.6 copy-done.2
  94.4 0.9 collective-permute-start.6
  95.3 1.4 slice.27
  96.8 1.7 collective-permute-start.7
  98.5 1.8 copy-done.3
  100.3 10.0 %near.2.acc = f32[1,384,384]{2,1,0:T(8,128)S(1)} custom-call(s32[24]{0:T(128)S(1)} %stack.188.at, f32[4,384,384]{2,1,0:T(8,128)} %pad_maximum_fusion.refs_0_, f32[4,384,384]{2,1,0:T(8,128)S(1)} %copy-done.3, f32[4,384,384]{2,1,0:T(8,128)} %collective-permute-done.5.refs_2_, f32[16,384,384]{2,1,0:T(8,128)} %bitcast.74), custom_call_target="tpu_custom_call" | custom-call | flops 48922361856 | bytes 198180864 | tf_op jit(solution)/shard_map/near/pallas_call | solution.py:144
  110.3 0.9 collective-permute-done.6.top
  111.2 2.3 collective-permute-done.7.low
  113.5 3.7 %update.1 = (f32[384,384]{1,0:T(8,128)S(1)}, f32[384,384]{1,0:T(8,128)S(1)}) custom-call(s32[24]{0:T(128)S(1)} %stack.188.at, f32[1,384,384]{2,1,0:T(8,128)S(1)} %near.2.acc, f32[2,384,384]{2,1,0:T(8,128)S(1)} %collective-permute-done.6.top, f32[2,384,384]{2,1,0:T(8,128)S(1)} %collective-permute-done.7.low, f32[16,384,384]{2,1,0:T(8,128)S(1)} %bitcast.77), custom_call_target="tpu_custom_call" | custom-call | flops 1358954496 | bytes 2359296 | tf_op jit(solution)/shard_map/update/pallas_call | solution.py:193
  117.3 6.2 %collective-permute-start.8 = (f32[384,384]{1,0:T(8,128)S(1)}, f32[384,384]{1,0:T(8,128)S(1)}, u32[]{:S(2)}, u32[]{:S(2)}) collective-permute-start(f32[384,384]{1,0:T(8,128)S(1)} %get-tuple-element.13), channel_id=1, source_target_pairs={{0,0},{1,1},{2,16},{3,17},{4,4},{5,5},{6,20},{7,21},{8,8},{9,9},{1... | collective-permute-start | bytes 1769480 | tf_op jit(solution)/shard_map/ppermute | solution.py:79
  123.5 3.5 %collective-permute-start.14 = (f32[12,32,384]{2,1,0:T(8,128)S(1)}, f32[12,32,384]{2,1,0:T(8,128)S(1)}, u32[]{:S(2)}, u32[]{:S(2)}) collective-permute-start(f32[12,32,384]{2,1,0:T(8,128)S(1)} %bitcast.84), channel_id=1, source_target_pairs={{0,32},{16,112},{32,64},{48,16},{64,96},{80,48},{96,0},{112,80},{1... | collective-permute-start | bytes 1769480 | tf_op jit(solution)/shard_map/ppermute | solution.py:37
  126.9 4.1 %collective-permute-done.8 = f32[384,384]{1,0:T(8,128)S(1)} collective-permute-done((f32[384,384]{1,0:T(8,128)S(1)}, f32[384,384]{1,0:T(8,128)S(1)}, u32[]{:S(2)}, u32[]{:S(2)}) %collective-permute-start.8) | collective-permute-done | bytes 589856 | tf_op jit(solution)/shard_map/ppermute | solution.py:79
  131.0 0.7 collective-permute-start.9
  131.7 2.0 collective-permute-done.14.refs_1_
  133.8 4.5 %collective-permute-start.15 = (f32[12,32,384]{2,1,0:T(8,128)S(1)}, f32[12,32,384]{2,1,0:T(8,128)}, u32[]{:S(2)}, u32[]{:S(2)}) collective-permute-start(f32[12,32,384]{2,1,0:T(8,128)S(1)} %collective-permute-done.14.refs_1_), channel_id=1, source_target_pairs={{0,32},{16,112},{32,64},{48,16},{64,96},{80,48},{96,0},{112,80},{1... | collective-permute-start | bytes 1769480 | tf_op jit(solution)/shard_map/ppermute | solution.py:37
  138.3 3.5 %collective-permute-start.10 = (f32[384,384]{1,0:T(8,128)S(1)}, f32[384,384]{1,0:T(8,128)S(1)}, u32[]{:S(2)}, u32[]{:S(2)}) collective-permute-start(f32[384,384]{1,0:T(8,128)S(1)} %collective-permute-done.9), channel_id=1, source_target_pairs={{0,1},{1,2},{2,3},{3,0},{4,5},{5,6},{6,7},{7,4},{8,9},{9,10},{10,1... | collective-permute-start | bytes 1769480 | tf_op jit(solution)/shard_map/ppermute | solution.py:58
  141.8 6.6 %collective-permute-start.11 = (f32[384,384]{1,0:T(8,128)S(1)}, f32[384,384]{1,0:T(8,128)S(1)}, u32[]{:S(2)}, u32[]{:S(2)}) collective-permute-start(f32[384,384]{1,0:T(8,128)S(1)} %collective-permute-done.9), channel_id=1, source_target_pairs={{0,3},{1,0},{2,1},{3,2},{4,7},{5,4},{6,5},{7,6},{8,11},{9,8},{10,9... | collective-permute-start | bytes 1769480 | tf_op jit(solution)/shard_map/ppermute | solution.py:58
  148.4 8.1 %collective-permute-done.15.refs_2_ = f32[12,32,384]{2,1,0:T(8,128)} collective-permute-done((f32[12,32,384]{2,1,0:T(8,128)S(1)}, f32[12,32,384]{2,1,0:T(8,128)}, u32[]{:S(2)}, u32[]{:S(2)}) %collective-permute-start.15) | collective-permute-done | bytes 589856 | tf_op jit(solution)/shard_map/ppermute | solution.py:37
  156.5 2.3 collective-permute-start.16
  158.8 9.8 %collective-permute-done.10 = f32[384,384]{1,0:T(8,128)S(1)} collective-permute-done((f32[384,384]{1,0:T(8,128)S(1)}, f32[384,384]{1,0:T(8,128)S(1)}, u32[]{:S(2)}, u32[]{:S(2)}) %collective-permute-start.10) | collective-permute-done | bytes 589856 | tf_op jit(solution)/shard_map/ppermute | solution.py:58
  168.7 0.1 collective-permute-start.17
  168.8 0.5 collective-permute-start.18
  169.3 0.1 collective-permute-start.19
  169.4 1.1 collective-permute-start.20
  170.6 4.9 %collective-permute-done.12 = f32[192,384]{1,0:T(8,128)S(1)} collective-permute-done((f32[192,384]{1,0:T(8,128)S(1)}, f32[192,384]{1,0:T(8,128)S(1)}, u32[]{:S(2)}, u32[]{:S(2)}) %collective-permute-start.12) | collective-permute-done | bytes 294944 | tf_op jit(solution)/shard_map/ppermute | solution.py:58
  175.6 0.1 pad_maximum_fusion.1.refs_0_
  175.7 5.4 %collective-permute-done.13 = f32[192,384]{1,0:T(8,128)S(1)} collective-permute-done((f32[192,384]{1,0:T(8,128)S(1)}, f32[192,384]{1,0:T(8,128)S(1)}, u32[]{:S(2)}, u32[]{:S(2)}) %collective-permute-start.13) | collective-permute-done | bytes 294944 | tf_op jit(solution)/shard_map/ppermute | solution.py:58
  181.1 0.1 pad_maximum_fusion.2.refs_1_
  181.3 2.3 copy-done.5
  183.6 7.9 %cross.1 = f32[384,384]{1,0:T(8,128)} custom-call(s32[24]{0:T(128)S(1)} %stack.188.at, f32[384,3072]{1,0:T(8,128)S(1)} %copy-done.5, f32[12,32,384]{2,1,0:T(8,128)S(1)} %bitcast.86, f32[12,32,384]{2,1,0:T(8,128)S(1)} %collective-permute-done.14.refs_1_, f32[12,32,384]{2,1,0:T(8,128)} %collective-permute-done.15.refs_2_, ...), custom_call_target="tpu_custom_call" | custom-call | flops 2717908992 | bytes 9437184 | tf_op jit(solution)/shard_map/cross/pallas_call | solution.py:250
  191.5 1.7 collective-permute-start.21
  193.2 1.0 collective-permute-start.24
  194.3 0.4 collective-permute-start.22
  194.7 2.3 collective-permute-start.23
  197.0 0.1 stack.215.at
  197.1 11.2 %collective-permute-done.21.refs_2_ = f32[2,384,384]{2,1,0:T(8,128)} collective-permute-done((f32[2,384,384]{2,1,0:T(8,128)S(1)}, f32[2,384,384]{2,1,0:T(8,128)}, u32[]{:S(2)}, u32[]{:S(2)}) %collective-permute-start.21) | collective-permute-done | bytes 1179680 | tf_op jit(solution)/shard_map/ppermute | solution.py:58
  208.3 0.4 collective-permute-start.25
  208.7 2.3 collective-permute-start.26
  210.9 10.0 %collective-permute-done.22.refs_3_ = f32[2,384,384]{2,1,0:T(8,128)} collective-permute-done((f32[2,384,384]{2,1,0:T(8,128)S(1)}, f32[2,384,384]{2,1,0:T(8,128)}, u32[]{:S(2)}, u32[]{:S(2)}) %collective-permute-start.22) | collective-permute-done | bytes 1179680 | tf_op jit(solution)/shard_map/ppermute | solution.py:58
  220.9 0.4 collective-permute-done.23.refs_4_
  221.3 7.1 %all-gather.8.cloned.1.call-done = f32[3072,384]{1,0:T(8,128)} async-done(((f32[384,384]{1,0:T(8,128)}), f32[3072,384]{1,0:T(8,128)}) %all-gather.8.cloned.1.call-update) | async-done | bytes 4718608 | tf_op jit(solution)/shard_map/all_gather | solution.py:355
  228.4 2.3 copy-done
  230.8 9.4 %near.3.acc = f32[2,384,384]{2,1,0:T(8,128)S(1)} custom-call(s32[24]{0:T(128)S(1)} %stack.215.at, f32[2,384,384]{2,1,0:T(8,128)S(1)} %pad_maximum_fusion.1.refs_0_, f32[2,384,384]{2,1,0:T(8,128)S(1)} %pad_maximum_fusion.2.refs_1_, f32[2,384,384]{2,1,0:T(8,128)} %collective-permute-done.21.refs_2_, f32[2,384,384]{2,1,0:T(8,128)} %collective-permute-done.22.refs_3_, ...), custom_call_target="tpu_custom_call" | custom-call | flops 48922361856 | bytes 141557760 | tf_op jit(solution)/shard_map/near/pallas_call | solution.py:144
  240.2 2.0 place_rows.1
  242.3 5.3 %child.1 = f32[768,384]{1,0:T(8,128)} custom-call(s32[24]{0:T(128)S(1)} %stack.215.at, f32[2,384,384]{2,1,0:T(8,128)S(1)} %near.3.acc, f32[2,384,384]{2,1,0:T(8,128)S(1)} %collective-permute-done.25.top, f32[2,384,384]{2,1,0:T(8,128)} %collective-permute-done.26.low, f32[8,384,384]{2,1,0:T(8,128)S(1)} %bitcast.73, f32[768,384]{1,0:T(8,128)S(1)} %copy-done.1), custom_call_target="tpu_custom_call" | custom-call | flops 1358954496 | bytes 3538944 | tf_op jit(solution)/shard_map/child/pallas_call | solution.py:215
  (48 shorter events, 0.6 us)
Async XLA Ops:
  7.2 91.3 %all-gather.6.cloned.1.call-start = ((), (), s32[]{:S(2)}) async-start(), calls=%async_computation.4 | async-start | bytes 10616832 | tf_op jit(solution)/shard_map/all_gather | solution.py:341
  8.6 22.4 %copy-start.4 = (s32[12]{0:T(128)S(1)}, s32[12]{0:T(128)}, u32[]{:S(2)}) copy-start(s32[12]{0:T(128)} %anc.7) | copy-start | bytes 148
  31.0 4.5 %copy-start.6 = (f32[768,384]{1,0:T(8,128)S(1)}, f32[768,384]{1,0:T(8,128)}, u32[]{:S(2)}) copy-start(f32[768,384]{1,0:T(8,128)} %param.5) | copy-start | bytes 3538948
  31.6 11.4 %collective-permute-start = (f32[384,384]{1,0:T(8,128)S(1)}, f32[384,384]{1,0:T(8,128)S(1)}, u32[]{:S(2)}, u32[]{:S(2)}) collective-permute-start(f32[384,384]{1,0:T(8,128)S(1)} %bitcast.80), channel_id=1, source_target_pairs={{0,1},{1,2},{2,3},{3,0},{4,5},{5,6},{6,7},{7,4},{8,9},{9,10},{10,1... | collective-permute-start | bytes 1769480 | tf_op jit(solution)/shard_map/ppermute | solution.py:58
  33.3 9.8 %collective-permute-start.1 = (f32[384,384]{1,0:T(8,128)S(1)}, f32[384,384]{1,0:T(8,128)S(1)}, u32[]{:S(2)}, u32[]{:S(2)}) collective-permute-start(f32[384,384]{1,0:T(8,128)S(1)} %bitcast.81), channel_id=1, source_target_pairs={{0,3},{1,0},{2,1},{3,2},{4,7},{5,4},{6,5},{7,6},{8,11},{9,8},{10,9... | collective-permute-start | bytes 1769480 | tf_op jit(solution)/shard_map/ppermute | solution.py:58
  36.6 29.8 %all-to-all-start.1 = ((f32[3,8,32,384]{3,2,0,1:T(8,128)}), f32[3,8,32,384]{3,2,0,1:T(8,128)S(1)}, u32[]{:S(2)}, u32[]{:S(2)}) async-start(f32[3,8,32,384]{3,2,0,1:T(8,128)} %copy.8), calls=%async_computation.1 | async-start | bytes 2359296 | tf_op jit(solution)/shard_map/all_to_all | solution.py:270
  40.3 140.9 %all-gather.4.cloned.1.call-start = ((), (), s32[]{:S(2)}) async-start(), calls=%async_computation.3 | async-start | bytes 5013504 | tf_op jit(solution)/shard_map/all_gather | solution.py:346
  43.0 7.3 %collective-permute-start.2 = (f32[192,384]{1,0:T(8,128)S(1)}, f32[192,384]{1,0:T(8,128)S(1)}, u32[]{:S(2)}, u32[]{:S(2)}) collective-permute-start(f32[192,384]{1,0:T(8,128)S(1)} %slice.24), channel_id=1, source_target_pairs={{0,1},{1,2},{2,3},{3,0},{4,5},{5,6},{6,7},{7,4},{8,9},{9,10},{10,1... | collective-permute-start | bytes 884744 | tf_op jit(solution)/shard_map/ppermute | solution.py:58
  43.1 7.1 %collective-permute-start.3 = (f32[192,384]{1,0:T(8,128)S(1)}, f32[192,384]{1,0:T(8,128)S(1)}, u32[]{:S(2)}, u32[]{:S(2)}) collective-permute-start(f32[192,384]{1,0:T(8,128)S(1)} %slice.25), channel_id=1, source_target_pairs={{0,3},{1,0},{2,1},{3,2},{4,7},{5,4},{6,5},{7,6},{8,11},{9,8},{10,9... | collective-permute-start | bytes 884744 | tf_op jit(solution)/shard_map/ppermute | solution.py:58
  51.9 40.7 %collective-permute-start.4 = (f32[4,384,384]{2,1,0:T(8,128)}, f32[4,384,384]{2,1,0:T(8,128)S(1)}, u32[]{:S(2)}, u32[]{:S(2)}) collective-permute-start(f32[4,384,384]{2,1,0:T(8,128)} %pad_maximum_fusion.refs_0_), channel_id=1, source_target_pairs={{0,4},{1,5},{2,6},{3,7},{4,8},{5,9},{6,10},{7,11},{8,12},{9,13},{1... | collective-permute-start | bytes 7077896 | tf_op jit(solution)/shard_map/ppermute | solution.py:58
  52.8 42.6 %collective-permute-start.5 = (f32[4,384,384]{2,1,0:T(8,128)}, f32[4,384,384]{2,1,0:T(8,128)}, u32[]{:S(2)}, u32[]{:S(2)}) collective-permute-start(f32[4,384,384]{2,1,0:T(8,128)} %pad_maximum_fusion.refs_0_), channel_id=1, source_target_pairs={{0,12},{1,13},{2,14},{3,15},{4,0},{5,1},{6,2},{7,3},{8,4},{9,5},{1... | collective-permute-start | bytes 7077896 | tf_op jit(solution)/shard_map/ppermute | solution.py:58
  92.2 136.3 %all-gather.8.cloned.1.call-start = ((), (), s32[]{:S(2)}) async-start(), calls=%async_computation.5 | async-start | bytes 5308416 | tf_op jit(solution)/shard_map/all_gather | solution.py:355
  92.6 1.8 copy-start.2
  94.4 16.8 %collective-permute-start.6 = (f32[2,384,384]{2,1,0:T(8,128)}, f32[2,384,384]{2,1,0:T(8,128)S(1)}, u32[]{:S(2)}, u32[]{:S(2)}) collective-permute-start(f32[2,384,384]{2,1,0:T(8,128)} %slice.26), channel_id=1, source_target_pairs={{0,4},{1,5},{2,6},{3,7},{4,8},{5,9},{6,10},{7,11},{8,12},{9,13},{1... | collective-permute-start | bytes 3538952 | tf_op jit(solution)/shard_map/ppermute | solution.py:58
  96.8 16.7 %collective-permute-start.7 = (f32[2,384,384]{2,1,0:T(8,128)S(1)}, f32[2,384,384]{2,1,0:T(8,128)S(1)}, u32[]{:S(2)}, u32[]{:S(2)}) collective-permute-start(f32[2,384,384]{2,1,0:T(8,128)S(1)} %slice.27), channel_id=1, source_target_pairs={{0,12},{1,13},{2,14},{3,15},{4,0},{5,1},{6,2},{7,3},{8,4},{9,5},{1... | collective-permute-start | bytes 3538952 | tf_op jit(solution)/shard_map/ppermute | solution.py:58
  98.5 15.0 %slice-start = ((s8[9437184]{0:T(1024)(128)(4,1)}), s8[4194304]{0:T(1024)(128)(4,1)S(1)}, s32[]{:S(2)}) async-start(s8[9437184]{0:T(1024)(128)(4,1)} %bitcast.75), calls=%async_computation.6 | async-start | bytes 8388608
  98.5 1.8 copy-start.3
  100.3 13.2 %slice-start.1 = ((s8[9437184]{0:T(1024)(128)(4,1)}), s8[4194304]{0:T(1024)(128)(4,1)S(1)}, s32[]{:S(2)}) async-start(s8[9437184]{0:T(1024)(128)(4,1)} %bitcast.75), calls=%async_computation.7 | async-start | bytes 8388608
  100.3 13.2 %slice-start.2 = ((s8[9437184]{0:T(1024)(128)(4,1)}), s8[1048576]{0:T(1024)(128)(4,1)S(1)}, s32[]{:S(2)}) async-start(s8[9437184]{0:T(1024)(128)(4,1)} %bitcast.75), calls=%async_computation.8 | async-start | bytes 2097152
  117.3 13.8 %collective-permute-start.8 = (f32[384,384]{1,0:T(8,128)S(1)}, f32[384,384]{1,0:T(8,128)S(1)}, u32[]{:S(2)}, u32[]{:S(2)}) collective-permute-start(f32[384,384]{1,0:T(8,128)S(1)} %get-tuple-element.13), channel_id=1, source_target_pairs={{0,0},{1,1},{2,16},{3,17},{4,4},{5,5},{6,20},{7,21},{8,8},{9,9},{1... | collective-permute-start | bytes 1769480 | tf_op jit(solution)/shard_map/ppermute | solution.py:79
  123.5 10.3 %collective-permute-start.14 = (f32[12,32,384]{2,1,0:T(8,128)S(1)}, f32[12,32,384]{2,1,0:T(8,128)S(1)}, u32[]{:S(2)}, u32[]{:S(2)}) collective-permute-start(f32[12,32,384]{2,1,0:T(8,128)S(1)} %bitcast.84), channel_id=1, source_target_pairs={{0,32},{16,112},{32,64},{48,16},{64,96},{80,48},{96,0},{112,80},{1... | collective-permute-start | bytes 1769480 | tf_op jit(solution)/shard_map/ppermute | solution.py:37
  131.0 7.3 %collective-permute-start.9 = (f32[384,384]{1,0:T(8,128)S(1)}, f32[384,384]{1,0:T(8,128)S(1)}, u32[]{:S(2)}, u32[]{:S(2)}) collective-permute-start(f32[384,384]{1,0:T(8,128)S(1)} %collective-permute-done.8), channel_id=1, source_target_pairs={{0,0},{1,1},{2,2},{3,3},{4,36},{5,37},{6,38},{7,39},{8,72},{9,73},... | collective-permute-start | bytes 1769480 | tf_op jit(solution)/shard_map/ppermute | solution.py:80
  133.8 22.7 %collective-permute-start.15 = (f32[12,32,384]{2,1,0:T(8,128)S(1)}, f32[12,32,384]{2,1,0:T(8,128)}, u32[]{:S(2)}, u32[]{:S(2)}) collective-permute-start(f32[12,32,384]{2,1,0:T(8,128)S(1)} %collective-permute-done.14.refs_1_), channel_id=1, source_target_pairs={{0,32},{16,112},{32,64},{48,16},{64,96},{80,48},{96,0},{112,80},{1... | collective-permute-start | bytes 1769480 | tf_op jit(solution)/shard_map/ppermute | solution.py:37
  138.3 30.3 %collective-permute-start.10 = (f32[384,384]{1,0:T(8,128)S(1)}, f32[384,384]{1,0:T(8,128)S(1)}, u32[]{:S(2)}, u32[]{:S(2)}) collective-permute-start(f32[384,384]{1,0:T(8,128)S(1)} %collective-permute-done.9), channel_id=1, source_target_pairs={{0,1},{1,2},{2,3},{3,0},{4,5},{5,6},{6,7},{7,4},{8,9},{9,10},{10,1... | collective-permute-start | bytes 1769480 | tf_op jit(solution)/shard_map/ppermute | solution.py:58
  141.8 27.6 %collective-permute-start.11 = (f32[384,384]{1,0:T(8,128)S(1)}, f32[384,384]{1,0:T(8,128)S(1)}, u32[]{:S(2)}, u32[]{:S(2)}) collective-permute-start(f32[384,384]{1,0:T(8,128)S(1)} %collective-permute-done.9), channel_id=1, source_target_pairs={{0,3},{1,0},{2,1},{3,2},{4,7},{5,4},{6,5},{7,6},{8,11},{9,8},{10,9... | collective-permute-start | bytes 1769480 | tf_op jit(solution)/shard_map/ppermute | solution.py:58
  156.5 13.0 %collective-permute-start.16 = (f32[12,32,384]{2,1,0:T(8,128)}, f32[12,32,384]{2,1,0:T(8,128)}, u32[]{:S(2)}, u32[]{:S(2)}) collective-permute-start(f32[12,32,384]{2,1,0:T(8,128)} %collective-permute-done.15.refs_2_), channel_id=1, source_target_pairs={{0,32},{16,112},{32,64},{48,16},{64,96},{80,48},{96,0},{112,80},{1... | collective-permute-start | bytes 1769480 | tf_op jit(solution)/shard_map/ppermute | solution.py:37
  168.7 6.9 %collective-permute-start.12 = (f32[192,384]{1,0:T(8,128)S(1)}, f32[192,384]{1,0:T(8,128)S(1)}, u32[]{:S(2)}, u32[]{:S(2)}) collective-permute-start(f32[192,384]{1,0:T(8,128)S(1)} %slice.28), channel_id=1, source_target_pairs={{0,1},{1,2},{2,3},{3,0},{4,5},{5,6},{6,7},{7,4},{8,9},{9,10},{10,1... | collective-permute-start | bytes 884744 | tf_op jit(solution)/shard_map/ppermute | solution.py:58
  168.7 12.5 %collective-permute-start.17 = (f32[12,32,384]{2,1,0:T(8,128)S(1)}, f32[12,32,384]{2,1,0:T(8,128)}, u32[]{:S(2)}, u32[]{:S(2)}) collective-permute-start(f32[12,32,384]{2,1,0:T(8,128)S(1)} %bitcast.85), channel_id=1, source_target_pairs={{0,16},{16,0},{1,17},{17,1},{2,18},{18,2},{3,19},{19,3},{4,20},{20... | collective-permute-start | bytes 1769480 | tf_op jit(solution)/shard_map/ppermute | solution.py:41
  168.8 12.4 %collective-permute-start.18 = (f32[12,32,384]{2,1,0:T(8,128)S(1)}, f32[12,32,384]{2,1,0:T(8,128)}, u32[]{:S(2)}, u32[]{:S(2)}) collective-permute-start(f32[12,32,384]{2,1,0:T(8,128)S(1)} %collective-permute-done.14.refs_1_), channel_id=1, source_target_pairs={{0,16},{16,0},{1,17},{17,1},{2,18},{18,2},{3,19},{19,3},{4,20},{20... | collective-permute-start | bytes 1769480 | tf_op jit(solution)/shard_map/ppermute | solution.py:41
  169.3 11.9 %collective-permute-start.19 = (f32[12,32,384]{2,1,0:T(8,128)}, f32[12,32,384]{2,1,0:T(8,128)}, u32[]{:S(2)}, u32[]{:S(2)}) collective-permute-start(f32[12,32,384]{2,1,0:T(8,128)} %collective-permute-done.15.refs_2_), channel_id=1, source_target_pairs={{0,16},{16,0},{1,17},{17,1},{2,18},{18,2},{3,19},{19,3},{4,20},{20... | collective-permute-start | bytes 1769480 | tf_op jit(solution)/shard_map/ppermute | solution.py:41
  169.4 11.8 %collective-permute-start.20 = (f32[12,32,384]{2,1,0:T(8,128)}, f32[12,32,384]{2,1,0:T(8,128)}, u32[]{:S(2)}, u32[]{:S(2)}) collective-permute-start(f32[12,32,384]{2,1,0:T(8,128)} %collective-permute-done.16.refs_3_), channel_id=1, source_target_pairs={{0,16},{16,0},{1,17},{17,1},{2,18},{18,2},{3,19},{19,3},{4,20},{20... | collective-permute-start | bytes 1769480 | tf_op jit(solution)/shard_map/ppermute | solution.py:41
  175.5 5.6 %collective-permute-start.13 = (f32[192,384]{1,0:T(8,128)S(1)}, f32[192,384]{1,0:T(8,128)S(1)}, u32[]{:S(2)}, u32[]{:S(2)}) collective-permute-start(f32[192,384]{1,0:T(8,128)S(1)} %slice.29), channel_id=1, source_target_pairs={{0,3},{1,0},{2,1},{3,2},{4,7},{5,4},{6,5},{7,6},{8,11},{9,8},{10,9... | collective-permute-start | bytes 884744 | tf_op jit(solution)/shard_map/ppermute | solution.py:58
  181.3 2.3 copy-start.5
  191.5 16.7 %collective-permute-start.21 = (f32[2,384,384]{2,1,0:T(8,128)S(1)}, f32[2,384,384]{2,1,0:T(8,128)}, u32[]{:S(2)}, u32[]{:S(2)}) collective-permute-start(f32[2,384,384]{2,1,0:T(8,128)S(1)} %pad_maximum_fusion.1.refs_0_), channel_id=1, source_target_pairs={{0,4},{1,5},{2,6},{3,7},{4,8},{5,9},{6,10},{7,11},{8,12},{9,13},{1... | collective-permute-start | bytes 3538952 | tf_op jit(solution)/shard_map/ppermute | solution.py:58
  193.2 15.5 %collective-permute-start.24 = (f32[2,384,384]{2,1,0:T(8,128)S(1)}, f32[2,384,384]{2,1,0:T(8,128)}, u32[]{:S(2)}, u32[]{:S(2)}) collective-permute-start(f32[2,384,384]{2,1,0:T(8,128)S(1)} %pad_maximum_fusion.2.refs_1_), channel_id=1, source_target_pairs={{0,12},{1,13},{2,14},{3,15},{4,0},{5,1},{6,2},{7,3},{8,4},{9,5},{1... | collective-permute-start | bytes 3538952 | tf_op jit(solution)/shard_map/ppermute | solution.py:58
  194.3 26.6 %collective-permute-start.22 = (f32[2,384,384]{2,1,0:T(8,128)S(1)}, f32[2,384,384]{2,1,0:T(8,128)}, u32[]{:S(2)}, u32[]{:S(2)}) collective-permute-start(f32[2,384,384]{2,1,0:T(8,128)S(1)} %pad_maximum_fusion.2.refs_1_), channel_id=1, source_target_pairs={{0,4},{1,5},{2,6},{3,7},{4,8},{5,9},{6,10},{7,11},{8,12},{9,13},{1... | collective-permute-start | bytes 3538952 | tf_op jit(solution)/shard_map/ppermute | solution.py:58
  194.7 26.6 %collective-permute-start.23 = (f32[2,384,384]{2,1,0:T(8,128)S(1)}, f32[2,384,384]{2,1,0:T(8,128)}, u32[]{:S(2)}, u32[]{:S(2)}) collective-permute-start(f32[2,384,384]{2,1,0:T(8,128)S(1)} %pad_maximum_fusion.1.refs_0_), channel_id=1, source_target_pairs={{0,12},{1,13},{2,14},{3,15},{4,0},{5,1},{6,2},{7,3},{8,4},{9,5},{1... | collective-permute-start | bytes 3538952 | tf_op jit(solution)/shard_map/ppermute | solution.py:58
  208.3 34.0 %collective-permute-start.25 = (f32[2,384,384]{2,1,0:T(8,128)}, f32[2,384,384]{2,1,0:T(8,128)S(1)}, u32[]{:S(2)}, u32[]{:S(2)}) collective-permute-start(f32[2,384,384]{2,1,0:T(8,128)} %collective-permute-done.21.refs_2_), channel_id=1, source_target_pairs={{0,4},{1,5},{2,6},{3,7},{4,8},{5,9},{6,10},{7,11},{8,12},{9,13},{1... | collective-permute-start | bytes 3538952 | tf_op jit(solution)/shard_map/ppermute | solution.py:58
  208.7 33.5 %collective-permute-start.26 = (f32[2,384,384]{2,1,0:T(8,128)}, f32[2,384,384]{2,1,0:T(8,128)}, u32[]{:S(2)}, u32[]{:S(2)}) collective-permute-start(f32[2,384,384]{2,1,0:T(8,128)} %collective-permute-done.24.refs_5_), channel_id=1, source_target_pairs={{0,12},{1,13},{2,14},{3,15},{4,0},{5,1},{6,2},{7,3},{8,4},{9,5},{1... | collective-permute-start | bytes 3538952 | tf_op jit(solution)/shard_map/ppermute | solution.py:58
  228.4 2.3 copy-start
  240.2 2.0 copy-start.1
Sparse Core Ops, SparseCore 0:
  31.7 65.2 all-gather.5
  99.7 69.7 all-gather.3
  191.7 36.7 all-gather.7

commit v11 on v10

--- a/solution.py
+++ b/solution.py
@@ -103,7 +103,26 @@
     return mul(a_hi, b_hi) + (mul(a_hi, b_lo) + mul(a_lo, b_hi))
 
 
-def near_kernel(per, count, at, *refs):
+def near_child_kernel(per, count, anc, first, at, *refs):
+    tiles, rows, sem = refs[count], refs[count + 2], refs[-1]
+    blocks, _, sub, _ = rows.shape
+    copies, living = [], []
+    for b in range(blocks):
+        hits = [jnp.where(anc[i] == first[0] + b, 1, 0) for i in range(NANC)]
+        index = sum(i * hit for i, hit in enumerate(hits))
+        living.append(sum(hits))
+        source = tiles.at[:, pl.ds(pl.multiple_of(index * sub, 8), sub)]
+        copies.append(pltpu.make_async_copy(source, rows.at[b], sem.at[b]))
+    near_kernel(per, count, at, *refs[: count + 2], *refs[count + 3 : -1], others=copies)
+    for b in range(blocks):
+        copies[b].wait()
+
+        @pl.when(living[b] == 0)
+        def _():
+            rows[b] = jnp.zeros_like(rows[b])
+
+
+def near_kernel(per, count, at, *refs, others=()):
     pieces, tiles, acc, (a_buf, b_buf, a_sem, b_sem) = refs[:count], refs[count], refs[count + 1], refs[count + 2 :]
     outs, many = acc.shape[0], 12 // count
 
@@ -117,6 +136,8 @@
         piece_copy(i, pieces[i]).start()
         for k in range(many):
             tile_copy(many * i + k).start()
+    for copy in others:
+        copy.start()
     acc[...] = jnp.zeros_like(acc)
 
     def body(i, carry):
@@ -138,24 +159,29 @@
     lax.fori_loop(0, 6, body, 0)
 
 
-def near_product(at, pieces, tiles, outs, weight):
+def near_product(at, pieces, tiles, outs, weight, ancestors=None):
     m, w = pieces[0].shape[1:]
     many, _, n = tiles.shape
-    return pl.pallas_call(
-        functools.partial(near_kernel, 16 // many, len(pieces)),
-        out_shape=jax.ShapeDtypeStruct((outs, m, n), F32),
-        in_specs=[SMEM] + [ANY] * len(pieces) + [HBM],
-        out_specs=VMEM,
+    kernel, extra, out_shape, more = near_kernel, (), [jax.ShapeDtypeStruct((outs, m, n), F32)], []
+    if ancestors is not None:
+        kernel, extra = near_child_kernel, (ancestors, (3 * lax.axis_index(ROW)).astype(jnp.int32).reshape(1))
+        out_shape += [jax.ShapeDtypeStruct((3, many, m // NANC, n), F32)]
+        more = [pltpu.SemaphoreType.DMA((3,))]
+    return pl.pallas_call(
+        functools.partial(kernel, 16 // many, len(pieces)),
+        out_shape=out_shape,
+        in_specs=[SMEM] * (1 + len(extra)) + [ANY] * len(pieces) + [HBM],
+        out_specs=[VMEM] * len(out_shape),
         scratch_shapes=[
             pltpu.VMEM((12, m, w), F32),
             pltpu.VMEM((12,) + tiles.shape[1:], F32),
             pltpu.SemaphoreType.DMA((len(pieces),)),
             pltpu.SemaphoreType.DMA((12,)),
-        ],
-        compiler_params=params(40),
+        ] + more,
+        compiler_params=params(56),
         cost_estimate=cost(weight * m, 12 * w, n, weight * 4 * w * (12 * m + many * n)),
         name="near",
-    )(at, *pieces, tiles)
+    )(*extra, at, *pieces, tiles)
 
 
 def far_sum(at, top, low, tiles, a_buf, b_buf, sem, per):
@@ -196,7 +222,7 @@
         in_specs=[SMEM, VMEM, ANY, ANY, HBM],
         out_specs=(VMEM, VMEM),
         scratch_shapes=far_scratch(top, tiles),
-        compiler_params=params(24),
+        compiler_params=params(56),
         cost_estimate=cost(m, 4 * top.shape[2], n, 16 * m * n),
         name="update",
     )(at, acc, top, low, tiles)
@@ -218,7 +244,7 @@
         in_specs=[SMEM, VMEM, ANY, ANY, HBM, VMEM],
         out_specs=VMEM,
         scratch_shapes=far_scratch(top, tiles),
-        compiler_params=params(24),
+        compiler_params=params(56),
         cost_estimate=cost(acc.shape[1], 4 * top.shape[2], acc.shape[2], 24 * acc.shape[1] * acc.shape[2]),
         name="child",
     )(at, acc, top, low, tiles, base)
@@ -258,7 +284,7 @@
             pltpu.SemaphoreType.DMA((4,)),
             pltpu.SemaphoreType.DMA((8,)),
         ],
-        compiler_params=params(40),
+        compiler_params=params(56),
         cost_estimate=cost(m, width, w, 4 * width * (m + w)),
         name="cross",
     )(at, s, *tiles)
@@ -306,32 +332,6 @@
     )(ancestors, x)
 
 
-def place_kernel(anc, first, x, out, sem):
-    out[...] = jnp.zeros_like(out)
-    for b in range(out.shape[0]):
-        for i in range(NANC):
-
-            @pl.when(anc[i] == first[0] + b)
-            def _():
-                copy = pltpu.make_async_copy(x.at[:, i], out.at[b], sem)
-                copy.start()
-                copy.wait()
-
-
-def place_rows(ancestors, x, h):
-    _, _, sub, w = x.shape
-    first = (3 * lax.axis_index(ROW)).astype(jnp.int32).reshape(1)
-    return pl.pallas_call(
-        place_kernel,
-        out_shape=jax.ShapeDtypeStruct((3, 8, sub, w), F32),
-        in_specs=[SMEM, SMEM, ANY],
-        out_specs=VMEM,
-        scratch_shapes=[pltpu.SemaphoreType.DMA],
-        compiler_params=params(8),
-        name="place_rows",
-    )(ancestors, first, x).reshape(h, w)
-
-
 def per_device(sigma_top, factor_cross, factor_inverse, block_inverse, ancestors):
     h, w = sigma_top.shape
     sub = h // 24
@@ -345,7 +345,7 @@
     s = lax.all_to_all(after(s, f_near[0]).reshape(16, -1, w), COL, 0, 0, tiled=True)
     s_all = lax.all_gather(pick_cols(ancestors, s), COL, axis=0, tiled=True)
 
-    acc = near_product(at, f_near, inverse, 1, W1)
+    (acc,) = near_product(at, f_near, inverse, 1, W1)
     u, ut = update_product(at, acc, *f_far, inverse)
 
     u_near, u_far = gather_cols(turn(ut), False)
@@ -353,11 +353,10 @@
 
     sigma = cross_product(at, after(s_all, u_near[0]), u_tiles)
     sigma_all = lax.all_gather(sigma, ROW, axis=0, tiled=True).reshape(8, w, w)
-    acc = near_product(at_turned, u_near, sigma_all, 2, W2)
+    acc, rows = near_product(at_turned, u_near, sigma_all, 2, W2, ancestors)
     sigma_child = child_product(at_turned, acc, *u_far, sigma_all, block_inverse)
 
-    sigma_cross = place_rows(ancestors, sigma_all.reshape(8, NANC, sub, w), h)
-    return (sigma_cross, sigma_child)
+    return (rows.reshape(h, w), sigma_child)
 
 
 def solution(mesh):

time: 255 us -> 267 us (1.047)
  starting transfers between devices: 53.2 us -> 66.4 us
  Pallas kernels: 40.8 us -> 48.3 us
  waiting for transfers between devices: 85.4 us -> 78.8 us
  local copies, waits for them, and re-layouts: 12.5 us -> 9.65 us
    ppermute x4, starting transfers between devices: 1.78 us -> 15.3 us  [swap(): return lax.ppermute(x, 'core', [(0, 1), (1, 0)])]
    ppermute x18, waiting for transfers between devices: 52 us -> 42.5 us  [hop(): return lax.ppermute(x, ('core',) + COL, pairs)]
    ppermute x1, waiting for transfers between devices: 4.09 us -> 12.8 us  [turn(): lax.ppermute(x, ALL, [(at(y, c, z, x), at(y, x // 2, (y + z) % 4, 2 * c +...]
    unnamed x20 -> x18, local copies, waits for them, and re-layouts: 7.15 us -> 2.07 us
    all_to_all x1, waiting for transfers between devices: 11.9 us -> 8.11 us  [spread(): lax.all_to_all(x.reshape(3, 8, sub, w), ROW, 1, 0, tiled=True)]
    pallas_call x1, Pallas kernels: 3.74 us -> 6.5 us  [update_product(): pl.pallas_call(update_kernel, out_shape=(jax.ShapeDtypeStruct((m, n), F32...]
    pallas_call x3 -> x2, Pallas kernels: 21.4 us -> 23 us  [near_product(): pl.pallas_call(functools.partial(kernel, 16 // many, len(pieces)), out_sh...]
  transfers between devices with their start and end apart: 31 -> 31, of which waited for: 15 -> 13; matrix products, arithmetic and copies ran while one was open for 2% -> 3% of each run, Pallas kernels for 11% -> 12%
where the time goes in v11:
time: 267 us
  waiting for transfers between devices  78.8 us (30%)
  starting transfers between devices  66.4 us (25%)
  Pallas kernels  48.3 us (18%)
  blocking collectives  47.3 us (18%)
  between operations  14.3 us (5%)
  local copies, waits for them, and re-layouts  9.65 us (4%)
    ppermute x18, waiting for transfers between devices, hop(): return lax.ppermute(x, ('core',) + COL, pairs)  42.5 us
    ppermute x18, starting transfers between devices, hop(): return lax.ppermute(x, ('core',) + COL, pairs)  30.3 us
    all_to_all x1, blocking collectives, per_device(): lax.all_to_all(after(s, f_near[0]).reshape(16, -1, w), COL, 0, 0, tiled=T...  24.9 us
    pallas_call x2, Pallas kernels, near_product(): pl.pallas_call(functools.partial(kernel, 16 // many, len(pieces)), out_sh...  23 us
    all_to_all x1, blocking collectives, spread(): lax.all_to_all(x.reshape(3, 8, sub, w), ROW, 1, 0, tiled=True)  22.4 us
    ppermute x4, starting transfers between devices, swap(): return lax.ppermute(x, 'core', [(0, 1), (1, 0)])  15.3 us
    ppermute x1, waiting for transfers between devices, turn(): lax.ppermute(x, ALL, [(at(y, c, z, x), at(y, x // 2, (y + z) % 4, 2 * c +...  12.8 us
    ppermute x3, starting transfers between devices, step(): lax.ppermute(x, ROW, [(2 * i + c, 2 * ((i + 1 - 2 * c) % 4) + c) for i in...  11.7 us
  transfers between devices with their start and end apart: 31, of which 13 were waited for; matrix products, arithmetic and copies ran while one was open for 3% of the time, Pallas kernels for 12%

profile of v11, /device:TPU:1, one launch (start us, length us, event | category | flops | bytes accessed | tf_op | source)
XLA Modules:
  0.0 266.6 jit_solution(3204995722366694274)
XLA Ops:
  7.2 0.0 all-gather.4.cloned.1.call-start
  7.2 1.3 copy.7
  8.6 22.4 %all_to_all.35 = f32[3,8,32,384]{3,2,0,1:T(8,128)S(1)} all-to-all(f32[3,8,32,384]{3,2,0,1:T(8,128)S(1)} %copy.7), channel_id=1, replica_groups=mesh['y'=4,'core'=2,'z'=4,'x'=4] {'y','core'}, dimensions={1} | all-to-all | bytes 2359296 | tf_op jit(solution)/shard_map/all_to_all | solution.py:296
  31.0 0.6 pick_rows.2
  31.6 0.0 all-gather.4.cloned.1.call-update
  31.6 3.8 %collective-permute-start.1 = (f32[384,384]{1,0:T(8,128)S(1)}, f32[384,384]{1,0:T(8,128)S(1)}, u32[]{:S(2)}, u32[]{:S(2)}) collective-permute-start(f32[384,384]{1,0:T(8,128)S(1)} %bitcast.72), channel_id=1, source_target_pairs={{0,3},{1,0},{2,1},{3,2},{4,7},{5,4},{6,5},{7,6},{8,11},{9,8},{10,9... | collective-permute-start | bytes 1769480 | tf_op jit(solution)/shard_map/ppermute | solution.py:58
  35.4 1.1 copy.8
  36.5 3.5 %all-to-all-start.1 = ((f32[3,8,32,384]{3,2,0,1:T(8,128)}), f32[3,8,32,384]{3,2,0,1:T(8,128)S(1)}, u32[]{:S(2)}, u32[]{:S(2)}) async-start(f32[3,8,32,384]{3,2,0,1:T(8,128)} %copy.8), calls=%async_computation.1 | async-start | bytes 2359296 | tf_op jit(solution)/shard_map/all_to_all | solution.py:296
  40.1 0.0 all-gather.6.cloned.1.call-start
  40.1 2.2 collective-permute-done.1
  42.3 3.5 %collective-permute-start.3 = (f32[192,384]{1,0:T(8,128)S(1)}, f32[192,384]{1,0:T(8,128)S(1)}, u32[]{:S(2)}, u32[]{:S(2)}) collective-permute-start(f32[192,384]{1,0:T(8,128)S(1)} %slice.25), channel_id=1, source_target_pairs={{0,3},{1,0},{2,1},{3,2},{4,7},{5,4},{6,5},{7,6},{8,11},{9,8},{10,9... | collective-permute-start | bytes 884744 | tf_op jit(solution)/shard_map/ppermute | solution.py:58
  45.8 0.1 collective-permute-start.2
  45.9 3.6 %collective-permute-done.3 = f32[192,384]{1,0:T(8,128)S(1)} collective-permute-done((f32[192,384]{1,0:T(8,128)S(1)}, f32[192,384]{1,0:T(8,128)S(1)}, u32[]{:S(2)}, u32[]{:S(2)}) %collective-permute-start.3) | collective-permute-done | bytes 294944 | tf_op jit(solution)/shard_map/ppermute | solution.py:58
  49.4 3.6 %collective-permute-done.2 = f32[192,384]{1,0:T(8,128)S(1)} collective-permute-done((f32[192,384]{1,0:T(8,128)S(1)}, f32[192,384]{1,0:T(8,128)S(1)}, u32[]{:S(2)}, u32[]{:S(2)}) %collective-permute-start.2) | collective-permute-done | bytes 294944 | tf_op jit(solution)/shard_map/ppermute | solution.py:58
  53.1 1.6 pad_maximum_fusion.refs_0_
  54.7 1.1 collective-permute-start.4
  55.8 1.6 collective-permute-start.5
  57.4 8.1 %all-to-all-done.1 = f32[3,8,32,384]{3,2,0,1:T(8,128)S(1)} async-done(((f32[3,8,32,384]{3,2,0,1:T(8,128)}), f32[3,8,32,384]{3,2,0,1:T(8,128)S(1)}, u32[]{:S(2)}, u32[]{:S(2)}) %all-to-all-start.1) | async-done | bytes 1179680 | tf_op jit(solution)/shard_map/all_to_all | solution.py:296
  65.5 0.6 pick_rows.3
  66.1 24.9 %all_to_all.36.x = f32[16,24,384]{2,1,0:T(8,128)S(1)} all-to-all(f32[16,24,384]{2,1,0:T(8,128)S(1)} %bitcast.75), channel_id=1, replica_groups=mesh['y'=4,'core'=2,'z'=4,'x'=4] {'z','x'}, dimensions={0} | all-to-all | bytes 1179648 | tf_op jit(solution)/shard_map/all_to_all | solution.py:345
  91.0 1.4 pick_cols.1
  92.4 0.0 all-gather.8.cloned.1.call-start
  92.7 0.6 stack.205.at
  93.3 1.3 slice.26
  94.7 1.3 collective-permute-start.6
  95.9 2.4 slice.27
  98.3 1.5 collective-permute-start.7
  99.8 11.4 %near.2.acc = f32[1,384,384]{2,1,0:T(8,128)} custom-call(s32[24]{0:T(128)} %stack.205.at, f32[4,384,384]{2,1,0:T(8,128)} %pad_maximum_fusion.refs_0_, f32[4,384,384]{2,1,0:T(8,128)} %collective-permute-done.4.refs_1_, f32[4,384,384]{2,1,0:T(8,128)} %collective-permute-done.5.refs_2_, f32[16,384,384]{2,1,0:T(8,128)} %bitcast.76), custom_call_target="tpu_custom_call" | custom-call | flops 48922361856 | bytes 198180864 | tf_op jit(solution)/shard_map/near/pallas_call | solution.py:170
  111.1 0.1 collective-permute-done.6.top
  111.3 4.3 %collective-permute-done.7.low = f32[2,384,384]{2,1,0:T(8,128)S(1)} collective-permute-done((f32[2,384,384]{2,1,0:T(8,128)}, f32[2,384,384]{2,1,0:T(8,128)S(1)}, u32[]{:S(2)}, u32[]{:S(2)}) %collective-permute-start.7) | collective-permute-done | bytes 1179680 | tf_op jit(solution)/shard_map/ppermute | solution.py:58
  115.6 1.0 copy-done.2
  116.6 6.5 %update.1 = (f32[384,384]{1,0:T(8,128)}, f32[384,384]{1,0:T(8,128)}) custom-call(s32[24]{0:T(128)} %stack.205.at, f32[1,384,384]{2,1,0:T(8,128)} %near.2.acc, f32[2,384,384]{2,1,0:T(8,128)} %copy-done.1, f32[2,384,384]{2,1,0:T(8,128)} %copy-done.2, f32[16,384,384]{2,1,0:T(8,128)} %bitcast.77), custom_call_target="tpu_custom_call" | custom-call | flops 1358954496 | bytes 2359296 | tf_op jit(solution)/shard_map/update/pallas_call | solution.py:219
  123.1 4.8 %collective-permute-start.8 = (f32[384,384]{1,0:T(8,128)}, f32[384,384]{1,0:T(8,128)S(1)}, u32[]{:S(2)}, u32[]{:S(2)}) collective-permute-start(f32[384,384]{1,0:T(8,128)} %get-tuple-element.13), channel_id=1, source_target_pairs={{0,0},{1,1},{2,16},{3,17},{4,4},{5,5},{6,20},{7,21},{8,8},{9,9},{1... | collective-permute-start | bytes 1769480 | tf_op jit(solution)/shard_map/ppermute | solution.py:79
  127.9 3.5 %collective-permute-start.18 = (f32[12,32,384]{2,1,0:T(8,128)}, f32[12,32,384]{2,1,0:T(8,128)S(1)}, u32[]{:S(2)}, u32[]{:S(2)}) collective-permute-start(f32[12,32,384]{2,1,0:T(8,128)} %bitcast.87), channel_id=1, source_target_pairs={{0,32},{16,112},{32,64},{48,16},{64,96},{80,48},{96,0},{112,80},{1... | collective-permute-start | bytes 1769480 | tf_op jit(solution)/shard_map/ppermute | solution.py:37
  131.4 12.8 %collective-permute-done.8 = f32[384,384]{1,0:T(8,128)S(1)} collective-permute-done((f32[384,384]{1,0:T(8,128)}, f32[384,384]{1,0:T(8,128)S(1)}, u32[]{:S(2)}, u32[]{:S(2)}) %collective-permute-start.8) | collective-permute-done | bytes 589856 | tf_op jit(solution)/shard_map/ppermute | solution.py:79
  144.2 0.7 collective-permute-start.9
  144.9 6.3 %collective-permute-start.19 = (f32[12,32,384]{2,1,0:T(8,128)S(1)}, f32[12,32,384]{2,1,0:T(8,128)S(1)}, u32[]{:S(2)}, u32[]{:S(2)}) collective-permute-start(f32[12,32,384]{2,1,0:T(8,128)S(1)} %collective-permute-done.18.refs_1_), channel_id=1, source_target_pairs={{0,32},{16,112},{32,64},{48,16},{64,96},{80,48},{96,0},{112,80},{1... | collective-permute-start | bytes 1769480 | tf_op jit(solution)/shard_map/ppermute | solution.py:37
  151.2 8.6 %collective-permute-start.11 = (f32[384,384]{1,0:T(8,128)S(1)}, f32[384,384]{1,0:T(8,128)S(1)}, u32[]{:S(2)}, u32[]{:S(2)}) collective-permute-start(f32[384,384]{1,0:T(8,128)S(1)} %collective-permute-done.9), channel_id=1, source_target_pairs={{0,3},{1,0},{2,1},{3,2},{4,7},{5,4},{6,5},{7,6},{8,11},{9,8},{10,9... | collective-permute-start | bytes 1769480 | tf_op jit(solution)/shard_map/ppermute | solution.py:58
  159.8 9.2 %collective-permute-done.19.refs_2_ = f32[12,32,384]{2,1,0:T(8,128)S(1)} collective-permute-done((f32[12,32,384]{2,1,0:T(8,128)S(1)}, f32[12,32,384]{2,1,0:T(8,128)S(1)}, u32[]{:S(2)}, u32[]{:S(2)}) %collective-permute-start.19) | collective-permute-done | bytes 589856 | tf_op jit(solution)/shard_map/ppermute | solution.py:37
  169.0 2.0 collective-permute-start.20
  171.0 0.1 collective-permute-start.13
  171.1 6.9 %collective-permute-start.21 = (f32[12,32,384]{2,1,0:T(8,128)}, f32[12,32,384]{2,1,0:T(8,128)}, u32[]{:S(2)}, u32[]{:S(2)}) collective-permute-start(f32[12,32,384]{2,1,0:T(8,128)} %bitcast.88), channel_id=1, source_target_pairs={{0,16},{16,0},{1,17},{17,1},{2,18},{18,2},{3,19},{19,3},{4,20},{20... | collective-permute-start | bytes 1769480 | tf_op jit(solution)/shard_map/ppermute | solution.py:41
  178.0 0.1 collective-permute-start.22
  178.1 0.4 collective-permute-start.23
  178.5 7.9 %collective-permute-start.24 = (f32[12,32,384]{2,1,0:T(8,128)}, f32[12,32,384]{2,1,0:T(8,128)}, u32[]{:S(2)}, u32[]{:S(2)}) collective-permute-start(f32[12,32,384]{2,1,0:T(8,128)} %collective-permute-done.20.refs_3_), channel_id=1, source_target_pairs={{0,16},{16,0},{1,17},{17,1},{2,18},{18,2},{3,19},{19,3},{4,20},{20... | collective-permute-start | bytes 1769480 | tf_op jit(solution)/shard_map/ppermute | solution.py:41
  186.4 0.3 collective-permute-start.12
  186.7 0.1 pad_maximum_fusion.1.refs_0_
  186.8 6.9 %collective-permute-done.12 = f32[192,384]{1,0:T(8,128)S(1)} collective-permute-done((f32[192,384]{1,0:T(8,128)S(1)}, f32[192,384]{1,0:T(8,128)S(1)}, u32[]{:S(2)}, u32[]{:S(2)}) %collective-permute-start.12) | collective-permute-done | bytes 294944 | tf_op jit(solution)/shard_map/ppermute | solution.py:58
  193.8 0.1 pad_maximum_fusion.2.refs_1_
  193.9 0.0 all-gather.6.cloned.1.call-done.s
  194.0 9.3 %cross.1 = f32[384,384]{1,0:T(8,128)} custom-call(s32[24]{0:T(128)} %stack.205.at, f32[384,3072]{1,0:T(8,128)} %all-gather.6.cloned.1.call-done.s, f32[12,32,384]{2,1,0:T(8,128)} %bitcast.89, f32[12,32,384]{2,1,0:T(8,128)} %copy-done.7, f32[12,32,384]{2,1,0:T(8,128)} %copy-done.8, f32[12,32,384]{2,1,0:T(8,128)} %collective-permute-done.20.refs_3_, ...), custom_call_target="tpu_custom_call" | custom-call | flops 2717908992 | bytes 9437184 | tf_op jit(solution)/shard_map/cross/pallas_call | solution.py:276
  203.3 3.0 %collective-permute-start.14 = (f32[2,384,384]{2,1,0:T(8,128)S(1)}, f32[2,384,384]{2,1,0:T(8,128)}, u32[]{:S(2)}, u32[]{:S(2)}) collective-permute-start(f32[2,384,384]{2,1,0:T(8,128)S(1)} %pad_maximum_fusion.1.refs_0_), channel_id=1, source_target_pairs={{0,4},{1,5},{2,6},{3,7},{4,8},{5,9},{6,10},{7,11},{8,12},{9,13},{1... | collective-permute-start | bytes 3538952 | tf_op jit(solution)/shard_map/ppermute | solution.py:58
  206.3 1.5 collective-permute-start.15
  207.7 1.2 collective-permute-start.16
  208.9 0.7 stack.188.at
  209.6 10.4 %collective-permute-done.14.refs_2_ = f32[2,384,384]{2,1,0:T(8,128)} collective-permute-done((f32[2,384,384]{2,1,0:T(8,128)S(1)}, f32[2,384,384]{2,1,0:T(8,128)}, u32[]{:S(2)}, u32[]{:S(2)}) %collective-permute-start.14) | collective-permute-done | bytes 1179680 | tf_op jit(solution)/shard_map/ppermute | solution.py:58
  220.0 1.7 collective-permute-start.25
  221.7 1.2 collective-permute-start.26
  222.9 9.7 %collective-permute-done.15.refs_3_ = f32[2,384,384]{2,1,0:T(8,128)} collective-permute-done((f32[2,384,384]{2,1,0:T(8,128)S(1)}, f32[2,384,384]{2,1,0:T(8,128)}, u32[]{:S(2)}, u32[]{:S(2)}) %collective-permute-start.15) | collective-permute-done | bytes 1179680 | tf_op jit(solution)/shard_map/ppermute | solution.py:58
  232.7 1.7 collective-permute-done.16.refs_4_
  234.4 6.0 %all-gather.8.cloned.1.call-done = f32[3072,384]{1,0:T(8,128)} async-done(((f32[384,384]{1,0:T(8,128)}), f32[3072,384]{1,0:T(8,128)}) %all-gather.8.cloned.1.call-update) | async-done | bytes 4718608 | tf_op jit(solution)/shard_map/all_gather | solution.py:355
  240.3 11.6 %near.3 = (f32[2,384,384]{2,1,0:T(8,128)}, f32[3,8,32,384]{3,2,1,0:T(8,128)}) custom-call(s32[12]{0:T(128)} %anc.7, s32[1]{0:T(128)} %bitcast.first, s32[24]{0:T(128)} %stack.188.at, f32[2,384,384]{2,1,0:T(8,128)} %copy-done.4, f32[2,384,384]{2,1,0:T(8,128)} %copy-done.5, f32[2,384,384]{2,1,0:T(8,128)} %collective-permute-done.14.refs_2_, ...), custom_call_target="tpu_custom_call" | custom-call | flops 48922361856 | bytes 141557760 | tf_op jit(solution)/shard_map/near/pallas_call | solution.py:170
  252.0 1.0 copy-done.6
  253.0 7.0 %child.1 = f32[768,384]{1,0:T(8,128)} custom-call(s32[24]{0:T(128)} %stack.188.at, f32[2,384,384]{2,1,0:T(8,128)} %get-tuple-element.21.acc, f32[2,384,384]{2,1,0:T(8,128)} %copy-done.6, f32[2,384,384]{2,1,0:T(8,128)} %collective-permute-done.26.low, f32[8,384,384]{2,1,0:T(8,128)} %bitcast.79, f32[768,384]{1,0:T(8,128)} %base.1), custom_call_target="tpu_custom_call" | custom-call | flops 1358954496 | bytes 3538944 | tf_op jit(solution)/shard_map/child/pallas_call | solution.py:241
  (44 shorter events, 0.3 us)
Async XLA Ops:
  7.2 92.6 %all-gather.4.cloned.1.call-start = ((), (), s32[]{:S(2)}) async-start(), calls=%async_computation.3 | async-start | bytes 10616832 | tf_op jit(solution)/shard_map/all_gather | solution.py:341
  8.6 22.4 %copy-start = (s32[12]{0:T(128)S(1)}, s32[12]{0:T(128)}, u32[]{:S(2)}) copy-start(s32[12]{0:T(128)} %anc.7) | copy-start | bytes 148
  31.0 4.5 %copy-start.3 = (f32[768,384]{1,0:T(8,128)S(1)}, f32[768,384]{1,0:T(8,128)}, u32[]{:S(2)}) copy-start(f32[768,384]{1,0:T(8,128)} %param.5) | copy-start | bytes 3538948
  31.6 10.7 %collective-permute-start.1 = (f32[384,384]{1,0:T(8,128)S(1)}, f32[384,384]{1,0:T(8,128)S(1)}, u32[]{:S(2)}, u32[]{:S(2)}) collective-permute-start(f32[384,384]{1,0:T(8,128)S(1)} %bitcast.72), channel_id=1, source_target_pairs={{0,3},{1,0},{2,1},{3,2},{4,7},{5,4},{6,5},{7,6},{8,11},{9,8},{10,9... | collective-permute-start | bytes 1769480 | tf_op jit(solution)/shard_map/ppermute | solution.py:58
  35.4 10.3 %collective-permute-start = (f32[384,384]{1,0:T(8,128)S(1)}, f32[384,384]{1,0:T(8,128)S(1)}, u32[]{:S(2)}, u32[]{:S(2)}) collective-permute-start(f32[384,384]{1,0:T(8,128)S(1)} %bitcast.73), channel_id=1, source_target_pairs={{0,1},{1,2},{2,3},{3,0},{4,5},{5,6},{6,7},{7,4},{8,9},{9,10},{10,1... | collective-permute-start | bytes 1769480 | tf_op jit(solution)/shard_map/ppermute | solution.py:58
  36.5 28.9 %all-to-all-start.1 = ((f32[3,8,32,384]{3,2,0,1:T(8,128)}), f32[3,8,32,384]{3,2,0,1:T(8,128)S(1)}, u32[]{:S(2)}, u32[]{:S(2)}) async-start(f32[3,8,32,384]{3,2,0,1:T(8,128)} %copy.8), calls=%async_computation.1 | async-start | bytes 2359296 | tf_op jit(solution)/shard_map/all_to_all | solution.py:296
  40.1 153.9 %all-gather.6.cloned.1.call-start = ((), (), s32[]{:S(2)}) async-start(), calls=%async_computation.4 | async-start | bytes 5013504 | tf_op jit(solution)/shard_map/all_gather | solution.py:346
  42.3 7.1 %collective-permute-start.3 = (f32[192,384]{1,0:T(8,128)S(1)}, f32[192,384]{1,0:T(8,128)S(1)}, u32[]{:S(2)}, u32[]{:S(2)}) collective-permute-start(f32[192,384]{1,0:T(8,128)S(1)} %slice.25), channel_id=1, source_target_pairs={{0,3},{1,0},{2,1},{3,2},{4,7},{5,4},{6,5},{7,6},{8,11},{9,8},{10,9... | collective-permute-start | bytes 884744 | tf_op jit(solution)/shard_map/ppermute | solution.py:58
  45.8 7.3 %collective-permute-start.2 = (f32[192,384]{1,0:T(8,128)S(1)}, f32[192,384]{1,0:T(8,128)S(1)}, u32[]{:S(2)}, u32[]{:S(2)}) collective-permute-start(f32[192,384]{1,0:T(8,128)S(1)} %slice.24), channel_id=1, source_target_pairs={{0,1},{1,2},{2,3},{3,0},{4,5},{5,6},{6,7},{7,4},{8,9},{9,10},{10,1... | collective-permute-start | bytes 884744 | tf_op jit(solution)/shard_map/ppermute | solution.py:58
  54.7 38.6 %collective-permute-start.4 = (f32[4,384,384]{2,1,0:T(8,128)}, f32[4,384,384]{2,1,0:T(8,128)}, u32[]{:S(2)}, u32[]{:S(2)}) collective-permute-start(f32[4,384,384]{2,1,0:T(8,128)} %pad_maximum_fusion.refs_0_), channel_id=1, source_target_pairs={{0,4},{1,5},{2,6},{3,7},{4,8},{5,9},{6,10},{7,11},{8,12},{9,13},{1... | collective-permute-start | bytes 7077896 | tf_op jit(solution)/shard_map/ppermute | solution.py:58
  55.8 40.2 %collective-permute-start.5 = (f32[4,384,384]{2,1,0:T(8,128)}, f32[4,384,384]{2,1,0:T(8,128)}, u32[]{:S(2)}, u32[]{:S(2)}) collective-permute-start(f32[4,384,384]{2,1,0:T(8,128)} %pad_maximum_fusion.refs_0_), channel_id=1, source_target_pairs={{0,12},{1,13},{2,14},{3,15},{4,0},{5,1},{6,2},{7,3},{8,4},{9,5},{1... | collective-permute-start | bytes 7077896 | tf_op jit(solution)/shard_map/ppermute | solution.py:58
  92.4 148.0 %all-gather.8.cloned.1.call-start = ((), (), s32[]{:S(2)}) async-start(), calls=%async_computation.5 | async-start | bytes 5308416 | tf_op jit(solution)/shard_map/all_gather | solution.py:355
  94.7 16.6 %collective-permute-start.6 = (f32[2,384,384]{2,1,0:T(8,128)S(1)}, f32[2,384,384]{2,1,0:T(8,128)S(1)}, u32[]{:S(2)}, u32[]{:S(2)}) collective-permute-start(f32[2,384,384]{2,1,0:T(8,128)S(1)} %slice.26), channel_id=1, source_target_pairs={{0,4},{1,5},{2,6},{3,7},{4,8},{5,9},{6,10},{7,11},{8,12},{9,13},{1... | collective-permute-start | bytes 3538952 | tf_op jit(solution)/shard_map/ppermute | solution.py:58
  98.3 17.3 %collective-permute-start.7 = (f32[2,384,384]{2,1,0:T(8,128)}, f32[2,384,384]{2,1,0:T(8,128)S(1)}, u32[]{:S(2)}, u32[]{:S(2)}) collective-permute-start(f32[2,384,384]{2,1,0:T(8,128)} %slice.27), channel_id=1, source_target_pairs={{0,12},{1,13},{2,14},{3,15},{4,0},{5,1},{6,2},{7,3},{8,4},{9,5},{1... | collective-permute-start | bytes 3538952 | tf_op jit(solution)/shard_map/ppermute | solution.py:58
  111.3 4.3 %copy-start.1 = (f32[2,384,384]{2,1,0:T(8,128)}, f32[2,384,384]{2,1,0:T(8,128)S(1)}, u32[]{:S(2)}) copy-start(f32[2,384,384]{2,1,0:T(8,128)S(1)} %collective-permute-done.6.top) | copy-start | bytes 3538948
  115.6 1.0 copy-start.2
  123.1 21.1 %collective-permute-start.8 = (f32[384,384]{1,0:T(8,128)}, f32[384,384]{1,0:T(8,128)S(1)}, u32[]{:S(2)}, u32[]{:S(2)}) collective-permute-start(f32[384,384]{1,0:T(8,128)} %get-tuple-element.13), channel_id=1, source_target_pairs={{0,0},{1,1},{2,16},{3,17},{4,4},{5,5},{6,20},{7,21},{8,8},{9,9},{1... | collective-permute-start | bytes 1769480 | tf_op jit(solution)/shard_map/ppermute | solution.py:79
  127.9 17.0 %collective-permute-start.18 = (f32[12,32,384]{2,1,0:T(8,128)}, f32[12,32,384]{2,1,0:T(8,128)S(1)}, u32[]{:S(2)}, u32[]{:S(2)}) collective-permute-start(f32[12,32,384]{2,1,0:T(8,128)} %bitcast.87), channel_id=1, source_target_pairs={{0,32},{16,112},{32,64},{48,16},{64,96},{80,48},{96,0},{112,80},{1... | collective-permute-start | bytes 1769480 | tf_op jit(solution)/shard_map/ppermute | solution.py:37
  144.2 7.0 %collective-permute-start.9 = (f32[384,384]{1,0:T(8,128)S(1)}, f32[384,384]{1,0:T(8,128)S(1)}, u32[]{:S(2)}, u32[]{:S(2)}) collective-permute-start(f32[384,384]{1,0:T(8,128)S(1)} %collective-permute-done.8), channel_id=1, source_target_pairs={{0,0},{1,1},{2,2},{3,3},{4,36},{5,37},{6,38},{7,39},{8,72},{9,73},... | collective-permute-start | bytes 1769480 | tf_op jit(solution)/shard_map/ppermute | solution.py:80
  144.9 41.9 %copy-start.7 = (f32[12,32,384]{2,1,0:T(8,128)}, f32[12,32,384]{2,1,0:T(8,128)S(1)}, u32[]{:S(2)}) copy-start(f32[12,32,384]{2,1,0:T(8,128)S(1)} %collective-permute-done.18.refs_1_) | copy-start | bytes 1769476
  144.9 24.1 %collective-permute-start.19 = (f32[12,32,384]{2,1,0:T(8,128)S(1)}, f32[12,32,384]{2,1,0:T(8,128)S(1)}, u32[]{:S(2)}, u32[]{:S(2)}) collective-permute-start(f32[12,32,384]{2,1,0:T(8,128)S(1)} %collective-permute-done.18.refs_1_), channel_id=1, source_target_pairs={{0,32},{16,112},{32,64},{48,16},{64,96},{80,48},{96,0},{112,80},{1... | collective-permute-start | bytes 1769480 | tf_op jit(solution)/shard_map/ppermute | solution.py:37
  151.2 19.8 %collective-permute-start.11 = (f32[384,384]{1,0:T(8,128)S(1)}, f32[384,384]{1,0:T(8,128)S(1)}, u32[]{:S(2)}, u32[]{:S(2)}) collective-permute-start(f32[384,384]{1,0:T(8,128)S(1)} %collective-permute-done.9), channel_id=1, source_target_pairs={{0,3},{1,0},{2,1},{3,2},{4,7},{5,4},{6,5},{7,6},{8,11},{9,8},{10,9... | collective-permute-start | bytes 1769480 | tf_op jit(solution)/shard_map/ppermute | solution.py:58
  159.8 18.3 %collective-permute-start.10 = (f32[384,384]{1,0:T(8,128)S(1)}, f32[384,384]{1,0:T(8,128)S(1)}, u32[]{:S(2)}, u32[]{:S(2)}) collective-permute-start(f32[384,384]{1,0:T(8,128)S(1)} %collective-permute-done.9), channel_id=1, source_target_pairs={{0,1},{1,2},{2,3},{3,0},{4,5},{5,6},{6,7},{7,4},{8,9},{9,10},{10,1... | collective-permute-start | bytes 1769480 | tf_op jit(solution)/shard_map/ppermute | solution.py:58
  169.0 17.8 %copy-start.8 = (f32[12,32,384]{2,1,0:T(8,128)}, f32[12,32,384]{2,1,0:T(8,128)S(1)}, u32[]{:S(2)}) copy-start(f32[12,32,384]{2,1,0:T(8,128)S(1)} %collective-permute-done.19.refs_2_) | copy-start | bytes 1769476
  169.0 9.5 %collective-permute-start.20 = (f32[12,32,384]{2,1,0:T(8,128)S(1)}, f32[12,32,384]{2,1,0:T(8,128)}, u32[]{:S(2)}, u32[]{:S(2)}) collective-permute-start(f32[12,32,384]{2,1,0:T(8,128)S(1)} %collective-permute-done.19.refs_2_), channel_id=1, source_target_pairs={{0,32},{16,112},{32,64},{48,16},{64,96},{80,48},{96,0},{112,80},{1... | collective-permute-start | bytes 1769480 | tf_op jit(solution)/shard_map/ppermute | solution.py:37
  171.0 15.4 %collective-permute-start.13 = (f32[192,384]{1,0:T(8,128)S(1)}, f32[192,384]{1,0:T(8,128)S(1)}, u32[]{:S(2)}, u32[]{:S(2)}) collective-permute-start(f32[192,384]{1,0:T(8,128)S(1)} %slice.29), channel_id=1, source_target_pairs={{0,3},{1,0},{2,1},{3,2},{4,7},{5,4},{6,5},{7,6},{8,11},{9,8},{10,9... | collective-permute-start | bytes 884744 | tf_op jit(solution)/shard_map/ppermute | solution.py:58
  171.1 22.8 %collective-permute-start.21 = (f32[12,32,384]{2,1,0:T(8,128)}, f32[12,32,384]{2,1,0:T(8,128)}, u32[]{:S(2)}, u32[]{:S(2)}) collective-permute-start(f32[12,32,384]{2,1,0:T(8,128)} %bitcast.88), channel_id=1, source_target_pairs={{0,16},{16,0},{1,17},{17,1},{2,18},{18,2},{3,19},{19,3},{4,20},{20... | collective-permute-start | bytes 1769480 | tf_op jit(solution)/shard_map/ppermute | solution.py:41
  178.0 15.9 %collective-permute-start.22 = (f32[12,32,384]{2,1,0:T(8,128)S(1)}, f32[12,32,384]{2,1,0:T(8,128)}, u32[]{:S(2)}, u32[]{:S(2)}) collective-permute-start(f32[12,32,384]{2,1,0:T(8,128)S(1)} %collective-permute-done.18.refs_1_), channel_id=1, source_target_pairs={{0,16},{16,0},{1,17},{17,1},{2,18},{18,2},{3,19},{19,3},{4,20},{20... | collective-permute-start | bytes 1769480 | tf_op jit(solution)/shard_map/ppermute | solution.py:41
  178.1 15.8 %collective-permute-start.23 = (f32[12,32,384]{2,1,0:T(8,128)S(1)}, f32[12,32,384]{2,1,0:T(8,128)}, u32[]{:S(2)}, u32[]{:S(2)}) collective-permute-start(f32[12,32,384]{2,1,0:T(8,128)S(1)} %collective-permute-done.19.refs_2_), channel_id=1, source_target_pairs={{0,16},{16,0},{1,17},{17,1},{2,18},{18,2},{3,19},{19,3},{4,20},{20... | collective-permute-start | bytes 1769480 | tf_op jit(solution)/shard_map/ppermute | solution.py:41
  178.5 15.4 %collective-permute-start.24 = (f32[12,32,384]{2,1,0:T(8,128)}, f32[12,32,384]{2,1,0:T(8,128)}, u32[]{:S(2)}, u32[]{:S(2)}) collective-permute-start(f32[12,32,384]{2,1,0:T(8,128)} %collective-permute-done.20.refs_3_), channel_id=1, source_target_pairs={{0,16},{16,0},{1,17},{17,1},{2,18},{18,2},{3,19},{19,3},{4,20},{20... | collective-permute-start | bytes 1769480 | tf_op jit(solution)/shard_map/ppermute | solution.py:41
  186.4 7.3 %collective-permute-start.12 = (f32[192,384]{1,0:T(8,128)S(1)}, f32[192,384]{1,0:T(8,128)S(1)}, u32[]{:S(2)}, u32[]{:S(2)}) collective-permute-start(f32[192,384]{1,0:T(8,128)S(1)} %slice.28), channel_id=1, source_target_pairs={{0,1},{1,2},{2,3},{3,0},{4,5},{5,6},{6,7},{7,4},{8,9},{9,10},{10,1... | collective-permute-start | bytes 884744 | tf_op jit(solution)/shard_map/ppermute | solution.py:58
  186.8 20.9 %copy-start.4 = (f32[2,384,384]{2,1,0:T(8,128)}, f32[2,384,384]{2,1,0:T(8,128)S(1)}, u32[]{:S(2)}) copy-start(f32[2,384,384]{2,1,0:T(8,128)S(1)} %pad_maximum_fusion.1.refs_0_) | copy-start | bytes 3538948
  193.9 12.4 %copy-start.5 = (f32[2,384,384]{2,1,0:T(8,128)}, f32[2,384,384]{2,1,0:T(8,128)S(1)}, u32[]{:S(2)}) copy-start(f32[2,384,384]{2,1,0:T(8,128)S(1)} %pad_maximum_fusion.2.refs_1_) | copy-start | bytes 3538948
  203.3 16.7 %collective-permute-start.14 = (f32[2,384,384]{2,1,0:T(8,128)S(1)}, f32[2,384,384]{2,1,0:T(8,128)}, u32[]{:S(2)}, u32[]{:S(2)}) collective-permute-start(f32[2,384,384]{2,1,0:T(8,128)S(1)} %pad_maximum_fusion.1.refs_0_), channel_id=1, source_target_pairs={{0,4},{1,5},{2,6},{3,7},{4,8},{5,9},{6,10},{7,11},{8,12},{9,13},{1... | collective-permute-start | bytes 3538952 | tf_op jit(solution)/shard_map/ppermute | solution.py:58
  206.3 15.5 %collective-permute-start.17 = (f32[2,384,384]{2,1,0:T(8,128)S(1)}, f32[2,384,384]{2,1,0:T(8,128)}, u32[]{:S(2)}, u32[]{:S(2)}) collective-permute-start(f32[2,384,384]{2,1,0:T(8,128)S(1)} %pad_maximum_fusion.2.refs_1_), channel_id=1, source_target_pairs={{0,12},{1,13},{2,14},{3,15},{4,0},{5,1},{6,2},{7,3},{8,4},{9,5},{1... | collective-permute-start | bytes 3538952 | tf_op jit(solution)/shard_map/ppermute | solution.py:58
  206.3 26.4 %collective-permute-start.15 = (f32[2,384,384]{2,1,0:T(8,128)S(1)}, f32[2,384,384]{2,1,0:T(8,128)}, u32[]{:S(2)}, u32[]{:S(2)}) collective-permute-start(f32[2,384,384]{2,1,0:T(8,128)S(1)} %pad_maximum_fusion.2.refs_1_), channel_id=1, source_target_pairs={{0,4},{1,5},{2,6},{3,7},{4,8},{5,9},{6,10},{7,11},{8,12},{9,13},{1... | collective-permute-start | bytes 3538952 | tf_op jit(solution)/shard_map/ppermute | solution.py:58
  207.7 26.6 %collective-permute-start.16 = (f32[2,384,384]{2,1,0:T(8,128)S(1)}, f32[2,384,384]{2,1,0:T(8,128)}, u32[]{:S(2)}, u32[]{:S(2)}) collective-permute-start(f32[2,384,384]{2,1,0:T(8,128)S(1)} %pad_maximum_fusion.1.refs_0_), channel_id=1, source_target_pairs={{0,12},{1,13},{2,14},{3,15},{4,0},{5,1},{6,2},{7,3},{8,4},{9,5},{1... | collective-permute-start | bytes 3538952 | tf_op jit(solution)/shard_map/ppermute | solution.py:58
  220.0 32.0 %collective-permute-start.25 = (f32[2,384,384]{2,1,0:T(8,128)}, f32[2,384,384]{2,1,0:T(8,128)S(1)}, u32[]{:S(2)}, u32[]{:S(2)}) collective-permute-start(f32[2,384,384]{2,1,0:T(8,128)} %collective-permute-done.14.refs_2_), channel_id=1, source_target_pairs={{0,4},{1,5},{2,6},{3,7},{4,8},{5,9},{6,10},{7,11},{8,12},{9,13},{1... | collective-permute-start | bytes 3538952 | tf_op jit(solution)/shard_map/ppermute | solution.py:58
  221.7 30.3 %collective-permute-start.26 = (f32[2,384,384]{2,1,0:T(8,128)}, f32[2,384,384]{2,1,0:T(8,128)}, u32[]{:S(2)}, u32[]{:S(2)}) collective-permute-start(f32[2,384,384]{2,1,0:T(8,128)} %collective-permute-done.17.refs_5_), channel_id=1, source_target_pairs={{0,12},{1,13},{2,14},{3,15},{4,0},{5,1},{6,2},{7,3},{8,4},{9,5},{1... | collective-permute-start | bytes 3538952 | tf_op jit(solution)/shard_map/ppermute | solution.py:58
  252.0 1.0 copy-start.6
Sparse Core Ops, SparseCore 0:
  31.7 64.7 all-gather.3
  98.7 59.1 all-gather.5
  203.4 36.8 all-gather.7

commit v12 on v11

--- a/solution.py
+++ b/solution.py
@@ -100,7 +100,9 @@
     a_lo = (a - a_hi.astype(F32)).astype(jnp.bfloat16)
     b_lo = (b - b_hi.astype(F32)).astype(jnp.bfloat16)
     mul = lambda p, q: jnp.dot(p, q, preferred_element_type=F32)
-    return mul(a_hi, b_hi) + (mul(a_hi, b_lo) + mul(a_lo, b_hi))
+    both = mul(a_hi, jnp.concatenate([b_hi, b_lo], axis=1))
+    n = b.shape[1]
+    return both[:, :n] + (both[:, n:] + mul(a_lo, b_hi))
 
 
 def near_child_kernel(per, count, anc, first, at, *refs):
@@ -178,7 +180,7 @@
             pltpu.SemaphoreType.DMA((len(pieces),)),
             pltpu.SemaphoreType.DMA((12,)),
         ] + more,
-        compiler_params=params(56),
+        compiler_params=params(40),
         cost_estimate=cost(weight * m, 12 * w, n, weight * 4 * w * (12 * m + many * n)),
         name="near",
     )(*extra, at, *pieces, tiles)
@@ -222,7 +224,7 @@
         in_specs=[SMEM, VMEM, ANY, ANY, HBM],
         out_specs=(VMEM, VMEM),
         scratch_shapes=far_scratch(top, tiles),
-        compiler_params=params(56),
+        compiler_params=params(24),
         cost_estimate=cost(m, 4 * top.shape[2], n, 16 * m * n),
         name="update",
     )(at, acc, top, low, tiles)
@@ -244,7 +246,7 @@
         in_specs=[SMEM, VMEM, ANY, ANY, HBM, VMEM],
         out_specs=VMEM,
         scratch_shapes=far_scratch(top, tiles),
-        compiler_params=params(56),
+        compiler_params=params(24),
         cost_estimate=cost(acc.shape[1], 4 * top.shape[2], acc.shape[2], 24 * acc.shape[1] * acc.shape[2]),
         name="child",
     )(at, acc, top, low, tiles, base)
@@ -284,7 +286,7 @@
             pltpu.SemaphoreType.DMA((4,)),
             pltpu.SemaphoreType.DMA((8,)),
         ],
-        compiler_params=params(56),
+        compiler_params=params(40),
         cost_estimate=cost(m, width, w, 4 * width * (m + w)),
         name="cross",
     )(at, s, *tiles)

time: 267 us -> 252 us (0.944)
  starting transfers between devices: 66.4 us -> 55.6 us
  Pallas kernels: 48.3 us -> 37.9 us
  waiting for transfers between devices: 78.8 us -> 82.7 us
  local copies, waits for them, and re-layouts: 9.65 us -> 12.4 us
    ppermute x4, starting transfers between devices: 15.3 us -> 1.02 us  [swap(): return lax.ppermute(x, 'core', [(0, 1), (1, 0)])]
    ppermute x18, waiting for transfers between devices: 42.5 us -> 52.4 us  [hop(): return lax.ppermute(x, ('core',) + COL, pairs)]
    ppermute x1, waiting for transfers between devices: 12.8 us -> 5.32 us  [turn(): lax.ppermute(x, ALL, [(at(y, c, z, x), at(y, x // 2, (y + z) % 4, 2 * c +...]
    unnamed x18 -> x20, local copies, waits for them, and re-layouts: 2.07 us -> 7.15 us
    ppermute x18, starting transfers between devices: 30.3 us -> 34.9 us  [hop(): return lax.ppermute(x, ('core',) + COL, pairs)]
    pallas_call x2, Pallas kernels: 23 us -> 19.1 us  [near_product(): pl.pallas_call(functools.partial(kernel, 16 // many, len(pieces)), out_sh...]
    pallas_call x1, Pallas kernels: 6.5 us -> 3.44 us  [update_product(): pl.pallas_call(update_kernel, out_shape=(jax.ShapeDtypeStruct((m, n), F32...]
  transfers between devices with their start and end apart: 31 -> 31, of which waited for: 13 -> 15; matrix products, arithmetic and copies ran while one was open for 3% -> 2% of each run, Pallas kernels for 12% -> 10%
where the time goes in v12:
time: 252 us
  waiting for transfers between devices  82.7 us (33%)
  starting transfers between devices  55.6 us (22%)
  blocking collectives  47.4 us (19%)
  Pallas kernels  37.9 us (15%)
  between operations  14.3 us (6%)
  local copies, waits for them, and re-layouts  12.4 us (5%)
    ppermute x18, waiting for transfers between devices, hop(): return lax.ppermute(x, ('core',) + COL, pairs)  52.4 us
    ppermute x18, starting transfers between devices, hop(): return lax.ppermute(x, ('core',) + COL, pairs)  34.9 us
    all_to_all x1, blocking collectives, per_device(): lax.all_to_all(after(s, f_near[0]).reshape(16, -1, w), COL, 0, 0, tiled=T...  25 us
    all_to_all x1, blocking collectives, spread(): lax.all_to_all(x.reshape(3, 8, sub, w), ROW, 1, 0, tiled=True)  22.4 us
    pallas_call x2, Pallas kernels, near_product(): pl.pallas_call(functools.partial(kernel, 16 // many, len(pieces)), out_sh...  19.1 us
    ppermute x3, starting transfers between devices, step(): lax.ppermute(x, ROW, [(2 * i + c, 2 * ((i + 1 - 2 * c) % 4) + c) for i in...  10.4 us
    ppermute x3, waiting for transfers between devices, step(): lax.ppermute(x, ROW, [(2 * i + c, 2 * ((i + 1 - 2 * c) % 4) + c) for i in...  8.82 us
    all_to_all x1, waiting for transfers between devices, spread(): lax.all_to_all(x.reshape(3, 8, sub, w), ROW, 1, 0, tiled=True)  8.16 us
  transfers between devices with their start and end apart: 31, of which 15 were waited for; matrix products, arithmetic and copies ran while one was open for 2% of the time, Pallas kernels for 10%

profile of v12, /device:TPU:1, one launch (start us, length us, event | category | flops | bytes accessed | tf_op | source)
XLA Modules:
  0.0 252.0 jit_solution(15912941229506748285)
XLA Ops:
  7.2 0.0 all-gather.4.cloned.1.call-start
  7.2 1.3 copy.7
  8.6 22.4 %all_to_all.35 = f32[3,8,32,384]{3,2,0,1:T(8,128)S(1)} all-to-all(f32[3,8,32,384]{3,2,0,1:T(8,128)S(1)} %copy.7), channel_id=1, replica_groups=mesh['y'=4,'core'=2,'z'=4,'x'=4] {'y','core'}, dimensions={1} | all-to-all | bytes 2359296 | tf_op jit(solution)/shard_map/all_to_all | solution.py:298
  31.0 0.6 pick_rows.2
  31.6 3.8 %collective-permute-start.1 = (f32[384,384]{1,0:T(8,128)S(1)}, f32[384,384]{1,0:T(8,128)S(1)}, u32[]{:S(2)}, u32[]{:S(2)}) collective-permute-start(f32[384,384]{1,0:T(8,128)S(1)} %bitcast.78), channel_id=1, source_target_pairs={{0,3},{1,0},{2,1},{3,2},{4,7},{5,4},{6,5},{7,6},{8,11},{9,8},{10,9... | collective-permute-start | bytes 1769480 | tf_op jit(solution)/shard_map/ppermute | solution.py:58
  35.4 1.1 copy.8
  36.5 3.5 %all-to-all-start.1 = ((f32[3,8,32,384]{3,2,0,1:T(8,128)}), f32[3,8,32,384]{3,2,0,1:T(8,128)S(1)}, u32[]{:S(2)}, u32[]{:S(2)}) async-start(f32[3,8,32,384]{3,2,0,1:T(8,128)} %copy.8), calls=%async_computation.1 | async-start | bytes 2359296 | tf_op jit(solution)/shard_map/all_to_all | solution.py:298
  40.1 0.0 all-gather.6.cloned.1.call-start
  40.1 2.2 collective-permute-done.1
  42.3 3.5 %collective-permute-start.3 = (f32[192,384]{1,0:T(8,128)S(1)}, f32[192,384]{1,0:T(8,128)S(1)}, u32[]{:S(2)}, u32[]{:S(2)}) collective-permute-start(f32[192,384]{1,0:T(8,128)S(1)} %slice.25), channel_id=1, source_target_pairs={{0,3},{1,0},{2,1},{3,2},{4,7},{5,4},{6,5},{7,6},{8,11},{9,8},{10,9... | collective-permute-start | bytes 884744 | tf_op jit(solution)/shard_map/ppermute | solution.py:58
  45.8 0.1 collective-permute-start.2
  45.9 3.6 %collective-permute-done.3 = f32[192,384]{1,0:T(8,128)S(1)} collective-permute-done((f32[192,384]{1,0:T(8,128)S(1)}, f32[192,384]{1,0:T(8,128)S(1)}, u32[]{:S(2)}, u32[]{:S(2)}) %collective-permute-start.3) | collective-permute-done | bytes 294944 | tf_op jit(solution)/shard_map/ppermute | solution.py:58
  49.4 3.6 %collective-permute-done.2 = f32[192,384]{1,0:T(8,128)S(1)} collective-permute-done((f32[192,384]{1,0:T(8,128)S(1)}, f32[192,384]{1,0:T(8,128)S(1)}, u32[]{:S(2)}, u32[]{:S(2)}) %collective-permute-start.2) | collective-permute-done | bytes 294944 | tf_op jit(solution)/shard_map/ppermute | solution.py:58
  53.1 1.5 pad_maximum_fusion.refs_0_
  54.6 1.1 collective-permute-start.4
  55.7 1.6 collective-permute-start.5
  57.3 8.2 %all-to-all-done.1 = f32[3,8,32,384]{3,2,0,1:T(8,128)S(1)} async-done(((f32[3,8,32,384]{3,2,0,1:T(8,128)}), f32[3,8,32,384]{3,2,0,1:T(8,128)S(1)}, u32[]{:S(2)}, u32[]{:S(2)}) %all-to-all-start.1) | async-done | bytes 1179680 | tf_op jit(solution)/shard_map/all_to_all | solution.py:298
  65.5 0.6 pick_rows.3
  66.1 25.0 %all_to_all.36.x = f32[16,24,384]{2,1,0:T(8,128)S(1)} all-to-all(f32[16,24,384]{2,1,0:T(8,128)S(1)} %bitcast.81), channel_id=1, replica_groups=mesh['y'=4,'core'=2,'z'=4,'x'=4] {'z','x'}, dimensions={0} | all-to-all | bytes 1179648 | tf_op jit(solution)/shard_map/all_to_all | solution.py:347
  91.0 1.4 pick_cols.1
  92.4 0.0 all-gather.8.cloned.1.call-start
  92.7 0.1 stack.205.at
  92.8 1.2 slice.26
  94.0 0.6 copy-done.2
  94.7 1.1 collective-permute-start.6
  95.8 1.3 slice.27
  97.1 1.6 collective-permute-start.7
  98.8 1.8 copy-done.3
  100.6 9.2 %near.2.acc = f32[1,384,384]{2,1,0:T(8,128)S(1)} custom-call(s32[24]{0:T(128)S(1)} %stack.205.at, f32[4,384,384]{2,1,0:T(8,128)} %pad_maximum_fusion.refs_0_, f32[4,384,384]{2,1,0:T(8,128)S(1)} %copy-done.3, f32[4,384,384]{2,1,0:T(8,128)} %collective-permute-done.5.refs_2_, f32[16,384,384]{2,1,0:T(8,128)} %bitcast.70), custom_call_target="tpu_custom_call" | custom-call | flops 48922361856 | bytes 198180864 | tf_op jit(solution)/shard_map/near/pallas_call | solution.py:172
  109.8 1.7 collective-permute-done.6.top
  111.4 2.1 collective-permute-done.7.low
  113.5 3.4 %update.1 = (f32[384,384]{1,0:T(8,128)S(1)}, f32[384,384]{1,0:T(8,128)S(1)}) custom-call(s32[24]{0:T(128)S(1)} %stack.205.at, f32[1,384,384]{2,1,0:T(8,128)S(1)} %near.2.acc, f32[2,384,384]{2,1,0:T(8,128)S(1)} %collective-permute-done.6.top, f32[2,384,384]{2,1,0:T(8,128)S(1)} %collective-permute-done.7.low, f32[16,384,384]{2,1,0:T(8,128)S(1)} %bitcast.73), custom_call_target="tpu_custom_call" | custom-call | flops 1358954496 | bytes 2359296 | tf_op jit(solution)/shard_map/update/pallas_call | solution.py:221
  116.9 4.9 %collective-permute-start.8 = (f32[384,384]{1,0:T(8,128)S(1)}, f32[384,384]{1,0:T(8,128)S(1)}, u32[]{:S(2)}, u32[]{:S(2)}) collective-permute-start(f32[384,384]{1,0:T(8,128)S(1)} %get-tuple-element.13), channel_id=1, source_target_pairs={{0,0},{1,1},{2,16},{3,17},{4,4},{5,5},{6,20},{7,21},{8,8},{9,9},{1... | collective-permute-start | bytes 1769480 | tf_op jit(solution)/shard_map/ppermute | solution.py:79
  121.9 2.5 collective-permute-start.18
  124.4 5.3 %collective-permute-done.8 = f32[384,384]{1,0:T(8,128)S(1)} collective-permute-done((f32[384,384]{1,0:T(8,128)S(1)}, f32[384,384]{1,0:T(8,128)S(1)}, u32[]{:S(2)}, u32[]{:S(2)}) %collective-permute-start.8) | collective-permute-done | bytes 589856 | tf_op jit(solution)/shard_map/ppermute | solution.py:79
  129.7 0.7 collective-permute-start.9
  130.4 0.8 collective-permute-done.18.refs_1_
  131.2 5.6 %collective-permute-start.19 = (f32[12,32,384]{2,1,0:T(8,128)S(1)}, f32[12,32,384]{2,1,0:T(8,128)}, u32[]{:S(2)}, u32[]{:S(2)}) collective-permute-start(f32[12,32,384]{2,1,0:T(8,128)S(1)} %collective-permute-done.18.refs_1_), channel_id=1, source_target_pairs={{0,32},{16,112},{32,64},{48,16},{64,96},{80,48},{96,0},{112,80},{1... | collective-permute-start | bytes 1769480 | tf_op jit(solution)/shard_map/ppermute | solution.py:37
  136.8 9.1 %collective-permute-start.11 = (f32[384,384]{1,0:T(8,128)S(1)}, f32[384,384]{1,0:T(8,128)S(1)}, u32[]{:S(2)}, u32[]{:S(2)}) collective-permute-start(f32[384,384]{1,0:T(8,128)S(1)} %collective-permute-done.9), channel_id=1, source_target_pairs={{0,3},{1,0},{2,1},{3,2},{4,7},{5,4},{6,5},{7,6},{8,11},{9,8},{10,9... | collective-permute-start | bytes 1769480 | tf_op jit(solution)/shard_map/ppermute | solution.py:58
  145.9 8.0 %collective-permute-done.19.refs_2_ = f32[12,32,384]{2,1,0:T(8,128)} collective-permute-done((f32[12,32,384]{2,1,0:T(8,128)S(1)}, f32[12,32,384]{2,1,0:T(8,128)}, u32[]{:S(2)}, u32[]{:S(2)}) %collective-permute-start.19) | collective-permute-done | bytes 589856 | tf_op jit(solution)/shard_map/ppermute | solution.py:37
  153.9 2.3 collective-permute-start.20
  156.2 9.1 %collective-permute-done.11 = f32[384,384]{1,0:T(8,128)S(1)} collective-permute-done((f32[384,384]{1,0:T(8,128)S(1)}, f32[384,384]{1,0:T(8,128)S(1)}, u32[]{:S(2)}, u32[]{:S(2)}) %collective-permute-start.11) | collective-permute-done | bytes 589856 | tf_op jit(solution)/shard_map/ppermute | solution.py:58
  165.3 3.6 %collective-permute-start.13 = (f32[192,384]{1,0:T(8,128)S(1)}, f32[192,384]{1,0:T(8,128)S(1)}, u32[]{:S(2)}, u32[]{:S(2)}) collective-permute-start(f32[192,384]{1,0:T(8,128)S(1)} %slice.29), channel_id=1, source_target_pairs={{0,3},{1,0},{2,1},{3,2},{4,7},{5,4},{6,5},{7,6},{8,11},{9,8},{10,9... | collective-permute-start | bytes 884744 | tf_op jit(solution)/shard_map/ppermute | solution.py:58
  168.9 0.5 collective-permute-start.22
  169.4 0.5 collective-permute-start.24
  169.9 2.6 %collective-permute-done.13 = f32[192,384]{1,0:T(8,128)S(1)} collective-permute-done((f32[192,384]{1,0:T(8,128)S(1)}, f32[192,384]{1,0:T(8,128)S(1)}, u32[]{:S(2)}, u32[]{:S(2)}) %collective-permute-start.13) | collective-permute-done | bytes 294944 | tf_op jit(solution)/shard_map/ppermute | solution.py:58
  172.6 0.6 collective-permute-start.12
  173.1 0.1 pad_maximum_fusion.1.refs_0_
  173.2 6.6 %collective-permute-done.12 = f32[192,384]{1,0:T(8,128)S(1)} collective-permute-done((f32[192,384]{1,0:T(8,128)S(1)}, f32[192,384]{1,0:T(8,128)S(1)}, u32[]{:S(2)}, u32[]{:S(2)}) %collective-permute-start.12) | collective-permute-done | bytes 294944 | tf_op jit(solution)/shard_map/ppermute | solution.py:58
  179.8 0.1 pad_maximum_fusion.2.refs_1_
  179.9 0.0 all-gather.6.cloned.1.call-done.s
  180.0 2.3 copy-done.5
  182.3 7.9 %cross.1 = f32[384,384]{1,0:T(8,128)} custom-call(s32[24]{0:T(128)S(1)} %stack.205.at, f32[384,3072]{1,0:T(8,128)S(1)} %copy-done.5, f32[12,32,384]{2,1,0:T(8,128)S(1)} %bitcast.84, f32[12,32,384]{2,1,0:T(8,128)S(1)} %collective-permute-done.18.refs_1_, f32[12,32,384]{2,1,0:T(8,128)} %collective-permute-done.19.refs_2_, ...), custom_call_target="tpu_custom_call" | custom-call | flops 2717908992 | bytes 9437184 | tf_op jit(solution)/shard_map/cross/pallas_call | solution.py:278
  190.2 1.9 collective-permute-start.14
  192.1 1.6 collective-permute-start.17
  193.7 2.7 %collective-permute-start.16 = (f32[2,384,384]{2,1,0:T(8,128)S(1)}, f32[2,384,384]{2,1,0:T(8,128)}, u32[]{:S(2)}, u32[]{:S(2)}) collective-permute-start(f32[2,384,384]{2,1,0:T(8,128)S(1)} %pad_maximum_fusion.1.refs_0_), channel_id=1, source_target_pairs={{0,12},{1,13},{2,14},{3,15},{4,0},{5,1},{6,2},{7,3},{8,4},{9,5},{1... | collective-permute-start | bytes 3538952 | tf_op jit(solution)/shard_map/ppermute | solution.py:58
  196.4 0.1 stack.188.at
  196.5 11.1 %collective-permute-done.14.refs_2_ = f32[2,384,384]{2,1,0:T(8,128)} collective-permute-done((f32[2,384,384]{2,1,0:T(8,128)S(1)}, f32[2,384,384]{2,1,0:T(8,128)}, u32[]{:S(2)}, u32[]{:S(2)}) %collective-permute-start.14) | collective-permute-done | bytes 1179680 | tf_op jit(solution)/shard_map/ppermute | solution.py:58
  207.6 2.7 %collective-permute-start.26 = (f32[2,384,384]{2,1,0:T(8,128)}, f32[2,384,384]{2,1,0:T(8,128)}, u32[]{:S(2)}, u32[]{:S(2)}) collective-permute-start(f32[2,384,384]{2,1,0:T(8,128)} %collective-permute-done.17.refs_5_), channel_id=1, source_target_pairs={{0,12},{1,13},{2,14},{3,15},{4,0},{5,1},{6,2},{7,3},{8,4},{9,5},{1... | collective-permute-start | bytes 3538952 | tf_op jit(solution)/shard_map/ppermute | solution.py:58
  210.4 9.9 %collective-permute-done.15.refs_3_ = f32[2,384,384]{2,1,0:T(8,128)} collective-permute-done((f32[2,384,384]{2,1,0:T(8,128)S(1)}, f32[2,384,384]{2,1,0:T(8,128)}, u32[]{:S(2)}, u32[]{:S(2)}) %collective-permute-start.15) | collective-permute-done | bytes 1179680 | tf_op jit(solution)/shard_map/ppermute | solution.py:58
  220.3 7.9 %all-gather.8.cloned.1.call-done = f32[3072,384]{1,0:T(8,128)} async-done(((f32[384,384]{1,0:T(8,128)}), f32[3072,384]{1,0:T(8,128)}) %all-gather.8.cloned.1.call-update) | async-done | bytes 4718608 | tf_op jit(solution)/shard_map/all_gather | solution.py:357
  228.2 2.3 copy-done
  230.5 10.0 %near.3 = (f32[2,384,384]{2,1,0:T(8,128)S(1)}, f32[3,8,32,384]{3,2,1,0:T(8,128)}) custom-call(s32[12]{0:T(128)S(1)} %copy-done.4, s32[1]{0:T(128)} %bitcast.first, s32[24]{0:T(128)S(1)} %stack.188.at, f32[2,384,384]{2,1,0:T(8,128)S(1)} %pad_maximum_fusion.1.refs_0_, f32[2,384,384]{2,1,0:T(8,128)S(1)} %pad_maximum_fusion.2.refs_1_, ...), custom_call_target="tpu_custom_call" | custom-call | flops 48922361856 | bytes 141557760 | tf_op jit(solution)/shard_map/near/pallas_call | solution.py:172
  240.5 4.9 %child.1 = f32[768,384]{1,0:T(8,128)} custom-call(s32[24]{0:T(128)S(1)} %stack.188.at, f32[2,384,384]{2,1,0:T(8,128)S(1)} %get-tuple-element.21.acc, f32[2,384,384]{2,1,0:T(8,128)S(1)} %collective-permute-done.25.top, f32[2,384,384]{2,1,0:T(8,128)} %collective-permute-done.26.low, f32[8,384,384]{2,1,0:T(8,128)S(1)} %bitcast.75, f32[768,384]{1,0:T(8,128)S(1)} %copy-done.1), custom_call_target="tpu_custom_call" | custom-call | flops 1358954496 | bytes 3538944 | tf_op jit(solution)/shard_map/child/pallas_call | solution.py:243
  (47 shorter events, 0.3 us)
Async XLA Ops:
  7.2 91.6 %all-gather.4.cloned.1.call-start = ((), (), s32[]{:S(2)}) async-start(), calls=%async_computation.3 | async-start | bytes 10616832 | tf_op jit(solution)/shard_map/all_gather | solution.py:343
  8.6 22.4 %copy-start.4 = (s32[12]{0:T(128)S(1)}, s32[12]{0:T(128)}, u32[]{:S(2)}) copy-start(s32[12]{0:T(128)} %anc.7) | copy-start | bytes 148
  31.0 4.5 %copy-start.6 = (f32[768,384]{1,0:T(8,128)S(1)}, f32[768,384]{1,0:T(8,128)}, u32[]{:S(2)}) copy-start(f32[768,384]{1,0:T(8,128)} %param.5) | copy-start | bytes 3538948
  31.6 10.7 %collective-permute-start.1 = (f32[384,384]{1,0:T(8,128)S(1)}, f32[384,384]{1,0:T(8,128)S(1)}, u32[]{:S(2)}, u32[]{:S(2)}) collective-permute-start(f32[384,384]{1,0:T(8,128)S(1)} %bitcast.78), channel_id=1, source_target_pairs={{0,3},{1,0},{2,1},{3,2},{4,7},{5,4},{6,5},{7,6},{8,11},{9,8},{10,9... | collective-permute-start | bytes 1769480 | tf_op jit(solution)/shard_map/ppermute | solution.py:58
  35.4 10.3 %collective-permute-start = (f32[384,384]{1,0:T(8,128)S(1)}, f32[384,384]{1,0:T(8,128)S(1)}, u32[]{:S(2)}, u32[]{:S(2)}) collective-permute-start(f32[384,384]{1,0:T(8,128)S(1)} %bitcast.79), channel_id=1, source_target_pairs={{0,1},{1,2},{2,3},{3,0},{4,5},{5,6},{6,7},{7,4},{8,9},{9,10},{10,1... | collective-permute-start | bytes 1769480 | tf_op jit(solution)/shard_map/ppermute | solution.py:58
  36.5 28.9 %all-to-all-start.1 = ((f32[3,8,32,384]{3,2,0,1:T(8,128)}), f32[3,8,32,384]{3,2,0,1:T(8,128)S(1)}, u32[]{:S(2)}, u32[]{:S(2)}) async-start(f32[3,8,32,384]{3,2,0,1:T(8,128)} %copy.8), calls=%async_computation.1 | async-start | bytes 2359296 | tf_op jit(solution)/shard_map/all_to_all | solution.py:298
  40.1 139.9 %all-gather.6.cloned.1.call-start = ((), (), s32[]{:S(2)}) async-start(), calls=%async_computation.4 | async-start | bytes 5013504 | tf_op jit(solution)/shard_map/all_gather | solution.py:348
  42.3 7.1 %collective-permute-start.3 = (f32[192,384]{1,0:T(8,128)S(1)}, f32[192,384]{1,0:T(8,128)S(1)}, u32[]{:S(2)}, u32[]{:S(2)}) collective-permute-start(f32[192,384]{1,0:T(8,128)S(1)} %slice.25), channel_id=1, source_target_pairs={{0,3},{1,0},{2,1},{3,2},{4,7},{5,4},{6,5},{7,6},{8,11},{9,8},{10,9... | collective-permute-start | bytes 884744 | tf_op jit(solution)/shard_map/ppermute | solution.py:58
  45.8 7.3 %collective-permute-start.2 = (f32[192,384]{1,0:T(8,128)S(1)}, f32[192,384]{1,0:T(8,128)S(1)}, u32[]{:S(2)}, u32[]{:S(2)}) collective-permute-start(f32[192,384]{1,0:T(8,128)S(1)} %slice.24), channel_id=1, source_target_pairs={{0,1},{1,2},{2,3},{3,0},{4,5},{5,6},{6,7},{7,4},{8,9},{9,10},{10,1... | collective-permute-start | bytes 884744 | tf_op jit(solution)/shard_map/ppermute | solution.py:58
  54.6 38.2 %collective-permute-start.4 = (f32[4,384,384]{2,1,0:T(8,128)}, f32[4,384,384]{2,1,0:T(8,128)S(1)}, u32[]{:S(2)}, u32[]{:S(2)}) collective-permute-start(f32[4,384,384]{2,1,0:T(8,128)} %pad_maximum_fusion.refs_0_), channel_id=1, source_target_pairs={{0,4},{1,5},{2,6},{3,7},{4,8},{5,9},{6,10},{7,11},{8,12},{9,13},{1... | collective-permute-start | bytes 7077896 | tf_op jit(solution)/shard_map/ppermute | solution.py:58
  55.7 40.0 %collective-permute-start.5 = (f32[4,384,384]{2,1,0:T(8,128)}, f32[4,384,384]{2,1,0:T(8,128)}, u32[]{:S(2)}, u32[]{:S(2)}) collective-permute-start(f32[4,384,384]{2,1,0:T(8,128)} %pad_maximum_fusion.refs_0_), channel_id=1, source_target_pairs={{0,12},{1,13},{2,14},{3,15},{4,0},{5,1},{6,2},{7,3},{8,4},{9,5},{1... | collective-permute-start | bytes 7077896 | tf_op jit(solution)/shard_map/ppermute | solution.py:58
  92.4 135.7 %all-gather.8.cloned.1.call-start = ((), (), s32[]{:S(2)}) async-start(), calls=%async_computation.5 | async-start | bytes 5308416 | tf_op jit(solution)/shard_map/all_gather | solution.py:357
  92.8 1.8 copy-start.2
  94.7 16.8 %collective-permute-start.6 = (f32[2,384,384]{2,1,0:T(8,128)}, f32[2,384,384]{2,1,0:T(8,128)S(1)}, u32[]{:S(2)}, u32[]{:S(2)}) collective-permute-start(f32[2,384,384]{2,1,0:T(8,128)} %slice.26), channel_id=1, source_target_pairs={{0,4},{1,5},{2,6},{3,7},{4,8},{5,9},{6,10},{7,11},{8,12},{9,13},{1... | collective-permute-start | bytes 3538952 | tf_op jit(solution)/shard_map/ppermute | solution.py:58
  97.1 16.4 %collective-permute-start.7 = (f32[2,384,384]{2,1,0:T(8,128)S(1)}, f32[2,384,384]{2,1,0:T(8,128)S(1)}, u32[]{:S(2)}, u32[]{:S(2)}) collective-permute-start(f32[2,384,384]{2,1,0:T(8,128)S(1)} %slice.27), channel_id=1, source_target_pairs={{0,12},{1,13},{2,14},{3,15},{4,0},{5,1},{6,2},{7,3},{8,4},{9,5},{1... | collective-permute-start | bytes 3538952 | tf_op jit(solution)/shard_map/ppermute | solution.py:58
  98.8 14.7 %slice-start = ((s8[9437184]{0:T(1024)(128)(4,1)}), s8[4194304]{0:T(1024)(128)(4,1)S(1)}, s32[]{:S(2)}) async-start(s8[9437184]{0:T(1024)(128)(4,1)} %bitcast.71), calls=%async_computation.6 | async-start | bytes 8388608
  98.8 1.8 copy-start.3
  100.6 12.9 %slice-start.1 = ((s8[9437184]{0:T(1024)(128)(4,1)}), s8[4194304]{0:T(1024)(128)(4,1)S(1)}, s32[]{:S(2)}) async-start(s8[9437184]{0:T(1024)(128)(4,1)} %bitcast.71), calls=%async_computation.7 | async-start | bytes 8388608
  100.6 12.9 %slice-start.2 = ((s8[9437184]{0:T(1024)(128)(4,1)}), s8[1048576]{0:T(1024)(128)(4,1)S(1)}, s32[]{:S(2)}) async-start(s8[9437184]{0:T(1024)(128)(4,1)} %bitcast.71), calls=%async_computation.8 | async-start | bytes 2097152
  116.9 12.8 %collective-permute-start.8 = (f32[384,384]{1,0:T(8,128)S(1)}, f32[384,384]{1,0:T(8,128)S(1)}, u32[]{:S(2)}, u32[]{:S(2)}) collective-permute-start(f32[384,384]{1,0:T(8,128)S(1)} %get-tuple-element.13), channel_id=1, source_target_pairs={{0,0},{1,1},{2,16},{3,17},{4,4},{5,5},{6,20},{7,21},{8,8},{9,9},{1... | collective-permute-start | bytes 1769480 | tf_op jit(solution)/shard_map/ppermute | solution.py:79
  121.9 9.3 %collective-permute-start.18 = (f32[12,32,384]{2,1,0:T(8,128)S(1)}, f32[12,32,384]{2,1,0:T(8,128)S(1)}, u32[]{:S(2)}, u32[]{:S(2)}) collective-permute-start(f32[12,32,384]{2,1,0:T(8,128)S(1)} %bitcast.82), channel_id=1, source_target_pairs={{0,32},{16,112},{32,64},{48,16},{64,96},{80,48},{96,0},{112,80},{1... | collective-permute-start | bytes 1769480 | tf_op jit(solution)/shard_map/ppermute | solution.py:37
  129.7 7.1 %collective-permute-start.9 = (f32[384,384]{1,0:T(8,128)S(1)}, f32[384,384]{1,0:T(8,128)S(1)}, u32[]{:S(2)}, u32[]{:S(2)}) collective-permute-start(f32[384,384]{1,0:T(8,128)S(1)} %collective-permute-done.8), channel_id=1, source_target_pairs={{0,0},{1,1},{2,2},{3,3},{4,36},{5,37},{6,38},{7,39},{8,72},{9,73},... | collective-permute-start | bytes 1769480 | tf_op jit(solution)/shard_map/ppermute | solution.py:80
  131.2 22.6 %collective-permute-start.19 = (f32[12,32,384]{2,1,0:T(8,128)S(1)}, f32[12,32,384]{2,1,0:T(8,128)}, u32[]{:S(2)}, u32[]{:S(2)}) collective-permute-start(f32[12,32,384]{2,1,0:T(8,128)S(1)} %collective-permute-done.18.refs_1_), channel_id=1, source_target_pairs={{0,32},{16,112},{32,64},{48,16},{64,96},{80,48},{96,0},{112,80},{1... | collective-permute-start | bytes 1769480 | tf_op jit(solution)/shard_map/ppermute | solution.py:37
  136.8 28.5 %collective-permute-start.11 = (f32[384,384]{1,0:T(8,128)S(1)}, f32[384,384]{1,0:T(8,128)S(1)}, u32[]{:S(2)}, u32[]{:S(2)}) collective-permute-start(f32[384,384]{1,0:T(8,128)S(1)} %collective-permute-done.9), channel_id=1, source_target_pairs={{0,3},{1,0},{2,1},{3,2},{4,7},{5,4},{6,5},{7,6},{8,11},{9,8},{10,9... | collective-permute-start | bytes 1769480 | tf_op jit(solution)/shard_map/ppermute | solution.py:58
  145.8 23.6 %collective-permute-start.10 = (f32[384,384]{1,0:T(8,128)S(1)}, f32[384,384]{1,0:T(8,128)S(1)}, u32[]{:S(2)}, u32[]{:S(2)}) collective-permute-start(f32[384,384]{1,0:T(8,128)S(1)} %collective-permute-done.9), channel_id=1, source_target_pairs={{0,1},{1,2},{2,3},{3,0},{4,5},{5,6},{6,7},{7,4},{8,9},{9,10},{10,1... | collective-permute-start | bytes 1769480 | tf_op jit(solution)/shard_map/ppermute | solution.py:58
  153.9 15.6 %collective-permute-start.20 = (f32[12,32,384]{2,1,0:T(8,128)}, f32[12,32,384]{2,1,0:T(8,128)}, u32[]{:S(2)}, u32[]{:S(2)}) collective-permute-start(f32[12,32,384]{2,1,0:T(8,128)} %collective-permute-done.19.refs_2_), channel_id=1, source_target_pairs={{0,32},{16,112},{32,64},{48,16},{64,96},{80,48},{96,0},{112,80},{1... | collective-permute-start | bytes 1769480 | tf_op jit(solution)/shard_map/ppermute | solution.py:37
  165.3 7.3 %collective-permute-start.13 = (f32[192,384]{1,0:T(8,128)S(1)}, f32[192,384]{1,0:T(8,128)S(1)}, u32[]{:S(2)}, u32[]{:S(2)}) collective-permute-start(f32[192,384]{1,0:T(8,128)S(1)} %slice.29), channel_id=1, source_target_pairs={{0,3},{1,0},{2,1},{3,2},{4,7},{5,4},{6,5},{7,6},{8,11},{9,8},{10,9... | collective-permute-start | bytes 884744 | tf_op jit(solution)/shard_map/ppermute | solution.py:58
  168.9 11.1 %collective-permute-start.21 = (f32[12,32,384]{2,1,0:T(8,128)S(1)}, f32[12,32,384]{2,1,0:T(8,128)}, u32[]{:S(2)}, u32[]{:S(2)}) collective-permute-start(f32[12,32,384]{2,1,0:T(8,128)S(1)} %bitcast.83), channel_id=1, source_target_pairs={{0,16},{16,0},{1,17},{17,1},{2,18},{18,2},{3,19},{19,3},{4,20},{20... | collective-permute-start | bytes 1769480 | tf_op jit(solution)/shard_map/ppermute | solution.py:41
  168.9 11.1 %collective-permute-start.22 = (f32[12,32,384]{2,1,0:T(8,128)S(1)}, f32[12,32,384]{2,1,0:T(8,128)}, u32[]{:S(2)}, u32[]{:S(2)}) collective-permute-start(f32[12,32,384]{2,1,0:T(8,128)S(1)} %collective-permute-done.18.refs_1_), channel_id=1, source_target_pairs={{0,16},{16,0},{1,17},{17,1},{2,18},{18,2},{3,19},{19,3},{4,20},{20... | collective-permute-start | bytes 1769480 | tf_op jit(solution)/shard_map/ppermute | solution.py:41
  169.4 10.6 %collective-permute-start.23 = (f32[12,32,384]{2,1,0:T(8,128)}, f32[12,32,384]{2,1,0:T(8,128)}, u32[]{:S(2)}, u32[]{:S(2)}) collective-permute-start(f32[12,32,384]{2,1,0:T(8,128)} %collective-permute-done.19.refs_2_), channel_id=1, source_target_pairs={{0,16},{16,0},{1,17},{17,1},{2,18},{18,2},{3,19},{19,3},{4,20},{20... | collective-permute-start | bytes 1769480 | tf_op jit(solution)/shard_map/ppermute | solution.py:41
  169.4 10.6 %collective-permute-start.24 = (f32[12,32,384]{2,1,0:T(8,128)}, f32[12,32,384]{2,1,0:T(8,128)}, u32[]{:S(2)}, u32[]{:S(2)}) collective-permute-start(f32[12,32,384]{2,1,0:T(8,128)} %collective-permute-done.20.refs_3_), channel_id=1, source_target_pairs={{0,16},{16,0},{1,17},{17,1},{2,18},{18,2},{3,19},{19,3},{4,20},{20... | collective-permute-start | bytes 1769480 | tf_op jit(solution)/shard_map/ppermute | solution.py:41
  172.6 7.2 %collective-permute-start.12 = (f32[192,384]{1,0:T(8,128)S(1)}, f32[192,384]{1,0:T(8,128)S(1)}, u32[]{:S(2)}, u32[]{:S(2)}) collective-permute-start(f32[192,384]{1,0:T(8,128)S(1)} %slice.28), channel_id=1, source_target_pairs={{0,1},{1,2},{2,3},{3,0},{4,5},{5,6},{6,7},{7,4},{8,9},{9,10},{10,1... | collective-permute-start | bytes 884744 | tf_op jit(solution)/shard_map/ppermute | solution.py:58
  180.0 2.3 copy-start.5
  190.2 17.4 %collective-permute-start.14 = (f32[2,384,384]{2,1,0:T(8,128)S(1)}, f32[2,384,384]{2,1,0:T(8,128)}, u32[]{:S(2)}, u32[]{:S(2)}) collective-permute-start(f32[2,384,384]{2,1,0:T(8,128)S(1)} %pad_maximum_fusion.1.refs_0_), channel_id=1, source_target_pairs={{0,4},{1,5},{2,6},{3,7},{4,8},{5,9},{6,10},{7,11},{8,12},{9,13},{1... | collective-permute-start | bytes 3538952 | tf_op jit(solution)/shard_map/ppermute | solution.py:58
  192.1 15.5 %collective-permute-start.17 = (f32[2,384,384]{2,1,0:T(8,128)S(1)}, f32[2,384,384]{2,1,0:T(8,128)}, u32[]{:S(2)}, u32[]{:S(2)}) collective-permute-start(f32[2,384,384]{2,1,0:T(8,128)S(1)} %pad_maximum_fusion.2.refs_1_), channel_id=1, source_target_pairs={{0,12},{1,13},{2,14},{3,15},{4,0},{5,1},{6,2},{7,3},{8,4},{9,5},{1... | collective-permute-start | bytes 3538952 | tf_op jit(solution)/shard_map/ppermute | solution.py:58
  193.7 26.6 %collective-permute-start.15 = (f32[2,384,384]{2,1,0:T(8,128)S(1)}, f32[2,384,384]{2,1,0:T(8,128)}, u32[]{:S(2)}, u32[]{:S(2)}) collective-permute-start(f32[2,384,384]{2,1,0:T(8,128)S(1)} %pad_maximum_fusion.2.refs_1_), channel_id=1, source_target_pairs={{0,4},{1,5},{2,6},{3,7},{4,8},{5,9},{6,10},{7,11},{8,12},{9,13},{1... | collective-permute-start | bytes 3538952 | tf_op jit(solution)/shard_map/ppermute | solution.py:58
  193.7 26.6 %collective-permute-start.16 = (f32[2,384,384]{2,1,0:T(8,128)S(1)}, f32[2,384,384]{2,1,0:T(8,128)}, u32[]{:S(2)}, u32[]{:S(2)}) collective-permute-start(f32[2,384,384]{2,1,0:T(8,128)S(1)} %pad_maximum_fusion.1.refs_0_), channel_id=1, source_target_pairs={{0,12},{1,13},{2,14},{3,15},{4,0},{5,1},{6,2},{7,3},{8,4},{9,5},{1... | collective-permute-start | bytes 3538952 | tf_op jit(solution)/shard_map/ppermute | solution.py:58
  207.6 32.9 %collective-permute-start.25 = (f32[2,384,384]{2,1,0:T(8,128)}, f32[2,384,384]{2,1,0:T(8,128)S(1)}, u32[]{:S(2)}, u32[]{:S(2)}) collective-permute-start(f32[2,384,384]{2,1,0:T(8,128)} %collective-permute-done.14.refs_2_), channel_id=1, source_target_pairs={{0,4},{1,5},{2,6},{3,7},{4,8},{5,9},{6,10},{7,11},{8,12},{9,13},{1... | collective-permute-start | bytes 3538952 | tf_op jit(solution)/shard_map/ppermute | solution.py:58
  207.6 32.9 %collective-permute-start.26 = (f32[2,384,384]{2,1,0:T(8,128)}, f32[2,384,384]{2,1,0:T(8,128)}, u32[]{:S(2)}, u32[]{:S(2)}) collective-permute-start(f32[2,384,384]{2,1,0:T(8,128)} %collective-permute-done.17.refs_5_), channel_id=1, source_target_pairs={{0,12},{1,13},{2,14},{3,15},{4,0},{5,1},{6,2},{7,3},{8,4},{9,5},{1... | collective-permute-start | bytes 3538952 | tf_op jit(solution)/shard_map/ppermute | solution.py:58
  228.2 2.3 copy-start
  230.5 10.0 %copy-start.1 = (f32[768,384]{1,0:T(8,128)S(1)}, f32[768,384]{1,0:T(8,128)}, u32[]{:S(2)}) copy-start(f32[768,384]{1,0:T(8,128)} %base.1) | copy-start | bytes 3538948
Sparse Core Ops, SparseCore 0:
  31.7 64.7 all-gather.3
  99.2 70.2 all-gather.5
  190.3 37.7 all-gather.7

commit v13 on v12

--- a/solution.py
+++ b/solution.py
@@ -65,12 +65,12 @@
     if whole:
         group = jnp.stack([x, up, down, jnp.concatenate([top, low])])
         up, down = hop(group, 1, 1), hop(group, 1, -1)
-        return (group, up, down), (hop(up[:2], 1, 1), hop(down[2:], 1, -1))
+        return (group, up, down), (hop(up[:2], 1, 1), hop(down[2:], 1, -1)), top
     one, two = jnp.stack([x, up]), jnp.stack([down, jnp.concatenate([top, low])])
     one, two = lax.optimization_barrier((one, two))
     up_one, down_two = hop(one, 1, 1), hop(two, 1, -1)
     up_two, down_one = hop(two, 1, 1), hop(one, 1, -1)
-    return (one, two, up_one, up_two, down_one, down_two), (hop(up_one, 1, 1), hop(down_two, 1, -1))
+    return (one, two, up_one, up_two, down_one, down_two), (hop(up_one, 1, 1), hop(down_two, 1, -1)), top
 
 
 def turn(x):
@@ -341,7 +341,7 @@
 
     f = pick_rows(ancestors, spread(factor_cross))
     inverse = lax.all_gather(after(factor_inverse, f), ROW, axis=0, tiled=True).reshape(16, w, w)
-    f_near, f_far = gather_cols(f, True)
+    f_near, f_far, _ = gather_cols(f, True)
 
     s = pick_rows(ancestors, spread(after(sigma_top, f)))
     s = lax.all_to_all(after(s, f_near[0]).reshape(16, -1, w), COL, 0, 0, tiled=True)
@@ -350,10 +350,10 @@
     (acc,) = near_product(at, f_near, inverse, 1, W1)
     u, ut = update_product(at, acc, *f_far, inverse)
 
-    u_near, u_far = gather_cols(turn(ut), False)
+    u_near, u_far, u_top = gather_cols(turn(ut), False)
     u_tiles = gather_rows(u.reshape(NANC, sub, w))
 
-    sigma = cross_product(at, after(s_all, u_near[0]), u_tiles)
+    sigma = cross_product(at, after(s_all, u_top), u_tiles)
     sigma_all = lax.all_gather(sigma, ROW, axis=0, tiled=True).reshape(8, w, w)
     acc, rows = near_product(at_turned, u_near, sigma_all, 2, W2, ancestors)
     sigma_child = child_product(at_turned, acc, *u_far, sigma_all, block_inverse)

time: 252 us -> 262 us (1.040); the launches traced: 252 us -> 258 us
  waiting for transfers between devices: 82.7 us -> 91.2 us
  starting transfers between devices: 55.6 us -> 49.7 us
    ppermute x18, waiting for transfers between devices: 52.4 us -> 64.7 us  [hop(): return lax.ppermute(x, ('core',) + COL, pairs)]
    all_gather x1, waiting for transfers between devices: 7.88 us -> 0.01 us  [per_device(): sigma_all = lax.all_gather(sigma, ROW, axis=0, tiled=True).reshape(8, w, w)]
    ppermute x3, waiting for transfers between devices: 8.82 us -> 16.1 us  [step(): lax.ppermute(x, ROW, [(2 * i + c, 2 * ((i + 1 - 2 * c) % 4) + c) for i in...]
    ppermute x3, starting transfers between devices: 10.4 us -> 5.19 us  [step(): lax.ppermute(x, ROW, [(2 * i + c, 2 * ((i + 1 - 2 * c) % 4) + c) for i in...]
    ppermute x1, waiting for transfers between devices: 5.32 us -> 2 us  [turn(): lax.ppermute(x, ALL, [(at(y, c, z, x), at(y, x // 2, (y + z) % 4, 2 * c +...]
    unnamed x20 -> x24, local copies, waits for them, and re-layouts: 7.15 us -> 7.95 us
  transfers between devices with their start and end apart: 31 -> 31, of which waited for: 15 -> 18; matrix products, arithmetic and copies ran while one was open for 2% -> 3% of each run, Pallas kernels for 10% -> 10%
where the time goes in v13:
time: 262 us; the launch traced here: 258 us
  waiting for transfers between devices  91.2 us (35%)
  starting transfers between devices  49.7 us (19%)
  blocking collectives  47.4 us (18%)
  Pallas kernels  37.5 us (14%)
  between operations  14.2 us (5%)
  local copies, waits for them, and re-layouts  13.9 us (5%)
  other arithmetic  3.8 us (1%)
    ppermute x18, waiting for transfers between devices, hop(): return lax.ppermute(x, ('core',) + COL, pairs)  64.7 us
    ppermute x18, starting transfers between devices, hop(): return lax.ppermute(x, ('core',) + COL, pairs)  33.5 us
    all_to_all x1, blocking collectives, per_device(): lax.all_to_all(after(s, f_near[0]).reshape(16, -1, w), COL, 0, 0, tiled=T...  25 us
    all_to_all x1, blocking collectives, spread(): lax.all_to_all(x.reshape(3, 8, sub, w), ROW, 1, 0, tiled=True)  22.4 us
    pallas_call x2, Pallas kernels, near_product(): pl.pallas_call(functools.partial(kernel, 16 // many, len(pieces)), out_sh...  19.2 us
    ppermute x3, waiting for transfers between devices, step(): lax.ppermute(x, ROW, [(2 * i + c, 2 * ((i + 1 - 2 * c) % 4) + c) for i in...  16.1 us
    all_to_all x1, waiting for transfers between devices, spread(): lax.all_to_all(x.reshape(3, 8, sub, w), ROW, 1, 0, tiled=True)  8.17 us
    unnamed x24, local copies, waits for them, and re-layouts  7.95 us
  transfers between devices with their start and end apart: 31, of which 18 were waited for; matrix products, arithmetic and copies ran while one was open for 3% of the time, Pallas kernels for 10%

profile of v13, /device:TPU:1, one launch (start us, length us, event | category | flops | bytes accessed | tf_op | source)
XLA Modules:
  0.0 257.7 jit_solution(16158583222624154932)
XLA Ops:
  7.2 1.3 copy.7
  8.6 22.4 %all_to_all.35 = f32[3,8,32,384]{3,2,0,1:T(8,128)S(1)} all-to-all(f32[3,8,32,384]{3,2,0,1:T(8,128)S(1)} %copy.7), channel_id=1, replica_groups=mesh['y'=4,'core'=2,'z'=4,'x'=4] {'y','core'}, dimensions={1} | all-to-all | bytes 2359296 | tf_op jit(solution)/shard_map/all_to_all | solution.py:298
  31.0 0.6 pick_rows.2
  31.6 3.8 %collective-permute-start.1 = (f32[384,384]{1,0:T(8,128)S(1)}, f32[384,384]{1,0:T(8,128)S(1)}, u32[]{:S(2)}, u32[]{:S(2)}) collective-permute-start(f32[384,384]{1,0:T(8,128)S(1)} %bitcast.78), channel_id=1, source_target_pairs={{0,3},{1,0},{2,1},{3,2},{4,7},{5,4},{6,5},{7,6},{8,11},{9,8},{10,9... | collective-permute-start | bytes 1769480 | tf_op jit(solution)/shard_map/ppermute | solution.py:58
  35.4 1.1 copy.8
  36.5 3.5 %all-to-all-start.1 = ((f32[3,8,32,384]{3,2,0,1:T(8,128)}), f32[3,8,32,384]{3,2,0,1:T(8,128)S(1)}, u32[]{:S(2)}, u32[]{:S(2)}) async-start(f32[3,8,32,384]{3,2,0,1:T(8,128)} %copy.8), calls=%async_computation.1 | async-start | bytes 2359296 | tf_op jit(solution)/shard_map/all_to_all | solution.py:298
  40.1 2.2 collective-permute-done.1
  42.3 3.5 %collective-permute-start.3 = (f32[192,384]{1,0:T(8,128)S(1)}, f32[192,384]{1,0:T(8,128)S(1)}, u32[]{:S(2)}, u32[]{:S(2)}) collective-permute-start(f32[192,384]{1,0:T(8,128)S(1)} %slice.25), channel_id=1, source_target_pairs={{0,3},{1,0},{2,1},{3,2},{4,7},{5,4},{6,5},{7,6},{8,11},{9,8},{10,9... | collective-permute-start | bytes 884744 | tf_op jit(solution)/shard_map/ppermute | solution.py:58
  45.9 3.6 %collective-permute-done.3 = f32[192,384]{1,0:T(8,128)S(1)} collective-permute-done((f32[192,384]{1,0:T(8,128)S(1)}, f32[192,384]{1,0:T(8,128)S(1)}, u32[]{:S(2)}, u32[]{:S(2)}) %collective-permute-start.3) | collective-permute-done | bytes 294944 | tf_op jit(solution)/shard_map/ppermute | solution.py:58
  49.4 3.6 %collective-permute-done.2 = f32[192,384]{1,0:T(8,128)S(1)} collective-permute-done((f32[192,384]{1,0:T(8,128)S(1)}, f32[192,384]{1,0:T(8,128)S(1)}, u32[]{:S(2)}, u32[]{:S(2)}) %collective-permute-start.2) | collective-permute-done | bytes 294944 | tf_op jit(solution)/shard_map/ppermute | solution.py:58
  53.1 1.5 pad_maximum_fusion.refs_0_
  54.6 1.1 collective-permute-start.4
  55.7 1.6 collective-permute-start.5
  57.3 8.2 %all-to-all-done.1 = f32[3,8,32,384]{3,2,0,1:T(8,128)S(1)} async-done(((f32[3,8,32,384]{3,2,0,1:T(8,128)}), f32[3,8,32,384]{3,2,0,1:T(8,128)S(1)}, u32[]{:S(2)}, u32[]{:S(2)}) %all-to-all-start.1) | async-done | bytes 1179680 | tf_op jit(solution)/shard_map/all_to_all | solution.py:298
  65.5 0.6 pick_rows.3
  66.1 25.0 %all_to_all.36.x = f32[16,24,384]{2,1,0:T(8,128)S(1)} all-to-all(f32[16,24,384]{2,1,0:T(8,128)S(1)} %bitcast.81), channel_id=1, replica_groups=mesh['y'=4,'core'=2,'z'=4,'x'=4] {'z','x'}, dimensions={0} | all-to-all | bytes 1179648 | tf_op jit(solution)/shard_map/all_to_all | solution.py:347
  91.0 1.4 pick_cols.1
  92.7 0.1 stack.205.at
  92.9 1.2 slice.26
  94.1 0.6 copy-done.2
  94.7 1.1 collective-permute-start.6
  95.8 1.3 slice.27
  97.1 1.6 collective-permute-start.7
  98.8 1.8 copy-done.3
  100.6 9.2 %near.2.acc = f32[1,384,384]{2,1,0:T(8,128)S(1)} custom-call(s32[24]{0:T(128)S(1)} %stack.205.at, f32[4,384,384]{2,1,0:T(8,128)} %pad_maximum_fusion.refs_0_, f32[4,384,384]{2,1,0:T(8,128)S(1)} %copy-done.3, f32[4,384,384]{2,1,0:T(8,128)} %collective-permute-done.5.refs_2_, f32[16,384,384]{2,1,0:T(8,128)} %bitcast.70), custom_call_target="tpu_custom_call" | custom-call | flops 48922361856 | bytes 198180864 | tf_op jit(solution)/shard_map/near/pallas_call | solution.py:172
  109.8 1.7 collective-permute-done.6.top
  111.5 2.4 collective-permute-done.7.low
  113.8 3.4 %update.1 = (f32[384,384]{1,0:T(8,128)S(1)}, f32[384,384]{1,0:T(8,128)S(1)}) custom-call(s32[24]{0:T(128)S(1)} %stack.205.at, f32[1,384,384]{2,1,0:T(8,128)S(1)} %near.2.acc, f32[2,384,384]{2,1,0:T(8,128)S(1)} %collective-permute-done.6.top, f32[2,384,384]{2,1,0:T(8,128)S(1)} %collective-permute-done.7.low, f32[16,384,384]{2,1,0:T(8,128)S(1)} %bitcast.73), custom_call_target="tpu_custom_call" | custom-call | flops 1358954496 | bytes 2359296 | tf_op jit(solution)/shard_map/update/pallas_call | solution.py:221
  117.3 0.2 collective-permute-start.18
  117.4 5.1 %collective-permute-start.8 = (f32[384,384]{1,0:T(8,128)S(1)}, f32[384,384]{1,0:T(8,128)S(1)}, u32[]{:S(2)}, u32[]{:S(2)}) collective-permute-start(f32[384,384]{1,0:T(8,128)S(1)} %get-tuple-element.13), channel_id=1, source_target_pairs={{0,0},{1,1},{2,16},{3,17},{4,4},{5,5},{6,20},{7,21},{8,8},{9,9},{1... | collective-permute-start | bytes 1769480 | tf_op jit(solution)/shard_map/ppermute | solution.py:79
  122.6 3.5 %collective-permute-done.18.refs_1_ = f32[12,32,384]{2,1,0:T(8,128)S(1)} collective-permute-done((f32[12,32,384]{2,1,0:T(8,128)S(1)}, f32[12,32,384]{2,1,0:T(8,128)S(1)}, u32[]{:S(2)}, u32[]{:S(2)}) %collective-permute-start.18) | collective-permute-done | bytes 589856 | tf_op jit(solution)/shard_map/ppermute | solution.py:37
  126.1 2.0 collective-permute-start.19
  128.1 2.0 collective-permute-done.8
  130.1 1.5 collective-permute-start.9
  131.6 3.5 %collective-permute-done.19.refs_2_ = f32[12,32,384]{2,1,0:T(8,128)S(1)} collective-permute-done((f32[12,32,384]{2,1,0:T(8,128)S(1)}, f32[12,32,384]{2,1,0:T(8,128)S(1)}, u32[]{:S(2)}, u32[]{:S(2)}) %collective-permute-start.19) | collective-permute-done | bytes 589856 | tf_op jit(solution)/shard_map/ppermute | solution.py:37
  135.1 3.0 %collective-permute-start.20 = (f32[12,32,384]{2,1,0:T(8,128)S(1)}, f32[12,32,384]{2,1,0:T(8,128)S(1)}, u32[]{:S(2)}, u32[]{:S(2)}) collective-permute-start(f32[12,32,384]{2,1,0:T(8,128)S(1)} %collective-permute-done.19.refs_2_), channel_id=1, source_target_pairs={{0,32},{16,112},{32,64},{48,16},{64,96},{80,48},{96,0},{112,80},{1... | collective-permute-start | bytes 1769480 | tf_op jit(solution)/shard_map/ppermute | solution.py:37
  138.1 9.9 %collective-permute-start.10 = (f32[384,384]{1,0:T(8,128)}, f32[384,384]{1,0:T(8,128)S(1)}, u32[]{:S(2)}, u32[]{:S(2)}) collective-permute-start(f32[384,384]{1,0:T(8,128)} %collective-permute-done.9), channel_id=1, source_target_pairs={{0,1},{1,2},{2,3},{3,0},{4,5},{5,6},{6,7},{7,4},{8,9},{9,10},{10,1... | collective-permute-start | bytes 1769480 | tf_op jit(solution)/shard_map/ppermute | solution.py:58
  148.1 0.5 collective-permute-start.22
  148.6 9.1 %collective-permute-done.20.refs_3_ = f32[12,32,384]{2,1,0:T(8,128)S(1)} collective-permute-done((f32[12,32,384]{2,1,0:T(8,128)S(1)}, f32[12,32,384]{2,1,0:T(8,128)S(1)}, u32[]{:S(2)}, u32[]{:S(2)}) %collective-permute-start.20) | collective-permute-done | bytes 589856 | tf_op jit(solution)/shard_map/ppermute | solution.py:37
  157.7 0.3 collective-permute-start.24
  158.0 10.5 %collective-permute-done.10 = f32[384,384]{1,0:T(8,128)S(1)} collective-permute-done((f32[384,384]{1,0:T(8,128)}, f32[384,384]{1,0:T(8,128)S(1)}, u32[]{:S(2)}, u32[]{:S(2)}) %collective-permute-start.10) | collective-permute-done | bytes 589856 | tf_op jit(solution)/shard_map/ppermute | solution.py:58
  168.5 0.8 copy-done.6
  169.3 0.7 slice.28
  170.0 0.1 all-gather.6.cloned.1.call-done.s
  170.1 7.3 %collective-permute-done.12 = f32[192,384]{1,0:T(8,128)} collective-permute-done((f32[192,384]{1,0:T(8,128)}, f32[192,384]{1,0:T(8,128)}, u32[]{:S(2)}, u32[]{:S(2)}) %collective-permute-start.12) | collective-permute-done | bytes 294944 | tf_op jit(solution)/shard_map/ppermute | solution.py:58
  177.4 2.3 copy-done.5
  179.8 7.4 %cross.1 = f32[384,384]{1,0:T(8,128)} custom-call(s32[24]{0:T(128)S(1)} %stack.205.at, f32[384,3072]{1,0:T(8,128)S(1)} %copy-done.5, f32[12,32,384]{2,1,0:T(8,128)S(1)} %bitcast.84, f32[12,32,384]{2,1,0:T(8,128)S(1)} %collective-permute-done.18.refs_1_, f32[12,32,384]{2,1,0:T(8,128)S(1)} %collective-permute-done.19.refs_2_, ...), custom_call_target="tpu_custom_call" | custom-call | flops 2717908992 | bytes 9437184 | tf_op jit(solution)/shard_map/cross/pallas_call | solution.py:278
  187.2 0.5 collective-permute-start.11
  187.7 8.8 %collective-permute-done.11 = f32[384,384]{1,0:T(8,128)S(1)} collective-permute-done((f32[384,384]{1,0:T(8,128)}, f32[384,384]{1,0:T(8,128)S(1)}, u32[]{:S(2)}, u32[]{:S(2)}) %collective-permute-start.11) | collective-permute-done | bytes 589856 | tf_op jit(solution)/shard_map/ppermute | solution.py:58
  196.5 1.4 collective-permute-start.13
  197.9 1.2 pad_maximum_fusion.1.refs_0_
  199.1 3.5 %collective-permute-done.13 = f32[192,384]{1,0:T(8,128)S(1)} collective-permute-done((f32[192,384]{1,0:T(8,128)S(1)}, f32[192,384]{1,0:T(8,128)S(1)}, u32[]{:S(2)}, u32[]{:S(2)}) %collective-permute-start.13) | collective-permute-done | bytes 294944 | tf_op jit(solution)/shard_map/ppermute | solution.py:58
  202.6 1.0 maximum_bitcast_fusion.1
  203.7 1.8 collective-permute-start.14
  205.5 1.6 collective-permute-start.17
  207.1 2.7 %collective-permute-start.16 = (f32[2,384,384]{2,1,0:T(8,128)S(1)}, f32[2,384,384]{2,1,0:T(8,128)}, u32[]{:S(2)}, u32[]{:S(2)}) collective-permute-start(f32[2,384,384]{2,1,0:T(8,128)S(1)} %pad_maximum_fusion.1.refs_0_), channel_id=1, source_target_pairs={{0,12},{1,13},{2,14},{3,15},{4,0},{5,1},{6,2},{7,3},{8,4},{9,5},{1... | collective-permute-start | bytes 3538952 | tf_op jit(solution)/shard_map/ppermute | solution.py:58
  209.8 0.1 stack.188.at
  209.9 11.1 %collective-permute-done.14.refs_2_ = f32[2,384,384]{2,1,0:T(8,128)} collective-permute-done((f32[2,384,384]{2,1,0:T(8,128)S(1)}, f32[2,384,384]{2,1,0:T(8,128)}, u32[]{:S(2)}, u32[]{:S(2)}) %collective-permute-start.14) | collective-permute-done | bytes 1179680 | tf_op jit(solution)/shard_map/ppermute | solution.py:58
  221.0 2.7 %collective-permute-start.26 = (f32[2,384,384]{2,1,0:T(8,128)}, f32[2,384,384]{2,1,0:T(8,128)}, u32[]{:S(2)}, u32[]{:S(2)}) collective-permute-start(f32[2,384,384]{2,1,0:T(8,128)} %collective-permute-done.17.refs_5_), channel_id=1, source_target_pairs={{0,12},{1,13},{2,14},{3,15},{4,0},{5,1},{6,2},{7,3},{8,4},{9,5},{1... | collective-permute-start | bytes 3538952 | tf_op jit(solution)/shard_map/ppermute | solution.py:58
  223.7 9.9 %collective-permute-done.15.refs_3_ = f32[2,384,384]{2,1,0:T(8,128)} collective-permute-done((f32[2,384,384]{2,1,0:T(8,128)S(1)}, f32[2,384,384]{2,1,0:T(8,128)}, u32[]{:S(2)}, u32[]{:S(2)}) %collective-permute-start.15) | collective-permute-done | bytes 1179680 | tf_op jit(solution)/shard_map/ppermute | solution.py:58
  233.6 2.3 copy-done
  236.0 10.0 %near.3 = (f32[2,384,384]{2,1,0:T(8,128)S(1)}, f32[3,8,32,384]{3,2,1,0:T(8,128)}) custom-call(s32[12]{0:T(128)S(1)} %copy-done.4, s32[1]{0:T(128)} %bitcast.first, s32[24]{0:T(128)S(1)} %stack.188.at, f32[2,384,384]{2,1,0:T(8,128)S(1)} %pad_maximum_fusion.1.refs_0_, f32[2,384,384]{2,1,0:T(8,128)S(1)} %pad_maximum_fusion.2.refs_1_, ...), custom_call_target="tpu_custom_call" | custom-call | flops 48922361856 | bytes 141557760 | tf_op jit(solution)/shard_map/near/pallas_call | solution.py:172
  246.0 0.2 collective-permute-done.25.top
  246.2 4.9 %child.1 = f32[768,384]{1,0:T(8,128)} custom-call(s32[24]{0:T(128)S(1)} %stack.188.at, f32[2,384,384]{2,1,0:T(8,128)S(1)} %get-tuple-element.21.acc, f32[2,384,384]{2,1,0:T(8,128)S(1)} %collective-permute-done.25.top, f32[2,384,384]{2,1,0:T(8,128)} %collective-permute-done.26.low, f32[8,384,384]{2,1,0:T(8,128)S(1)} %bitcast.75, f32[768,384]{1,0:T(8,128)S(1)} %copy-done.1), custom_call_target="tpu_custom_call" | custom-call | flops 1358954496 | bytes 3538944 | tf_op jit(solution)/shard_map/child/pallas_call | solution.py:243
  (51 shorter events, 0.6 us)
Async XLA Ops:
  7.2 91.6 %all-gather.4.cloned.1.call-start = ((), (), s32[]{:S(2)}) async-start(), calls=%async_computation.3 | async-start | bytes 10616832 | tf_op jit(solution)/shard_map/all_gather | solution.py:343
  8.6 22.4 %copy-start.4 = (s32[12]{0:T(128)S(1)}, s32[12]{0:T(128)}, u32[]{:S(2)}) copy-start(s32[12]{0:T(128)} %anc.7) | copy-start | bytes 148
  31.0 4.5 %copy-start.8 = (f32[768,384]{1,0:T(8,128)S(1)}, f32[768,384]{1,0:T(8,128)}, u32[]{:S(2)}) copy-start(f32[768,384]{1,0:T(8,128)} %param.5) | copy-start | bytes 3538948
  31.6 10.7 %collective-permute-start.1 = (f32[384,384]{1,0:T(8,128)S(1)}, f32[384,384]{1,0:T(8,128)S(1)}, u32[]{:S(2)}, u32[]{:S(2)}) collective-permute-start(f32[384,384]{1,0:T(8,128)S(1)} %bitcast.78), channel_id=1, source_target_pairs={{0,3},{1,0},{2,1},{3,2},{4,7},{5,4},{6,5},{7,6},{8,11},{9,8},{10,9... | collective-permute-start | bytes 1769480 | tf_op jit(solution)/shard_map/ppermute | solution.py:58
  35.4 10.3 %collective-permute-start = (f32[384,384]{1,0:T(8,128)S(1)}, f32[384,384]{1,0:T(8,128)S(1)}, u32[]{:S(2)}, u32[]{:S(2)}) collective-permute-start(f32[384,384]{1,0:T(8,128)S(1)} %bitcast.79), channel_id=1, source_target_pairs={{0,1},{1,2},{2,3},{3,0},{4,5},{5,6},{6,7},{7,4},{8,9},{9,10},{10,1... | collective-permute-start | bytes 1769480 | tf_op jit(solution)/shard_map/ppermute | solution.py:58
  36.5 28.9 %all-to-all-start.1 = ((f32[3,8,32,384]{3,2,0,1:T(8,128)}), f32[3,8,32,384]{3,2,0,1:T(8,128)S(1)}, u32[]{:S(2)}, u32[]{:S(2)}) async-start(f32[3,8,32,384]{3,2,0,1:T(8,128)} %copy.8), calls=%async_computation.1 | async-start | bytes 2359296 | tf_op jit(solution)/shard_map/all_to_all | solution.py:298
  40.1 130.1 %all-gather.6.cloned.1.call-start = ((), (), s32[]{:S(2)}) async-start(), calls=%async_computation.4 | async-start | bytes 5013504 | tf_op jit(solution)/shard_map/all_gather | solution.py:348
  42.3 7.1 %collective-permute-start.3 = (f32[192,384]{1,0:T(8,128)S(1)}, f32[192,384]{1,0:T(8,128)S(1)}, u32[]{:S(2)}, u32[]{:S(2)}) collective-permute-start(f32[192,384]{1,0:T(8,128)S(1)} %slice.25), channel_id=1, source_target_pairs={{0,3},{1,0},{2,1},{3,2},{4,7},{5,4},{6,5},{7,6},{8,11},{9,8},{10,9... | collective-permute-start | bytes 884744 | tf_op jit(solution)/shard_map/ppermute | solution.py:58
  45.8 7.3 %collective-permute-start.2 = (f32[192,384]{1,0:T(8,128)S(1)}, f32[192,384]{1,0:T(8,128)S(1)}, u32[]{:S(2)}, u32[]{:S(2)}) collective-permute-start(f32[192,384]{1,0:T(8,128)S(1)} %slice.24), channel_id=1, source_target_pairs={{0,1},{1,2},{2,3},{3,0},{4,5},{5,6},{6,7},{7,4},{8,9},{9,10},{10,1... | collective-permute-start | bytes 884744 | tf_op jit(solution)/shard_map/ppermute | solution.py:58
  54.6 38.2 %collective-permute-start.4 = (f32[4,384,384]{2,1,0:T(8,128)}, f32[4,384,384]{2,1,0:T(8,128)S(1)}, u32[]{:S(2)}, u32[]{:S(2)}) collective-permute-start(f32[4,384,384]{2,1,0:T(8,128)} %pad_maximum_fusion.refs_0_), channel_id=1, source_target_pairs={{0,4},{1,5},{2,6},{3,7},{4,8},{5,9},{6,10},{7,11},{8,12},{9,13},{1... | collective-permute-start | bytes 7077896 | tf_op jit(solution)/shard_map/ppermute | solution.py:58
  55.7 40.1 %collective-permute-start.5 = (f32[4,384,384]{2,1,0:T(8,128)}, f32[4,384,384]{2,1,0:T(8,128)}, u32[]{:S(2)}, u32[]{:S(2)}) collective-permute-start(f32[4,384,384]{2,1,0:T(8,128)} %pad_maximum_fusion.refs_0_), channel_id=1, source_target_pairs={{0,12},{1,13},{2,14},{3,15},{4,0},{5,1},{6,2},{7,3},{8,4},{9,5},{1... | collective-permute-start | bytes 7077896 | tf_op jit(solution)/shard_map/ppermute | solution.py:58
  92.5 141.2 %all-gather.8.cloned.1.call-start = ((), (), s32[]{:S(2)}) async-start(), calls=%async_computation.5 | async-start | bytes 5308416 | tf_op jit(solution)/shard_map/all_gather | solution.py:357
  92.9 1.8 copy-start.2
  94.7 16.8 %collective-permute-start.6 = (f32[2,384,384]{2,1,0:T(8,128)}, f32[2,384,384]{2,1,0:T(8,128)S(1)}, u32[]{:S(2)}, u32[]{:S(2)}) collective-permute-start(f32[2,384,384]{2,1,0:T(8,128)} %slice.26), channel_id=1, source_target_pairs={{0,4},{1,5},{2,6},{3,7},{4,8},{5,9},{6,10},{7,11},{8,12},{9,13},{1... | collective-permute-start | bytes 3538952 | tf_op jit(solution)/shard_map/ppermute | solution.py:58
  97.1 16.7 %collective-permute-start.7 = (f32[2,384,384]{2,1,0:T(8,128)S(1)}, f32[2,384,384]{2,1,0:T(8,128)S(1)}, u32[]{:S(2)}, u32[]{:S(2)}) collective-permute-start(f32[2,384,384]{2,1,0:T(8,128)S(1)} %slice.27), channel_id=1, source_target_pairs={{0,12},{1,13},{2,14},{3,15},{4,0},{5,1},{6,2},{7,3},{8,4},{9,5},{1... | collective-permute-start | bytes 3538952 | tf_op jit(solution)/shard_map/ppermute | solution.py:58
  98.8 15.0 %slice-start = ((s8[9437184]{0:T(1024)(128)(4,1)}), s8[4194304]{0:T(1024)(128)(4,1)S(1)}, s32[]{:S(2)}) async-start(s8[9437184]{0:T(1024)(128)(4,1)} %bitcast.71), calls=%async_computation.6 | async-start | bytes 8388608
  98.8 1.8 copy-start.3
  100.6 13.2 %slice-start.1 = ((s8[9437184]{0:T(1024)(128)(4,1)}), s8[4194304]{0:T(1024)(128)(4,1)S(1)}, s32[]{:S(2)}) async-start(s8[9437184]{0:T(1024)(128)(4,1)} %bitcast.71), calls=%async_computation.7 | async-start | bytes 8388608
  100.6 13.2 %slice-start.2 = ((s8[9437184]{0:T(1024)(128)(4,1)}), s8[1048576]{0:T(1024)(128)(4,1)S(1)}, s32[]{:S(2)}) async-start(s8[9437184]{0:T(1024)(128)(4,1)} %bitcast.71), calls=%async_computation.8 | async-start | bytes 2097152
  117.3 8.8 %collective-permute-start.18 = (f32[12,32,384]{2,1,0:T(8,128)S(1)}, f32[12,32,384]{2,1,0:T(8,128)S(1)}, u32[]{:S(2)}, u32[]{:S(2)}) collective-permute-start(f32[12,32,384]{2,1,0:T(8,128)S(1)} %bitcast.82), channel_id=1, source_target_pairs={{0,32},{16,112},{32,64},{48,16},{64,96},{80,48},{96,0},{112,80},{1... | collective-permute-start | bytes 1769480 | tf_op jit(solution)/shard_map/ppermute | solution.py:37
  117.4 12.7 %collective-permute-start.8 = (f32[384,384]{1,0:T(8,128)S(1)}, f32[384,384]{1,0:T(8,128)S(1)}, u32[]{:S(2)}, u32[]{:S(2)}) collective-permute-start(f32[384,384]{1,0:T(8,128)S(1)} %get-tuple-element.13), channel_id=1, source_target_pairs={{0,0},{1,1},{2,16},{3,17},{4,4},{5,5},{6,20},{7,21},{8,8},{9,9},{1... | collective-permute-start | bytes 1769480 | tf_op jit(solution)/shard_map/ppermute | solution.py:79
  126.1 9.0 %collective-permute-start.19 = (f32[12,32,384]{2,1,0:T(8,128)S(1)}, f32[12,32,384]{2,1,0:T(8,128)S(1)}, u32[]{:S(2)}, u32[]{:S(2)}) collective-permute-start(f32[12,32,384]{2,1,0:T(8,128)S(1)} %collective-permute-done.18.refs_1_), channel_id=1, source_target_pairs={{0,32},{16,112},{32,64},{48,16},{64,96},{80,48},{96,0},{112,80},{1... | collective-permute-start | bytes 1769480 | tf_op jit(solution)/shard_map/ppermute | solution.py:37
  130.1 8.0 %collective-permute-start.9 = (f32[384,384]{1,0:T(8,128)S(1)}, f32[384,384]{1,0:T(8,128)}, u32[]{:S(2)}, u32[]{:S(2)}) collective-permute-start(f32[384,384]{1,0:T(8,128)S(1)} %collective-permute-done.8), channel_id=1, source_target_pairs={{0,0},{1,1},{2,2},{3,3},{4,36},{5,37},{6,38},{7,39},{8,72},{9,73},... | collective-permute-start | bytes 1769480 | tf_op jit(solution)/shard_map/ppermute | solution.py:80
  135.1 22.6 %collective-permute-start.20 = (f32[12,32,384]{2,1,0:T(8,128)S(1)}, f32[12,32,384]{2,1,0:T(8,128)S(1)}, u32[]{:S(2)}, u32[]{:S(2)}) collective-permute-start(f32[12,32,384]{2,1,0:T(8,128)S(1)} %collective-permute-done.19.refs_2_), channel_id=1, source_target_pairs={{0,32},{16,112},{32,64},{48,16},{64,96},{80,48},{96,0},{112,80},{1... | collective-permute-start | bytes 1769480 | tf_op jit(solution)/shard_map/ppermute | solution.py:37
  138.1 30.3 %collective-permute-start.10 = (f32[384,384]{1,0:T(8,128)}, f32[384,384]{1,0:T(8,128)S(1)}, u32[]{:S(2)}, u32[]{:S(2)}) collective-permute-start(f32[384,384]{1,0:T(8,128)} %collective-permute-done.9), channel_id=1, source_target_pairs={{0,1},{1,2},{2,3},{3,0},{4,5},{5,6},{6,7},{7,4},{8,9},{9,10},{10,1... | collective-permute-start | bytes 1769480 | tf_op jit(solution)/shard_map/ppermute | solution.py:58
  148.1 29.3 %collective-permute-start.21 = (f32[12,32,384]{2,1,0:T(8,128)S(1)}, f32[12,32,384]{2,1,0:T(8,128)S(1)}, u32[]{:S(2)}, u32[]{:S(2)}) collective-permute-start(f32[12,32,384]{2,1,0:T(8,128)S(1)} %bitcast.83), channel_id=1, source_target_pairs={{0,16},{16,0},{1,17},{17,1},{2,18},{18,2},{3,19},{19,3},{4,20},{20... | collective-permute-start | bytes 1769480 | tf_op jit(solution)/shard_map/ppermute | solution.py:41
  148.1 29.3 %collective-permute-start.22 = (f32[12,32,384]{2,1,0:T(8,128)S(1)}, f32[12,32,384]{2,1,0:T(8,128)S(1)}, u32[]{:S(2)}, u32[]{:S(2)}) collective-permute-start(f32[12,32,384]{2,1,0:T(8,128)S(1)} %collective-permute-done.18.refs_1_), channel_id=1, source_target_pairs={{0,16},{16,0},{1,17},{17,1},{2,18},{18,2},{3,19},{19,3},{4,20},{20... | collective-permute-start | bytes 1769480 | tf_op jit(solution)/shard_map/ppermute | solution.py:41
  148.6 28.8 %collective-permute-start.23 = (f32[12,32,384]{2,1,0:T(8,128)S(1)}, f32[12,32,384]{2,1,0:T(8,128)}, u32[]{:S(2)}, u32[]{:S(2)}) collective-permute-start(f32[12,32,384]{2,1,0:T(8,128)S(1)} %collective-permute-done.19.refs_2_), channel_id=1, source_target_pairs={{0,16},{16,0},{1,17},{17,1},{2,18},{18,2},{3,19},{19,3},{4,20},{20... | collective-permute-start | bytes 1769480 | tf_op jit(solution)/shard_map/ppermute | solution.py:41
  157.7 19.7 %collective-permute-start.24 = (f32[12,32,384]{2,1,0:T(8,128)S(1)}, f32[12,32,384]{2,1,0:T(8,128)}, u32[]{:S(2)}, u32[]{:S(2)}) collective-permute-start(f32[12,32,384]{2,1,0:T(8,128)S(1)} %collective-permute-done.20.refs_3_), channel_id=1, source_target_pairs={{0,16},{16,0},{1,17},{17,1},{2,18},{18,2},{3,19},{19,3},{4,20},{20... | collective-permute-start | bytes 1769480 | tf_op jit(solution)/shard_map/ppermute | solution.py:41
  168.5 0.8 copy-start.6
  170.0 7.4 %collective-permute-start.12 = (f32[192,384]{1,0:T(8,128)}, f32[192,384]{1,0:T(8,128)}, u32[]{:S(2)}, u32[]{:S(2)}) collective-permute-start(f32[192,384]{1,0:T(8,128)} %slice.28), channel_id=1, source_target_pairs={{0,1},{1,2},{2,3},{3,0},{4,5},{5,6},{6,7},{7,4},{8,9},{9,10},{10,1... | collective-permute-start | bytes 884744 | tf_op jit(solution)/shard_map/ppermute | solution.py:58
  177.4 2.3 copy-start.5
  187.2 10.8 %copy-start.7 = (f32[384,384]{1,0:T(8,128)S(1)}, f32[384,384]{1,0:T(8,128)}, u32[]{:S(2)}) copy-start(f32[384,384]{1,0:T(8,128)} %copy-done.6) | copy-start | bytes 1769476
  187.2 9.3 %collective-permute-start.11 = (f32[384,384]{1,0:T(8,128)}, f32[384,384]{1,0:T(8,128)S(1)}, u32[]{:S(2)}, u32[]{:S(2)}) collective-permute-start(f32[384,384]{1,0:T(8,128)} %collective-permute-done.9), channel_id=1, source_target_pairs={{0,3},{1,0},{2,1},{3,2},{4,7},{5,4},{6,5},{7,6},{8,11},{9,8},{10,9... | collective-permute-start | bytes 1769480 | tf_op jit(solution)/shard_map/ppermute | solution.py:58
  196.5 6.0 %collective-permute-start.13 = (f32[192,384]{1,0:T(8,128)S(1)}, f32[192,384]{1,0:T(8,128)S(1)}, u32[]{:S(2)}, u32[]{:S(2)}) collective-permute-start(f32[192,384]{1,0:T(8,128)S(1)} %slice.29), channel_id=1, source_target_pairs={{0,3},{1,0},{2,1},{3,2},{4,7},{5,4},{6,5},{7,6},{8,11},{9,8},{10,9... | collective-permute-start | bytes 884744 | tf_op jit(solution)/shard_map/ppermute | solution.py:58
  203.7 17.3 %collective-permute-start.14 = (f32[2,384,384]{2,1,0:T(8,128)S(1)}, f32[2,384,384]{2,1,0:T(8,128)}, u32[]{:S(2)}, u32[]{:S(2)}) collective-permute-start(f32[2,384,384]{2,1,0:T(8,128)S(1)} %pad_maximum_fusion.1.refs_0_), channel_id=1, source_target_pairs={{0,4},{1,5},{2,6},{3,7},{4,8},{5,9},{6,10},{7,11},{8,12},{9,13},{1... | collective-permute-start | bytes 3538952 | tf_op jit(solution)/shard_map/ppermute | solution.py:58
  205.5 15.5 %collective-permute-start.17 = (f32[2,384,384]{2,1,0:T(8,128)S(1)}, f32[2,384,384]{2,1,0:T(8,128)}, u32[]{:S(2)}, u32[]{:S(2)}) collective-permute-start(f32[2,384,384]{2,1,0:T(8,128)S(1)} %pad_maximum_fusion.2.refs_1_), channel_id=1, source_target_pairs={{0,12},{1,13},{2,14},{3,15},{4,0},{5,1},{6,2},{7,3},{8,4},{9,5},{1... | collective-permute-start | bytes 3538952 | tf_op jit(solution)/shard_map/ppermute | solution.py:58
  207.1 26.6 %collective-permute-start.15 = (f32[2,384,384]{2,1,0:T(8,128)S(1)}, f32[2,384,384]{2,1,0:T(8,128)}, u32[]{:S(2)}, u32[]{:S(2)}) collective-permute-start(f32[2,384,384]{2,1,0:T(8,128)S(1)} %pad_maximum_fusion.2.refs_1_), channel_id=1, source_target_pairs={{0,4},{1,5},{2,6},{3,7},{4,8},{5,9},{6,10},{7,11},{8,12},{9,13},{1... | collective-permute-start | bytes 3538952 | tf_op jit(solution)/shard_map/ppermute | solution.py:58
  207.1 26.6 %collective-permute-start.16 = (f32[2,384,384]{2,1,0:T(8,128)S(1)}, f32[2,384,384]{2,1,0:T(8,128)}, u32[]{:S(2)}, u32[]{:S(2)}) collective-permute-start(f32[2,384,384]{2,1,0:T(8,128)S(1)} %pad_maximum_fusion.1.refs_0_), channel_id=1, source_target_pairs={{0,12},{1,13},{2,14},{3,15},{4,0},{5,1},{6,2},{7,3},{8,4},{9,5},{1... | collective-permute-start | bytes 3538952 | tf_op jit(solution)/shard_map/ppermute | solution.py:58
  221.0 25.2 %collective-permute-start.25 = (f32[2,384,384]{2,1,0:T(8,128)}, f32[2,384,384]{2,1,0:T(8,128)S(1)}, u32[]{:S(2)}, u32[]{:S(2)}) collective-permute-start(f32[2,384,384]{2,1,0:T(8,128)} %collective-permute-done.14.refs_2_), channel_id=1, source_target_pairs={{0,4},{1,5},{2,6},{3,7},{4,8},{5,9},{6,10},{7,11},{8,12},{9,13},{1... | collective-permute-start | bytes 3538952 | tf_op jit(solution)/shard_map/ppermute | solution.py:58
  221.0 25.2 %collective-permute-start.26 = (f32[2,384,384]{2,1,0:T(8,128)}, f32[2,384,384]{2,1,0:T(8,128)}, u32[]{:S(2)}, u32[]{:S(2)}) collective-permute-start(f32[2,384,384]{2,1,0:T(8,128)} %collective-permute-done.17.refs_5_), channel_id=1, source_target_pairs={{0,12},{1,13},{2,14},{3,15},{4,0},{5,1},{6,2},{7,3},{8,4},{9,5},{1... | collective-permute-start | bytes 3538952 | tf_op jit(solution)/shard_map/ppermute | solution.py:58
  233.6 2.3 copy-start
  236.0 10.2 %copy-start.1 = (f32[768,384]{1,0:T(8,128)S(1)}, f32[768,384]{1,0:T(8,128)}, u32[]{:S(2)}) copy-start(f32[768,384]{1,0:T(8,128)} %base.1) | copy-start | bytes 3538948
Sparse Core Ops, SparseCore 0:
  31.7 64.7 all-gather.3
  98.7 71.4 all-gather.5
  187.3 35.3 all-gather.7

commit v14 on v13

--- a/solution.py
+++ b/solution.py
@@ -61,6 +61,8 @@
 def gather_cols(x, whole):
     half = x.shape[0] // 2
     up, down = hop(x, 0, 1), hop(x, 0, -1)
+    if not whole:
+        up, down = lax.optimization_barrier((up, down))
     top, low = hop(up[:half], 0, 1), hop(down[half:], 0, -1)
     if whole:
         group = jnp.stack([x, up, down, jnp.concatenate([top, low])])

time: 262 us -> 254 us (0.969)
  waiting for transfers between devices: 91.2 us -> 77 us
  starting transfers between devices: 49.7 us -> 55.9 us
    ppermute x18, waiting for transfers between devices: 64.7 us -> 50.4 us  [hop(): return lax.ppermute(x, ('core',) + COL, pairs)]
    ppermute x3, starting transfers between devices: 5.19 us -> 11 us  [step(): lax.ppermute(x, ROW, [(2 * i + c, 2 * ((i + 1 - 2 * c) % 4) + c) for i in...]
    ppermute x4, starting transfers between devices: 0.8 us -> 5.47 us  [swap(): return lax.ppermute(x, 'core', [(0, 1), (1, 0)])]
    ppermute x1, waiting for transfers between devices: 2 us -> 5.19 us  [turn(): lax.ppermute(x, ALL, [(at(y, c, z, x), at(y, x // 2, (y + z) % 4, 2 * c +...]
    ppermute x18, starting transfers between devices: 33.5 us -> 30.5 us  [hop(): return lax.ppermute(x, ('core',) + COL, pairs)]
    ppermute x3, waiting for transfers between devices: 16.1 us -> 13.2 us  [step(): lax.ppermute(x, ROW, [(2 * i + c, 2 * ((i + 1 - 2 * c) % 4) + c) for i in...]
    unnamed x24 -> x28, local copies, waits for them, and re-layouts: 7.95 us -> 7.15 us
  transfers between devices with their start and end apart: 31 -> 31, of which waited for: 18 -> 16; matrix products, arithmetic and copies ran while one was open for 3% -> 4% of each run, Pallas kernels for 10% -> 10%
where the time goes in v14:
time: 254 us; the launch traced here: 250 us
  waiting for transfers between devices  77 us (30%)
  starting transfers between devices  55.9 us (22%)
  blocking collectives  47.4 us (19%)
  Pallas kernels  37.5 us (15%)
  local copies, waits for them, and re-layouts  14.2 us (6%)
  between operations  14.2 us (6%)
  other arithmetic  3.81 us (2%)
    ppermute x18, waiting for transfers between devices, hop(): return lax.ppermute(x, ('core',) + COL, pairs)  50.4 us
    ppermute x18, starting transfers between devices, hop(): return lax.ppermute(x, ('core',) + COL, pairs)  30.5 us
    all_to_all x1, blocking collectives, per_device(): lax.all_to_all(after(s, f_near[0]).reshape(16, -1, w), COL, 0, 0, tiled=T...  25 us
    all_to_all x1, blocking collectives, spread(): lax.all_to_all(x.reshape(3, 8, sub, w), ROW, 1, 0, tiled=True)  22.4 us
    pallas_call x2, Pallas kernels, near_product(): pl.pallas_call(functools.partial(kernel, 16 // many, len(pieces)), out_sh...  19.2 us
    ppermute x3, waiting for transfers between devices, step(): lax.ppermute(x, ROW, [(2 * i + c, 2 * ((i + 1 - 2 * c) % 4) + c) for i in...  13.2 us
    ppermute x3, starting transfers between devices, step(): lax.ppermute(x, ROW, [(2 * i + c, 2 * ((i + 1 - 2 * c) % 4) + c) for i in...  11 us
    all_to_all x1, waiting for transfers between devices, spread(): lax.all_to_all(x.reshape(3, 8, sub, w), ROW, 1, 0, tiled=True)  8.15 us
  transfers between devices with their start and end apart: 31, of which 16 were waited for; matrix products, arithmetic and copies ran while one was open for 4% of the time, Pallas kernels for 10%

profile of v14, /device:TPU:1, one launch (start us, length us, event | category | flops | bytes accessed | tf_op | source)
XLA Modules:
  0.0 250.0 jit_solution(14933094495050933647)
XLA Ops:
  7.2 1.3 copy.7
  8.6 22.4 %all_to_all.35 = f32[3,8,32,384]{3,2,0,1:T(8,128)S(1)} all-to-all(f32[3,8,32,384]{3,2,0,1:T(8,128)S(1)} %copy.7), channel_id=1, replica_groups=mesh['y'=4,'core'=2,'z'=4,'x'=4] {'y','core'}, dimensions={1} | all-to-all | bytes 2359296 | tf_op jit(solution)/shard_map/all_to_all | solution.py:300
  31.0 0.6 pick_rows.2
  31.6 3.8 %collective-permute-start.1 = (f32[384,384]{1,0:T(8,128)S(1)}, f32[384,384]{1,0:T(8,128)S(1)}, u32[]{:S(2)}, u32[]{:S(2)}) collective-permute-start(f32[384,384]{1,0:T(8,128)S(1)} %bitcast.78), channel_id=1, source_target_pairs={{0,3},{1,0},{2,1},{3,2},{4,7},{5,4},{6,5},{7,6},{8,11},{9,8},{10,9... | collective-permute-start | bytes 1769480 | tf_op jit(solution)/shard_map/ppermute | solution.py:58
  35.4 1.1 copy.8
  36.5 3.5 %all-to-all-start.1 = ((f32[3,8,32,384]{3,2,0,1:T(8,128)}), f32[3,8,32,384]{3,2,0,1:T(8,128)S(1)}, u32[]{:S(2)}, u32[]{:S(2)}) async-start(f32[3,8,32,384]{3,2,0,1:T(8,128)} %copy.8), calls=%async_computation.1 | async-start | bytes 2359296 | tf_op jit(solution)/shard_map/all_to_all | solution.py:300
  40.1 2.2 collective-permute-done.1
  42.3 3.5 %collective-permute-start.3 = (f32[192,384]{1,0:T(8,128)S(1)}, f32[192,384]{1,0:T(8,128)S(1)}, u32[]{:S(2)}, u32[]{:S(2)}) collective-permute-start(f32[192,384]{1,0:T(8,128)S(1)} %slice.25), channel_id=1, source_target_pairs={{0,3},{1,0},{2,1},{3,2},{4,7},{5,4},{6,5},{7,6},{8,11},{9,8},{10,9... | collective-permute-start | bytes 884744 | tf_op jit(solution)/shard_map/ppermute | solution.py:58
  45.8 0.1 collective-permute-start.2
  45.9 3.6 %collective-permute-done.3 = f32[192,384]{1,0:T(8,128)S(1)} collective-permute-done((f32[192,384]{1,0:T(8,128)S(1)}, f32[192,384]{1,0:T(8,128)S(1)}, u32[]{:S(2)}, u32[]{:S(2)}) %collective-permute-start.3) | collective-permute-done | bytes 294944 | tf_op jit(solution)/shard_map/ppermute | solution.py:58
  49.4 3.6 %collective-permute-done.2 = f32[192,384]{1,0:T(8,128)S(1)} collective-permute-done((f32[192,384]{1,0:T(8,128)S(1)}, f32[192,384]{1,0:T(8,128)S(1)}, u32[]{:S(2)}, u32[]{:S(2)}) %collective-permute-start.2) | collective-permute-done | bytes 294944 | tf_op jit(solution)/shard_map/ppermute | solution.py:58
  53.1 1.5 pad_maximum_fusion.refs_0_
  54.6 1.1 collective-permute-start.4
  55.8 1.6 collective-permute-start.5
  57.3 8.2 %all-to-all-done.1 = f32[3,8,32,384]{3,2,0,1:T(8,128)S(1)} async-done(((f32[3,8,32,384]{3,2,0,1:T(8,128)}), f32[3,8,32,384]{3,2,0,1:T(8,128)S(1)}, u32[]{:S(2)}, u32[]{:S(2)}) %all-to-all-start.1) | async-done | bytes 1179680 | tf_op jit(solution)/shard_map/all_to_all | solution.py:300
  65.5 0.6 pick_rows.3
  66.1 25.0 %all_to_all.36.x = f32[16,24,384]{2,1,0:T(8,128)S(1)} all-to-all(f32[16,24,384]{2,1,0:T(8,128)S(1)} %bitcast.81), channel_id=1, replica_groups=mesh['y'=4,'core'=2,'z'=4,'x'=4] {'z','x'}, dimensions={0} | all-to-all | bytes 1179648 | tf_op jit(solution)/shard_map/all_to_all | solution.py:349
  91.0 1.4 pick_cols.1
  92.7 0.1 stack.205.at
  92.8 1.2 slice.26
  94.0 0.6 copy-done.2
  94.7 1.1 collective-permute-start.6
  95.8 1.3 slice.27
  97.1 1.6 collective-permute-start.7
  98.8 1.8 copy-done.3
  100.6 9.2 %near.2.acc = f32[1,384,384]{2,1,0:T(8,128)S(1)} custom-call(s32[24]{0:T(128)S(1)} %stack.205.at, f32[4,384,384]{2,1,0:T(8,128)} %pad_maximum_fusion.refs_0_, f32[4,384,384]{2,1,0:T(8,128)S(1)} %copy-done.3, f32[4,384,384]{2,1,0:T(8,128)} %collective-permute-done.5.refs_2_, f32[16,384,384]{2,1,0:T(8,128)} %bitcast.70), custom_call_target="tpu_custom_call" | custom-call | flops 48922361856 | bytes 198180864 | tf_op jit(solution)/shard_map/near/pallas_call | solution.py:174
  109.8 1.7 collective-permute-done.6.top
  111.4 2.4 collective-permute-done.7.low
  113.9 3.4 %update.1 = (f32[384,384]{1,0:T(8,128)S(1)}, f32[384,384]{1,0:T(8,128)S(1)}) custom-call(s32[24]{0:T(128)S(1)} %stack.205.at, f32[1,384,384]{2,1,0:T(8,128)S(1)} %near.2.acc, f32[2,384,384]{2,1,0:T(8,128)S(1)} %collective-permute-done.6.top, f32[2,384,384]{2,1,0:T(8,128)S(1)} %collective-permute-done.7.low, f32[16,384,384]{2,1,0:T(8,128)S(1)} %bitcast.73), custom_call_target="tpu_custom_call" | custom-call | flops 1358954496 | bytes 2359296 | tf_op jit(solution)/shard_map/update/pallas_call | solution.py:223
  117.3 4.6 %collective-permute-start.8 = (f32[384,384]{1,0:T(8,128)S(1)}, f32[384,384]{1,0:T(8,128)S(1)}, u32[]{:S(2)}, u32[]{:S(2)}) collective-permute-start(f32[384,384]{1,0:T(8,128)S(1)} %get-tuple-element.15), channel_id=1, source_target_pairs={{0,0},{1,1},{2,16},{3,17},{4,4},{5,5},{6,20},{7,21},{8,8},{9,9},{1... | collective-permute-start | bytes 1769480 | tf_op jit(solution)/shard_map/ppermute | solution.py:81
  121.9 2.9 %collective-permute-start.18 = (f32[12,32,384]{2,1,0:T(8,128)S(1)}, f32[12,32,384]{2,1,0:T(8,128)S(1)}, u32[]{:S(2)}, u32[]{:S(2)}) collective-permute-start(f32[12,32,384]{2,1,0:T(8,128)S(1)} %bitcast.82), channel_id=1, source_target_pairs={{0,32},{16,112},{32,64},{48,16},{64,96},{80,48},{96,0},{112,80},{1... | collective-permute-start | bytes 1769480 | tf_op jit(solution)/shard_map/ppermute | solution.py:37
  124.8 5.2 %collective-permute-done.8 = f32[384,384]{1,0:T(8,128)S(1)} collective-permute-done((f32[384,384]{1,0:T(8,128)S(1)}, f32[384,384]{1,0:T(8,128)S(1)}, u32[]{:S(2)}, u32[]{:S(2)}) %collective-permute-start.8) | collective-permute-done | bytes 589856 | tf_op jit(solution)/shard_map/ppermute | solution.py:81
  130.0 0.7 collective-permute-start.9
  130.7 0.9 collective-permute-done.18.refs_1_
  131.7 5.8 %collective-permute-start.19 = (f32[12,32,384]{2,1,0:T(8,128)S(1)}, f32[12,32,384]{2,1,0:T(8,128)S(1)}, u32[]{:S(2)}, u32[]{:S(2)}) collective-permute-start(f32[12,32,384]{2,1,0:T(8,128)S(1)} %collective-permute-done.18.refs_1_), channel_id=1, source_target_pairs={{0,32},{16,112},{32,64},{48,16},{64,96},{80,48},{96,0},{112,80},{1... | collective-permute-start | bytes 1769480 | tf_op jit(solution)/shard_map/ppermute | solution.py:37
  137.4 4.8 %collective-permute-start.10 = (f32[384,384]{1,0:T(8,128)S(1)}, f32[384,384]{1,0:T(8,128)S(1)}, u32[]{:S(2)}, u32[]{:S(2)}) collective-permute-start(f32[384,384]{1,0:T(8,128)S(1)} %collective-permute-done.9), channel_id=1, source_target_pairs={{0,1},{1,2},{2,3},{3,0},{4,5},{5,6},{6,7},{7,4},{8,9},{9,10},{10,1... | collective-permute-start | bytes 1769480 | tf_op jit(solution)/shard_map/ppermute | solution.py:58
  142.2 12.3 %collective-permute-done.19.refs_2_ = f32[12,32,384]{2,1,0:T(8,128)S(1)} collective-permute-done((f32[12,32,384]{2,1,0:T(8,128)S(1)}, f32[12,32,384]{2,1,0:T(8,128)S(1)}, u32[]{:S(2)}, u32[]{:S(2)}) %collective-permute-start.19) | collective-permute-done | bytes 589856 | tf_op jit(solution)/shard_map/ppermute | solution.py:37
  154.5 2.3 collective-permute-start.20
  156.8 0.9 collective-permute-start.11
  157.7 4.4 %collective-permute-start.21 = (f32[12,32,384]{2,1,0:T(8,128)S(1)}, f32[12,32,384]{2,1,0:T(8,128)S(1)}, u32[]{:S(2)}, u32[]{:S(2)}) collective-permute-start(f32[12,32,384]{2,1,0:T(8,128)S(1)} %bitcast.83), channel_id=1, source_target_pairs={{0,16},{16,0},{1,17},{17,1},{2,18},{18,2},{3,19},{19,3},{4,20},{20... | collective-permute-start | bytes 1769480 | tf_op jit(solution)/shard_map/ppermute | solution.py:41
  162.1 5.3 %collective-permute-done.10 = f32[384,384]{1,0:T(8,128)S(1)} collective-permute-done((f32[384,384]{1,0:T(8,128)S(1)}, f32[384,384]{1,0:T(8,128)S(1)}, u32[]{:S(2)}, u32[]{:S(2)}) %collective-permute-start.10) | collective-permute-done | bytes 589856 | tf_op jit(solution)/shard_map/ppermute | solution.py:58
  167.4 1.1 collective-permute-start.24
  168.5 0.7 slice.22
  169.3 2.2 collective-permute-start.12
  171.4 6.1 %collective-permute-done.12 = f32[192,384]{1,0:T(8,128)} collective-permute-done((f32[192,384]{1,0:T(8,128)}, f32[192,384]{1,0:T(8,128)}, u32[]{:S(2)}, u32[]{:S(2)}) %collective-permute-start.12) | collective-permute-done | bytes 294944 | tf_op jit(solution)/shard_map/ppermute | solution.py:58
  177.6 2.3 copy-done.5
  179.9 7.4 %cross.1 = f32[384,384]{1,0:T(8,128)} custom-call(s32[24]{0:T(128)S(1)} %stack.205.at, f32[384,3072]{1,0:T(8,128)S(1)} %copy-done.5, f32[12,32,384]{2,1,0:T(8,128)S(1)} %bitcast.84, f32[12,32,384]{2,1,0:T(8,128)S(1)} %collective-permute-done.18.refs_1_, f32[12,32,384]{2,1,0:T(8,128)S(1)} %collective-permute-done.19.refs_2_, ...), custom_call_target="tpu_custom_call" | custom-call | flops 2717908992 | bytes 9437184 | tf_op jit(solution)/shard_map/cross/pallas_call | solution.py:280
  187.3 1.1 slice.23
  188.4 1.5 collective-permute-start.13
  189.9 0.1 pad_maximum_fusion.1.refs_0_
  190.0 4.3 %collective-permute-done.13 = f32[192,384]{1,0:T(8,128)S(1)} collective-permute-done((f32[192,384]{1,0:T(8,128)S(1)}, f32[192,384]{1,0:T(8,128)S(1)}, u32[]{:S(2)}, u32[]{:S(2)}) %collective-permute-start.13) | collective-permute-done | bytes 294944 | tf_op jit(solution)/shard_map/ppermute | solution.py:58
  194.3 1.0 maximum_bitcast_fusion.1
  195.3 1.1 pad_maximum_fusion.2.refs_1_
  196.5 1.2 collective-permute-start.14
  197.7 1.7 collective-permute-start.17
  199.4 2.7 %collective-permute-start.16 = (f32[2,384,384]{2,1,0:T(8,128)S(1)}, f32[2,384,384]{2,1,0:T(8,128)}, u32[]{:S(2)}, u32[]{:S(2)}) collective-permute-start(f32[2,384,384]{2,1,0:T(8,128)S(1)} %pad_maximum_fusion.1.refs_0_), channel_id=1, source_target_pairs={{0,12},{1,13},{2,14},{3,15},{4,0},{5,1},{6,2},{7,3},{8,4},{9,5},{1... | collective-permute-start | bytes 3538952 | tf_op jit(solution)/shard_map/ppermute | solution.py:58
  202.1 0.1 stack.188.at
  202.2 11.1 %collective-permute-done.14.refs_2_ = f32[2,384,384]{2,1,0:T(8,128)} collective-permute-done((f32[2,384,384]{2,1,0:T(8,128)S(1)}, f32[2,384,384]{2,1,0:T(8,128)}, u32[]{:S(2)}, u32[]{:S(2)}) %collective-permute-start.14) | collective-permute-done | bytes 1179680 | tf_op jit(solution)/shard_map/ppermute | solution.py:58
  213.3 2.7 %collective-permute-start.26 = (f32[2,384,384]{2,1,0:T(8,128)}, f32[2,384,384]{2,1,0:T(8,128)}, u32[]{:S(2)}, u32[]{:S(2)}) collective-permute-start(f32[2,384,384]{2,1,0:T(8,128)} %collective-permute-done.17.refs_5_), channel_id=1, source_target_pairs={{0,12},{1,13},{2,14},{3,15},{4,0},{5,1},{6,2},{7,3},{8,4},{9,5},{1... | collective-permute-start | bytes 3538952 | tf_op jit(solution)/shard_map/ppermute | solution.py:58
  216.1 9.9 %collective-permute-done.15.refs_3_ = f32[2,384,384]{2,1,0:T(8,128)} collective-permute-done((f32[2,384,384]{2,1,0:T(8,128)S(1)}, f32[2,384,384]{2,1,0:T(8,128)}, u32[]{:S(2)}, u32[]{:S(2)}) %collective-permute-start.15) | collective-permute-done | bytes 1179680 | tf_op jit(solution)/shard_map/ppermute | solution.py:58
  226.0 2.3 copy-done
  228.3 10.0 %near.3 = (f32[2,384,384]{2,1,0:T(8,128)S(1)}, f32[3,8,32,384]{3,2,1,0:T(8,128)}) custom-call(s32[12]{0:T(128)S(1)} %copy-done.4, s32[1]{0:T(128)} %bitcast.first, s32[24]{0:T(128)S(1)} %stack.188.at, f32[2,384,384]{2,1,0:T(8,128)S(1)} %pad_maximum_fusion.1.refs_0_, f32[2,384,384]{2,1,0:T(8,128)S(1)} %pad_maximum_fusion.2.refs_1_, ...), custom_call_target="tpu_custom_call" | custom-call | flops 48922361856 | bytes 141557760 | tf_op jit(solution)/shard_map/near/pallas_call | solution.py:174
  238.3 0.2 collective-permute-done.25.top
  238.5 4.9 %child.1 = f32[768,384]{1,0:T(8,128)} custom-call(s32[24]{0:T(128)S(1)} %stack.188.at, f32[2,384,384]{2,1,0:T(8,128)S(1)} %get-tuple-element.25.acc, f32[2,384,384]{2,1,0:T(8,128)S(1)} %collective-permute-done.25.top, f32[2,384,384]{2,1,0:T(8,128)} %collective-permute-done.26.low, f32[8,384,384]{2,1,0:T(8,128)S(1)} %bitcast.75, f32[768,384]{1,0:T(8,128)S(1)} %copy-done.1), custom_call_target="tpu_custom_call" | custom-call | flops 1358954496 | bytes 3538944 | tf_op jit(solution)/shard_map/child/pallas_call | solution.py:245
  (55 shorter events, 0.4 us)
Async XLA Ops:
  7.2 91.6 %all-gather.4.cloned.1.call-start = ((), (), s32[]{:S(2)}) async-start(), calls=%async_computation.3 | async-start | bytes 10616832 | tf_op jit(solution)/shard_map/all_gather | solution.py:345
  8.6 22.4 %copy-start.4 = (s32[12]{0:T(128)S(1)}, s32[12]{0:T(128)}, u32[]{:S(2)}) copy-start(s32[12]{0:T(128)} %anc.7) | copy-start | bytes 148
  31.0 4.5 %copy-start.8 = (f32[768,384]{1,0:T(8,128)S(1)}, f32[768,384]{1,0:T(8,128)}, u32[]{:S(2)}) copy-start(f32[768,384]{1,0:T(8,128)} %param.5) | copy-start | bytes 3538948
  31.6 10.7 %collective-permute-start.1 = (f32[384,384]{1,0:T(8,128)S(1)}, f32[384,384]{1,0:T(8,128)S(1)}, u32[]{:S(2)}, u32[]{:S(2)}) collective-permute-start(f32[384,384]{1,0:T(8,128)S(1)} %bitcast.78), channel_id=1, source_target_pairs={{0,3},{1,0},{2,1},{3,2},{4,7},{5,4},{6,5},{7,6},{8,11},{9,8},{10,9... | collective-permute-start | bytes 1769480 | tf_op jit(solution)/shard_map/ppermute | solution.py:58
  35.4 10.3 %collective-permute-start = (f32[384,384]{1,0:T(8,128)S(1)}, f32[384,384]{1,0:T(8,128)S(1)}, u32[]{:S(2)}, u32[]{:S(2)}) collective-permute-start(f32[384,384]{1,0:T(8,128)S(1)} %bitcast.79), channel_id=1, source_target_pairs={{0,1},{1,2},{2,3},{3,0},{4,5},{5,6},{6,7},{7,4},{8,9},{9,10},{10,1... | collective-permute-start | bytes 1769480 | tf_op jit(solution)/shard_map/ppermute | solution.py:58
  36.5 28.9 %all-to-all-start.1 = ((f32[3,8,32,384]{3,2,0,1:T(8,128)}), f32[3,8,32,384]{3,2,0,1:T(8,128)S(1)}, u32[]{:S(2)}, u32[]{:S(2)}) async-start(f32[3,8,32,384]{3,2,0,1:T(8,128)} %copy.8), calls=%async_computation.1 | async-start | bytes 2359296 | tf_op jit(solution)/shard_map/all_to_all | solution.py:300
  40.1 131.4 %all-gather.6.cloned.1.call-start = ((), (), s32[]{:S(2)}) async-start(), calls=%async_computation.4 | async-start | bytes 5013504 | tf_op jit(solution)/shard_map/all_gather | solution.py:350
  42.3 7.1 %collective-permute-start.3 = (f32[192,384]{1,0:T(8,128)S(1)}, f32[192,384]{1,0:T(8,128)S(1)}, u32[]{:S(2)}, u32[]{:S(2)}) collective-permute-start(f32[192,384]{1,0:T(8,128)S(1)} %slice.25), channel_id=1, source_target_pairs={{0,3},{1,0},{2,1},{3,2},{4,7},{5,4},{6,5},{7,6},{8,11},{9,8},{10,9... | collective-permute-start | bytes 884744 | tf_op jit(solution)/shard_map/ppermute | solution.py:58
  45.8 7.3 %collective-permute-start.2 = (f32[192,384]{1,0:T(8,128)S(1)}, f32[192,384]{1,0:T(8,128)S(1)}, u32[]{:S(2)}, u32[]{:S(2)}) collective-permute-start(f32[192,384]{1,0:T(8,128)S(1)} %slice.24), channel_id=1, source_target_pairs={{0,1},{1,2},{2,3},{3,0},{4,5},{5,6},{6,7},{7,4},{8,9},{9,10},{10,1... | collective-permute-start | bytes 884744 | tf_op jit(solution)/shard_map/ppermute | solution.py:58
  54.6 38.2 %collective-permute-start.4 = (f32[4,384,384]{2,1,0:T(8,128)}, f32[4,384,384]{2,1,0:T(8,128)S(1)}, u32[]{:S(2)}, u32[]{:S(2)}) collective-permute-start(f32[4,384,384]{2,1,0:T(8,128)} %pad_maximum_fusion.refs_0_), channel_id=1, source_target_pairs={{0,4},{1,5},{2,6},{3,7},{4,8},{5,9},{6,10},{7,11},{8,12},{9,13},{1... | collective-permute-start | bytes 7077896 | tf_op jit(solution)/shard_map/ppermute | solution.py:58
  55.8 40.0 %collective-permute-start.5 = (f32[4,384,384]{2,1,0:T(8,128)}, f32[4,384,384]{2,1,0:T(8,128)}, u32[]{:S(2)}, u32[]{:S(2)}) collective-permute-start(f32[4,384,384]{2,1,0:T(8,128)} %pad_maximum_fusion.refs_0_), channel_id=1, source_target_pairs={{0,12},{1,13},{2,14},{3,15},{4,0},{5,1},{6,2},{7,3},{8,4},{9,5},{1... | collective-permute-start | bytes 7077896 | tf_op jit(solution)/shard_map/ppermute | solution.py:58
  92.4 133.5 %all-gather.8.cloned.1.call-start = ((), (), s32[]{:S(2)}) async-start(), calls=%async_computation.5 | async-start | bytes 5308416 | tf_op jit(solution)/shard_map/all_gather | solution.py:359
  92.8 1.8 copy-start.2
  94.7 16.8 %collective-permute-start.6 = (f32[2,384,384]{2,1,0:T(8,128)}, f32[2,384,384]{2,1,0:T(8,128)S(1)}, u32[]{:S(2)}, u32[]{:S(2)}) collective-permute-start(f32[2,384,384]{2,1,0:T(8,128)} %slice.26), channel_id=1, source_target_pairs={{0,4},{1,5},{2,6},{3,7},{4,8},{5,9},{6,10},{7,11},{8,12},{9,13},{1... | collective-permute-start | bytes 3538952 | tf_op jit(solution)/shard_map/ppermute | solution.py:58
  97.1 16.7 %collective-permute-start.7 = (f32[2,384,384]{2,1,0:T(8,128)S(1)}, f32[2,384,384]{2,1,0:T(8,128)S(1)}, u32[]{:S(2)}, u32[]{:S(2)}) collective-permute-start(f32[2,384,384]{2,1,0:T(8,128)S(1)} %slice.27), channel_id=1, source_target_pairs={{0,12},{1,13},{2,14},{3,15},{4,0},{5,1},{6,2},{7,3},{8,4},{9,5},{1... | collective-permute-start | bytes 3538952 | tf_op jit(solution)/shard_map/ppermute | solution.py:58
  98.8 15.1 %slice-start = ((s8[9437184]{0:T(1024)(128)(4,1)}), s8[4194304]{0:T(1024)(128)(4,1)S(1)}, s32[]{:S(2)}) async-start(s8[9437184]{0:T(1024)(128)(4,1)} %bitcast.71), calls=%async_computation.6 | async-start | bytes 8388608
  98.8 1.8 copy-start.3
  100.6 13.3 %slice-start.1 = ((s8[9437184]{0:T(1024)(128)(4,1)}), s8[4194304]{0:T(1024)(128)(4,1)S(1)}, s32[]{:S(2)}) async-start(s8[9437184]{0:T(1024)(128)(4,1)} %bitcast.71), calls=%async_computation.7 | async-start | bytes 8388608
  100.6 13.3 %slice-start.2 = ((s8[9437184]{0:T(1024)(128)(4,1)}), s8[1048576]{0:T(1024)(128)(4,1)S(1)}, s32[]{:S(2)}) async-start(s8[9437184]{0:T(1024)(128)(4,1)} %bitcast.71), calls=%async_computation.8 | async-start | bytes 2097152
  117.3 12.7 %collective-permute-start.8 = (f32[384,384]{1,0:T(8,128)S(1)}, f32[384,384]{1,0:T(8,128)S(1)}, u32[]{:S(2)}, u32[]{:S(2)}) collective-permute-start(f32[384,384]{1,0:T(8,128)S(1)} %get-tuple-element.15), channel_id=1, source_target_pairs={{0,0},{1,1},{2,16},{3,17},{4,4},{5,5},{6,20},{7,21},{8,8},{9,9},{1... | collective-permute-start | bytes 1769480 | tf_op jit(solution)/shard_map/ppermute | solution.py:81
  121.9 9.7 %collective-permute-start.18 = (f32[12,32,384]{2,1,0:T(8,128)S(1)}, f32[12,32,384]{2,1,0:T(8,128)S(1)}, u32[]{:S(2)}, u32[]{:S(2)}) collective-permute-start(f32[12,32,384]{2,1,0:T(8,128)S(1)} %bitcast.82), channel_id=1, source_target_pairs={{0,32},{16,112},{32,64},{48,16},{64,96},{80,48},{96,0},{112,80},{1... | collective-permute-start | bytes 1769480 | tf_op jit(solution)/shard_map/ppermute | solution.py:37
  130.0 7.4 %collective-permute-start.9 = (f32[384,384]{1,0:T(8,128)S(1)}, f32[384,384]{1,0:T(8,128)S(1)}, u32[]{:S(2)}, u32[]{:S(2)}) collective-permute-start(f32[384,384]{1,0:T(8,128)S(1)} %collective-permute-done.8), channel_id=1, source_target_pairs={{0,0},{1,1},{2,2},{3,3},{4,36},{5,37},{6,38},{7,39},{8,72},{9,73},... | collective-permute-start | bytes 1769480 | tf_op jit(solution)/shard_map/ppermute | solution.py:82
  131.7 22.8 %collective-permute-start.19 = (f32[12,32,384]{2,1,0:T(8,128)S(1)}, f32[12,32,384]{2,1,0:T(8,128)S(1)}, u32[]{:S(2)}, u32[]{:S(2)}) collective-permute-start(f32[12,32,384]{2,1,0:T(8,128)S(1)} %collective-permute-done.18.refs_1_), channel_id=1, source_target_pairs={{0,32},{16,112},{32,64},{48,16},{64,96},{80,48},{96,0},{112,80},{1... | collective-permute-start | bytes 1769480 | tf_op jit(solution)/shard_map/ppermute | solution.py:37
  137.4 29.9 %copy-start.9 = (f32[384,384]{1,0:T(8,128)}, f32[384,384]{1,0:T(8,128)S(1)}, u32[]{:S(2)}) copy-start(f32[384,384]{1,0:T(8,128)S(1)} %collective-permute-done.9) | copy-start | bytes 1769476
  137.4 29.9 %collective-permute-start.10 = (f32[384,384]{1,0:T(8,128)S(1)}, f32[384,384]{1,0:T(8,128)S(1)}, u32[]{:S(2)}, u32[]{:S(2)}) collective-permute-start(f32[384,384]{1,0:T(8,128)S(1)} %collective-permute-done.9), channel_id=1, source_target_pairs={{0,1},{1,2},{2,3},{3,0},{4,5},{5,6},{6,7},{7,4},{8,9},{9,10},{10,1... | collective-permute-start | bytes 1769480 | tf_op jit(solution)/shard_map/ppermute | solution.py:58
  154.5 12.9 %collective-permute-start.20 = (f32[12,32,384]{2,1,0:T(8,128)S(1)}, f32[12,32,384]{2,1,0:T(8,128)S(1)}, u32[]{:S(2)}, u32[]{:S(2)}) collective-permute-start(f32[12,32,384]{2,1,0:T(8,128)S(1)} %collective-permute-done.19.refs_2_), channel_id=1, source_target_pairs={{0,32},{16,112},{32,64},{48,16},{64,96},{80,48},{96,0},{112,80},{1... | collective-permute-start | bytes 1769480 | tf_op jit(solution)/shard_map/ppermute | solution.py:37
  156.8 11.7 %collective-permute-start.11 = (f32[384,384]{1,0:T(8,128)S(1)}, f32[384,384]{1,0:T(8,128)}, u32[]{:S(2)}, u32[]{:S(2)}) collective-permute-start(f32[384,384]{1,0:T(8,128)S(1)} %collective-permute-done.9), channel_id=1, source_target_pairs={{0,3},{1,0},{2,1},{3,2},{4,7},{5,4},{6,5},{7,6},{8,11},{9,8},{10,9... | collective-permute-start | bytes 1769480 | tf_op jit(solution)/shard_map/ppermute | solution.py:58
  157.7 19.9 %collective-permute-start.21 = (f32[12,32,384]{2,1,0:T(8,128)S(1)}, f32[12,32,384]{2,1,0:T(8,128)S(1)}, u32[]{:S(2)}, u32[]{:S(2)}) collective-permute-start(f32[12,32,384]{2,1,0:T(8,128)S(1)} %bitcast.83), channel_id=1, source_target_pairs={{0,16},{16,0},{1,17},{17,1},{2,18},{18,2},{3,19},{19,3},{4,20},{20... | collective-permute-start | bytes 1769480 | tf_op jit(solution)/shard_map/ppermute | solution.py:41
  162.1 15.5 %collective-permute-start.22 = (f32[12,32,384]{2,1,0:T(8,128)S(1)}, f32[12,32,384]{2,1,0:T(8,128)S(1)}, u32[]{:S(2)}, u32[]{:S(2)}) collective-permute-start(f32[12,32,384]{2,1,0:T(8,128)S(1)} %collective-permute-done.18.refs_1_), channel_id=1, source_target_pairs={{0,16},{16,0},{1,17},{17,1},{2,18},{18,2},{3,19},{19,3},{4,20},{20... | collective-permute-start | bytes 1769480 | tf_op jit(solution)/shard_map/ppermute | solution.py:41
  167.4 1.2 copy-start.6
  167.4 10.2 %collective-permute-start.23 = (f32[12,32,384]{2,1,0:T(8,128)S(1)}, f32[12,32,384]{2,1,0:T(8,128)}, u32[]{:S(2)}, u32[]{:S(2)}) collective-permute-start(f32[12,32,384]{2,1,0:T(8,128)S(1)} %collective-permute-done.19.refs_2_), channel_id=1, source_target_pairs={{0,16},{16,0},{1,17},{17,1},{2,18},{18,2},{3,19},{19,3},{4,20},{20... | collective-permute-start | bytes 1769480 | tf_op jit(solution)/shard_map/ppermute | solution.py:41
  167.4 10.2 %collective-permute-start.24 = (f32[12,32,384]{2,1,0:T(8,128)S(1)}, f32[12,32,384]{2,1,0:T(8,128)}, u32[]{:S(2)}, u32[]{:S(2)}) collective-permute-start(f32[12,32,384]{2,1,0:T(8,128)S(1)} %collective-permute-done.20.refs_3_), channel_id=1, source_target_pairs={{0,16},{16,0},{1,17},{17,1},{2,18},{18,2},{3,19},{19,3},{4,20},{20... | collective-permute-start | bytes 1769480 | tf_op jit(solution)/shard_map/ppermute | solution.py:41
  169.3 8.3 %collective-permute-start.12 = (f32[192,384]{1,0:T(8,128)}, f32[192,384]{1,0:T(8,128)}, u32[]{:S(2)}, u32[]{:S(2)}) collective-permute-start(f32[192,384]{1,0:T(8,128)} %slice.22), channel_id=1, source_target_pairs={{0,1},{1,2},{2,3},{3,0},{4,5},{5,6},{6,7},{7,4},{8,9},{9,10},{10,1... | collective-permute-start | bytes 884744 | tf_op jit(solution)/shard_map/ppermute | solution.py:58
  177.6 2.3 copy-start.5
  187.3 2.7 %copy-start.7 = (f32[384,384]{1,0:T(8,128)S(1)}, f32[384,384]{1,0:T(8,128)}, u32[]{:S(2)}) copy-start(f32[384,384]{1,0:T(8,128)} %copy-done.6) | copy-start | bytes 1769476
  187.3 2.6 %copy-start.10 = (f32[384,384]{1,0:T(8,128)S(1)}, f32[384,384]{1,0:T(8,128)}, u32[]{:S(2)}) copy-start(f32[384,384]{1,0:T(8,128)} %copy-done.9) | copy-start | bytes 1769476
  188.4 5.9 %collective-permute-start.13 = (f32[192,384]{1,0:T(8,128)S(1)}, f32[192,384]{1,0:T(8,128)S(1)}, u32[]{:S(2)}, u32[]{:S(2)}) collective-permute-start(f32[192,384]{1,0:T(8,128)S(1)} %slice.23), channel_id=1, source_target_pairs={{0,3},{1,0},{2,1},{3,2},{4,7},{5,4},{6,5},{7,6},{8,11},{9,8},{10,9... | collective-permute-start | bytes 884744 | tf_op jit(solution)/shard_map/ppermute | solution.py:58
  196.5 16.8 %collective-permute-start.14 = (f32[2,384,384]{2,1,0:T(8,128)S(1)}, f32[2,384,384]{2,1,0:T(8,128)}, u32[]{:S(2)}, u32[]{:S(2)}) collective-permute-start(f32[2,384,384]{2,1,0:T(8,128)S(1)} %pad_maximum_fusion.1.refs_0_), channel_id=1, source_target_pairs={{0,4},{1,5},{2,6},{3,7},{4,8},{5,9},{6,10},{7,11},{8,12},{9,13},{1... | collective-permute-start | bytes 3538952 | tf_op jit(solution)/shard_map/ppermute | solution.py:58
  197.7 15.6 %collective-permute-start.17 = (f32[2,384,384]{2,1,0:T(8,128)S(1)}, f32[2,384,384]{2,1,0:T(8,128)}, u32[]{:S(2)}, u32[]{:S(2)}) collective-permute-start(f32[2,384,384]{2,1,0:T(8,128)S(1)} %pad_maximum_fusion.2.refs_1_), channel_id=1, source_target_pairs={{0,12},{1,13},{2,14},{3,15},{4,0},{5,1},{6,2},{7,3},{8,4},{9,5},{1... | collective-permute-start | bytes 3538952 | tf_op jit(solution)/shard_map/ppermute | solution.py:58
  199.4 26.6 %collective-permute-start.15 = (f32[2,384,384]{2,1,0:T(8,128)S(1)}, f32[2,384,384]{2,1,0:T(8,128)}, u32[]{:S(2)}, u32[]{:S(2)}) collective-permute-start(f32[2,384,384]{2,1,0:T(8,128)S(1)} %pad_maximum_fusion.2.refs_1_), channel_id=1, source_target_pairs={{0,4},{1,5},{2,6},{3,7},{4,8},{5,9},{6,10},{7,11},{8,12},{9,13},{1... | collective-permute-start | bytes 3538952 | tf_op jit(solution)/shard_map/ppermute | solution.py:58
  199.4 26.6 %collective-permute-start.16 = (f32[2,384,384]{2,1,0:T(8,128)S(1)}, f32[2,384,384]{2,1,0:T(8,128)}, u32[]{:S(2)}, u32[]{:S(2)}) collective-permute-start(f32[2,384,384]{2,1,0:T(8,128)S(1)} %pad_maximum_fusion.1.refs_0_), channel_id=1, source_target_pairs={{0,12},{1,13},{2,14},{3,15},{4,0},{5,1},{6,2},{7,3},{8,4},{9,5},{1... | collective-permute-start | bytes 3538952 | tf_op jit(solution)/shard_map/ppermute | solution.py:58
  213.3 25.2 %collective-permute-start.25 = (f32[2,384,384]{2,1,0:T(8,128)}, f32[2,384,384]{2,1,0:T(8,128)S(1)}, u32[]{:S(2)}, u32[]{:S(2)}) collective-permute-start(f32[2,384,384]{2,1,0:T(8,128)} %collective-permute-done.14.refs_2_), channel_id=1, source_target_pairs={{0,4},{1,5},{2,6},{3,7},{4,8},{5,9},{6,10},{7,11},{8,12},{9,13},{1... | collective-permute-start | bytes 3538952 | tf_op jit(solution)/shard_map/ppermute | solution.py:58
  213.3 25.2 %collective-permute-start.26 = (f32[2,384,384]{2,1,0:T(8,128)}, f32[2,384,384]{2,1,0:T(8,128)}, u32[]{:S(2)}, u32[]{:S(2)}) collective-permute-start(f32[2,384,384]{2,1,0:T(8,128)} %collective-permute-done.17.refs_5_), channel_id=1, source_target_pairs={{0,12},{1,13},{2,14},{3,15},{4,0},{5,1},{6,2},{7,3},{8,4},{9,5},{1... | collective-permute-start | bytes 3538952 | tf_op jit(solution)/shard_map/ppermute | solution.py:58
  226.0 2.3 copy-start
  228.3 10.2 %copy-start.1 = (f32[768,384]{1,0:T(8,128)S(1)}, f32[768,384]{1,0:T(8,128)}, u32[]{:S(2)}) copy-start(f32[768,384]{1,0:T(8,128)} %base.1) | copy-start | bytes 3538948
Sparse Core Ops, SparseCore 0:
  31.7 64.7 all-gather.3
  98.7 70.6 all-gather.5
  187.4 36.1 all-gather.7
